TPU v7x, 512 devices: a whole 4x4x16 slice. The times are simulated.
512 devices in a mesh: row: 4 (over x), col: 16 (over z_lo, y), layer: 8 (over z_hi, core).
Axes of the slice: x: 4, y: 4, z: 16 (z_hi: 4, z_lo: 4; z = z_hi * 4 + z_lo), core: 2. Of those that a mesh axis runs over, the one named last changes fastest.
Arguments:
- earlier_warming_amount: float32 [32, 512, 2048], P('layer', 'row', 'col'), may hold values from -2 to 2
- conductive_capability: float32 [32, 512, 2048], P('layer', 'row', 'col'), may hold values from 0.5 to 2
- thermal_mass_timewise: float32 [32, 512, 2048], P('layer', 'row', 'col'), may hold values from 0.5 to 2
- toggling_wattage_map: bfloat16 [512, 64, 4096], P(('row', 'col', 'layer')), may hold values from 0.049804688 to 1
- baseline_loss_wattage: bfloat16 [512, 64, 4096], P(('row', 'col', 'layer')), may hold values from 0.049804688 to 1
- receiving_panel: int32 [512, 64, 1], P(('row', 'col', 'layer')), may hold values from 0 to 63; in each aligned block of 64 rows (0 to 63, 64 to 127, ..., all dimensions but the last counted through in order) at most 4 rows name the same one
- subsquare_placement: int32 [512, 64], P(('row', 'col', 'layer')), may hold values from 0 to 3
- holder_chip_module: int32 [512, 64], P(('row', 'col', 'layer')), may hold values from 0 to 15, never falling along the last dimension, each value on 1 to 8 neighbouring positions
- module_tier_order: int32 [512, 16], P(('row', 'col', 'layer')), may hold values from 0 to 3
- warming_sensitivity: float32 [512, 16], P(('row', 'col', 'layer')), may hold values from 0.5 to 2
Outputs:
- new_temperature: float32 [32, 512, 2048], P('layer', 'row', 'col')
- supplied_wattage_density: float32 [32, 512, 2048], P('layer', 'row', 'col')
Inputs may be any that keep to these rules, and one draw needn't show every extreme that they name: `receiving_panel`: the tile is numbered row tile times the number of column tiles plus column tile, inside the owning device's layer group; among the slots of one device at most 4 name the same tile, and exactly 4 do on some device in every draw. `subsquare_placement`: row-major over the tile's patch rows and patch columns. `holder_chip_module`: never falls along a device's slots; every block of a device has 1 to 8 slots.
All inputs are finite; a program needn't handle non-finite values.
Results may differ from a plain program's by a relative error of at most 0.0012.
Values may be sent and summed in bfloat16 or wider, within the bound.
No kernel may reach another device: no remote copies, remote signals or barrier semaphores. Data moves between devices by JAX's collectives and lax.ppermute only.
A program may use at most 64 MiB of HBM per device.

v0:
```python
import math

import jax
import jax.numpy as jnp
from jax import lax
from jax.sharding import PartitionSpec as P

SUBSQUARE_EXTENT = 64
SWEEPS = 3
CAP = 4


eig_low = 0.1
eig_high = 2.0


def copy_for_each(array, axis):
    copies = jnp.broadcast_to(array, (lax.axis_size(axis), *array.shape))
    return lax.all_to_all(copies, axis, split_axis=0, concat_axis=0, tiled=True)


def joined_along(tiles, dim):
    dims = list(tiles.shape[1:])
    dims[dim] *= tiles.shape[0]
    return jnp.moveaxis(tiles, 0, dim).reshape(dims)


def gather_directly(array, axis, dim):
    tiles = copy_for_each(array, axis)
    return joined_along(tiles, dim)


def side_by_side(arrays, axis, split_dim, concat_dim, along):
    widths = [math.prod(a.shape[along:]) for a in arrays]
    both = jnp.concatenate(
        [a.reshape(*a.shape[:along], w) for a, w in zip(arrays, widths)], axis=along
    )
    out = lax.all_to_all(both, axis, split_axis=split_dim, concat_axis=concat_dim, tiled=True)
    tiles = jnp.split(out, [sum(widths[:k]) for k in range(1, len(widths))], axis=along)
    return tuple((b.reshape(*out.shape[:along], *a.shape[along:]) for a, b in zip(arrays, tiles)))


def with_halo(array, sides, width):
    edges = {}
    for axis, dim in sides:
        count, length = (lax.axis_size(axis), array.shape[dim])
        up = [(i, (i + 1) % count) for i in range(count - 1)]
        last = lax.slice_in_dim(array, length - width, length, axis=dim)
        leading = lax.slice_in_dim(array, 0, width, axis=dim)
        edges[dim] = (
            lax.ppermute(last, axis, up),
            lax.ppermute(leading, axis, [(b, a) for a, b in up]),
        )
    done = []
    for _, dim in sides:
        low, high = edges[dim]
        around = [(width, width) if d in done else (0, 0) for d in range(array.ndim)]
        array = jnp.concatenate([jnp.pad(low, around), array, jnp.pad(high, around)], axis=dim)
        done.append(dim)
    return array


def neighbours(padded):
    return [
        padded[2:, 1:-1, 1:-1],
        padded[:-2, 1:-1, 1:-1],
        padded[1:-1, 2:, 1:-1],
        padded[1:-1, :-2, 1:-1],
        padded[1:-1, 1:-1, 2:],
        padded[1:-1, 1:-1, :-2],
    ]


def face_terms(padded_cond):
    center = padded_cond[1:-1, 1:-1, 1:-1]
    return [0.5 * (center + beside) for beside in neighbours(padded_cond)]


def diagonal_of(thermal_mass_timewise, nearby_conductance_factors):
    running = thermal_mass_timewise
    for face_term in nearby_conductance_factors:
        running = running + face_term
    return running


def linear_mapping_result(padded, nearby_conductance_factors, linear_pivot_coefficients):
    result = linear_pivot_coefficients * padded[1:-1, 1:-1, 1:-1]
    for face_term, beside in zip(nearby_conductance_factors, neighbours(padded)):
        result = result - face_term * beside
    return result


def exact_dot(former, latter):
    return jnp.dot(
        former, latter, precision=lax.Precision.HIGHEST, preferred_element_type=jnp.float32
    )


def shards(
    earlier_warming_amount,
    conductive_capability,
    thermal_mass_timewise,
    toggling_wattage_map,
    baseline_loss_wattage,
    receiving_panel,
    subsquare_placement,
    holder_chip_module,
    module_tier_order,
    warming_sensitivity,
):
    tile_total = lax.axis_size(("row", "col"))
    number_sheetwise, number_lengthwise, tier_total_number = earlier_warming_amount.shape
    in_plane = number_lengthwise // SUBSQUARE_EXTENT * (tier_total_number // SUBSQUARE_EXTENT)
    tile_patches = number_sheetwise * in_plane
    target = receiving_panel[0, :, 0]
    tile_hits = (target[:, None] == jnp.arange(tile_total, dtype=jnp.int32)[None, :]).astype(
        jnp.int32
    )
    order_rank = jnp.sum(jnp.cumsum(tile_hits, axis=0) * tile_hits, axis=1) - 1
    slot_place = target * CAP + order_rank
    placing = (
        jnp.arange(tile_total * CAP, dtype=jnp.int32)[:, None] == slot_place[None, :]
    ).astype(jnp.float32)
    placing_half = placing.astype(jnp.bfloat16)
    local_block = holder_chip_module[0]
    block_total = module_tier_order.shape[1]
    block_match = local_block[:, None] == jnp.arange(block_total, dtype=jnp.int32)[None, :]
    member = jnp.transpose(block_match.astype(jnp.float32))
    slot_layer = jnp.sum(jnp.where(block_match, module_tier_order[0][None, :], 0), axis=1)
    position = slot_layer * in_plane + subsquare_placement[0]
    position_buf = exact_dot(placing, (position + 1).astype(jnp.float32)) - 1.0
    tile_means = (
        earlier_warming_amount.reshape(
            number_sheetwise,
            number_lengthwise // SUBSQUARE_EXTENT,
            SUBSQUARE_EXTENT,
            tier_total_number // SUBSQUARE_EXTENT,
            SUBSQUARE_EXTENT,
        )
        .mean(axis=(2, 4))
        .reshape(tile_patches)
    )
    block_sizes = jnp.sum(member, axis=1)
    patch_ids = jnp.arange(tile_patches, dtype=jnp.int32).astype(jnp.float32)
    all_means = gather_directly(tile_means, ("row", "col"), 0)
    block_means = exact_dot(member, all_means[target * tile_patches + position]) / block_sizes
    slot_factor = exact_dot(jnp.exp(warming_sensitivity[0] * block_means), member)
    own_power = (
        toggling_wattage_map[0].astype(jnp.float32)
        + slot_factor[:, None] * baseline_loss_wattage[0].astype(jnp.float32)
    ).astype(jnp.bfloat16)
    power_send = (
        jnp.dot(placing_half, own_power, preferred_element_type=jnp.float32)
        .astype(jnp.bfloat16)
        .reshape(tile_total, CAP, -1)
    )
    place_send = position_buf.astype(jnp.bfloat16).reshape(tile_total, CAP)
    power_recv, place_recv = side_by_side((power_send, place_send), ("row", "col"), 0, 0, 2)
    slot_power = power_recv.reshape(tile_total * CAP, -1)
    selector = (patch_ids[:, None] == place_recv.reshape(-1).astype(jnp.float32)[None, :]).astype(
        jnp.float32
    )
    footprint_wattage = jnp.dot(
        selector.astype(jnp.bfloat16), slot_power, preferred_element_type=jnp.float32
    )
    supplied_wattage_density = (
        footprint_wattage.reshape(
            number_sheetwise,
            number_lengthwise // SUBSQUARE_EXTENT,
            tier_total_number // SUBSQUARE_EXTENT,
            SUBSQUARE_EXTENT,
            SUBSQUARE_EXTENT,
        )
        .transpose(0, 1, 3, 2, 4)
        .reshape(number_sheetwise, number_lengthwise, tier_total_number)
    )
    middle = (eig_low + eig_high) / 2.0
    spread = (eig_high - eig_low) / 2.0
    ratio_sigma = middle / spread
    weight_now = 1.0 / ratio_sigma
    both_sides = with_halo(
        jnp.stack([earlier_warming_amount, conductive_capability]),
        (("row", 2), ("col", 3), ("layer", 1)),
        1,
    )
    nearby_conductance_factors = face_terms(both_sides[1])
    linear_pivot_coefficients = diagonal_of(thermal_mass_timewise, nearby_conductance_factors)
    iterate_guess = earlier_warming_amount
    remaining_imbalance = (
        thermal_mass_timewise * earlier_warming_amount
        + supplied_wattage_density
        - linear_mapping_result(
            both_sides[0], nearby_conductance_factors, linear_pivot_coefficients
        )
    )
    direction = remaining_imbalance / (linear_pivot_coefficients * middle)
    for sweep in range(SWEEPS):
        iterate_guess = iterate_guess + direction
        if sweep < SWEEPS - 1:
            padded_dir = with_halo(direction, (("row", 1), ("col", 2), ("layer", 0)), 1)
            remaining_imbalance = remaining_imbalance - linear_mapping_result(
                padded_dir, nearby_conductance_factors, linear_pivot_coefficients
            )
            weight_new = 1.0 / (2.0 * ratio_sigma - weight_now)
            direction = weight_new * weight_now * direction + 2.0 * weight_new / spread * (
                remaining_imbalance / linear_pivot_coefficients
            )
            weight_now = weight_new
    return (iterate_guess, supplied_wattage_density)


def solution(mesh):
    return jax.shard_map(
        shards,
        mesh=mesh,
        in_specs=(
            P("layer", "row", "col"),
            P("layer", "row", "col"),
            P("layer", "row", "col"),
            P(("row", "col", "layer"), None, None),
            P(("row", "col", "layer"), None, None),
            P(("row", "col", "layer"), None, None),
            P(("row", "col", "layer"), None),
            P(("row", "col", "layer"), None),
            P(("row", "col", "layer"), None),
            P(("row", "col", "layer"), None),
        ),
        out_specs=(P("layer", "row", "col"), P("layer", "row", "col")),
        check_vma=False,
    )
```

profile of v0, /device:TPU:65, one launch (start us, length us, event | category | flops | bytes accessed | tf_op | source)
XLA Modules:
  0.0 174.9 jit_solution(6995854463736808313)
XLA Ops:
  0.7 1.4 reshape.116
  3.1 10.6 %all-to-all-start = ((f32[64,1,16]{2,1,0:T(1,128)}), f32[64,1,16]{2,1,0:T(1,128)S(1)}, u32[]{:S(2)}, u32[]{:S(2)}) async-start(f32[64,1,16]{2,1,0:T(1,128)} %broadcast_in_dim.16), calls=%async_computation | async-start | bytes 65536 | tf_op jit(solution)/shard_map/all_to_all | solution.py:19
  19.4 1.4 all-to-all-done
  23.9 2.2 %reshape.118 = bf16[64,4,4096]{2,1,0:T(4,128)(2,1)} reshape(bf16[256,4096]{1,0:T(8,128)(2,1)S(1)} %convolution_convert_fusion) | data formatting | bytes 4194304 | tf_op jit(solution)/shard_map/reshape | solution.py:155
  26.1 4.0 %pad_maximum_fusion = bf16[64,4,4097]{2,1,0:T(4,128)(2,1)} fusion(bf16[64,4,1]{2,1,0:T(4,128)(2,1)S(1)} %reshape_reshape.5, bf16[64,4,4096]{2,1,0:T(4,128)(2,1)} %reshape.118), kind=kLoop, calls=%fused_computation.4 | loop fusion | flops 4195328 | bytes 4195328 | tf_op jit(solution)/shard_map/concatenate | solution.py:35
  30.1 8.9 %all-to-all-start.1 = ((bf16[64,4,4097]{2,1,0:T(4,128)(2,1)}), bf16[64,4,4097]{2,1,0:T(4,128)(2,1)S(1)}, u32[]{:S(2)}, u32[]{:S(2)}) async-start(bf16[64,4,4097]{2,1,0:T(4,128)(2,1)} %pad_maximum_fusion), calls=%async_computation.1 | async-start | bytes 4325376 | tf_op jit(solution)/shard_map/all_to_all | solution.py:38
  39.0 3.1 %collective-permute-start.2 = (f32[2,4,1,128]{3,2,1,0:T(1,128)S(1)}, f32[2,4,1,128]{3,2,1,0:T(1,128)S(1)}, u32[]{:S(2)}, u32[]{:S(2)}) collective-permute-start(f32[2,4,1,128]{3,2,1,0:T(1,128)S(1)} %get-tuple-element.12), channel_id=1, source_target_pairs={{0,128},{128,256},{256,384},{1,129},{129,257},{257,385},{2,130},{1... | collective-permute-start | bytes 12296 | tf_op jit(solution)/shard_map/ppermute | solution.py:51
  42.2 1.3 collective-permute-start.3
  43.5 10.8 %collective-permute-start = (f32[2,1,128,128]{3,2,1,0:T(8,128)S(1)}, f32[2,1,128,128]{3,2,1,0:T(8,128)S(1)}, u32[]{:S(2)}, u32[]{:S(2)}) collective-permute-start(f32[2,1,128,128]{3,2,1,0:T(8,128)S(1)} %get-tuple-element.14), channel_id=1, source_target_pairs={{0,1},{1,2},{2,3},{3,4},{4,5},{5,6},{6,7},{8,9},{9,10},{10,11},{11... | collective-permute-start | bytes 393224 | tf_op jit(solution)/shard_map/ppermute | solution.py:51
  54.3 1.9 %collective-permute-start.5 = (f32[2,1,128,128]{3,2,1,0:T(8,128)S(1)}, f32[2,1,128,128]{3,2,1,0:T(8,128)S(1)}, u32[]{:S(2)}, u32[]{:S(2)}) collective-permute-start(f32[2,1,128,128]{3,2,1,0:T(8,128)S(1)} %get-tuple-element.15), channel_id=1, source_target_pairs={{1,0},{2,1},{3,2},{4,3},{5,4},{6,5},{7,6},{9,8},{10,9},{11,10},{12... | collective-permute-start | bytes 393224 | tf_op jit(solution)/shard_map/ppermute | solution.py:52
  56.4 3.1 %collective-permute-start.1 = (f32[2,4,128,1]{3,2,1,0:T(8,128)S(1)}, f32[2,4,128,1]{3,2,1,0:T(8,128)S(1)}, u32[]{:S(2)}, u32[]{:S(2)}) collective-permute-start(f32[2,4,128,1]{3,2,1,0:T(8,128)S(1)} %get-tuple-element.16), channel_id=1, source_target_pairs={{0,8},{8,16},{16,24},{24,32},{32,40},{40,48},{48,56},{56,64},{64,7... | collective-permute-start | bytes 12296 | tf_op jit(solution)/shard_map/ppermute | solution.py:51
  59.5 4.3 %collective-permute-start.4 = (f32[2,4,128,1]{3,2,1,0:T(8,128)S(1)}, f32[2,4,128,1]{3,2,1,0:T(8,128)S(1)}, u32[]{:S(2)}, u32[]{:S(2)}) collective-permute-start(f32[2,4,128,1]{3,2,1,0:T(8,128)S(1)} %get-tuple-element.17), channel_id=1, source_target_pairs={{8,0},{16,8},{24,16},{32,24},{40,32},{48,40},{56,48},{64,56},{72,6... | collective-permute-start | bytes 12296 | tf_op jit(solution)/shard_map/ppermute | solution.py:52
  63.9 38.9 %collective-permute-done.1 = f32[2,4,128,1]{3,2,1,0:T(8,128)S(1)} collective-permute-done((f32[2,4,128,1]{3,2,1,0:T(8,128)S(1)}, f32[2,4,128,1]{3,2,1,0:T(8,128)S(1)}, u32[]{:S(2)}, u32[]{:S(2)}) %collective-permute-start.1) | collective-permute-done | bytes 4128 | tf_op jit(solution)/shard_map/ppermute | solution.py:51
  104.7 2.5 %split.9 = bf16[64,4,4096]{2,1,0:T(4,128)(2,1)} slice(bf16[64,4,4097]{2,1,0:T(4,128)(2,1)S(1)} %all-to-all-done.1), slice={[0:64], [0:4], [0:4096]} | slice | bytes 4194304 | tf_op jit(solution)/shard_map/split | solution.py:39
  107.2 2.5 %reshape.119 = bf16[256,4096]{1,0:T(8,128)(2,1)S(1)} reshape(bf16[64,4,4096]{2,1,0:T(4,128)(2,1)} %split.9) | data formatting | bytes 4194304 | tf_op jit(solution)/shard_map/reshape | solution.py:159
  109.8 2.5 %copy.22 = bf16[4096,256]{1,0:T(8,128)(2,1)} copy(bf16[4096,256]{0,1:T(8,128)(2,1)S(1)} %bitcast.86) | data formatting | bytes 4194304 | tf_op jit(solution)/shard_map/dot_general | solution.py:163
  112.3 2.6 %convolution_bitcast_fusion = f32[4,2,64,2,64]{4,0,2,3,1:T(4,128)S(1)} fusion(bf16[64,64,256,1,1]{2,1,0,4,3:T(8,128)(2,1)} %bitcast.85, f32[256]{0:T(256)S(1)} %reshape.123, f32[4,2,2]{0,2,1:T(2,128)S(1)} %add_convert_fusion), kind=kOutput, calls=%fused_computation.16 | convolution fusion | flops 33566720 | bytes 2360384 | tf_op jit(solution)/shard_map/dot_general | solution.py:163
  116.1 1.3 reshape.120
  118.6 2.0 %collective-permute-start.10 = (f32[1,128,128]{2,1,0:T(8,128)S(1)}, f32[1,128,128]{2,1,0:T(8,128)S(1)}, u32[]{:S(2)}, u32[]{:S(2)}) collective-permute-start(f32[1,128,128]{2,1,0:T(8,128)S(1)} %get-tuple-element.24), channel_id=1, source_target_pairs={{1,0},{2,1},{3,2},{4,3},{5,4},{6,5},{7,6},{9,8},{10,9},{11,10},{12... | collective-permute-start | bytes 196616 | tf_op jit(solution)/shard_map/ppermute | solution.py:52
  120.5 11.3 %collective-permute-start.11 = (f32[1,128,128]{2,1,0:T(8,128)S(1)}, f32[1,128,128]{2,1,0:T(8,128)S(1)}, u32[]{:S(2)}, u32[]{:S(2)}) collective-permute-start(f32[1,128,128]{2,1,0:T(8,128)S(1)} %get-tuple-element.25), channel_id=1, source_target_pairs={{0,1},{1,2},{2,3},{3,4},{4,5},{5,6},{6,7},{8,9},{9,10},{10,11},{11... | collective-permute-start | bytes 196616 | tf_op jit(solution)/shard_map/ppermute | solution.py:51
  131.9 3.8 %collective-permute-start.9 = (f32[4,128,1]{2,1,0:T(8,128)S(1)}, f32[4,128,1]{2,1,0:T(8,128)S(1)}, u32[]{:S(2)}, u32[]{:S(2)}) collective-permute-start(f32[4,128,1]{2,1,0:T(8,128)S(1)} %get-tuple-element.26), channel_id=1, source_target_pairs={{8,0},{16,8},{24,16},{32,24},{40,32},{48,40},{56,48},{64,56},{72,6... | collective-permute-start | bytes 6152 | tf_op jit(solution)/shard_map/ppermute | solution.py:52
  135.7 3.1 %collective-permute-start.7 = (f32[4,1,128]{2,1,0:T(1,128)S(1)}, f32[4,1,128]{2,1,0:T(1,128)S(1)}, u32[]{:S(2)}, u32[]{:S(2)}) collective-permute-start(f32[4,1,128]{2,1,0:T(1,128)S(1)} %get-tuple-element.28), channel_id=1, source_target_pairs={{0,128},{128,256},{256,384},{1,129},{129,257},{257,385},{2,130},{1... | collective-permute-start | bytes 6152 | tf_op jit(solution)/shard_map/ppermute | solution.py:51
  138.8 1.9 %collective-permute-start.6 = (f32[4,128,1]{2,1,0:T(8,128)S(1)}, f32[4,128,1]{2,1,0:T(8,128)S(1)}, u32[]{:S(2)}, u32[]{:S(2)}) collective-permute-start(f32[4,128,1]{2,1,0:T(8,128)S(1)} %get-tuple-element.27), channel_id=1, source_target_pairs={{0,8},{8,16},{16,24},{24,32},{32,40},{40,48},{48,56},{56,64},{64,7... | collective-permute-start | bytes 6152 | tf_op jit(solution)/shard_map/ppermute | solution.py:51
  140.8 1.3 collective-permute-start.8
  142.1 5.9 %collective-permute-done.6 = f32[4,128,1]{2,1,0:T(8,128)S(1)} collective-permute-done((f32[4,128,1]{2,1,0:T(8,128)S(1)}, f32[4,128,1]{2,1,0:T(8,128)S(1)}, u32[]{:S(2)}, u32[]{:S(2)}) %collective-permute-start.6) | collective-permute-done | bytes 2080 | tf_op jit(solution)/shard_map/ppermute | solution.py:51
  148.8 1.9 %collective-permute-start.16 = (f32[1,128,128]{2,1,0:T(8,128)S(1)}, f32[1,128,128]{2,1,0:T(8,128)S(1)}, u32[]{:S(2)}, u32[]{:S(2)}) collective-permute-start(f32[1,128,128]{2,1,0:T(8,128)S(1)} %get-tuple-element.18), channel_id=1, source_target_pairs={{1,0},{2,1},{3,2},{4,3},{5,4},{6,5},{7,6},{9,8},{10,9},{11,10},{12... | collective-permute-start | bytes 196616 | tf_op jit(solution)/shard_map/ppermute | solution.py:52
  150.7 7.5 %collective-permute-start.17 = (f32[1,128,128]{2,1,0:T(8,128)S(1)}, f32[1,128,128]{2,1,0:T(8,128)S(1)}, u32[]{:S(2)}, u32[]{:S(2)}) collective-permute-start(f32[1,128,128]{2,1,0:T(8,128)S(1)} %get-tuple-element.19), channel_id=1, source_target_pairs={{0,1},{1,2},{2,3},{3,4},{4,5},{5,6},{6,7},{8,9},{9,10},{10,11},{11... | collective-permute-start | bytes 196616 | tf_op jit(solution)/shard_map/ppermute | solution.py:51
  158.3 2.4 %collective-permute-start.15 = (f32[4,128,1]{2,1,0:T(8,128)S(1)}, f32[4,128,1]{2,1,0:T(8,128)S(1)}, u32[]{:S(2)}, u32[]{:S(2)}) collective-permute-start(f32[4,128,1]{2,1,0:T(8,128)S(1)} %get-tuple-element.20), channel_id=1, source_target_pairs={{8,0},{16,8},{24,16},{32,24},{40,32},{48,40},{56,48},{64,56},{72,6... | collective-permute-start | bytes 6152 | tf_op jit(solution)/shard_map/ppermute | solution.py:52
  160.8 3.2 %collective-permute-start.13 = (f32[4,1,128]{2,1,0:T(1,128)S(1)}, f32[4,1,128]{2,1,0:T(1,128)S(1)}, u32[]{:S(2)}, u32[]{:S(2)}) collective-permute-start(f32[4,1,128]{2,1,0:T(1,128)S(1)} %get-tuple-element.22), channel_id=1, source_target_pairs={{0,128},{128,256},{256,384},{1,129},{129,257},{257,385},{2,130},{1... | collective-permute-start | bytes 6152 | tf_op jit(solution)/shard_map/ppermute | solution.py:51
  164.0 2.8 %collective-permute-start.12 = (f32[4,128,1]{2,1,0:T(8,128)S(1)}, f32[4,128,1]{2,1,0:T(8,128)S(1)}, u32[]{:S(2)}, u32[]{:S(2)}) collective-permute-start(f32[4,128,1]{2,1,0:T(8,128)S(1)} %get-tuple-element.21), channel_id=1, source_target_pairs={{0,8},{8,16},{16,24},{24,32},{32,40},{40,48},{48,56},{56,64},{64,7... | collective-permute-start | bytes 6152 | tf_op jit(solution)/shard_map/ppermute | solution.py:51
  168.2 5.0 %collective-permute-done.12 = f32[4,128,1]{2,1,0:T(8,128)S(1)} collective-permute-done((f32[4,128,1]{2,1,0:T(8,128)S(1)}, f32[4,128,1]{2,1,0:T(8,128)S(1)}, u32[]{:S(2)}, u32[]{:S(2)}) %collective-permute-start.12) | collective-permute-done | bytes 2080 | tf_op jit(solution)/shard_map/ppermute | solution.py:51
  173.3 1.6 fusion.22
  (78 shorter events, 16.4 us)
Async XLA Ops:
  0.6 22.2 %copy-start.8 = (s32[1,64]{1,0:T(1,128)S(1)}, s32[1,64]{1,0:T(1,128)}, u32[]{:S(2)}) copy-start(s32[1,64]{1,0:T(1,128)} %param.17) | copy-start | bytes 772
  0.6 22.2 %copy-start.7 = (f32[1,16]{1,0:T(1,128)S(1)}, f32[1,16]{1,0:T(1,128)}, u32[]{:S(2)}) copy-start(f32[1,16]{1,0:T(1,128)} %param.19) | copy-start | bytes 196
  0.7 22.4 %copy-start.5 = (bf16[1,64,4096]{2,1,0:T(8,128)(2,1)S(1)}, bf16[1,64,4096]{2,1,0:T(8,128)(2,1)}, u32[]{:S(2)}) copy-start(bf16[1,64,4096]{2,1,0:T(8,128)(2,1)} %param.14) | copy-start | bytes 1572868
  0.7 22.4 %copy-start.6 = (bf16[1,64,4096]{2,1,0:T(8,128)(2,1)S(1)}, bf16[1,64,4096]{2,1,0:T(8,128)(2,1)}, u32[]{:S(2)}) copy-start(bf16[1,64,4096]{2,1,0:T(8,128)(2,1)} %param.13) | copy-start | bytes 1572868
  3.1 17.7 %all-to-all-start = ((f32[64,1,16]{2,1,0:T(1,128)}), f32[64,1,16]{2,1,0:T(1,128)S(1)}, u32[]{:S(2)}, u32[]{:S(2)}) async-start(f32[64,1,16]{2,1,0:T(1,128)} %broadcast_in_dim.16), calls=%async_computation | async-start | bytes 65536 | tf_op jit(solution)/shard_map/all_to_all | solution.py:19
  30.1 8.9 %copy-start = (f32[4,128,128]{2,1,0:T(8,128)S(1)}, f32[4,128,128]{2,1,0:T(8,128)}, u32[]{:S(2)}) copy-start(f32[4,128,128]{2,1,0:T(8,128)} %param.10) | copy-start | bytes 786436
  30.1 8.9 %copy-start.2 = (f32[4,128,128]{2,1,0:T(8,128)S(1)}, f32[4,128,128]{2,1,0:T(8,128)}, u32[]{:S(2)}) copy-start(f32[4,128,128]{2,1,0:T(8,128)} %param.11) | copy-start | bytes 786436
  30.1 74.3 %all-to-all-start.1 = ((bf16[64,4,4097]{2,1,0:T(4,128)(2,1)}), bf16[64,4,4097]{2,1,0:T(4,128)(2,1)S(1)}, u32[]{:S(2)}, u32[]{:S(2)}) async-start(bf16[64,4,4097]{2,1,0:T(4,128)(2,1)} %pad_maximum_fusion), calls=%async_computation.1 | async-start | bytes 4325376 | tf_op jit(solution)/shard_map/all_to_all | solution.py:38
  39.0 20.5 %collective-permute-start.2 = (f32[2,4,1,128]{3,2,1,0:T(1,128)S(1)}, f32[2,4,1,128]{3,2,1,0:T(1,128)S(1)}, u32[]{:S(2)}, u32[]{:S(2)}) collective-permute-start(f32[2,4,1,128]{3,2,1,0:T(1,128)S(1)} %get-tuple-element.12), channel_id=1, source_target_pairs={{0,128},{128,256},{256,384},{1,129},{129,257},{257,385},{2,130},{1... | collective-permute-start | bytes 12296 | tf_op jit(solution)/shard_map/ppermute | solution.py:51
  42.2 21.7 %collective-permute-start.3 = (f32[2,4,1,128]{3,2,1,0:T(1,128)S(1)}, f32[2,4,1,128]{3,2,1,0:T(1,128)S(1)}, u32[]{:S(2)}, u32[]{:S(2)}) collective-permute-start(f32[2,4,1,128]{3,2,1,0:T(1,128)S(1)} %get-tuple-element.13), channel_id=1, source_target_pairs={{128,0},{256,128},{384,256},{129,1},{257,129},{385,257},{130,2},{2... | collective-permute-start | bytes 12296 | tf_op jit(solution)/shard_map/ppermute | solution.py:52
  43.5 59.3 %collective-permute-start = (f32[2,1,128,128]{3,2,1,0:T(8,128)S(1)}, f32[2,1,128,128]{3,2,1,0:T(8,128)S(1)}, u32[]{:S(2)}, u32[]{:S(2)}) collective-permute-start(f32[2,1,128,128]{3,2,1,0:T(8,128)S(1)} %get-tuple-element.14), channel_id=1, source_target_pairs={{0,1},{1,2},{2,3},{3,4},{4,5},{5,6},{6,7},{8,9},{9,10},{10,11},{11... | collective-permute-start | bytes 393224 | tf_op jit(solution)/shard_map/ppermute | solution.py:51
  54.3 48.5 %collective-permute-start.5 = (f32[2,1,128,128]{3,2,1,0:T(8,128)S(1)}, f32[2,1,128,128]{3,2,1,0:T(8,128)S(1)}, u32[]{:S(2)}, u32[]{:S(2)}) collective-permute-start(f32[2,1,128,128]{3,2,1,0:T(8,128)S(1)} %get-tuple-element.15), channel_id=1, source_target_pairs={{1,0},{2,1},{3,2},{4,3},{5,4},{6,5},{7,6},{9,8},{10,9},{11,10},{12... | collective-permute-start | bytes 393224 | tf_op jit(solution)/shard_map/ppermute | solution.py:52
  56.4 46.3 %collective-permute-start.1 = (f32[2,4,128,1]{3,2,1,0:T(8,128)S(1)}, f32[2,4,128,1]{3,2,1,0:T(8,128)S(1)}, u32[]{:S(2)}, u32[]{:S(2)}) collective-permute-start(f32[2,4,128,1]{3,2,1,0:T(8,128)S(1)} %get-tuple-element.16), channel_id=1, source_target_pairs={{0,8},{8,16},{16,24},{24,32},{32,40},{40,48},{48,56},{56,64},{64,7... | collective-permute-start | bytes 12296 | tf_op jit(solution)/shard_map/ppermute | solution.py:51
  59.5 43.2 %collective-permute-start.4 = (f32[2,4,128,1]{3,2,1,0:T(8,128)S(1)}, f32[2,4,128,1]{3,2,1,0:T(8,128)S(1)}, u32[]{:S(2)}, u32[]{:S(2)}) collective-permute-start(f32[2,4,128,1]{3,2,1,0:T(8,128)S(1)} %get-tuple-element.17), channel_id=1, source_target_pairs={{8,0},{16,8},{24,16},{32,24},{40,32},{48,40},{56,48},{64,56},{72,6... | collective-permute-start | bytes 12296 | tf_op jit(solution)/shard_map/ppermute | solution.py:52
  112.3 5.2 %copy-start.1 = (f32[6,130,130]{2,1,0:T(8,128)S(1)}, f32[6,130,130]{2,1,0:T(8,128)}, u32[]{:S(2)}) copy-start(f32[6,130,130]{2,1,0:T(8,128)} %get-tuple-element.11) | copy-start | bytes 1216804
  112.3 5.2 %copy-start.3 = (f32[4,128,128]{2,1,0:T(8,128)S(1)}, f32[4,128,128]{2,1,0:T(8,128)}, u32[]{:S(2)}) copy-start(f32[4,128,128]{2,1,0:T(8,128)} %param.12) | copy-start | bytes 786436
  117.5 0.9 copy-start.4
  118.6 29.5 %collective-permute-start.10 = (f32[1,128,128]{2,1,0:T(8,128)S(1)}, f32[1,128,128]{2,1,0:T(8,128)S(1)}, u32[]{:S(2)}, u32[]{:S(2)}) collective-permute-start(f32[1,128,128]{2,1,0:T(8,128)S(1)} %get-tuple-element.24), channel_id=1, source_target_pairs={{1,0},{2,1},{3,2},{4,3},{5,4},{6,5},{7,6},{9,8},{10,9},{11,10},{12... | collective-permute-start | bytes 196616 | tf_op jit(solution)/shard_map/ppermute | solution.py:52
  120.5 27.6 %collective-permute-start.11 = (f32[1,128,128]{2,1,0:T(8,128)S(1)}, f32[1,128,128]{2,1,0:T(8,128)S(1)}, u32[]{:S(2)}, u32[]{:S(2)}) collective-permute-start(f32[1,128,128]{2,1,0:T(8,128)S(1)} %get-tuple-element.25), channel_id=1, source_target_pairs={{0,1},{1,2},{2,3},{3,4},{4,5},{5,6},{6,7},{8,9},{9,10},{10,11},{11... | collective-permute-start | bytes 196616 | tf_op jit(solution)/shard_map/ppermute | solution.py:51
  131.9 8.9 %collective-permute-start.9 = (f32[4,128,1]{2,1,0:T(8,128)S(1)}, f32[4,128,1]{2,1,0:T(8,128)S(1)}, u32[]{:S(2)}, u32[]{:S(2)}) collective-permute-start(f32[4,128,1]{2,1,0:T(8,128)S(1)} %get-tuple-element.26), channel_id=1, source_target_pairs={{8,0},{16,8},{24,16},{32,24},{40,32},{48,40},{56,48},{64,56},{72,6... | collective-permute-start | bytes 6152 | tf_op jit(solution)/shard_map/ppermute | solution.py:52
  135.7 12.4 %collective-permute-start.7 = (f32[4,1,128]{2,1,0:T(1,128)S(1)}, f32[4,1,128]{2,1,0:T(1,128)S(1)}, u32[]{:S(2)}, u32[]{:S(2)}) collective-permute-start(f32[4,1,128]{2,1,0:T(1,128)S(1)} %get-tuple-element.28), channel_id=1, source_target_pairs={{0,128},{128,256},{256,384},{1,129},{129,257},{257,385},{2,130},{1... | collective-permute-start | bytes 6152 | tf_op jit(solution)/shard_map/ppermute | solution.py:51
  138.8 9.2 %collective-permute-start.6 = (f32[4,128,1]{2,1,0:T(8,128)S(1)}, f32[4,128,1]{2,1,0:T(8,128)S(1)}, u32[]{:S(2)}, u32[]{:S(2)}) collective-permute-start(f32[4,128,1]{2,1,0:T(8,128)S(1)} %get-tuple-element.27), channel_id=1, source_target_pairs={{0,8},{8,16},{16,24},{24,32},{32,40},{40,48},{48,56},{56,64},{64,7... | collective-permute-start | bytes 6152 | tf_op jit(solution)/shard_map/ppermute | solution.py:51
  140.8 7.3 %collective-permute-start.8 = (f32[4,1,128]{2,1,0:T(1,128)S(1)}, f32[4,1,128]{2,1,0:T(1,128)S(1)}, u32[]{:S(2)}, u32[]{:S(2)}) collective-permute-start(f32[4,1,128]{2,1,0:T(1,128)S(1)} %get-tuple-element.29), channel_id=1, source_target_pairs={{128,0},{256,128},{384,256},{129,1},{257,129},{385,257},{130,2},{2... | collective-permute-start | bytes 6152 | tf_op jit(solution)/shard_map/ppermute | solution.py:52
  148.8 24.4 %collective-permute-start.16 = (f32[1,128,128]{2,1,0:T(8,128)S(1)}, f32[1,128,128]{2,1,0:T(8,128)S(1)}, u32[]{:S(2)}, u32[]{:S(2)}) collective-permute-start(f32[1,128,128]{2,1,0:T(8,128)S(1)} %get-tuple-element.18), channel_id=1, source_target_pairs={{1,0},{2,1},{3,2},{4,3},{5,4},{6,5},{7,6},{9,8},{10,9},{11,10},{12... | collective-permute-start | bytes 196616 | tf_op jit(solution)/shard_map/ppermute | solution.py:52
  150.7 22.5 %collective-permute-start.17 = (f32[1,128,128]{2,1,0:T(8,128)S(1)}, f32[1,128,128]{2,1,0:T(8,128)S(1)}, u32[]{:S(2)}, u32[]{:S(2)}) collective-permute-start(f32[1,128,128]{2,1,0:T(8,128)S(1)} %get-tuple-element.19), channel_id=1, source_target_pairs={{0,1},{1,2},{2,3},{3,4},{4,5},{5,6},{6,7},{8,9},{9,10},{10,11},{11... | collective-permute-start | bytes 196616 | tf_op jit(solution)/shard_map/ppermute | solution.py:51
  158.3 8.5 %collective-permute-start.15 = (f32[4,128,1]{2,1,0:T(8,128)S(1)}, f32[4,128,1]{2,1,0:T(8,128)S(1)}, u32[]{:S(2)}, u32[]{:S(2)}) collective-permute-start(f32[4,128,1]{2,1,0:T(8,128)S(1)} %get-tuple-element.20), channel_id=1, source_target_pairs={{8,0},{16,8},{24,16},{32,24},{40,32},{48,40},{56,48},{64,56},{72,6... | collective-permute-start | bytes 6152 | tf_op jit(solution)/shard_map/ppermute | solution.py:52
  160.8 12.5 %collective-permute-start.13 = (f32[4,1,128]{2,1,0:T(1,128)S(1)}, f32[4,1,128]{2,1,0:T(1,128)S(1)}, u32[]{:S(2)}, u32[]{:S(2)}) collective-permute-start(f32[4,1,128]{2,1,0:T(1,128)S(1)} %get-tuple-element.22), channel_id=1, source_target_pairs={{0,128},{128,256},{256,384},{1,129},{129,257},{257,385},{2,130},{1... | collective-permute-start | bytes 6152 | tf_op jit(solution)/shard_map/ppermute | solution.py:51
  164.0 9.2 %collective-permute-start.12 = (f32[4,128,1]{2,1,0:T(8,128)S(1)}, f32[4,128,1]{2,1,0:T(8,128)S(1)}, u32[]{:S(2)}, u32[]{:S(2)}) collective-permute-start(f32[4,128,1]{2,1,0:T(8,128)S(1)} %get-tuple-element.21), channel_id=1, source_target_pairs={{0,8},{8,16},{16,24},{24,32},{32,40},{40,48},{48,56},{56,64},{64,7... | collective-permute-start | bytes 6152 | tf_op jit(solution)/shard_map/ppermute | solution.py:51
  166.8 6.4 %collective-permute-start.14 = (f32[4,1,128]{2,1,0:T(1,128)S(1)}, f32[4,1,128]{2,1,0:T(1,128)S(1)}, u32[]{:S(2)}, u32[]{:S(2)}) collective-permute-start(f32[4,1,128]{2,1,0:T(1,128)S(1)} %get-tuple-element.23), channel_id=1, source_target_pairs={{128,0},{256,128},{384,256},{129,1},{257,129},{385,257},{130,2},{2... | collective-permute-start | bytes 6152 | tf_op jit(solution)/shard_map/ppermute | solution.py:52
where the time goes:
time: 176 us; the launch traced here: 175 us
  starting transfers between devices  86.7 us (49%)
  waiting for transfers between devices  51.3 us (29%)
  local copies, waits for them, and re-layouts  17.5 us (10%)
  other arithmetic  13.8 us (8%)
  matrix products  4.46 us (3%)
    ppermute x9, waiting for transfers between devices, with_halo(): lax.ppermute(last, axis, up)  49.9 us
    ppermute x9, starting transfers between devices, with_halo(): lax.ppermute(last, axis, up)  47 us
    ppermute x9, starting transfers between devices, with_halo(): lax.ppermute(leading, axis, [(b, a) for a, b in up])  20.2 us
    all_to_all x1, starting transfers between devices, copy_for_each(): return lax.all_to_all(copies, axis, split_axis=0, concat_axis=0, tiled=True)  10.6 us
    all_to_all x1, starting transfers between devices, side_by_side(): lax.all_to_all(both, axis, split_axis=split_dim, concat_axis=concat_dim,...  8.87 us
    concatenate x1, other arithmetic, side_by_side(): jnp.concatenate([a.reshape(*a.shape[:along], w) for a, w in zip(arrays, w...  4.03 us
  transfers between devices with their start and end apart: 20, of which 4 were waited for; matrix products, arithmetic and copies ran while one was open for 4% of the time, Pallas kernels for 0%

commit v1 on v0

v1 whole, which is shorter than its diff:
```python
import jax
import jax.numpy as jnp
from jax import lax
from jax.experimental import pallas as pl
from jax.experimental.pallas import tpu as pltpu
from jax.sharding import Mesh
from jax.sharding import PartitionSpec as P

SWEEPS = 3
eig_low = 0.1
eig_high = 2.0

LAYER = ("zhi", "core")
COL = ("zlo", "y")
CUBE = ("row", "zlo", "y")
PLANE = ("row", "y")

F32, BF16, I32 = jnp.float32, jnp.bfloat16, jnp.int32


def params(mib):
    return pltpu.CompilerParams(vmem_limit_bytes=mib * 2**20)


def iota(shape, dim):
    return lax.broadcasted_iota(I32, shape, dim)


def as_column(row):
    n = row.shape[1]
    return jnp.sum(jnp.where(iota((n, n), 0) == iota((n, n), 1), row, 0), axis=1, keepdims=True)


def slot_rows(panel, place, holder, tier):
    layer = jnp.sum(jnp.where(iota((16, 64), 0) == holder, as_column(tier), 0), axis=0, keepdims=True)
    pos = layer * 4 + place
    ident = ((panel >> 2) & 3) * 16 + pos
    column = (panel >> 4) * 4 + (panel & 3)
    same = (as_column(column) == column) & (iota((64, 64), 0) < iota((64, 64), 1))
    rank = jnp.sum(same.astype(I32), axis=0, keepdims=True)
    return pos, ident, column * 16 + rank


def message_kernel(temp, panel, place, holder, tier, out):
    _, ident, dest = slot_rows(panel[...], place[...], holder[...], tier[...])
    sums = jnp.sum(temp[...].reshape(8, 64, 128), axis=1)
    lane = iota((8, 128), 1)
    first = jnp.sum(jnp.where(lane < 64, sums, 0.0), axis=1, keepdims=True)
    second = jnp.sum(jnp.where(lane < 64, 0.0, sums), axis=1, keepdims=True)
    at = iota((8, 128), 0) * 2
    means = jnp.where(lane == at, first, jnp.where(lane == at + 1, second, 0.0))
    means = jnp.sum(means, axis=0, keepdims=True) * (1.0 / 4096.0)
    code = (dest * 64 + ident).astype(F32)
    row = jnp.where(iota((1, 128), 1) < 64, means, jnp.concatenate([code, code], axis=1))
    out[...] = jnp.broadcast_to(row, (64, 128))


def placing_kernel(panel, place, holder, tier, placing, columns):
    pos, _, dest = slot_rows(panel[...], place[...], holder[...], tier[...])
    placing[...] = jnp.where(iota((256, 64), 0) == dest, 1.0, 0.0).astype(BF16)
    lane = iota((64, 128), 1)
    columns[...] = jnp.where(
        lane == 0,
        as_column(panel[...]),
        jnp.where(lane == 1, as_column(pos), as_column(holder[...])),
    )


def power_kernel(messages, columns, warming, toggling, baseline, placing, out):
    tile, pos, holder = (columns[:, k : k + 1] for k in range(3))
    pick = jnp.where(iota((64, 64), 1) == tile, 1.0, 0.0)
    means = jnp.dot(pick, messages[...], precision=lax.Precision.HIGHEST, preferred_element_type=F32)
    slot_mean = jnp.sum(jnp.where(iota((64, 128), 1) == pos, means, 0.0), axis=1, keepdims=True)
    member = iota((64, 16), 1) == holder
    total = jnp.sum(jnp.where(member, slot_mean, 0.0), axis=0, keepdims=True)
    count = jnp.sum(jnp.where(member, 1.0, 0.0), axis=0, keepdims=True)
    leak = jnp.exp(warming[...] * (total / count))
    factor = jnp.sum(jnp.where(member, leak, 0.0), axis=1, keepdims=True)
    width = 512
    for k in range(4096 // width):
        at = pl.ds(k * width, width)
        power = toggling[:, at].astype(F32) + factor * baseline[:, at].astype(F32)
        out[:, at] = jnp.dot(placing[...], power.astype(BF16), preferred_element_type=F32).astype(BF16)


def selector_kernel(messages, out):
    mine = lax.axis_index("row") * 4 + lax.axis_index("y")
    plane = lax.axis_index("zlo")
    code = jnp.concatenate(
        [messages[pl.ds(r * 16 + plane * 4, 4), :] for r in range(4)], axis=0
    )
    code = jnp.where(iota((16, 128), 1) < 64, -1.0, code).astype(I32)
    dest, ident = code >> 6, code & 63
    lane = iota((16, 256), 1)
    ids = jnp.zeros((16, 256), I32)
    for r in range(16):
        hit = jnp.sum(jnp.where(dest == mine * 16 + r, ident + 1, 0), axis=1, keepdims=True)
        ids = jnp.where((lane & 15) == r, hit, ids)
    ids = jnp.sum(jnp.where((lane >> 4) == iota((16, 256), 0), ids, 0), axis=0, keepdims=True)
    out[...] = jnp.where(iota((64, 256), 0) + 1 == ids, 1.0, 0.0).astype(BF16)


def combine_kernel(selector, received, out):
    width = 512
    for k in range(4096 // width):
        at = pl.ds(k * width, width)
        out[:, at] = jnp.dot(selector[...], received[:, at], preferred_element_type=F32).astype(BF16)


def unpack_kernel(parts, out, turned):
    for k in range(32):
        at = pl.ds(k * 128, 128)
        whole = parts[0, :, at].astype(F32)
        for z in range(1, 4):
            whole = whole + parts[z, :, at].astype(F32)
        turned[pl.ds(k * 16, 16), :] = whole
    low = iota((32, 128), 1) < 64
    for layer in range(4):
        for r in range(2):
            left = turned[pl.ds(layer * 4 + r * 2, 32, stride=16), :]
            right = turned[pl.ds(layer * 4 + r * 2 + 1, 32, stride=16), :]
            base = layer * 128 + r * 64
            out[pl.ds(base, 32, stride=2), :] = jnp.where(low, left, pltpu.roll(right, 64, 1))
            out[pl.ds(base + 1, 32, stride=2), :] = jnp.where(low, pltpu.roll(left, 64, 1), right)


def call(kernel, shape, args, mib=16, scratch=()):
    return pl.pallas_call(
        kernel,
        out_shape=shape,
        in_specs=[pl.BlockSpec(memory_space=pltpu.VMEM)] * len(args),
        out_specs=jax.tree.map(lambda _: pl.BlockSpec(memory_space=pltpu.VMEM), shape),
        scratch_shapes=list(scratch),
        compiler_params=params(mib),
    )(*args)


def sds(shape, dtype):
    return jax.ShapeDtypeStruct(shape, dtype)


def with_halo(array, sides, width):
    edges = {}
    for axis, dim in sides:
        count, length = (lax.axis_size(axis), array.shape[dim])
        up = [(i, (i + 1) % count) for i in range(count - 1)]
        last = lax.slice_in_dim(array, length - width, length, axis=dim)
        leading = lax.slice_in_dim(array, 0, width, axis=dim)
        edges[dim] = (
            lax.ppermute(last, axis, up),
            lax.ppermute(leading, axis, [(b, a) for a, b in up]),
        )
    done = []
    for _, dim in sides:
        low, high = edges[dim]
        around = [(width, width) if d in done else (0, 0) for d in range(array.ndim)]
        array = jnp.concatenate([jnp.pad(low, around), array, jnp.pad(high, around)], axis=dim)
        done.append(dim)
    return array


def neighbours(padded):
    return [
        padded[2:, 1:-1, 1:-1],
        padded[:-2, 1:-1, 1:-1],
        padded[1:-1, 2:, 1:-1],
        padded[1:-1, :-2, 1:-1],
        padded[1:-1, 1:-1, 2:],
        padded[1:-1, 1:-1, :-2],
    ]


def face_terms(padded_cond):
    center = padded_cond[1:-1, 1:-1, 1:-1]
    return [0.5 * (center + beside) for beside in neighbours(padded_cond)]


def linear_mapping_result(padded, faces, diagonal):
    result = diagonal * padded[1:-1, 1:-1, 1:-1]
    for face_term, beside in zip(faces, neighbours(padded)):
        result = result - face_term * beside
    return result


def shards(temp, cond, mass, toggling, baseline, panel, place, holder, tier, warming):
    panel = panel.reshape(1, 64)
    slots = (panel, place, holder, tier)
    message = call(message_kernel, sds((64, 128), F32), (temp, *slots))
    messages = lax.all_to_all(message.reshape(64, 1, 128), CUBE, split_axis=0, concat_axis=0, tiled=True)
    messages = messages.reshape(64, 128)
    placing, columns = call(placing_kernel, (sds((256, 64), BF16), sds((64, 128), I32)), slots)
    send = call(
        power_kernel,
        sds((256, 4096), BF16),
        (messages, columns, warming, toggling[0], baseline[0], placing),
    )
    received = lax.all_to_all(send.reshape(16, 16, 4096), PLANE, split_axis=0, concat_axis=0, tiled=True)
    selector = call(selector_kernel, sds((64, 256), BF16), (messages,))
    partial = call(combine_kernel, sds((64, 4096), BF16), (selector, received.reshape(256, 4096)))
    parts = lax.all_to_all(partial.reshape(4, 16, 4096), "zlo", split_axis=0, concat_axis=0, tiled=True)
    density = call(
        unpack_kernel, sds((512, 128), F32), (parts,), scratch=[pltpu.VMEM((512, 128), F32)]
    ).reshape(4, 128, 128)

    middle = (eig_low + eig_high) / 2.0
    spread = (eig_high - eig_low) / 2.0
    ratio_sigma = middle / spread
    weight_now = 1.0 / ratio_sigma
    both_sides = with_halo(jnp.stack([temp, cond]), (("row", 2), (COL, 3), (LAYER, 1)), 1)
    faces = face_terms(both_sides[1])
    diagonal = mass
    for face in faces:
        diagonal = diagonal + face
    guess = temp
    imbalance = mass * temp + density - linear_mapping_result(both_sides[0], faces, diagonal)
    direction = imbalance / (diagonal * middle)
    for sweep in range(SWEEPS):
        guess = guess + direction
        if sweep < SWEEPS - 1:
            padded = with_halo(direction, (("row", 1), (COL, 2), (LAYER, 0)), 1)
            imbalance = imbalance - linear_mapping_result(padded, faces, diagonal)
            weight_new = 1.0 / (2.0 * ratio_sigma - weight_now)
            direction = weight_new * weight_now * direction + 2.0 * weight_new / spread * (
                imbalance / diagonal
            )
            weight_now = weight_new
    return guess, density


def solution(mesh):
    fine = Mesh(mesh.devices.reshape(4, 4, 4, 4, 2), ("row", "zlo", "y", "zhi", "core"))
    grid = P(LAYER, "row", COL)
    slot = ("row", "zlo", "y", "zhi", "core")
    return jax.shard_map(
        shards,
        mesh=fine,
        in_specs=(
            grid,
            grid,
            grid,
            P(slot, None, None),
            P(slot, None, None),
            P(slot, None, None),
            P(slot, None),
            P(slot, None),
            P(slot, None),
            P(slot, None),
        ),
        out_specs=(grid, grid),
        check_vma=False,
    )
```

time: 176 us -> 162 us (0.920)
  the two profiles are of different devices: /device:TPU:65 before, /device:TPU:33 now
where the time goes in v1:
time: 162 us; the launch traced here: 161 us
  starting transfers between devices  92.4 us (57%)
  waiting for transfers between devices  47.7 us (29%)
  local copies, waits for them, and re-layouts  10.8 us (7%)
  other arithmetic  4.89 us (3%)
  Pallas kernels  4.51 us (3%)
    ppermute x9, starting transfers between devices, with_halo(): lax.ppermute(last, axis, up)  49.3 us
    all_to_all x1, waiting for transfers between devices, shards(): lax.all_to_all(send.reshape(16, 16, 4096), PLANE, split_axis=0, concat_ax...  25.5 us
    ppermute x9, starting transfers between devices, with_halo(): lax.ppermute(leading, axis, [(b, a) for a, b in up])  23.5 us
    ppermute x9, waiting for transfers between devices, with_halo(): lax.ppermute(last, axis, up)  15.6 us
    all_to_all x1, starting transfers between devices, shards(): lax.all_to_all(message.reshape(64, 1, 128), CUBE, split_axis=0, concat_ax...  11.1 us
    unnamed x32, local copies, waits for them, and re-layouts  10.3 us
    all_to_all x1, waiting for transfers between devices, shards(): lax.all_to_all(message.reshape(64, 1, 128), CUBE, split_axis=0, concat_ax...  5.09 us
    all_to_all x1, starting transfers between devices, shards(): lax.all_to_all(partial.reshape(4, 16, 4096), 'zlo', split_axis=0, concat_...  4.78 us
  transfers between devices with their start and end apart: 21, of which 6 were waited for; matrix products, arithmetic and copies ran while one was open for 1% of the time, Pallas kernels for 0%

profile of v1, /device:TPU:33, one launch (start us, length us, event | category | flops | bytes accessed | tf_op | source)
XLA Modules:
  0.0 161.3 jit_solution(8732111258346950136)
XLA Ops:
  5.0 11.1 %all-to-all-start = ((f32[64,1,128]{2,1,0:T(1,128)}), f32[64,1,128]{2,1,0:T(1,128)S(1)}, u32[]{:S(2)}, u32[]{:S(2)}) async-start(f32[64,1,128]{2,1,0:T(1,128)} %bitcast.2), calls=%async_computation | async-start | bytes 65536 | tf_op jit(solution)/shard_map/all_to_all | solution.py:189
  18.9 5.1 %all-to-all-done = f32[64,1,128]{2,1,0:T(1,128)S(1)} async-done(((f32[64,1,128]{2,1,0:T(1,128)}), f32[64,1,128]{2,1,0:T(1,128)S(1)}, u32[]{:S(2)}, u32[]{:S(2)}) %all-to-all-start) | async-done | bytes 32800 | tf_op jit(solution)/shard_map/all_to_all | solution.py:189
  26.8 1.1 shard_map.116
  27.9 1.3 copy-done.2
  29.3 3.7 %all-to-all-start.1 = ((bf16[16,16,4096]{2,1,0:T(8,128)(2,1)}), bf16[16,16,4096]{2,1,0:T(8,128)(2,1)S(1)}, u32[]{:S(2)}, u32[]{:S(2)}) async-start(bf16[16,16,4096]{2,1,0:T(8,128)(2,1)} %bitcast.22), calls=%async_computation.1 | async-start | bytes 4194304 | tf_op jit(solution)/shard_map/all_to_all | solution.py:197
  33.2 25.5 %all-to-all-done.1 = bf16[16,16,4096]{2,1,0:T(8,128)(2,1)S(1)} async-done(((bf16[16,16,4096]{2,1,0:T(8,128)(2,1)}), bf16[16,16,4096]{2,1,0:T(8,128)(2,1)S(1)}, u32[]{:S(2)}, u32[]{:S(2)}) %all-to-all-start.1) | async-done | bytes 2097184 | tf_op jit(solution)/shard_map/all_to_all | solution.py:197
  58.7 1.3 shard_map.117
  59.9 4.8 %all-to-all-start.2 = ((bf16[4,16,4096]{2,1,0:T(8,128)(2,1)}), bf16[4,16,4096]{2,1,0:T(8,128)(2,1)S(1)}, u32[]{:S(2)}, u32[]{:S(2)}) async-start(bf16[4,16,4096]{2,1,0:T(8,128)(2,1)} %bitcast.8), calls=%async_computation.2 | async-start | bytes 1048576 | tf_op jit(solution)/shard_map/all_to_all | solution.py:200
  64.7 1.6 %collective-permute-start.2 = (f32[2,4,1,128]{3,2,1,0:T(1,128)S(1)}, f32[2,4,1,128]{3,2,1,0:T(1,128)S(1)}, u32[]{:S(2)}, u32[]{:S(2)}) collective-permute-start(f32[2,4,1,128]{3,2,1,0:T(1,128)S(1)} %get-tuple-element.16), channel_id=1, source_target_pairs={{0,128},{128,256},{256,384},{1,129},{129,257},{257,385},{2,130},{1... | collective-permute-start | bytes 12296 | tf_op jit(solution)/shard_map/ppermute | solution.py:150
  66.4 1.3 collective-permute-start.3
  67.7 13.6 %collective-permute-start = (f32[2,1,128,128]{3,2,1,0:T(8,128)S(1)}, f32[2,1,128,128]{3,2,1,0:T(8,128)S(1)}, u32[]{:S(2)}, u32[]{:S(2)}) collective-permute-start(f32[2,1,128,128]{3,2,1,0:T(8,128)S(1)} %get-tuple-element.18), channel_id=1, source_target_pairs={{0,1},{1,2},{2,3},{3,4},{4,5},{5,6},{6,7},{8,9},{9,10},{10,11},{11... | collective-permute-start | bytes 393224 | tf_op jit(solution)/shard_map/ppermute | solution.py:150
  81.3 1.9 %collective-permute-start.5 = (f32[2,1,128,128]{3,2,1,0:T(8,128)S(1)}, f32[2,1,128,128]{3,2,1,0:T(8,128)S(1)}, u32[]{:S(2)}, u32[]{:S(2)}) collective-permute-start(f32[2,1,128,128]{3,2,1,0:T(8,128)S(1)} %get-tuple-element.19), channel_id=1, source_target_pairs={{1,0},{2,1},{3,2},{4,3},{5,4},{6,5},{7,6},{9,8},{10,9},{11,10},{12... | collective-permute-start | bytes 393224 | tf_op jit(solution)/shard_map/ppermute | solution.py:151
  83.5 2.2 %collective-permute-start.1 = (f32[2,4,128,1]{3,2,1,0:T(8,128)S(1)}, f32[2,4,128,1]{3,2,1,0:T(8,128)S(1)}, u32[]{:S(2)}, u32[]{:S(2)}) collective-permute-start(f32[2,4,128,1]{3,2,1,0:T(8,128)S(1)} %get-tuple-element.20), channel_id=1, source_target_pairs={{0,8},{8,16},{16,24},{24,32},{32,40},{40,48},{48,56},{56,64},{64,7... | collective-permute-start | bytes 12296 | tf_op jit(solution)/shard_map/ppermute | solution.py:150
  85.7 5.2 %collective-permute-start.4 = (f32[2,4,128,1]{3,2,1,0:T(8,128)S(1)}, f32[2,4,128,1]{3,2,1,0:T(8,128)S(1)}, u32[]{:S(2)}, u32[]{:S(2)}) collective-permute-start(f32[2,4,128,1]{3,2,1,0:T(8,128)S(1)} %get-tuple-element.21), channel_id=1, source_target_pairs={{8,0},{16,8},{24,16},{32,24},{40,32},{48,40},{56,48},{64,56},{72,6... | collective-permute-start | bytes 12296 | tf_op jit(solution)/shard_map/ppermute | solution.py:151
  90.9 4.6 %collective-permute-done.1 = f32[2,4,128,1]{3,2,1,0:T(8,128)S(1)} collective-permute-done((f32[2,4,128,1]{3,2,1,0:T(8,128)S(1)}, f32[2,4,128,1]{3,2,1,0:T(8,128)S(1)}, u32[]{:S(2)}, u32[]{:S(2)}) %collective-permute-start.1) | collective-permute-done | bytes 4128 | tf_op jit(solution)/shard_map/ppermute | solution.py:150
  95.5 1.5 collective-permute-done.4
  98.8 1.8 %multiply_divide_fusion = (f32[4,128,128]{2,1,0:T(8,128)S(1)}, f32[4,128,128]{2,1,0:T(8,128)S(1)}, f32[4,128,128]{2,1,0:T(8,128)S(1)}, f32[4,128,128]{2,1,0:T(8,...) fusion(f32[4,128,128]{2,1,0:T(8,128)S(1)} %copy-done.15, ...), kind=kLoop, calls=%fused_computation.126 | loop fusion | flops 2359296 | bytes 6553600 | tf_op jit(solution)/shard_map/div | solution.py:216
  100.7 1.9 %collective-permute-start.10 = (f32[1,128,128]{2,1,0:T(8,128)S(1)}, f32[1,128,128]{2,1,0:T(8,128)S(1)}, u32[]{:S(2)}, u32[]{:S(2)}) collective-permute-start(f32[1,128,128]{2,1,0:T(8,128)S(1)} %get-tuple-element.28), channel_id=1, source_target_pairs={{1,0},{2,1},{3,2},{4,3},{5,4},{6,5},{7,6},{9,8},{10,9},{11,10},{12... | collective-permute-start | bytes 196616 | tf_op jit(solution)/shard_map/ppermute | solution.py:151
  102.7 12.0 %collective-permute-start.11 = (f32[1,128,128]{2,1,0:T(8,128)S(1)}, f32[1,128,128]{2,1,0:T(8,128)S(1)}, u32[]{:S(2)}, u32[]{:S(2)}) collective-permute-start(f32[1,128,128]{2,1,0:T(8,128)S(1)} %get-tuple-element.29), channel_id=1, source_target_pairs={{0,1},{1,2},{2,3},{3,4},{4,5},{5,6},{6,7},{8,9},{9,10},{10,11},{11... | collective-permute-start | bytes 196616 | tf_op jit(solution)/shard_map/ppermute | solution.py:150
  114.7 6.2 %collective-permute-start.9 = (f32[4,128,1]{2,1,0:T(8,128)S(1)}, f32[4,128,1]{2,1,0:T(8,128)S(1)}, u32[]{:S(2)}, u32[]{:S(2)}) collective-permute-start(f32[4,128,1]{2,1,0:T(8,128)S(1)} %get-tuple-element.30), channel_id=1, source_target_pairs={{8,0},{16,8},{24,16},{32,24},{40,32},{48,40},{56,48},{64,56},{72,6... | collective-permute-start | bytes 6152 | tf_op jit(solution)/shard_map/ppermute | solution.py:151
  120.9 4.3 %collective-permute-start.7 = (f32[4,1,128]{2,1,0:T(1,128)S(1)}, f32[4,1,128]{2,1,0:T(1,128)S(1)}, u32[]{:S(2)}, u32[]{:S(2)}) collective-permute-start(f32[4,1,128]{2,1,0:T(1,128)S(1)} %get-tuple-element.32), channel_id=1, source_target_pairs={{0,128},{128,256},{256,384},{1,129},{129,257},{257,385},{2,130},{1... | collective-permute-start | bytes 6152 | tf_op jit(solution)/shard_map/ppermute | solution.py:150
  125.2 1.9 %collective-permute-start.6 = (f32[4,128,1]{2,1,0:T(8,128)S(1)}, f32[4,128,1]{2,1,0:T(8,128)S(1)}, u32[]{:S(2)}, u32[]{:S(2)}) collective-permute-start(f32[4,128,1]{2,1,0:T(8,128)S(1)} %get-tuple-element.31), channel_id=1, source_target_pairs={{0,8},{8,16},{16,24},{24,32},{32,40},{40,48},{48,56},{56,64},{64,7... | collective-permute-start | bytes 6152 | tf_op jit(solution)/shard_map/ppermute | solution.py:150
  127.2 1.3 collective-permute-start.8
  128.5 5.9 %collective-permute-done.6 = f32[4,128,1]{2,1,0:T(8,128)S(1)} collective-permute-done((f32[4,128,1]{2,1,0:T(8,128)S(1)}, f32[4,128,1]{2,1,0:T(8,128)S(1)}, u32[]{:S(2)}, u32[]{:S(2)}) %collective-permute-start.6) | collective-permute-done | bytes 2080 | tf_op jit(solution)/shard_map/ppermute | solution.py:150
  135.2 1.9 %collective-permute-start.16 = (f32[1,128,128]{2,1,0:T(8,128)S(1)}, f32[1,128,128]{2,1,0:T(8,128)S(1)}, u32[]{:S(2)}, u32[]{:S(2)}) collective-permute-start(f32[1,128,128]{2,1,0:T(8,128)S(1)} %get-tuple-element.22), channel_id=1, source_target_pairs={{1,0},{2,1},{3,2},{4,3},{5,4},{6,5},{7,6},{9,8},{10,9},{11,10},{12... | collective-permute-start | bytes 196616 | tf_op jit(solution)/shard_map/ppermute | solution.py:151
  137.1 7.5 %collective-permute-start.17 = (f32[1,128,128]{2,1,0:T(8,128)S(1)}, f32[1,128,128]{2,1,0:T(8,128)S(1)}, u32[]{:S(2)}, u32[]{:S(2)}) collective-permute-start(f32[1,128,128]{2,1,0:T(8,128)S(1)} %get-tuple-element.23), channel_id=1, source_target_pairs={{0,1},{1,2},{2,3},{3,4},{4,5},{5,6},{6,7},{8,9},{9,10},{10,11},{11... | collective-permute-start | bytes 196616 | tf_op jit(solution)/shard_map/ppermute | solution.py:150
  144.7 2.4 %collective-permute-start.15 = (f32[4,128,1]{2,1,0:T(8,128)S(1)}, f32[4,128,1]{2,1,0:T(8,128)S(1)}, u32[]{:S(2)}, u32[]{:S(2)}) collective-permute-start(f32[4,128,1]{2,1,0:T(8,128)S(1)} %get-tuple-element.24), channel_id=1, source_target_pairs={{8,0},{16,8},{24,16},{32,24},{40,32},{48,40},{56,48},{64,56},{72,6... | collective-permute-start | bytes 6152 | tf_op jit(solution)/shard_map/ppermute | solution.py:151
  147.2 3.2 %collective-permute-start.13 = (f32[4,1,128]{2,1,0:T(1,128)S(1)}, f32[4,1,128]{2,1,0:T(1,128)S(1)}, u32[]{:S(2)}, u32[]{:S(2)}) collective-permute-start(f32[4,1,128]{2,1,0:T(1,128)S(1)} %get-tuple-element.26), channel_id=1, source_target_pairs={{0,128},{128,256},{256,384},{1,129},{129,257},{257,385},{2,130},{1... | collective-permute-start | bytes 6152 | tf_op jit(solution)/shard_map/ppermute | solution.py:150
  150.4 2.8 %collective-permute-start.12 = (f32[4,128,1]{2,1,0:T(8,128)S(1)}, f32[4,128,1]{2,1,0:T(8,128)S(1)}, u32[]{:S(2)}, u32[]{:S(2)}) collective-permute-start(f32[4,128,1]{2,1,0:T(8,128)S(1)} %get-tuple-element.25), channel_id=1, source_target_pairs={{0,8},{8,16},{16,24},{24,32},{32,40},{40,48},{48,56},{56,64},{64,7... | collective-permute-start | bytes 6152 | tf_op jit(solution)/shard_map/ppermute | solution.py:150
  153.2 1.3 collective-permute-start.14
  154.6 5.0 %collective-permute-done.12 = f32[4,128,1]{2,1,0:T(8,128)S(1)} collective-permute-done((f32[4,128,1]{2,1,0:T(8,128)S(1)}, f32[4,128,1]{2,1,0:T(8,128)S(1)}, u32[]{:S(2)}, u32[]{:S(2)}) %collective-permute-start.12) | collective-permute-done | bytes 2080 | tf_op jit(solution)/shard_map/ppermute | solution.py:150
  159.7 1.6 %fusion.12 = f32[4,128,128]{2,1,0:T(8,128)} fusion(f32[4,128,128]{2,1,0:T(8,128)S(1)} %get-tuple-element.13, f32[4,130,1]{2,1,0:T(8,128)S(1)} %pad.48, f32[4,1,128]{2,1,0:T(1,128)S(1)} %collective-permute-done.14, f32[4,128,128]{2,1,0:T(8,128)S(1)} %multiply_add_fusion, f32[4,1,128]{2,1,0:T(1,128)S(1)} %collective-permute-done.13, ...), kind=kLoop, calls=%fused_computation.34 | loop fusion | flops 5701632 | bytes 3424384 | tf_op jit(solution)/shard_map/add | solution.py:218
  (66 shorter events, 13.0 us)
Async XLA Ops:
  0.6 1.0 copy-start
  1.6 0.7 copy-start.5
  2.2 0.7 copy-start.7
  2.9 0.7 copy-start.9
  5.0 19.0 %all-to-all-start = ((f32[64,1,128]{2,1,0:T(1,128)}), f32[64,1,128]{2,1,0:T(1,128)S(1)}, u32[]{:S(2)}, u32[]{:S(2)}) async-start(f32[64,1,128]{2,1,0:T(1,128)} %bitcast.2), calls=%async_computation | async-start | bytes 65536 | tf_op jit(solution)/shard_map/all_to_all | solution.py:189
  16.1 0.7 copy-start.6
  24.0 1.0 copy-start.3
  25.1 1.0 copy-start.4
  27.9 1.3 copy-start.2
  29.3 29.4 %all-to-all-start.1 = ((bf16[16,16,4096]{2,1,0:T(8,128)(2,1)}), bf16[16,16,4096]{2,1,0:T(8,128)(2,1)S(1)}, u32[]{:S(2)}, u32[]{:S(2)}) async-start(bf16[16,16,4096]{2,1,0:T(8,128)(2,1)} %bitcast.22), calls=%async_computation.1 | async-start | bytes 4194304 | tf_op jit(solution)/shard_map/all_to_all | solution.py:197
  58.7 6.1 %copy-start.1 = (f32[4,128,128]{2,1,0:T(8,128)S(1)}, f32[4,128,128]{2,1,0:T(8,128)}, u32[]{:S(2)}) copy-start(f32[4,128,128]{2,1,0:T(8,128)} %temp.1) | copy-start | bytes 786436
  58.7 6.1 %copy-start.14 = (f32[4,128,128]{2,1,0:T(8,128)S(1)}, f32[4,128,128]{2,1,0:T(8,128)}, u32[]{:S(2)}) copy-start(f32[4,128,128]{2,1,0:T(8,128)} %param.11) | copy-start | bytes 786436
  59.9 37.9 %all-to-all-start.2 = ((bf16[4,16,4096]{2,1,0:T(8,128)(2,1)}), bf16[4,16,4096]{2,1,0:T(8,128)(2,1)S(1)}, u32[]{:S(2)}, u32[]{:S(2)}) async-start(bf16[4,16,4096]{2,1,0:T(8,128)(2,1)} %bitcast.8), calls=%async_computation.2 | async-start | bytes 1048576 | tf_op jit(solution)/shard_map/all_to_all | solution.py:200
  64.7 20.9 %collective-permute-start.2 = (f32[2,4,1,128]{3,2,1,0:T(1,128)S(1)}, f32[2,4,1,128]{3,2,1,0:T(1,128)S(1)}, u32[]{:S(2)}, u32[]{:S(2)}) collective-permute-start(f32[2,4,1,128]{3,2,1,0:T(1,128)S(1)} %get-tuple-element.16), channel_id=1, source_target_pairs={{0,128},{128,256},{256,384},{1,129},{129,257},{257,385},{2,130},{1... | collective-permute-start | bytes 12296 | tf_op jit(solution)/shard_map/ppermute | solution.py:150
  66.4 24.5 %collective-permute-start.3 = (f32[2,4,1,128]{3,2,1,0:T(1,128)S(1)}, f32[2,4,1,128]{3,2,1,0:T(1,128)S(1)}, u32[]{:S(2)}, u32[]{:S(2)}) collective-permute-start(f32[2,4,1,128]{3,2,1,0:T(1,128)S(1)} %get-tuple-element.17), channel_id=1, source_target_pairs={{128,0},{256,128},{384,256},{129,1},{257,129},{385,257},{130,2},{2... | collective-permute-start | bytes 12296 | tf_op jit(solution)/shard_map/ppermute | solution.py:151
  67.7 29.3 %collective-permute-start = (f32[2,1,128,128]{3,2,1,0:T(8,128)S(1)}, f32[2,1,128,128]{3,2,1,0:T(8,128)S(1)}, u32[]{:S(2)}, u32[]{:S(2)}) collective-permute-start(f32[2,1,128,128]{3,2,1,0:T(8,128)S(1)} %get-tuple-element.18), channel_id=1, source_target_pairs={{0,1},{1,2},{2,3},{3,4},{4,5},{5,6},{6,7},{8,9},{9,10},{10,11},{11... | collective-permute-start | bytes 393224 | tf_op jit(solution)/shard_map/ppermute | solution.py:150
  81.3 15.7 %collective-permute-start.5 = (f32[2,1,128,128]{3,2,1,0:T(8,128)S(1)}, f32[2,1,128,128]{3,2,1,0:T(8,128)S(1)}, u32[]{:S(2)}, u32[]{:S(2)}) collective-permute-start(f32[2,1,128,128]{3,2,1,0:T(8,128)S(1)} %get-tuple-element.19), channel_id=1, source_target_pairs={{1,0},{2,1},{3,2},{4,3},{5,4},{6,5},{7,6},{9,8},{10,9},{11,10},{12... | collective-permute-start | bytes 393224 | tf_op jit(solution)/shard_map/ppermute | solution.py:151
  83.5 12.0 %collective-permute-start.1 = (f32[2,4,128,1]{3,2,1,0:T(8,128)S(1)}, f32[2,4,128,1]{3,2,1,0:T(8,128)S(1)}, u32[]{:S(2)}, u32[]{:S(2)}) collective-permute-start(f32[2,4,128,1]{3,2,1,0:T(8,128)S(1)} %get-tuple-element.20), channel_id=1, source_target_pairs={{0,8},{8,16},{16,24},{24,32},{32,40},{40,48},{48,56},{56,64},{64,7... | collective-permute-start | bytes 12296 | tf_op jit(solution)/shard_map/ppermute | solution.py:150
  85.7 11.3 %collective-permute-start.4 = (f32[2,4,128,1]{3,2,1,0:T(8,128)S(1)}, f32[2,4,128,1]{3,2,1,0:T(8,128)S(1)}, u32[]{:S(2)}, u32[]{:S(2)}) collective-permute-start(f32[2,4,128,1]{3,2,1,0:T(8,128)S(1)} %get-tuple-element.21), channel_id=1, source_target_pairs={{8,0},{16,8},{24,16},{32,24},{40,32},{48,40},{56,48},{64,56},{72,6... | collective-permute-start | bytes 12296 | tf_op jit(solution)/shard_map/ppermute | solution.py:151
  97.7 1.1 copy-start.15
  100.7 33.8 %collective-permute-start.10 = (f32[1,128,128]{2,1,0:T(8,128)S(1)}, f32[1,128,128]{2,1,0:T(8,128)S(1)}, u32[]{:S(2)}, u32[]{:S(2)}) collective-permute-start(f32[1,128,128]{2,1,0:T(8,128)S(1)} %get-tuple-element.28), channel_id=1, source_target_pairs={{1,0},{2,1},{3,2},{4,3},{5,4},{6,5},{7,6},{9,8},{10,9},{11,10},{12... | collective-permute-start | bytes 196616 | tf_op jit(solution)/shard_map/ppermute | solution.py:151
  102.7 31.8 %collective-permute-start.11 = (f32[1,128,128]{2,1,0:T(8,128)S(1)}, f32[1,128,128]{2,1,0:T(8,128)S(1)}, u32[]{:S(2)}, u32[]{:S(2)}) collective-permute-start(f32[1,128,128]{2,1,0:T(8,128)S(1)} %get-tuple-element.29), channel_id=1, source_target_pairs={{0,1},{1,2},{2,3},{3,4},{4,5},{5,6},{6,7},{8,9},{9,10},{10,11},{11... | collective-permute-start | bytes 196616 | tf_op jit(solution)/shard_map/ppermute | solution.py:150
  114.7 12.4 %collective-permute-start.9 = (f32[4,128,1]{2,1,0:T(8,128)S(1)}, f32[4,128,1]{2,1,0:T(8,128)S(1)}, u32[]{:S(2)}, u32[]{:S(2)}) collective-permute-start(f32[4,128,1]{2,1,0:T(8,128)S(1)} %get-tuple-element.30), channel_id=1, source_target_pairs={{8,0},{16,8},{24,16},{32,24},{40,32},{48,40},{56,48},{64,56},{72,6... | collective-permute-start | bytes 6152 | tf_op jit(solution)/shard_map/ppermute | solution.py:151
  120.9 13.5 %collective-permute-start.7 = (f32[4,1,128]{2,1,0:T(1,128)S(1)}, f32[4,1,128]{2,1,0:T(1,128)S(1)}, u32[]{:S(2)}, u32[]{:S(2)}) collective-permute-start(f32[4,1,128]{2,1,0:T(1,128)S(1)} %get-tuple-element.32), channel_id=1, source_target_pairs={{0,128},{128,256},{256,384},{1,129},{129,257},{257,385},{2,130},{1... | collective-permute-start | bytes 6152 | tf_op jit(solution)/shard_map/ppermute | solution.py:150
  125.2 9.2 %collective-permute-start.6 = (f32[4,128,1]{2,1,0:T(8,128)S(1)}, f32[4,128,1]{2,1,0:T(8,128)S(1)}, u32[]{:S(2)}, u32[]{:S(2)}) collective-permute-start(f32[4,128,1]{2,1,0:T(8,128)S(1)} %get-tuple-element.31), channel_id=1, source_target_pairs={{0,8},{8,16},{16,24},{24,32},{32,40},{40,48},{48,56},{56,64},{64,7... | collective-permute-start | bytes 6152 | tf_op jit(solution)/shard_map/ppermute | solution.py:150
  127.2 7.3 %collective-permute-start.8 = (f32[4,1,128]{2,1,0:T(1,128)S(1)}, f32[4,1,128]{2,1,0:T(1,128)S(1)}, u32[]{:S(2)}, u32[]{:S(2)}) collective-permute-start(f32[4,1,128]{2,1,0:T(1,128)S(1)} %get-tuple-element.33), channel_id=1, source_target_pairs={{128,0},{256,128},{384,256},{129,1},{257,129},{385,257},{130,2},{2... | collective-permute-start | bytes 6152 | tf_op jit(solution)/shard_map/ppermute | solution.py:151
  135.2 24.5 %collective-permute-start.16 = (f32[1,128,128]{2,1,0:T(8,128)S(1)}, f32[1,128,128]{2,1,0:T(8,128)S(1)}, u32[]{:S(2)}, u32[]{:S(2)}) collective-permute-start(f32[1,128,128]{2,1,0:T(8,128)S(1)} %get-tuple-element.22), channel_id=1, source_target_pairs={{1,0},{2,1},{3,2},{4,3},{5,4},{6,5},{7,6},{9,8},{10,9},{11,10},{12... | collective-permute-start | bytes 196616 | tf_op jit(solution)/shard_map/ppermute | solution.py:151
  137.1 22.5 %collective-permute-start.17 = (f32[1,128,128]{2,1,0:T(8,128)S(1)}, f32[1,128,128]{2,1,0:T(8,128)S(1)}, u32[]{:S(2)}, u32[]{:S(2)}) collective-permute-start(f32[1,128,128]{2,1,0:T(8,128)S(1)} %get-tuple-element.23), channel_id=1, source_target_pairs={{0,1},{1,2},{2,3},{3,4},{4,5},{5,6},{6,7},{8,9},{9,10},{10,11},{11... | collective-permute-start | bytes 196616 | tf_op jit(solution)/shard_map/ppermute | solution.py:150
  144.7 8.5 %collective-permute-start.15 = (f32[4,128,1]{2,1,0:T(8,128)S(1)}, f32[4,128,1]{2,1,0:T(8,128)S(1)}, u32[]{:S(2)}, u32[]{:S(2)}) collective-permute-start(f32[4,128,1]{2,1,0:T(8,128)S(1)} %get-tuple-element.24), channel_id=1, source_target_pairs={{8,0},{16,8},{24,16},{32,24},{40,32},{48,40},{56,48},{64,56},{72,6... | collective-permute-start | bytes 6152 | tf_op jit(solution)/shard_map/ppermute | solution.py:151
  147.2 12.5 %collective-permute-start.13 = (f32[4,1,128]{2,1,0:T(1,128)S(1)}, f32[4,1,128]{2,1,0:T(1,128)S(1)}, u32[]{:S(2)}, u32[]{:S(2)}) collective-permute-start(f32[4,1,128]{2,1,0:T(1,128)S(1)} %get-tuple-element.26), channel_id=1, source_target_pairs={{0,128},{128,256},{256,384},{1,129},{129,257},{257,385},{2,130},{1... | collective-permute-start | bytes 6152 | tf_op jit(solution)/shard_map/ppermute | solution.py:150
  150.4 9.2 %collective-permute-start.12 = (f32[4,128,1]{2,1,0:T(8,128)S(1)}, f32[4,128,1]{2,1,0:T(8,128)S(1)}, u32[]{:S(2)}, u32[]{:S(2)}) collective-permute-start(f32[4,128,1]{2,1,0:T(8,128)S(1)} %get-tuple-element.25), channel_id=1, source_target_pairs={{0,8},{8,16},{16,24},{24,32},{32,40},{40,48},{48,56},{56,64},{64,7... | collective-permute-start | bytes 6152 | tf_op jit(solution)/shard_map/ppermute | solution.py:150
  153.2 6.4 %collective-permute-start.14 = (f32[4,1,128]{2,1,0:T(1,128)S(1)}, f32[4,1,128]{2,1,0:T(1,128)S(1)}, u32[]{:S(2)}, u32[]{:S(2)}) collective-permute-start(f32[4,1,128]{2,1,0:T(1,128)S(1)} %get-tuple-element.27), channel_id=1, source_target_pairs={{128,0},{256,128},{384,256},{129,1},{257,129},{385,257},{130,2},{2... | collective-permute-start | bytes 6152 | tf_op jit(solution)/shard_map/ppermute | solution.py:151
  (5 other events, 3.3 us)

commit v2 on v1

v2 whole, which is shorter than its diff:
```python
import jax
import jax.numpy as jnp
from jax import lax
from jax.experimental import pallas as pl
from jax.experimental.pallas import tpu as pltpu
from jax.sharding import Mesh
from jax.sharding import PartitionSpec as P

eig_low = 0.1
eig_high = 2.0

LAYER = ("zhi", "core")
COL = ("zlo", "y")
CUBE = ("row", "zlo", "y")
PLANE = ("row", "y")

F32, BF16, I32 = jnp.float32, jnp.bfloat16, jnp.int32


def iota(shape, dim):
    return lax.broadcasted_iota(I32, shape, dim)


def as_column(row):
    n = row.shape[1]
    return jnp.sum(jnp.where(iota((n, n), 0) == iota((n, n), 1), row, 0), axis=1, keepdims=True)


def slot_rows(panel, place, holder, tier):
    layer = jnp.sum(jnp.where(iota((16, 64), 0) == holder, as_column(tier), 0), axis=0, keepdims=True)
    pos = layer * 4 + place
    ident = ((panel >> 2) & 3) * 16 + pos
    column = (panel >> 4) * 4 + (panel & 3)
    same = (as_column(column) == column) & (iota((64, 64), 0) < iota((64, 64), 1))
    rank = jnp.sum(same.astype(I32), axis=0, keepdims=True)
    return pos, ident, column * 16 + rank


def message_kernel(temp, panel, place, holder, tier, out, meta, temp_v, panel_v, place_v, holder_v, tier_v, sems):
    pairs = [(panel, panel_v), (place, place_v), (holder, holder_v), (tier, tier_v), (temp, temp_v)]
    copies = [pltpu.make_async_copy(a, b, sems.at[i]) for i, (a, b) in enumerate(pairs)]
    for copy in copies:
        copy.start()
    for copy in copies[:4]:
        copy.wait()
    panel_row, holder_row = panel_v[...], holder_v[...]
    pos, ident, dest = slot_rows(panel_row, place_v[...], holder_row, tier_v[...])
    for k, row in enumerate((panel_row, pos, dest, holder_row)):
        meta[k : k + 1, :] = jnp.concatenate([row, row], axis=1)
    meta[4:8, :] = jnp.zeros((4, 128), I32)
    code = (dest * 64 + ident).astype(F32)
    copies[4].wait()
    sums = jnp.sum(temp_v[...].reshape(8, 64, 128), axis=1)
    lane = iota((8, 128), 1)
    first = jnp.sum(jnp.where(lane < 64, sums, 0.0), axis=1, keepdims=True)
    second = jnp.sum(jnp.where(lane < 64, 0.0, sums), axis=1, keepdims=True)
    at = iota((8, 128), 0) * 2
    means = jnp.where(lane == at, first, jnp.where(lane == at + 1, second, 0.0))
    means = jnp.sum(means, axis=0, keepdims=True) * (1.0 / 4096.0)
    row = jnp.where(iota((1, 128), 1) < 64, means, jnp.concatenate([code, code], axis=1))
    out[...] = jnp.broadcast_to(row, (64, 128))


def placing_kernel(meta, toggling, baseline, warming, placing, columns, toggling_v, baseline_v, warming_v, sems):
    pairs = [(toggling, toggling_v), (baseline, baseline_v), (warming, warming_v)]
    copies = [pltpu.make_async_copy(a, b, sems.at[i]) for i, (a, b) in enumerate(pairs)]
    for copy in copies:
        copy.start()
    panel, pos, dest, holder = (meta[k : k + 1, 0:64] for k in range(4))
    x, y, rank = panel >> 4, panel & 3, dest & 15
    lower, right = (pos >> 1) & 1, pos & 1
    next_x = x + lower * 2 - 1
    next_y = (y + right * 2 + 3) & 3
    inside = (next_x >= 0) & (next_x <= 3)
    targets = (
        dest,
        jnp.where(inside, (next_x * 4 + y) * 16 + rank, -1),
        (x * 4 + next_y) * 16 + rank,
        jnp.where(inside, (next_x * 4 + next_y) * 16 + rank, -1),
    )
    for k, target in enumerate(targets):
        placing[pl.ds(k * 256, 256), :] = jnp.where(iota((256, 64), 0) == target, 1.0, 0.0).astype(BF16)
    lane = iota((64, 128), 1)
    columns[...] = jnp.where(
        lane == 0, as_column(panel), jnp.where(lane == 1, as_column(pos), as_column(holder))
    )
    for copy in copies:
        copy.wait()


def power_kernel(messages, columns, warming, toggling, baseline, placing, out, sent, sems):
    tile, pos, holder = (columns[:, k : k + 1] for k in range(3))
    lower, right = (pos >> 1) & 1, pos & 1
    pick = jnp.where(iota((64, 64), 1) == tile, 1.0, 0.0)
    means = jnp.dot(pick, messages[...], precision=lax.Precision.HIGHEST, preferred_element_type=F32)
    lane = iota((64, 128), 1)
    slot_mean = jnp.sum(jnp.where(lane == pos, means, 0.0), axis=1, keepdims=True)
    member = iota((64, 16), 1) == holder
    total = jnp.sum(jnp.where(member, slot_mean, 0.0), axis=0, keepdims=True)
    count = jnp.sum(jnp.where(member, 1.0, 0.0), axis=0, keepdims=True)
    leak = jnp.exp(warming[...] * (total / count))
    factor = jnp.sum(jnp.where(member, leak, 0.0), axis=1, keepdims=True)

    def place(kind, values):
        at = placing[kind * 256 : (kind + 1) * 256, :]
        return jnp.dot(at, values.astype(BF16), preferred_element_type=F32).astype(BF16)

    copies = []

    def send(start, width):
        at = pl.ds(start, width)
        copy = pltpu.make_async_copy(sent.at[:, at], out.at[:, at], sems.at[len(copies)])
        copy.start()
        copies.append(copy)

    edge = ((lane & 63) >> 1) == right * 31
    sides = jnp.zeros((64, 128), F32)
    width = 512
    for k in range(8):
        at = pl.ds(k * width, width)
        power = (toggling[:, at].astype(F32) + factor * baseline[:, at].astype(F32)).astype(BF16)
        sent[:, at] = place(0, power)
        send(k * width, width)
        power = power.astype(F32)
        for t in range(4):
            piece = power[:, t * 128 : (t + 1) * 128]
            shift = 2 * (4 * k + t)
            kept = jnp.where(edge, piece, 0.0)
            sides = sides + (pltpu.roll(kept, shift, 1) if shift else kept)
            if k == 0 and t == 0:
                top = piece
    rows = jnp.where(lower == 0, top, piece)
    sides = jnp.where(right == 0, sides, pltpu.roll(sides, 66, 1))
    corner = jnp.sum(jnp.where(lane == lower * 64 + right * 63, rows, 0.0), axis=1, keepdims=True)
    quarter = (1 - lower) * 2 + 1 - right
    both = jnp.concatenate([jnp.where(lower == 1, rows, 0.0), jnp.where(lower == 0, rows, 0.0)], axis=1)
    sent[:, 4096:4352] = place(1, both)
    both = jnp.concatenate([jnp.where(right == 1, sides, 0.0), jnp.where(right == 0, sides, 0.0)], axis=1)
    sent[:, 4352:4608] = place(2, both)
    sent[:, 4608:4736] = place(3, jnp.where(lane == quarter, corner, 0.0))
    send(4096, 640)
    for copy in copies:
        copy.wait()


def selector_kernel(messages, out):
    x, y = lax.axis_index("row"), lax.axis_index("y")
    plane = lax.axis_index("zlo")
    code = jnp.concatenate([messages[pl.ds(r * 16 + plane * 4, 4), :] for r in range(4)], axis=0)
    code = jnp.where(iota((16, 128), 1) < 64, -1.0, code).astype(I32)
    dest, ident = code >> 6, code & 63
    lane = iota((16, 256), 1)

    def idents(dx, dy):
        base = ((x + dx) * 4 + ((y + dy + 4) & 3)) * 16
        ids = jnp.zeros((16, 256), I32)
        for r in range(16):
            hit = jnp.sum(jnp.where(dest == base + r, ident + 1, 0), axis=1, keepdims=True)
            ids = jnp.where((lane & 15) == r, hit, ids)
        ids = jnp.sum(jnp.where((lane >> 4) == iota((16, 256), 0), ids, 0), axis=0, keepdims=True) - 1
        turn = jnp.where(y == 0, 1, 0) if dy < 0 else jnp.where(y == 3, -1, 0) if dy > 0 else 0
        return ids, (ids >> 4) + turn, (ids >> 2) & 3, (ids >> 1) & 1, ids & 1

    def put(k, ids, target):
        out[pl.ds(k * 64, 64), :] = jnp.where(
            (iota((64, 256), 0) == target) & (ids >= 0), 1.0, 0.0
        ).astype(BF16)

    ids, *_ = idents(0, 0)
    put(0, ids, ids)
    for k, dx in enumerate((-1, 1)):
        ids, z, layer, _, pc = idents(dx, 0)
        put(1 + k, ids, z * 16 + k * 8 + layer * 2 + pc)
    for k, dy in enumerate((-1, 1)):
        ids, z, layer, pr, _ = idents(0, dy)
        put(3 + k, ids, z * 16 + k * 8 + layer * 2 + pr)
    for k in range(4):
        ids, z, layer, _, _ = idents((k >> 1) * 2 - 1, (k & 1) * 2 - 1)
        put(5 + k, ids, z * 16 + layer)


def combine_kernel(selector, received, out):
    def add(k, start, width):
        return jnp.dot(
            selector[k * 64 : (k + 1) * 64, :],
            received[:, start : start + width],
            preferred_element_type=F32,
        )

    for k in range(8):
        out[:, k * 512 : (k + 1) * 512] = add(0, k * 512, 512)
    out[:, 4096:4224] = add(1, 4096, 128) + add(2, 4224, 128)
    out[:, 4224:4352] = add(3, 4352, 128) + add(4, 4480, 128)
    lane = iota((64, 128), 1)
    corners = jnp.zeros((64, 128), F32)
    for k in range(4):
        corners = jnp.where(lane == k, add(5 + k, 4608, 128), corners)
    out[:, 4352:4480] = corners


def unpack_kernel(whole, density, main, side, up, down, turned):
    for k in range(32):
        turned[k * 16 : (k + 1) * 16, :] = whole[:, k * 128 : (k + 1) * 128]
    low = iota((32, 128), 1) < 64
    lane = iota((64, 128), 1)
    low_row = iota((1, 128), 1) < 64
    lane16, row16 = iota((16, 128), 1), iota((16, 128), 0)
    rows, columns, corners = whole[:, 4096:4224], whole[:, 4224:4352], whole[:, 4352:4480]
    cell = iota((64, 128), 0)
    turn = []
    for c in range(2):
        pick = jnp.where(lane == (cell & 1) * 64 + (cell - (cell & 1)) + c, 1.0, 0.0)
        turn.append(
            lax.dot_general(
                pick, columns, (((1,), (1,)), ((), ())),
                precision=lax.Precision.HIGHEST, preferred_element_type=F32,
            )
        )
    for layer in range(4):
        base = layer * 144
        for r in range(2):
            left = turned[pl.ds(layer * 4 + r * 2, 32, stride=16), :]
            right = turned[pl.ds(layer * 4 + r * 2 + 1, 32, stride=16), :]
            at = base + r * 64
            main[pl.ds(at, 32, stride=2), :] = jnp.where(low, left, pltpu.roll(right, 64, 1))
            main[pl.ds(at + 1, 32, stride=2), :] = jnp.where(low, pltpu.roll(left, 64, 1), right)
            k = layer * 2 + r
            strip = jnp.where(lane == 0, turn[0][:, 8 + k : 9 + k], 0.0)
            strip = jnp.where(lane == 1, turn[1][:, 8 + k : 9 + k], strip)
            strip = jnp.where(lane == 126, turn[0][:, k : k + 1], strip)
            side[at : at + 64, :] = jnp.where(lane == 127, turn[1][:, k : k + 1], strip)
        block = jnp.zeros((16, 128), F32)
        for kind, first_row in ((0, 14), (1, 0)):
            k = kind * 8 + layer * 2
            a, b = rows[k : k + 1, :], rows[k + 1 : k + 2, :]
            first = jnp.where(low_row, a, pltpu.roll(b, 64, 1))
            second = jnp.where(low_row, pltpu.roll(a, 64, 1), b)
            block = jnp.where(row16 == first_row, first, block)
            block = jnp.where(row16 == first_row + 1, second, block)
        main[base + 128 : base + 144, :] = block
        block = jnp.zeros((16, 128), F32)
        for k, (r, at_lane) in enumerate(((15, 127), (15, 0), (0, 127), (0, 0))):
            value = corners[layer : layer + 1, k : k + 1]
            block = jnp.where((row16 == r) & (lane16 == at_lane), value, block)
        side[base + 128 : base + 144, :] = block
        density[layer * 128 : (layer + 1) * 128, :] = main[base : base + 128, :]
    for out, first in ((up, 288), (down, 0)):
        out[0:288, :] = main[first : first + 288, :].astype(BF16)
        second = side[first + 144 : first + 288, :]
        out[288:432, :] = (side[first : first + 144, :] + pltpu.roll(second, 4, 1)).astype(BF16)


def gather_kernel(temp, cond, mass, lo, hi, above, below, out, to_left, to_right, own, sems):
    copies = [pltpu.make_async_copy(a, own.at[i], sems.at[i]) for i, a in enumerate((temp, cond, mass))]
    for copy in copies:
        copy.start()
    over, under = above[...].astype(F32), below[...].astype(F32)
    lane = iota((144, 128), 1)
    left, right = jnp.zeros((144, 128), F32), jnp.zeros((144, 128), F32)
    for copy in copies:
        copy.wait()
    for a in range(3):
        for layer in range(10):
            i = a * 10 + layer
            if layer < 3:
                source = lo[3 * a + layer].astype(F32)
            elif layer < 7:
                source = own[a, layer - 3]
            else:
                source = hi[3 * a + layer - 7].astype(F32)
            piece = jnp.concatenate([source, under[8 * i : 8 * i + 8], over[8 * i : 8 * i + 8]], axis=0)
            out[i] = piece
            base = a * 40 + layer * 4
            here = (lane >= base) & (lane < base + 3)
            left = jnp.where(here, pltpu.roll(piece, base, 1) if base else piece, left)
            right = jnp.where(here, pltpu.roll(piece, base + 3, 1), right)
    to_left[...] = left.astype(BF16)
    to_right[...] = right.astype(BF16)


def turned_by(x, shift, axis):
    return pltpu.roll(x, shift % x.shape[axis], axis)


def around(face_row, face_col, v):
    return (
        face_row * turned_by(v, -1, 0)
        + turned_by(face_row * v, 1, 0)
        + face_col * turned_by(v, -1, 1)
        + turned_by(face_col * v, 1, 1)
    )


def operator_kernel(grids, from_left, from_right, face_layer, face_row, face_col, inverse, residual, wide):
    left, right = from_left[...].astype(F32), from_right[...].astype(F32)
    lane = iota((144, 128), 1)
    for a in range(3):
        for layer in range(10):
            i, base = a * 10 + layer, a * 40 + layer * 4
            high = turned_by(right, -base, 1) if base else right
            side = jnp.where(lane < 3, high, jnp.where(lane >= 125, turned_by(left, 125 - base, 1), 0.0))
            wide[i, :, 0:128] = grids[i]
            wide[i, :, 128:256] = side
    for layer in range(9):
        face_layer[layer] = 0.5 * (wide[10 + layer] + wide[11 + layer])
    for layer in range(1, 9):
        temp, cond, mass = (wide[a * 10 + layer] for a in range(3))
        rows = 0.5 * (cond + turned_by(cond, -1, 0))
        cols = 0.5 * (cond + turned_by(cond, -1, 1))
        face_row[layer - 1] = rows
        face_col[layer - 1] = cols
        after, before = face_layer[layer], face_layer[layer - 1]
        diagonal = mass + after + before + rows + turned_by(rows, 1, 0) + cols + turned_by(cols, 1, 1)
        share = after * wide[layer + 1] + before * wide[layer - 1] + around(rows, cols, temp)
        residual[layer - 1] = mass * temp + (share - diagonal * temp)
        inverse[layer - 1] = jnp.where(mass > 0.0, 1.0 / diagonal, 0.0)


MIDDLE = (eig_low + eig_high) / 2.0
SPREAD = (eig_high - eig_low) / 2.0
W0 = SPREAD / MIDDLE
W1 = 1.0 / (2.0 * MIDDLE / SPREAD - W0)
W2 = 1.0 / (2.0 * MIDDLE / SPREAD - W1)


def sweep_kernel(main, side, lo, hi, grids, face_layer, face_row, face_col, inverse, residual, out, d0, d1, rest):
    lane = iota((144, 128), 1)
    kept = (lane < 2) | (lane >= 126)

    def supplied(i):
        if 3 <= i <= 6:
            at = (i - 3) * 144
            return main[at : at + 144, :], side[at : at + 144, :]
        source, second = (lo, i == 2) if i < 3 else (hi, i == 8)
        at = 144 if second else 0
        beside = source[288:432, :].astype(F32)
        if second:
            beside = turned_by(beside, -4, 1)
        return source[at : at + 144, :].astype(F32), jnp.where(kept, beside, 0.0)

    for i in range(1, 9):
        start = residual[i - 1] + jnp.concatenate(supplied(i), axis=1)
        rest[i - 1] = start
        d0[i - 1] = start * inverse[i - 1] * (1.0 / MIDDLE)

    def share(i, d):
        return (
            face_layer[i] * d[i]
            + face_layer[i - 1] * d[i - 2]
            + around(face_row[i - 1], face_col[i - 1], d[i - 1])
        )

    for i in range(2, 8):
        start = rest[i - 1]
        later = start * (1.0 - 1.0 / MIDDLE) + share(i, d0)
        d1[i - 1] = W1 * W0 * d0[i - 1] + (2.0 * W1 / SPREAD) * (later * inverse[i - 1])
        rest[i - 1] = later - (W1 * W0 / MIDDLE) * start - (2.0 * W1 / SPREAD) * later
    for i in range(3, 7):
        last = rest[i - 1] + share(i, d1)
        step = d0[i - 1] + d1[i - 1] * (1.0 + W2 * W1) + (2.0 * W2 / SPREAD) * (last * inverse[i - 1])
        at = (i - 3) * 128
        out[at : at + 128, :] = grids[i, 0:128, :] + step[0:128, 0:128]


def sds(shape, dtype):
    return jax.ShapeDtypeStruct(shape, dtype)


def call(kernel, shape, args, mib=16, scratch=(), far=(), far_out=False):
    vmem, anywhere = pl.BlockSpec(memory_space=pltpu.VMEM), pl.BlockSpec(memory_space=pl.ANY)
    return pl.pallas_call(
        kernel,
        out_shape=shape,
        in_specs=[anywhere if i in far else vmem for i in range(len(args))],
        out_specs=jax.tree.map(lambda _: anywhere if far_out else vmem, shape),
        scratch_shapes=list(scratch),
        compiler_params=pltpu.CompilerParams(vmem_limit_bytes=mib * 2**20),
    )(*args)


def pairs(axis):
    up = [(i, i + 1) for i in range(lax.axis_size(axis) - 1)]
    return up, [(b, a) for a, b in up]


def exchange(to_next, to_last, axis):
    up, down = pairs(axis)
    return lax.ppermute(to_next, axis, up), lax.ppermute(to_last, axis, down)


def extended_operator(temp, cond, mass):
    grids = (temp, cond, mass)
    lo, hi = exchange(
        jnp.concatenate([g[1:4] for g in grids]).astype(BF16),
        jnp.concatenate([g[0:3] for g in grids]).astype(BF16),
        LAYER,
    )

    def rows(at):
        parts = []
        for a, g in enumerate(grids):
            parts += [lo[3 * a : 3 * a + 3, at], g[:, at].astype(BF16), hi[3 * a : 3 * a + 3, at]]
        return jnp.concatenate(parts).reshape(240, 128)

    above, below = exchange(rows(slice(120, 128)), rows(slice(0, 8)), "row")
    wide, to_left, to_right = call(
        gather_kernel,
        (sds((30, 144, 128), F32), sds((144, 128), BF16), sds((144, 128), BF16)),
        (*grids, lo, hi, above, below),
        mib=24,
        scratch=[pltpu.VMEM((3, 4, 128, 128), F32), pltpu.SemaphoreType.DMA((3,))],
        far=(0, 1, 2),
    )
    from_left, from_right = exchange(to_right, to_left, COL)
    eight = sds((8, 144, 256), F32)
    terms = call(
        operator_kernel,
        (sds((9, 144, 256), F32), eight, eight, eight, eight),
        (wide, from_left, from_right),
        mib=32,
        scratch=[pltpu.VMEM((30, 144, 256), F32)],
    )
    return wide, terms


def shards(temp, cond, mass, toggling, baseline, panel, place, holder, tier, warming):
    row64 = pltpu.VMEM((1, 64), I32)
    message, meta = call(
        message_kernel,
        (sds((64, 128), F32), sds((8, 128), I32)),
        (temp, panel.reshape(1, 64), place, holder, tier),
        scratch=[
            pltpu.VMEM((4, 128, 128), F32), row64, row64, row64,
            pltpu.VMEM((1, 16), I32), pltpu.SemaphoreType.DMA((5,)),
        ],
        far=range(5),
    )
    messages = lax.all_to_all(message.reshape(64, 1, 128), CUBE, split_axis=0, concat_axis=0, tiled=True)
    messages = messages.reshape(64, 128)
    placing, columns, toggling, baseline, warming = call(
        placing_kernel,
        (
            sds((1024, 64), BF16), sds((64, 128), I32),
            sds((64, 4096), BF16), sds((64, 4096), BF16), sds((1, 16), F32),
        ),
        (meta, toggling[0], baseline[0], warming),
        scratch=[pltpu.SemaphoreType.DMA((3,))],
        far=(1, 2, 3),
    )
    send = call(
        power_kernel,
        sds((256, 4736), BF16),
        (messages, columns, warming, toggling, baseline, placing),
        mib=24,
        scratch=[pltpu.VMEM((256, 4736), BF16), pltpu.SemaphoreType.DMA((9,))],
        far_out=True,
    )
    received = lax.all_to_all(send.reshape(16, 16, 4736), PLANE, split_axis=0, concat_axis=0, tiled=True)
    selector = call(selector_kernel, sds((576, 256), BF16), (messages,))
    partial = call(combine_kernel, sds((64, 4480), F32), (selector, received.reshape(256, 4736)))
    parts = lax.all_to_all(
        partial.astype(jnp.float16).reshape(4, 16, 4480), "zlo", split_axis=0, concat_axis=0, tiled=True
    )
    wide, terms = extended_operator(temp, cond, mass)
    block, strip = sds((576, 128), F32), sds((432, 128), BF16)
    density, main, side, up, down = call(
        unpack_kernel,
        (sds((512, 128), F32), block, block, strip, strip),
        (jnp.sum(parts.astype(F32), axis=0),),
        scratch=[pltpu.VMEM((512, 128), F32)],
    )
    lo, hi = exchange(up, down, LAYER)
    eight = pltpu.VMEM((8, 144, 256), F32)
    guess = call(
        sweep_kernel,
        sds((512, 128), F32),
        (main, side, lo, hi, wide, *terms),
        mib=40,
        scratch=[eight, eight, eight],
    )
    return guess.reshape(4, 128, 128), density.reshape(4, 128, 128)


def solution(mesh):
    fine = Mesh(mesh.devices.reshape(4, 4, 4, 4, 2), ("row", "zlo", "y", "zhi", "core"))
    grid = P(LAYER, "row", COL)
    slot = ("row", "zlo", "y", "zhi", "core")
    return jax.shard_map(
        shards,
        mesh=fine,
        in_specs=(
            grid,
            grid,
            grid,
            P(slot, None, None),
            P(slot, None, None),
            P(slot, None, None),
            P(slot, None),
            P(slot, None),
            P(slot, None),
            P(slot, None),
        ),
        out_specs=(grid, grid),
        check_vma=False,
    )
```

time: 162 us -> 120 us (0.74)
  the two profiles are of different devices: /device:TPU:33 before, /device:TPU:1 now
where the time goes in v2:
time: 120 us; the launch traced here: 119 us
  starting transfers between devices  57.4 us (48%)
  waiting for transfers between devices  32.6 us (27%)
  local copies, waits for them, and re-layouts  12.9 us (11%)
  Pallas kernels  12.9 us (11%)
  other arithmetic  2.5 us (2%)
    ppermute x8, starting transfers between devices, exchange(): return (lax.ppermute(to_next, axis, up), lax.ppermute(to_last, axis, down))  37.5 us
    all_to_all x1, waiting for transfers between devices, shards(): lax.all_to_all(send.reshape(16, 16, 4736), PLANE, split_axis=0, concat_ax...  13.6 us
    pallas_call x9, Pallas kernels, call(): pl.pallas_call(kernel, out_shape=shape, in_specs=[anywhere if i in far el...  12.9 us
    all_to_all x1, starting transfers between devices, shards(): lax.all_to_all(message.reshape(64, 1, 128), CUBE, split_axis=0, concat_ax...  12.6 us
    unnamed x36, local copies, waits for them, and re-layouts  12.1 us
    ppermute x8, waiting for transfers between devices, exchange(): return (lax.ppermute(to_next, axis, up), lax.ppermute(to_last, axis, down))  9.27 us
    all_to_all x1, waiting for transfers between devices, shards(): lax.all_to_all(message.reshape(64, 1, 128), CUBE, split_axis=0, concat_ax...  5.73 us
    all_to_all x1, waiting for transfers between devices, shards(): lax.all_to_all(partial.astype(jnp.float16).reshape(4, 16, 4480), 'zlo', s...  3.96 us
  transfers between devices with their start and end apart: 11, of which 5 were waited for; matrix products, arithmetic and copies ran while one was open for 8% of the time, Pallas kernels for 5%

profile of v2, /device:TPU:1, one launch (start us, length us, event | category | flops | bytes accessed | tf_op | source)
XLA Modules:
  0.0 119.2 jit_solution(14382361981805567717)
XLA Ops:
  0.6 0.9 copy-done
  4.2 1.0 shard_map.113
  5.2 12.6 %all-to-all-start = ((f32[64,1,128]{2,1,0:T(1,128)}), f32[64,1,128]{2,1,0:T(1,128)S(1)}, u32[]{:S(2)}, u32[]{:S(2)}) async-start(f32[64,1,128]{2,1,0:T(1,128)} %bitcast.2), calls=%async_computation | async-start | bytes 65536 | tf_op jit(solution)/shard_map/all_to_all | solution.py:438
  17.8 1.0 copy-done.4
  18.8 1.0 copy-done.5
  20.9 5.7 %all-to-all-done = f32[64,1,128]{2,1,0:T(1,128)S(1)} async-done(((f32[64,1,128]{2,1,0:T(1,128)}), f32[64,1,128]{2,1,0:T(1,128)S(1)}, u32[]{:S(2)}, u32[]{:S(2)}) %all-to-all-start) | async-done | bytes 32800 | tf_op jit(solution)/shard_map/all_to_all | solution.py:438
  26.6 2.3 %shard_map.116 = bf16[256,4736]{1,0:T(8,128)(2,1)} custom-call(f32[64,128]{1,0:T(8,128)S(1)} %bitcast.17, s32[64,128]{1,0:T(8,128)S(1)} %get-tuple-element.24.columns, f32[1,16]{1,0:T(1,128)S(1)} %get-tuple-element.25.warming, bf16[64,4096]{1,0:T(8,128)(2,1)S(1)} %get-tuple-element.26.toggling, bf16[64,4096]{1,0:T(8,128)(2,1)S(1)} %get-tuple-element.27.baseline, ...), custom_call_target="tpu_custom_call" | custom-call | tf_op jit(solution)/shard_map/pallas_call | solution.py:371
  28.9 3.9 %all-to-all-start.1 = ((bf16[16,16,4736]{2,1,0:T(8,128)(2,1)}), bf16[16,16,4736]{2,1,0:T(8,128)(2,1)S(1)}, u32[]{:S(2)}, u32[]{:S(2)}) async-start(bf16[16,16,4736]{2,1,0:T(8,128)(2,1)} %bitcast.6), calls=%async_computation.1 | async-start | bytes 4849664 | tf_op jit(solution)/shard_map/all_to_all | solution.py:458
  33.1 0.7 pad_maximum_fusion
  33.8 10.8 %collective-permute-start.2 = (bf16[9,128,128]{2,1,0:T(8,128)(2,1)}, bf16[9,128,128]{2,1,0:T(8,128)(2,1)}, u32[]{:S(2)}, u32[]{:S(2)}) collective-permute-start(bf16[9,128,128]{2,1,0:T(8,128)(2,1)} %pad_maximum_fusion), channel_id=1, source_target_pairs={{0,1},{1,2},{2,3},{3,4},{4,5},{5,6},{6,7},{8,9},{9,10},{10,11},{11... | collective-permute-start | bytes 884744 | tf_op jit(solution)/shard_map/ppermute | solution.py:388
  44.6 0.7 pad_maximum_fusion.1
  45.4 1.9 %collective-permute-start.3 = (bf16[9,128,128]{2,1,0:T(8,128)(2,1)}, bf16[9,128,128]{2,1,0:T(8,128)(2,1)}, u32[]{:S(2)}, u32[]{:S(2)}) collective-permute-start(bf16[9,128,128]{2,1,0:T(8,128)(2,1)} %pad_maximum_fusion.1), channel_id=1, source_target_pairs={{1,0},{2,1},{3,2},{4,3},{5,4},{6,5},{7,6},{9,8},{10,9},{11,10},{12... | collective-permute-start | bytes 884744 | tf_op jit(solution)/shard_map/ppermute | solution.py:388
  47.3 0.7 shard_map.114.selector
  48.0 13.6 %all-to-all-done.1 = bf16[16,16,4736]{2,1,0:T(8,128)(2,1)S(1)} async-done(((bf16[16,16,4736]{2,1,0:T(8,128)(2,1)}), bf16[16,16,4736]{2,1,0:T(8,128)(2,1)S(1)}, u32[]{:S(2)}, u32[]{:S(2)}) %all-to-all-start.1) | async-done | bytes 2424864 | tf_op jit(solution)/shard_map/all_to_all | solution.py:458
  62.2 0.9 convert_element_type.4
  63.1 3.5 %all-to-all-start.2 = ((f16[4,16,4480]{2,1,0:T(8,128)(2,1)}), f16[4,16,4480]{2,1,0:T(8,128)(2,1)S(1)}, u32[]{:S(2)}, u32[]{:S(2)}) async-start(f16[4,16,4480]{2,1,0:T(8,128)(2,1)} %bitcast.8), calls=%async_computation.2 | async-start | bytes 1146880 | tf_op jit(solution)/shard_map/all_to_all | solution.py:461
  67.3 0.7 constant_dynamic-update-slice_fusion.16
  68.7 0.7 constant_dynamic-update-slice_fusion.14
  71.6 0.7 constant_dynamic-update-slice_fusion.10
  72.3 4.0 %all-to-all-done.2 = f16[4,16,4480]{2,1,0:T(8,128)(2,1)S(1)} async-done(((f16[4,16,4480]{2,1,0:T(8,128)(2,1)}), f16[4,16,4480]{2,1,0:T(8,128)(2,1)S(1)}, u32[]{:S(2)}, u32[]{:S(2)}) %all-to-all-start.2) | async-done | bytes 573472 | tf_op jit(solution)/shard_map/all_to_all | solution.py:461
  76.4 1.4 %shard_map.118 = (f32[512,128]{1,0:T(8,128)}, f32[576,128]{1,0:T(8,128)S(1)}, f32[576,128]{1,0:T(8,128)S(1)}, bf16[432,128]{1,0:T(8,128)(2,1)S(1)}, bf16[432,128]{1,0:T(8,128)(2,1)S(1)}) custom-call(f32[16,4480]{1,0:T(8,128)S(1)} %convert_reduce_fusion.whole), custom_call_target="tpu_custom_call" | custom-call | tf_op jit(solution)/shard_map/pallas_call | solution.py:371
  77.8 15.4 %collective-permute-start = (bf16[432,128]{1,0:T(8,128)(2,1)S(1)}, bf16[432,128]{1,0:T(8,128)(2,1)S(1)}, u32[]{:S(2)}, u32[]{:S(2)}) collective-permute-start(bf16[432,128]{1,0:T(8,128)(2,1)S(1)} %get-tuple-element.31), channel_id=1, source_target_pairs={{0,1},{1,2},{2,3},{3,4},{4,5},{5,6},{6,7},{8,9},{9,10},{10,11},{11... | collective-permute-start | bytes 331784 | tf_op jit(solution)/shard_map/ppermute | solution.py:388
  93.2 1.9 %collective-permute-start.1 = (bf16[432,128]{1,0:T(8,128)(2,1)S(1)}, bf16[432,128]{1,0:T(8,128)(2,1)S(1)}, u32[]{:S(2)}, u32[]{:S(2)}) collective-permute-start(bf16[432,128]{1,0:T(8,128)(2,1)S(1)} %get-tuple-element.32), channel_id=1, source_target_pairs={{1,0},{2,1},{3,2},{4,3},{5,4},{6,5},{7,6},{9,8},{10,9},{11,10},{12... | collective-permute-start | bytes 331784 | tf_op jit(solution)/shard_map/ppermute | solution.py:388
  95.8 2.0 %collective-permute-start.4 = (bf16[240,128]{1,0:T(8,128)(2,1)S(1)}, bf16[240,128]{1,0:T(8,128)(2,1)S(1)}, u32[]{:S(2)}, u32[]{:S(2)}) collective-permute-start(bf16[240,128]{1,0:T(8,128)(2,1)S(1)} %bitcast.22), channel_id=1, source_target_pairs={{0,128},{128,256},{256,384},{1,129},{129,257},{257,385},{2,130},{1... | collective-permute-start | bytes 184328 | tf_op jit(solution)/shard_map/ppermute | solution.py:388
  97.9 1.3 %collective-permute-start.5 = (bf16[240,128]{1,0:T(8,128)(2,1)S(1)}, bf16[240,128]{1,0:T(8,128)(2,1)S(1)}, u32[]{:S(2)}, u32[]{:S(2)}) collective-permute-start(bf16[240,128]{1,0:T(8,128)(2,1)S(1)} %bitcast.21), channel_id=1, source_target_pairs={{128,0},{256,128},{384,256},{129,1},{257,129},{385,257},{130,2},{2... | collective-permute-start | bytes 184328 | tf_op jit(solution)/shard_map/ppermute | solution.py:388
  99.2 3.7 %collective-permute-done.5.below = bf16[240,128]{1,0:T(8,128)(2,1)S(1)} collective-permute-done((bf16[240,128]{1,0:T(8,128)(2,1)S(1)}, bf16[240,128]{1,0:T(8,128)(2,1)S(1)}, u32[]{:S(2)}, u32[]{:S(2)}) %collective-permute-start.5) | collective-permute-done | bytes 61472 | tf_op jit(solution)/shard_map/ppermute | solution.py:388
  102.8 1.8 %shard_map.119 = (f32[30,144,128]{2,1,0:T(8,128)S(1)}, bf16[144,128]{1,0:T(8,128)(2,1)S(1)}, bf16[144,128]{1,0:T(8,128)(2,1)S(1)}) custom-call(f32[4,128,128]{2,1,0:T(8,128)S(1)} %copy-done.1, f32[4,128,128]{2,1,0:T(8,128)S(1)} %copy-done.2, f32[4,128,128]{2,1,0:T(8,128)S(1)} %copy-done.3, bf16[9,128,128]{2,1,0:T(8,128)(2,1)} %collective-permute-done.2.lo, ...), custom_call_target="tpu_custom_call" | custom-call | tf_op jit(solution)/shard_map/pallas_call | solution.py:371
  104.6 2.8 %collective-permute-start.6 = (bf16[144,128]{1,0:T(8,128)(2,1)S(1)}, bf16[144,128]{1,0:T(8,128)(2,1)S(1)}, u32[]{:S(2)}, u32[]{:S(2)}) collective-permute-start(bf16[144,128]{1,0:T(8,128)(2,1)S(1)} %get-tuple-element.34), channel_id=1, source_target_pairs={{0,8},{8,16},{16,24},{24,32},{32,40},{40,48},{48,56},{56,64},{64,7... | collective-permute-start | bytes 110600 | tf_op jit(solution)/shard_map/ppermute | solution.py:388
  107.5 1.3 %collective-permute-start.7 = (bf16[144,128]{1,0:T(8,128)(2,1)S(1)}, bf16[144,128]{1,0:T(8,128)(2,1)S(1)}, u32[]{:S(2)}, u32[]{:S(2)}) collective-permute-start(bf16[144,128]{1,0:T(8,128)(2,1)S(1)} %get-tuple-element.35), channel_id=1, source_target_pairs={{8,0},{16,8},{24,16},{32,24},{40,32},{48,40},{56,48},{64,56},{72,6... | collective-permute-start | bytes 110600 | tf_op jit(solution)/shard_map/ppermute | solution.py:388
  108.8 5.6 %collective-permute-done.7.from_right = bf16[144,128]{1,0:T(8,128)(2,1)S(1)} collective-permute-done((bf16[144,128]{1,0:T(8,128)(2,1)S(1)}, bf16[144,128]{1,0:T(8,128)(2,1)S(1)}, u32[]{:S(2)}, u32[]{:S(2)}) %collective-permute-start.7) | collective-permute-done | bytes 36896 | tf_op jit(solution)/shard_map/ppermute | solution.py:388
  114.4 2.8 %shard_map.120 = (f32[9,144,256]{2,1,0:T(8,128)S(1)}, f32[8,144,256]{2,1,0:T(8,128)S(1)}, f32[8,144,256]{2,1,0:T(8,128)S(1)}, f32[8,144,256]{2,1,0:T(8,128)S(1)}, f32[8,144,256]{2,1,0:T(8,128)S(1)}) custom-call(f32[30,144,128]{2,1,0:T(8,128)S(1)} %get-tuple-element.33.grids, bf16[144,128]{1,0:T(8,128)(2,1)S(1)} %collective-permute-done.6.from_left, ...), custom_call_target="tpu_custom_call" | custom-call | tf_op jit(solution)/shard_map/pallas_call | solution.py:371
  117.2 2.0 %shard_map.121 = f32[512,128]{1,0:T(8,128)} custom-call(f32[576,128]{1,0:T(8,128)S(1)} %get-tuple-element.29.main, f32[576,128]{1,0:T(8,128)S(1)} %get-tuple-element.30.side, bf16[432,128]{1,0:T(8,128)(2,1)S(1)} %collective-permute-done.lo, bf16[432,128]{1,0:T(8,128)(2,1)S(1)} %collective-permute-done.1.hi, f32[30,144,128]{2,1,0:T(8,128)S(1)} %get-tuple-element.33.grids, ...), custom_call_target="tpu_custom_call" | custom-call | tf_op jit(solution)/shard_map/pallas_call | solution.py:371
  (45 shorter events, 8.8 us)
Async XLA Ops:
  0.6 1.0 copy-start
  1.6 0.7 copy-start.6
  2.2 0.7 copy-start.7
  2.9 0.7 copy-start.8
  3.6 0.7 copy-start.9
  5.2 21.4 %all-to-all-start = ((f32[64,1,128]{2,1,0:T(1,128)}), f32[64,1,128]{2,1,0:T(1,128)S(1)}, u32[]{:S(2)}, u32[]{:S(2)}) async-start(f32[64,1,128]{2,1,0:T(1,128)} %bitcast.2), calls=%async_computation | async-start | bytes 65536 | tf_op jit(solution)/shard_map/all_to_all | solution.py:438
  17.8 1.0 copy-start.4
  18.8 1.0 copy-start.5
  19.9 0.7 copy-start.10
  28.9 3.9 %copy-start.1 = (f32[4,128,128]{2,1,0:T(8,128)S(1)}, f32[4,128,128]{2,1,0:T(8,128)}, u32[]{:S(2)}) copy-start(f32[4,128,128]{2,1,0:T(8,128)} %temp.3) | copy-start | bytes 786436
  28.9 3.9 %copy-start.2 = (f32[4,128,128]{2,1,0:T(8,128)S(1)}, f32[4,128,128]{2,1,0:T(8,128)}, u32[]{:S(2)}) copy-start(f32[4,128,128]{2,1,0:T(8,128)} %cond.1) | copy-start | bytes 786436
  28.9 4.0 %copy-start.3 = (f32[4,128,128]{2,1,0:T(8,128)S(1)}, f32[4,128,128]{2,1,0:T(8,128)}, u32[]{:S(2)}) copy-start(f32[4,128,128]{2,1,0:T(8,128)} %mass.1) | copy-start | bytes 786436
  28.9 32.7 %all-to-all-start.1 = ((bf16[16,16,4736]{2,1,0:T(8,128)(2,1)}), bf16[16,16,4736]{2,1,0:T(8,128)(2,1)S(1)}, u32[]{:S(2)}, u32[]{:S(2)}) async-start(bf16[16,16,4736]{2,1,0:T(8,128)(2,1)} %bitcast.6), calls=%async_computation.1 | async-start | bytes 4849664 | tf_op jit(solution)/shard_map/all_to_all | solution.py:458
  32.9 0.9 copy-start.11
  32.9 12.4 %copy-start.13 = (bf16[4,128,128]{2,1,0:T(8,128)(2,1)}, bf16[4,128,128]{2,1,0:T(8,128)(2,1)S(1)}, u32[]{:S(2)}) copy-start(bf16[4,128,128]{2,1,0:T(8,128)(2,1)S(1)} %convert.25) | copy-start | bytes 393220
  33.0 12.4 %copy-start.12 = (bf16[4,128,128]{2,1,0:T(8,128)(2,1)}, bf16[4,128,128]{2,1,0:T(8,128)(2,1)S(1)}, u32[]{:S(2)}) copy-start(bf16[4,128,128]{2,1,0:T(8,128)(2,1)S(1)} %convert.26) | copy-start | bytes 393220
  33.8 32.8 %collective-permute-start.2 = (bf16[9,128,128]{2,1,0:T(8,128)(2,1)}, bf16[9,128,128]{2,1,0:T(8,128)(2,1)}, u32[]{:S(2)}, u32[]{:S(2)}) collective-permute-start(bf16[9,128,128]{2,1,0:T(8,128)(2,1)} %pad_maximum_fusion), channel_id=1, source_target_pairs={{0,1},{1,2},{2,3},{3,4},{4,5},{5,6},{6,7},{8,9},{9,10},{10,11},{11... | collective-permute-start | bytes 884744 | tf_op jit(solution)/shard_map/ppermute | solution.py:388
  45.4 22.7 %collective-permute-start.3 = (bf16[9,128,128]{2,1,0:T(8,128)(2,1)}, bf16[9,128,128]{2,1,0:T(8,128)(2,1)}, u32[]{:S(2)}, u32[]{:S(2)}) collective-permute-start(bf16[9,128,128]{2,1,0:T(8,128)(2,1)} %pad_maximum_fusion.1), channel_id=1, source_target_pairs={{1,0},{2,1},{3,2},{4,3},{5,4},{6,5},{7,6},{9,8},{10,9},{11,10},{12... | collective-permute-start | bytes 884744 | tf_op jit(solution)/shard_map/ppermute | solution.py:388
  63.1 13.2 %all-to-all-start.2 = ((f16[4,16,4480]{2,1,0:T(8,128)(2,1)}), f16[4,16,4480]{2,1,0:T(8,128)(2,1)S(1)}, u32[]{:S(2)}, u32[]{:S(2)}) async-start(f16[4,16,4480]{2,1,0:T(8,128)(2,1)} %bitcast.8), calls=%async_computation.2 | async-start | bytes 1146880 | tf_op jit(solution)/shard_map/all_to_all | solution.py:461
  77.8 39.5 %collective-permute-start = (bf16[432,128]{1,0:T(8,128)(2,1)S(1)}, bf16[432,128]{1,0:T(8,128)(2,1)S(1)}, u32[]{:S(2)}, u32[]{:S(2)}) collective-permute-start(bf16[432,128]{1,0:T(8,128)(2,1)S(1)} %get-tuple-element.31), channel_id=1, source_target_pairs={{0,1},{1,2},{2,3},{3,4},{4,5},{5,6},{6,7},{8,9},{9,10},{10,11},{11... | collective-permute-start | bytes 331784 | tf_op jit(solution)/shard_map/ppermute | solution.py:388
  93.2 24.1 %collective-permute-start.1 = (bf16[432,128]{1,0:T(8,128)(2,1)S(1)}, bf16[432,128]{1,0:T(8,128)(2,1)S(1)}, u32[]{:S(2)}, u32[]{:S(2)}) collective-permute-start(bf16[432,128]{1,0:T(8,128)(2,1)S(1)} %get-tuple-element.32), channel_id=1, source_target_pairs={{1,0},{2,1},{3,2},{4,3},{5,4},{6,5},{7,6},{9,8},{10,9},{11,10},{12... | collective-permute-start | bytes 331784 | tf_op jit(solution)/shard_map/ppermute | solution.py:388
  95.8 3.3 %collective-permute-start.4 = (bf16[240,128]{1,0:T(8,128)(2,1)S(1)}, bf16[240,128]{1,0:T(8,128)(2,1)S(1)}, u32[]{:S(2)}, u32[]{:S(2)}) collective-permute-start(bf16[240,128]{1,0:T(8,128)(2,1)S(1)} %bitcast.22), channel_id=1, source_target_pairs={{0,128},{128,256},{256,384},{1,129},{129,257},{257,385},{2,130},{1... | collective-permute-start | bytes 184328 | tf_op jit(solution)/shard_map/ppermute | solution.py:388
  97.9 5.0 %collective-permute-start.5 = (bf16[240,128]{1,0:T(8,128)(2,1)S(1)}, bf16[240,128]{1,0:T(8,128)(2,1)S(1)}, u32[]{:S(2)}, u32[]{:S(2)}) collective-permute-start(bf16[240,128]{1,0:T(8,128)(2,1)S(1)} %bitcast.21), channel_id=1, source_target_pairs={{128,0},{256,128},{384,256},{129,1},{257,129},{385,257},{130,2},{2... | collective-permute-start | bytes 184328 | tf_op jit(solution)/shard_map/ppermute | solution.py:388
  104.6 4.2 %collective-permute-start.6 = (bf16[144,128]{1,0:T(8,128)(2,1)S(1)}, bf16[144,128]{1,0:T(8,128)(2,1)S(1)}, u32[]{:S(2)}, u32[]{:S(2)}) collective-permute-start(bf16[144,128]{1,0:T(8,128)(2,1)S(1)} %get-tuple-element.34), channel_id=1, source_target_pairs={{0,8},{8,16},{16,24},{24,32},{32,40},{40,48},{48,56},{56,64},{64,7... | collective-permute-start | bytes 110600 | tf_op jit(solution)/shard_map/ppermute | solution.py:388
  107.5 6.9 %collective-permute-start.7 = (bf16[144,128]{1,0:T(8,128)(2,1)S(1)}, bf16[144,128]{1,0:T(8,128)(2,1)S(1)}, u32[]{:S(2)}, u32[]{:S(2)}) collective-permute-start(bf16[144,128]{1,0:T(8,128)(2,1)S(1)} %get-tuple-element.35), channel_id=1, source_target_pairs={{8,0},{16,8},{24,16},{32,24},{40,32},{48,40},{56,48},{64,56},{72,6... | collective-permute-start | bytes 110600 | tf_op jit(solution)/shard_map/ppermute | solution.py:388

commit v3 on v2

--- a/solution.py
+++ b/solution.py
@@ -179,7 +179,7 @@
         put(5 + k, ids, z * 16 + layer)
 
 
-def combine_kernel(selector, received, out):
+def combine_kernel(selector, received, _left, _right, out):
     def add(k, start, width):
         return jnp.dot(
             selector[k * 64 : (k + 1) * 64, :],
@@ -250,15 +250,36 @@
         out[288:432, :] = (side[first : first + 144, :] + pltpu.roll(second, 4, 1)).astype(BF16)
 
 
-def gather_kernel(temp, cond, mass, lo, hi, above, below, out, to_left, to_right, own, sems):
+def layers_kernel(temp, cond, mass, own, up, down, sems):
     copies = [pltpu.make_async_copy(a, own.at[i], sems.at[i]) for i, a in enumerate((temp, cond, mass))]
     for copy in copies:
         copy.start()
+    for a, copy in enumerate(copies):
+        copy.wait()
+        for k in range(3):
+            up[3 * a + k] = own[a, 1 + k].astype(BF16)
+            down[3 * a + k] = own[a, k].astype(BF16)
+
+
+def rows_kernel(own, lo, hi, last, first):
+    lasts, firsts = [], []
+    for a in range(3):
+        for layer in range(10):
+            if 3 <= layer < 7:
+                lasts.append(own[a, layer - 3, 120:128, :])
+                firsts.append(own[a, layer - 3, 0:8, :])
+            else:
+                source, k = (lo, 3 * a + layer) if layer < 3 else (hi, 3 * a + layer - 7)
+                lasts.append(source[k, 112:128, :].astype(F32)[8:16])
+                firsts.append(source[k, 0:16, :].astype(F32)[0:8])
+    last[...] = jnp.concatenate(lasts, axis=0).astype(BF16)
+    first[...] = jnp.concatenate(firsts, axis=0).astype(BF16)
+
+
+def gather_kernel(own, lo, hi, above, below, out, to_left, to_right):
     over, under = above[...].astype(F32), below[...].astype(F32)
     lane = iota((144, 128), 1)
     left, right = jnp.zeros((144, 128), F32), jnp.zeros((144, 128), F32)
-    for copy in copies:
-        copy.wait()
     for a in range(3):
         for layer in range(10):
             i = a * 10 + layer
@@ -367,7 +388,7 @@
 
 
 def call(kernel, shape, args, mib=16, scratch=(), far=(), far_out=False):
-    vmem, anywhere = pl.BlockSpec(memory_space=pltpu.VMEM), pl.BlockSpec(memory_space=pl.ANY)
+    vmem, anywhere = pl.BlockSpec(memory_space=pltpu.VMEM), pl.BlockSpec(memory_space=pltpu.HBM)
     return pl.pallas_call(
         kernel,
         out_shape=shape,
@@ -388,39 +409,32 @@
     return lax.ppermute(to_next, axis, up), lax.ppermute(to_last, axis, down)
 
 
-def extended_operator(temp, cond, mass):
-    grids = (temp, cond, mass)
-    lo, hi = exchange(
-        jnp.concatenate([g[1:4] for g in grids]).astype(BF16),
-        jnp.concatenate([g[0:3] for g in grids]).astype(BF16),
-        LAYER,
-    )
-
-    def rows(at):
-        parts = []
-        for a, g in enumerate(grids):
-            parts += [lo[3 * a : 3 * a + 3, at], g[:, at].astype(BF16), hi[3 * a : 3 * a + 3, at]]
-        return jnp.concatenate(parts).reshape(240, 128)
-
-    above, below = exchange(rows(slice(120, 128)), rows(slice(0, 8)), "row")
+def extended_grids(temp, cond, mass):
+    nine, rows, edge = sds((9, 128, 128), BF16), sds((240, 128), BF16), sds((144, 128), BF16)
+    own, up, down = call(
+        layers_kernel,
+        (sds((3, 4, 128, 128), F32), nine, nine),
+        (temp, cond, mass),
+        scratch=[pltpu.SemaphoreType.DMA((3,))],
+        far=range(3),
+    )
+    lo, hi = exchange(up, down, LAYER)
+    above, below = exchange(*call(rows_kernel, (rows, rows), (own, lo, hi)), "row")
     wide, to_left, to_right = call(
-        gather_kernel,
-        (sds((30, 144, 128), F32), sds((144, 128), BF16), sds((144, 128), BF16)),
-        (*grids, lo, hi, above, below),
-        mib=24,
-        scratch=[pltpu.VMEM((3, 4, 128, 128), F32), pltpu.SemaphoreType.DMA((3,))],
-        far=(0, 1, 2),
-    )
-    from_left, from_right = exchange(to_right, to_left, COL)
+        gather_kernel, (sds((30, 144, 128), F32), edge, edge), (own, lo, hi, above, below), mib=24
+    )
+    return wide, exchange(to_right, to_left, COL)
+
+
+def operator(wide, from_left, from_right):
     eight = sds((8, 144, 256), F32)
-    terms = call(
+    return call(
         operator_kernel,
         (sds((9, 144, 256), F32), eight, eight, eight, eight),
         (wide, from_left, from_right),
         mib=32,
         scratch=[pltpu.VMEM((30, 144, 256), F32)],
     )
-    return wide, terms
 
 
 def shards(temp, cond, mass, toggling, baseline, panel, place, holder, tier, warming):
@@ -429,6 +443,7 @@
         message_kernel,
         (sds((64, 128), F32), sds((8, 128), I32)),
         (temp, panel.reshape(1, 64), place, holder, tier),
+        mib=60,
         scratch=[
             pltpu.VMEM((4, 128, 128), F32), row64, row64, row64,
             pltpu.VMEM((1, 16), I32), pltpu.SemaphoreType.DMA((5,)),
@@ -457,11 +472,14 @@
     )
     received = lax.all_to_all(send.reshape(16, 16, 4736), PLANE, split_axis=0, concat_axis=0, tiled=True)
     selector = call(selector_kernel, sds((576, 256), BF16), (messages,))
-    partial = call(combine_kernel, sds((64, 4480), F32), (selector, received.reshape(256, 4736)))
+    wide, beside = extended_grids(temp, cond, mass)
+    partial = call(
+        combine_kernel, sds((64, 4480), F32), (selector, received.reshape(256, 4736), *beside)
+    )
     parts = lax.all_to_all(
         partial.astype(jnp.float16).reshape(4, 16, 4480), "zlo", split_axis=0, concat_axis=0, tiled=True
     )
-    wide, terms = extended_operator(temp, cond, mass)
+    terms = operator(wide, *beside)
     block, strip = sds((576, 128), F32), sds((432, 128), BF16)
     density, main, side, up, down = call(
         unpack_kernel,

time: 120 us -> 122 us (1.017)
  blocking collectives: 0 us -> 12.2 us
  local copies, waits for them, and re-layouts: 12.9 us -> 4.81 us
  waiting for transfers between devices: 32.6 us -> 39.7 us
  starting transfers between devices: 57.4 us -> 50.5 us
  other arithmetic: 2.5 us -> 0.14 us
    ppermute x8, waiting for transfers between devices: 9.27 us -> 34.7 us  [exchange(): return (lax.ppermute(to_next, axis, up), lax.ppermute(to_last, axis, down))]
    all_to_all x1, waiting for transfers between devices: 13.6 us -> 0.01 us  [shards(): lax.all_to_all(send.reshape(16, 16, 4736), PLANE, split_axis=0, concat_ax...]
    all_to_all x0 -> x1, blocking collectives: none -> 12.2 us  [shards(): lax.all_to_all(partial.astype(jnp.float16).reshape(4, 16, 4480), 'zlo', s...]
    unnamed x36 -> x18, local copies, waits for them, and re-layouts: 12.1 us -> 4.81 us
    all_to_all x1 -> x0, waiting for transfers between devices: 3.96 us -> none  [shards(): lax.all_to_all(partial.astype(jnp.float16).reshape(4, 16, 4480), 'zlo', s...]
    all_to_all x1 -> x0, starting transfers between devices: 3.47 us -> none  [shards(): lax.all_to_all(partial.astype(jnp.float16).reshape(4, 16, 4480), 'zlo', s...]
    ppermute x8, starting transfers between devices: 37.5 us -> 34.1 us  [exchange(): return (lax.ppermute(to_next, axis, up), lax.ppermute(to_last, axis, down))]
    concatenate x2 -> x0, other arithmetic: 1.49 us -> none  [the longest x1 0.74 us: extended_operator(): jnp.concatenate([g[0:3] for g in grids]).astype(BF16)]
  transfers between devices with their start and end apart: 11 -> 10, of which waited for: 5 -> 6; matrix products, arithmetic and copies ran while one was open for 8% -> 0% of each run, Pallas kernels for 5% -> 4%
where the time goes in v3:
time: 122 us; the launch traced here: 121 us
  starting transfers between devices  50.5 us (41%)
  waiting for transfers between devices  39.7 us (33%)
  Pallas kernels  13 us (11%)
  blocking collectives  12.2 us (10%)
  local copies, waits for them, and re-layouts  4.81 us (4%)
    ppermute x8, waiting for transfers between devices, exchange(): return (lax.ppermute(to_next, axis, up), lax.ppermute(to_last, axis, down))  34.7 us
    ppermute x8, starting transfers between devices, exchange(): return (lax.ppermute(to_next, axis, up), lax.ppermute(to_last, axis, down))  34.1 us
    pallas_call x11, Pallas kernels, call(): pl.pallas_call(kernel, out_shape=shape, in_specs=[anywhere if i in far el...  13 us
    all_to_all x1, starting transfers between devices, shards(): lax.all_to_all(message.reshape(64, 1, 128), CUBE, split_axis=0, concat_ax...  12.6 us
    all_to_all x1, blocking collectives, shards(): lax.all_to_all(partial.astype(jnp.float16).reshape(4, 16, 4480), 'zlo', s...  12.2 us
    all_to_all x1, waiting for transfers between devices, shards(): lax.all_to_all(message.reshape(64, 1, 128), CUBE, split_axis=0, concat_ax...  5.04 us
    unnamed x18, local copies, waits for them, and re-layouts  4.81 us
    all_to_all x1, starting transfers between devices, shards(): lax.all_to_all(send.reshape(16, 16, 4736), PLANE, split_axis=0, concat_ax...  3.87 us
  transfers between devices with their start and end apart: 10, of which 6 were waited for; matrix products, arithmetic and copies ran while one was open for 0% of the time, Pallas kernels for 4%

profile of v3, /device:TPU:1, one launch (start us, length us, event | category | flops | bytes accessed | tf_op | source)
XLA Modules:
  0.0 121.2 jit_solution(9109340789745018371)
XLA Ops:
  0.6 1.8 %shard_map.113 = (f32[64,128]{1,0:T(8,128)}, s32[8,128]{1,0:T(8,128)}) custom-call(f32[4,128,128]{2,1,0:T(8,128)} %temp.3, s32[1,64]{1,0:T(1,128)} %bitcast.20, s32[1,64]{1,0:T(1,128)} %place.1, s32[1,64]{1,0:T(1,128)} %holder.1, s32[1,16]{1,0:T(1,128)} %tier.1), custom_call_target="tpu_custom_call" | custom-call | tf_op jit(solution)/shard_map/pallas_call | solution.py:392
  2.4 12.6 %all-to-all-start = ((f32[64,1,128]{2,1,0:T(1,128)}), f32[64,1,128]{2,1,0:T(1,128)S(1)}, u32[]{:S(2)}, u32[]{:S(2)}) async-start(f32[64,1,128]{2,1,0:T(1,128)} %bitcast.19), calls=%async_computation | async-start | bytes 65536 | tf_op jit(solution)/shard_map/all_to_all | solution.py:453
  15.0 1.0 copy-done.3
  16.0 1.0 copy-done.4
  17.1 0.7 copy-done.7
  17.8 0.7 copy-done.8
  18.4 0.3 shard_map.115
  18.8 5.0 %all-to-all-done = f32[64,1,128]{2,1,0:T(1,128)S(1)} async-done(((f32[64,1,128]{2,1,0:T(1,128)}), f32[64,1,128]{2,1,0:T(1,128)S(1)}, u32[]{:S(2)}, u32[]{:S(2)}) %all-to-all-start) | async-done | bytes 32800 | tf_op jit(solution)/shard_map/all_to_all | solution.py:453
  23.8 2.3 %shard_map.116 = bf16[256,4736]{1,0:T(8,128)(2,1)} custom-call(f32[64,128]{1,0:T(8,128)S(1)} %bitcast.15, s32[64,128]{1,0:T(8,128)S(1)} %get-tuple-element.29.columns, f32[1,16]{1,0:T(1,128)S(1)} %get-tuple-element.30.warming, bf16[64,4096]{1,0:T(8,128)(2,1)S(1)} %get-tuple-element.31.toggling, bf16[64,4096]{1,0:T(8,128)(2,1)S(1)} %get-tuple-element.32.baseline, ...), custom_call_target="tpu_custom_call" | custom-call | tf_op jit(solution)/shard_map/pallas_call | solution.py:392
  26.1 3.9 %all-to-all-start.1 = ((bf16[16,16,4736]{2,1,0:T(8,128)(2,1)}), bf16[16,16,4736]{2,1,0:T(8,128)(2,1)S(1)}, u32[]{:S(2)}, u32[]{:S(2)}) async-start(bf16[16,16,4736]{2,1,0:T(8,128)(2,1)} %bitcast.6), calls=%async_computation.1 | async-start | bytes 4849664 | tf_op jit(solution)/shard_map/all_to_all | solution.py:473
  30.0 0.1 shard_map.117
  30.2 10.8 %collective-permute-start = (bf16[9,128,128]{2,1,0:T(8,128)(2,1)S(1)}, bf16[9,128,128]{2,1,0:T(8,128)(2,1)S(1)}, u32[]{:S(2)}, u32[]{:S(2)}) collective-permute-start(bf16[9,128,128]{2,1,0:T(8,128)(2,1)S(1)} %get-tuple-element.35), channel_id=1, source_target_pairs={{0,1},{1,2},{2,3},{3,4},{4,5},{5,6},{6,7},{8,9},{9,10},{10,11},{11... | collective-permute-start | bytes 884744 | tf_op jit(solution)/shard_map/ppermute | solution.py:409
  41.0 1.9 %collective-permute-start.1 = (bf16[9,128,128]{2,1,0:T(8,128)(2,1)S(1)}, bf16[9,128,128]{2,1,0:T(8,128)(2,1)S(1)}, u32[]{:S(2)}, u32[]{:S(2)}) collective-permute-start(bf16[9,128,128]{2,1,0:T(8,128)(2,1)S(1)} %get-tuple-element.36), channel_id=1, source_target_pairs={{1,0},{2,1},{3,2},{4,3},{5,4},{6,5},{7,6},{9,8},{10,9},{11,10},{12... | collective-permute-start | bytes 884744 | tf_op jit(solution)/shard_map/ppermute | solution.py:409
  42.9 1.8 %collective-permute-done.lo = bf16[9,128,128]{2,1,0:T(8,128)(2,1)S(1)} collective-permute-done((bf16[9,128,128]{2,1,0:T(8,128)(2,1)S(1)}, bf16[9,128,128]{2,1,0:T(8,128)(2,1)S(1)}, u32[]{:S(2)}, u32[]{:S(2)}) %collective-permute-start) | collective-permute-done | bytes 294944 | tf_op jit(solution)/shard_map/ppermute | solution.py:409
  44.7 17.9 %collective-permute-done.1.hi = bf16[9,128,128]{2,1,0:T(8,128)(2,1)S(1)} collective-permute-done((bf16[9,128,128]{2,1,0:T(8,128)(2,1)S(1)}, bf16[9,128,128]{2,1,0:T(8,128)(2,1)S(1)}, u32[]{:S(2)}, u32[]{:S(2)}) %collective-permute-start.1) | collective-permute-done | bytes 294944 | tf_op jit(solution)/shard_map/ppermute | solution.py:409
  62.6 3.2 %collective-permute-start.2 = (bf16[240,128]{1,0:T(8,128)(2,1)S(1)}, bf16[240,128]{1,0:T(8,128)(2,1)S(1)}, u32[]{:S(2)}, u32[]{:S(2)}) collective-permute-start(bf16[240,128]{1,0:T(8,128)(2,1)S(1)} %get-tuple-element.37), channel_id=1, source_target_pairs={{0,128},{128,256},{256,384},{1,129},{129,257},{257,385},{2,130},{1... | collective-permute-start | bytes 184328 | tf_op jit(solution)/shard_map/ppermute | solution.py:409
  65.7 1.3 %collective-permute-start.3 = (bf16[240,128]{1,0:T(8,128)(2,1)S(1)}, bf16[240,128]{1,0:T(8,128)(2,1)S(1)}, u32[]{:S(2)}, u32[]{:S(2)}) collective-permute-start(bf16[240,128]{1,0:T(8,128)(2,1)S(1)} %get-tuple-element.38), channel_id=1, source_target_pairs={{128,0},{256,128},{384,256},{129,1},{257,129},{385,257},{130,2},{2... | collective-permute-start | bytes 184328 | tf_op jit(solution)/shard_map/ppermute | solution.py:409
  67.0 3.7 %collective-permute-done.3.below = bf16[240,128]{1,0:T(8,128)(2,1)S(1)} collective-permute-done((bf16[240,128]{1,0:T(8,128)(2,1)S(1)}, bf16[240,128]{1,0:T(8,128)(2,1)S(1)}, u32[]{:S(2)}, u32[]{:S(2)}) %collective-permute-start.3) | collective-permute-done | bytes 61472 | tf_op jit(solution)/shard_map/ppermute | solution.py:409
  70.7 0.6 shard_map.119
  71.3 1.4 %copy-done = f32[30,144,128]{2,1,0:T(8,128)} copy-done((f32[30,144,128]{2,1,0:T(8,128)}, f32[30,144,128]{2,1,0:T(8,128)S(1)}, u32[]{:S(2)}) %copy-start) | copy-done | bytes 2211864
  72.7 3.1 %collective-permute-start.4 = (bf16[144,128]{1,0:T(8,128)(2,1)S(1)}, bf16[144,128]{1,0:T(8,128)(2,1)S(1)}, u32[]{:S(2)}, u32[]{:S(2)}) collective-permute-start(bf16[144,128]{1,0:T(8,128)(2,1)S(1)} %get-tuple-element.39), channel_id=1, source_target_pairs={{0,8},{8,16},{16,24},{24,32},{32,40},{40,48},{48,56},{56,64},{64,7... | collective-permute-start | bytes 110600 | tf_op jit(solution)/shard_map/ppermute | solution.py:409
  75.8 1.3 %collective-permute-start.5 = (bf16[144,128]{1,0:T(8,128)(2,1)S(1)}, bf16[144,128]{1,0:T(8,128)(2,1)S(1)}, u32[]{:S(2)}, u32[]{:S(2)}) collective-permute-start(bf16[144,128]{1,0:T(8,128)(2,1)S(1)} %get-tuple-element.40), channel_id=1, source_target_pairs={{8,0},{16,8},{24,16},{32,24},{40,32},{48,40},{56,48},{64,56},{72,6... | collective-permute-start | bytes 110600 | tf_op jit(solution)/shard_map/ppermute | solution.py:409
  77.1 0.7 shard_map.114.selector
  77.9 3.0 %collective-permute-done.5._right.from_right = bf16[144,128]{1,0:T(8,128)(2,1)S(1)} collective-permute-done((bf16[144,128]{1,0:T(8,128)(2,1)S(1)}, bf16[144,128]{1,0:T(8,128)(2,1)S(1)}, u32[]{:S(2)}, u32[]{:S(2)}) %collective-permute-start.5) | collective-permute-done | bytes 36896 | tf_op jit(solution)/shard_map/ppermute | solution.py:409
  80.8 0.6 shard_map.120
  81.5 12.2 %all_to_all.15 = f16[4,16,4480]{2,1,0:T(8,128)(2,1)S(1)} all-to-all(f16[4,16,4480]{2,1,0:T(8,128)(2,1)S(1)} %bitcast.17), channel_id=1, replica_groups=mesh['row'=4,'zlo'=4,'y'=4,'zhi'=4,'core'=2] {'zlo'}, dimensions={0} | all-to-all | bytes 1146880 | tf_op jit(solution)/shard_map/all_to_all | solution.py:479
  93.8 1.4 %shard_map.121 = (f32[512,128]{1,0:T(8,128)}, f32[576,128]{1,0:T(8,128)S(1)}, f32[576,128]{1,0:T(8,128)S(1)}, bf16[432,128]{1,0:T(8,128)(2,1)S(1)}, bf16[432,128]{1,0:T(8,128)(2,1)S(1)}) custom-call(f32[16,4480]{1,0:T(8,128)S(1)} %convert_reduce_fusion.whole), custom_call_target="tpu_custom_call" | custom-call | tf_op jit(solution)/shard_map/pallas_call | solution.py:392
  95.1 10.6 %collective-permute-start.6 = (bf16[432,128]{1,0:T(8,128)(2,1)S(1)}, bf16[432,128]{1,0:T(8,128)(2,1)S(1)}, u32[]{:S(2)}, u32[]{:S(2)}) collective-permute-start(bf16[432,128]{1,0:T(8,128)(2,1)S(1)} %get-tuple-element.43), channel_id=1, source_target_pairs={{0,1},{1,2},{2,3},{3,4},{4,5},{5,6},{6,7},{8,9},{9,10},{10,11},{11... | collective-permute-start | bytes 331784 | tf_op jit(solution)/shard_map/ppermute | solution.py:409
  105.8 1.9 %collective-permute-start.7 = (bf16[432,128]{1,0:T(8,128)(2,1)S(1)}, bf16[432,128]{1,0:T(8,128)(2,1)S(1)}, u32[]{:S(2)}, u32[]{:S(2)}) collective-permute-start(bf16[432,128]{1,0:T(8,128)(2,1)S(1)} %get-tuple-element.44), channel_id=1, source_target_pairs={{1,0},{2,1},{3,2},{4,3},{5,4},{6,5},{7,6},{9,8},{10,9},{11,10},{12... | collective-permute-start | bytes 331784 | tf_op jit(solution)/shard_map/ppermute | solution.py:409
  107.7 2.9 %shard_map.122 = (f32[9,144,256]{2,1,0:T(8,128)S(1)}, f32[8,144,256]{2,1,0:T(8,128)S(1)}, f32[8,144,256]{2,1,0:T(8,128)S(1)}, f32[8,144,256]{2,1,0:T(8,128)S(1)}, f32[8,144,256]{2,1,0:T(8,128)S(1)}) custom-call(f32[30,144,128]{2,1,0:T(8,128)S(1)} %copy-done.1, bf16[144,128]{1,0:T(8,128)(2,1)S(1)} %collective-permute-done.4._left.from_left, ...), custom_call_target="tpu_custom_call" | custom-call | tf_op jit(solution)/shard_map/pallas_call | solution.py:392
  110.6 8.4 %collective-permute-done.7.hi = bf16[432,128]{1,0:T(8,128)(2,1)S(1)} collective-permute-done((bf16[432,128]{1,0:T(8,128)(2,1)S(1)}, bf16[432,128]{1,0:T(8,128)(2,1)S(1)}, u32[]{:S(2)}, u32[]{:S(2)}) %collective-permute-start.7) | collective-permute-done | bytes 110624 | tf_op jit(solution)/shard_map/ppermute | solution.py:409
  119.0 2.2 %shard_map.123 = f32[512,128]{1,0:T(8,128)} custom-call(f32[576,128]{1,0:T(8,128)S(1)} %get-tuple-element.41.main, f32[576,128]{1,0:T(8,128)S(1)} %get-tuple-element.42.side, bf16[432,128]{1,0:T(8,128)(2,1)S(1)} %collective-permute-done.6.lo, bf16[432,128]{1,0:T(8,128)(2,1)S(1)} %collective-permute-done.7.hi, f32[30,144,128]{2,1,0:T(8,128)S(1)} %copy-done.1, ...), custom_call_target="tpu_custom_call" | custom-call | tf_op jit(solution)/shard_map/pallas_call | solution.py:392
  (20 shorter events, 0.2 us)
Async XLA Ops:
  2.4 21.4 %all-to-all-start = ((f32[64,1,128]{2,1,0:T(1,128)}), f32[64,1,128]{2,1,0:T(1,128)S(1)}, u32[]{:S(2)}, u32[]{:S(2)}) async-start(f32[64,1,128]{2,1,0:T(1,128)} %bitcast.19), calls=%async_computation | async-start | bytes 65536 | tf_op jit(solution)/shard_map/all_to_all | solution.py:453
  15.0 1.0 copy-start.3
  16.0 1.0 copy-start.4
  17.1 0.7 copy-start.7
  17.8 0.7 copy-start.8
  26.1 3.9 %copy-start.2 = (f32[4,128,128]{2,1,0:T(8,128)S(1)}, f32[4,128,128]{2,1,0:T(8,128)}, u32[]{:S(2)}) copy-start(f32[4,128,128]{2,1,0:T(8,128)} %temp.3) | copy-start | bytes 786436
  26.1 3.9 %copy-start.5 = (f32[4,128,128]{2,1,0:T(8,128)S(1)}, f32[4,128,128]{2,1,0:T(8,128)}, u32[]{:S(2)}) copy-start(f32[4,128,128]{2,1,0:T(8,128)} %cond.1) | copy-start | bytes 786436
  26.1 3.9 %copy-start.6 = (f32[4,128,128]{2,1,0:T(8,128)S(1)}, f32[4,128,128]{2,1,0:T(8,128)}, u32[]{:S(2)}) copy-start(f32[4,128,128]{2,1,0:T(8,128)} %mass.1) | copy-start | bytes 786436
  26.1 54.7 %all-to-all-start.1 = ((bf16[16,16,4736]{2,1,0:T(8,128)(2,1)}), bf16[16,16,4736]{2,1,0:T(8,128)(2,1)S(1)}, u32[]{:S(2)}, u32[]{:S(2)}) async-start(bf16[16,16,4736]{2,1,0:T(8,128)(2,1)} %bitcast.6), calls=%async_computation.1 | async-start | bytes 4849664 | tf_op jit(solution)/shard_map/all_to_all | solution.py:473
  30.2 14.5 %collective-permute-start = (bf16[9,128,128]{2,1,0:T(8,128)(2,1)S(1)}, bf16[9,128,128]{2,1,0:T(8,128)(2,1)S(1)}, u32[]{:S(2)}, u32[]{:S(2)}) collective-permute-start(bf16[9,128,128]{2,1,0:T(8,128)(2,1)S(1)} %get-tuple-element.35), channel_id=1, source_target_pairs={{0,1},{1,2},{2,3},{3,4},{4,5},{5,6},{6,7},{8,9},{9,10},{10,11},{11... | collective-permute-start | bytes 884744 | tf_op jit(solution)/shard_map/ppermute | solution.py:409
  41.0 21.6 %collective-permute-start.1 = (bf16[9,128,128]{2,1,0:T(8,128)(2,1)S(1)}, bf16[9,128,128]{2,1,0:T(8,128)(2,1)S(1)}, u32[]{:S(2)}, u32[]{:S(2)}) collective-permute-start(bf16[9,128,128]{2,1,0:T(8,128)(2,1)S(1)} %get-tuple-element.36), channel_id=1, source_target_pairs={{1,0},{2,1},{3,2},{4,3},{5,4},{6,5},{7,6},{9,8},{10,9},{11,10},{12... | collective-permute-start | bytes 884744 | tf_op jit(solution)/shard_map/ppermute | solution.py:409
  62.6 4.5 %collective-permute-start.2 = (bf16[240,128]{1,0:T(8,128)(2,1)S(1)}, bf16[240,128]{1,0:T(8,128)(2,1)S(1)}, u32[]{:S(2)}, u32[]{:S(2)}) collective-permute-start(bf16[240,128]{1,0:T(8,128)(2,1)S(1)} %get-tuple-element.37), channel_id=1, source_target_pairs={{0,128},{128,256},{256,384},{1,129},{129,257},{257,385},{2,130},{1... | collective-permute-start | bytes 184328 | tf_op jit(solution)/shard_map/ppermute | solution.py:409
  65.7 5.0 %collective-permute-start.3 = (bf16[240,128]{1,0:T(8,128)(2,1)S(1)}, bf16[240,128]{1,0:T(8,128)(2,1)S(1)}, u32[]{:S(2)}, u32[]{:S(2)}) collective-permute-start(bf16[240,128]{1,0:T(8,128)(2,1)S(1)} %get-tuple-element.38), channel_id=1, source_target_pairs={{128,0},{256,128},{384,256},{129,1},{257,129},{385,257},{130,2},{2... | collective-permute-start | bytes 184328 | tf_op jit(solution)/shard_map/ppermute | solution.py:409
  71.3 1.4 %copy-start = (f32[30,144,128]{2,1,0:T(8,128)}, f32[30,144,128]{2,1,0:T(8,128)S(1)}, u32[]{:S(2)}) copy-start(f32[30,144,128]{2,1,0:T(8,128)S(1)} %get-tuple-element.45.grids) | copy-start | bytes 6635524
  72.7 5.1 %collective-permute-start.4 = (bf16[144,128]{1,0:T(8,128)(2,1)S(1)}, bf16[144,128]{1,0:T(8,128)(2,1)S(1)}, u32[]{:S(2)}, u32[]{:S(2)}) collective-permute-start(bf16[144,128]{1,0:T(8,128)(2,1)S(1)} %get-tuple-element.39), channel_id=1, source_target_pairs={{0,8},{8,16},{16,24},{24,32},{32,40},{40,48},{48,56},{56,64},{64,7... | collective-permute-start | bytes 110600 | tf_op jit(solution)/shard_map/ppermute | solution.py:409
  75.8 5.0 %collective-permute-start.5 = (bf16[144,128]{1,0:T(8,128)(2,1)S(1)}, bf16[144,128]{1,0:T(8,128)(2,1)S(1)}, u32[]{:S(2)}, u32[]{:S(2)}) collective-permute-start(bf16[144,128]{1,0:T(8,128)(2,1)S(1)} %get-tuple-element.40), channel_id=1, source_target_pairs={{8,0},{16,8},{24,16},{32,24},{40,32},{48,40},{56,48},{64,56},{72,6... | collective-permute-start | bytes 110600 | tf_op jit(solution)/shard_map/ppermute | solution.py:409
  81.5 26.2 %copy-start.1 = (f32[30,144,128]{2,1,0:T(8,128)S(1)}, f32[30,144,128]{2,1,0:T(8,128)}, u32[]{:S(2)}) copy-start(f32[30,144,128]{2,1,0:T(8,128)} %copy-done) | copy-start | bytes 6635524
  95.1 15.5 %collective-permute-start.6 = (bf16[432,128]{1,0:T(8,128)(2,1)S(1)}, bf16[432,128]{1,0:T(8,128)(2,1)S(1)}, u32[]{:S(2)}, u32[]{:S(2)}) collective-permute-start(bf16[432,128]{1,0:T(8,128)(2,1)S(1)} %get-tuple-element.43), channel_id=1, source_target_pairs={{0,1},{1,2},{2,3},{3,4},{4,5},{5,6},{6,7},{8,9},{9,10},{10,11},{11... | collective-permute-start | bytes 331784 | tf_op jit(solution)/shard_map/ppermute | solution.py:409
  105.8 13.3 %collective-permute-start.7 = (bf16[432,128]{1,0:T(8,128)(2,1)S(1)}, bf16[432,128]{1,0:T(8,128)(2,1)S(1)}, u32[]{:S(2)}, u32[]{:S(2)}) collective-permute-start(bf16[432,128]{1,0:T(8,128)(2,1)S(1)} %get-tuple-element.44), channel_id=1, source_target_pairs={{1,0},{2,1},{3,2},{4,3},{5,4},{6,5},{7,6},{9,8},{10,9},{11,10},{12... | collective-permute-start | bytes 331784 | tf_op jit(solution)/shard_map/ppermute | solution.py:409

commit v4 on v3

--- a/solution.py
+++ b/solution.py
@@ -36,7 +36,27 @@
     return pos, ident, column * 16 + rank
 
 
-def message_kernel(temp, panel, place, holder, tier, out, meta, temp_v, panel_v, place_v, holder_v, tier_v, sems):
+def place_slots(panel, pos, dest, holder, placing, columns):
+    x, y, rank = panel >> 4, panel & 3, dest & 15
+    lower, right = (pos >> 1) & 1, pos & 1
+    next_x = x + lower * 2 - 1
+    next_y = (y + right * 2 + 3) & 3
+    inside = (next_x >= 0) & (next_x <= 3)
+    targets = (
+        dest,
+        jnp.where(inside, (next_x * 4 + y) * 16 + rank, -1),
+        (x * 4 + next_y) * 16 + rank,
+        jnp.where(inside, (next_x * 4 + next_y) * 16 + rank, -1),
+    )
+    for k, target in enumerate(targets):
+        placing[pl.ds(k * 256, 256), :] = jnp.where(iota((256, 64), 0) == target, 1.0, 0.0).astype(BF16)
+    lane = iota((64, 128), 1)
+    columns[...] = jnp.where(
+        lane == 0, as_column(panel), jnp.where(lane == 1, as_column(pos), as_column(holder))
+    )
+
+
+def message_kernel(temp, panel, place, holder, tier, out, placing, columns, temp_v, panel_v, place_v, holder_v, tier_v, sems):
     pairs = [(panel, panel_v), (place, place_v), (holder, holder_v), (tier, tier_v), (temp, temp_v)]
     copies = [pltpu.make_async_copy(a, b, sems.at[i]) for i, (a, b) in enumerate(pairs)]
     for copy in copies:
@@ -45,9 +65,7 @@
         copy.wait()
     panel_row, holder_row = panel_v[...], holder_v[...]
     pos, ident, dest = slot_rows(panel_row, place_v[...], holder_row, tier_v[...])
-    for k, row in enumerate((panel_row, pos, dest, holder_row)):
-        meta[k : k + 1, :] = jnp.concatenate([row, row], axis=1)
-    meta[4:8, :] = jnp.zeros((4, 128), I32)
+    place_slots(panel_row, pos, dest, holder_row, placing, columns)
     code = (dest * 64 + ident).astype(F32)
     copies[4].wait()
     sums = jnp.sum(temp_v[...].reshape(8, 64, 128), axis=1)
@@ -61,34 +79,23 @@
     out[...] = jnp.broadcast_to(row, (64, 128))
 
 
-def placing_kernel(meta, toggling, baseline, warming, placing, columns, toggling_v, baseline_v, warming_v, sems):
-    pairs = [(toggling, toggling_v), (baseline, baseline_v), (warming, warming_v)]
-    copies = [pltpu.make_async_copy(a, b, sems.at[i]) for i, (a, b) in enumerate(pairs)]
-    for copy in copies:
-        copy.start()
-    panel, pos, dest, holder = (meta[k : k + 1, 0:64] for k in range(4))
-    x, y, rank = panel >> 4, panel & 3, dest & 15
-    lower, right = (pos >> 1) & 1, pos & 1
-    next_x = x + lower * 2 - 1
-    next_y = (y + right * 2 + 3) & 3
-    inside = (next_x >= 0) & (next_x <= 3)
-    targets = (
-        dest,
-        jnp.where(inside, (next_x * 4 + y) * 16 + rank, -1),
-        (x * 4 + next_y) * 16 + rank,
-        jnp.where(inside, (next_x * 4 + next_y) * 16 + rank, -1),
-    )
-    for k, target in enumerate(targets):
-        placing[pl.ds(k * 256, 256), :] = jnp.where(iota((256, 64), 0) == target, 1.0, 0.0).astype(BF16)
-    lane = iota((64, 128), 1)
-    columns[...] = jnp.where(
-        lane == 0, as_column(panel), jnp.where(lane == 1, as_column(pos), as_column(holder))
-    )
-    for copy in copies:
-        copy.wait()
-
-
-def power_kernel(messages, columns, warming, toggling, baseline, placing, out, sent, sems):
+def power_kernel(
+    far_messages, far_columns, far_warming, far_toggling, far_baseline, far_placing, out,
+    messages, columns, warming, toggling, baseline, placing, sent, sems,
+):
+    pairs = [
+        (far_messages, messages),
+        (far_columns, columns),
+        (far_warming, warming),
+        (far_toggling, toggling),
+        (far_baseline, baseline),
+        (far_placing, placing),
+    ]
+    loads = [pltpu.make_async_copy(a, b, sems.at[9 + i]) for i, (a, b) in enumerate(pairs)]
+    for load in loads:
+        load.start()
+    loads[0].wait()
+    loads[1].wait()
     tile, pos, holder = (columns[:, k : k + 1] for k in range(3))
     lower, right = (pos >> 1) & 1, pos & 1
     pick = jnp.where(iota((64, 64), 1) == tile, 1.0, 0.0)
@@ -98,6 +105,7 @@
     member = iota((64, 16), 1) == holder
     total = jnp.sum(jnp.where(member, slot_mean, 0.0), axis=0, keepdims=True)
     count = jnp.sum(jnp.where(member, 1.0, 0.0), axis=0, keepdims=True)
+    loads[2].wait()
     leak = jnp.exp(warming[...] * (total / count))
     factor = jnp.sum(jnp.where(member, leak, 0.0), axis=1, keepdims=True)
 
@@ -113,6 +121,8 @@
         copy.start()
         copies.append(copy)
 
+    for load in loads[3:]:
+        load.wait()
     edge = ((lane & 63) >> 1) == right * 31
     sides = jnp.zeros((64, 128), F32)
     width = 512
@@ -179,7 +189,7 @@
         put(5 + k, ids, z * 16 + layer)
 
 
-def combine_kernel(selector, received, _left, _right, out):
+def combine_kernel(selector, received, _to_left, _to_right, out):
     def add(k, start, width):
         return jnp.dot(
             selector[k * 64 : (k + 1) * 64, :],
@@ -198,7 +208,7 @@
     out[:, 4352:4480] = corners
 
 
-def unpack_kernel(whole, density, main, side, up, down, turned):
+def unpack_kernel(whole, _left, _right, density, main, side, up, down, turned):
     for k in range(32):
         turned[k * 16 : (k + 1) * 16, :] = whole[:, k * 128 : (k + 1) * 128]
     low = iota((32, 128), 1) < 64
@@ -250,14 +260,26 @@
         out[288:432, :] = (side[first : first + 144, :] + pltpu.roll(second, 4, 1)).astype(BF16)
 
 
+def depth(a):
+    return 3 if a < 2 else 2
+
+
+def beyond(lo, hi, a, layer):
+    if layer < 3:
+        k = layer - 3 + depth(a)
+        return (lo, 3 * a + k) if k >= 0 else None
+    k = layer - 7
+    return (hi, 3 * a + k) if k < depth(a) else None
+
+
 def layers_kernel(temp, cond, mass, own, up, down, sems):
     copies = [pltpu.make_async_copy(a, own.at[i], sems.at[i]) for i, a in enumerate((temp, cond, mass))]
     for copy in copies:
         copy.start()
     for a, copy in enumerate(copies):
         copy.wait()
-        for k in range(3):
-            up[3 * a + k] = own[a, 1 + k].astype(BF16)
+        for k in range(depth(a)):
+            up[3 * a + k] = own[a, 4 - depth(a) + k].astype(BF16)
             down[3 * a + k] = own[a, k].astype(BF16)
 
 
@@ -268,10 +290,13 @@
             if 3 <= layer < 7:
                 lasts.append(own[a, layer - 3, 120:128, :])
                 firsts.append(own[a, layer - 3, 0:8, :])
-            else:
-                source, k = (lo, 3 * a + layer) if layer < 3 else (hi, 3 * a + layer - 7)
+            elif found := beyond(lo, hi, a, layer):
+                source, k = found
                 lasts.append(source[k, 112:128, :].astype(F32)[8:16])
                 firsts.append(source[k, 0:16, :].astype(F32)[0:8])
+            else:
+                lasts.append(jnp.zeros((8, 128), F32))
+                firsts.append(jnp.zeros((8, 128), F32))
     last[...] = jnp.concatenate(lasts, axis=0).astype(BF16)
     first[...] = jnp.concatenate(firsts, axis=0).astype(BF16)
 
@@ -283,12 +308,12 @@
     for a in range(3):
         for layer in range(10):
             i = a * 10 + layer
-            if layer < 3:
-                source = lo[3 * a + layer].astype(F32)
-            elif layer < 7:
+            if 3 <= layer < 7:
                 source = own[a, layer - 3]
+            elif found := beyond(lo, hi, a, layer):
+                source = found[0][found[1]].astype(F32)
             else:
-                source = hi[3 * a + layer - 7].astype(F32)
+                source = jnp.zeros((128, 128), F32)
             piece = jnp.concatenate([source, under[8 * i : 8 * i + 8], over[8 * i : 8 * i + 8]], axis=0)
             out[i] = piece
             base = a * 40 + layer * 4
@@ -410,10 +435,10 @@
 
 
 def extended_grids(temp, cond, mass):
-    nine, rows, edge = sds((9, 128, 128), BF16), sds((240, 128), BF16), sds((144, 128), BF16)
+    eight, rows, edge = sds((8, 128, 128), BF16), sds((240, 128), BF16), sds((144, 128), BF16)
     own, up, down = call(
         layers_kernel,
-        (sds((3, 4, 128, 128), F32), nine, nine),
+        (sds((3, 4, 128, 128), F32), eight, eight),
         (temp, cond, mass),
         scratch=[pltpu.SemaphoreType.DMA((3,))],
         far=range(3),
@@ -423,7 +448,7 @@
     wide, to_left, to_right = call(
         gather_kernel, (sds((30, 144, 128), F32), edge, edge), (own, lo, hi, above, below), mib=24
     )
-    return wide, exchange(to_right, to_left, COL)
+    return wide, (to_left, to_right), exchange(to_right, to_left, COL)
 
 
 def operator(wide, from_left, from_right):
@@ -439,9 +464,9 @@
 
 def shards(temp, cond, mass, toggling, baseline, panel, place, holder, tier, warming):
     row64 = pltpu.VMEM((1, 64), I32)
-    message, meta = call(
+    message, placing, columns = call(
         message_kernel,
-        (sds((64, 128), F32), sds((8, 128), I32)),
+        (sds((64, 128), F32), sds((1024, 64), BF16), sds((64, 128), I32)),
         (temp, panel.reshape(1, 64), place, holder, tier),
         mib=60,
         scratch=[
@@ -452,29 +477,24 @@
     )
     messages = lax.all_to_all(message.reshape(64, 1, 128), CUBE, split_axis=0, concat_axis=0, tiled=True)
     messages = messages.reshape(64, 128)
-    placing, columns, toggling, baseline, warming = call(
-        placing_kernel,
-        (
-            sds((1024, 64), BF16), sds((64, 128), I32),
-            sds((64, 4096), BF16), sds((64, 4096), BF16), sds((1, 16), F32),
-        ),
-        (meta, toggling[0], baseline[0], warming),
-        scratch=[pltpu.SemaphoreType.DMA((3,))],
-        far=(1, 2, 3),
-    )
     send = call(
         power_kernel,
         sds((256, 4736), BF16),
-        (messages, columns, warming, toggling, baseline, placing),
-        mib=24,
-        scratch=[pltpu.VMEM((256, 4736), BF16), pltpu.SemaphoreType.DMA((9,))],
+        (messages, columns, warming, toggling[0], baseline[0], placing),
+        mib=60,
+        scratch=[
+            pltpu.VMEM((64, 128), F32), pltpu.VMEM((64, 128), I32), pltpu.VMEM((1, 16), F32),
+            pltpu.VMEM((64, 4096), BF16), pltpu.VMEM((64, 4096), BF16), pltpu.VMEM((1024, 64), BF16),
+            pltpu.VMEM((256, 4736), BF16), pltpu.SemaphoreType.DMA((15,)),
+        ],
+        far=range(6),
         far_out=True,
     )
     received = lax.all_to_all(send.reshape(16, 16, 4736), PLANE, split_axis=0, concat_axis=0, tiled=True)
     selector = call(selector_kernel, sds((576, 256), BF16), (messages,))
-    wide, beside = extended_grids(temp, cond, mass)
+    wide, edges, beside = extended_grids(temp, cond, mass)
     partial = call(
-        combine_kernel, sds((64, 4480), F32), (selector, received.reshape(256, 4736), *beside)
+        combine_kernel, sds((64, 4480), F32), (selector, received.reshape(256, 4736), *edges)
     )
     parts = lax.all_to_all(
         partial.astype(jnp.float16).reshape(4, 16, 4480), "zlo", split_axis=0, concat_axis=0, tiled=True
@@ -484,7 +504,7 @@
     density, main, side, up, down = call(
         unpack_kernel,
         (sds((512, 128), F32), block, block, strip, strip),
-        (jnp.sum(parts.astype(F32), axis=0),),
+        (jnp.sum(parts.astype(F32), axis=0), *beside),
         scratch=[pltpu.VMEM((512, 128), F32)],
     )
     lo, hi = exchange(up, down, LAYER)

time: 122 us -> 112 us (0.918)
  starting transfers between devices: 50.5 us -> 40.7 us
  blocking collectives: 12.2 us -> 21.6 us
  waiting for transfers between devices: 39.7 us -> 32.1 us
  local copies, waits for them, and re-layouts: 4.81 us -> 1.39 us
    all_to_all x1, blocking collectives: 12.2 us -> 21.6 us  [shards(): lax.all_to_all(message.reshape(64, 1, 128), CUBE, split_axis=0, concat_ax...]
    all_to_all x1, starting transfers between devices: 12.6 us -> 3.61 us  [shards(): lax.all_to_all(partial.astype(jnp.float16).reshape(4, 16, 4480), 'zlo', s...]
    ppermute x8, waiting for transfers between devices: 34.7 us -> 27.3 us  [exchange(): return (lax.ppermute(to_next, axis, up), lax.ppermute(to_last, axis, down))]
    unnamed x18 -> x12, local copies, waits for them, and re-layouts: 4.81 us -> 1.39 us
    pallas_call x11 -> x10, Pallas kernels: 13 us -> 13.5 us  [call(): pl.pallas_call(kernel, out_shape=shape, in_specs=[anywhere if i in far el...]
  transfers between devices with their start and end apart: 10 -> 10, of which waited for: 6 -> 5; matrix products, arithmetic and copies ran while one was open for 0% -> 0% of each run, Pallas kernels for 4% -> 4%
where the time goes in v4:
time: 112 us; the launch traced here: 111 us
  starting transfers between devices  40.7 us (36%)
  waiting for transfers between devices  32.1 us (29%)
  blocking collectives  21.6 us (19%)
  Pallas kernels  13.5 us (12%)
  local copies, waits for them, and re-layouts  1.39 us (1%)
    ppermute x8, starting transfers between devices, exchange(): return (lax.ppermute(to_next, axis, up), lax.ppermute(to_last, axis, down))  33.2 us
    ppermute x8, waiting for transfers between devices, exchange(): return (lax.ppermute(to_next, axis, up), lax.ppermute(to_last, axis, down))  27.3 us
    all_to_all x1, blocking collectives, shards(): lax.all_to_all(message.reshape(64, 1, 128), CUBE, split_axis=0, concat_ax...  21.6 us
    pallas_call x10, Pallas kernels, call(): pl.pallas_call(kernel, out_shape=shape, in_specs=[anywhere if i in far el...  13.5 us
    all_to_all x1, waiting for transfers between devices, shards(): lax.all_to_all(partial.astype(jnp.float16).reshape(4, 16, 4480), 'zlo', s...  4.73 us
    all_to_all x1, starting transfers between devices, shards(): lax.all_to_all(send.reshape(16, 16, 4736), PLANE, split_axis=0, concat_ax...  3.87 us
    all_to_all x1, starting transfers between devices, shards(): lax.all_to_all(partial.astype(jnp.float16).reshape(4, 16, 4480), 'zlo', s...  3.61 us
  transfers between devices with their start and end apart: 10, of which 5 were waited for; matrix products, arithmetic and copies ran while one was open for 0% of the time, Pallas kernels for 4%

profile of v4, /device:TPU:1, one launch (start us, length us, event | category | flops | bytes accessed | tf_op | source)
XLA Modules:
  0.0 111.1 jit_solution(6482110393691426625)
XLA Ops:
  0.6 1.8 %shard_map.113 = (f32[64,128]{1,0:T(8,128)}, bf16[1024,64]{1,0:T(8,128)(2,1)}, s32[64,128]{1,0:T(8,128)}) custom-call(f32[4,128,128]{2,1,0:T(8,128)} %temp.3, s32[1,64]{1,0:T(1,128)} %bitcast.21, s32[1,64]{1,0:T(1,128)} %place.1, s32[1,64]{1,0:T(1,128)} %holder.1, s32[1,16]{1,0:T(1,128)} %tier.1), custom_call_target="tpu_custom_call" | custom-call | tf_op jit(solution)/shard_map/pallas_call | solution.py:417
  2.4 21.6 %all_to_all.15 = f32[64,1,128]{2,1,0:T(1,128)} all-to-all(f32[64,1,128]{2,1,0:T(1,128)} %bitcast.20), channel_id=1, replica_groups=mesh['row'=4,'zlo'=4,'y'=4,'zhi'=4,'core'=2] {'row','zlo','y'}, dimensions={0} | all-to-all | bytes 65536 | tf_op jit(solution)/shard_map/all_to_all | solution.py:478
  24.1 3.2 %shard_map.115 = bf16[256,4736]{1,0:T(8,128)(2,1)} custom-call(f32[64,128]{1,0:T(8,128)} %bitcast.13, s32[64,128]{1,0:T(8,128)} %get-tuple-element.24.far_columns, f32[1,16]{1,0:T(1,128)} %far_warming.1, bf16[64,4096]{1,0:T(8,128)(2,1)} %bitcast.17, bf16[64,4096]{1,0:T(8,128)(2,1)} %bitcast.18, bf16[1024,64]{1,0:T(8,128)(2,1)} %get-tuple-element.25.far_placing), custom_call_target="tpu_custom_call" | custom-call | tf_op jit(solution)/shard_map/pallas_call | solution.py:417
  27.2 0.0 copy-start.2
  27.3 0.0 copy-start.4
  27.3 0.0 copy-start.5
  27.3 3.9 %all-to-all-start.1 = ((bf16[16,16,4736]{2,1,0:T(8,128)(2,1)}), bf16[16,16,4736]{2,1,0:T(8,128)(2,1)S(1)}, u32[]{:S(2)}, u32[]{:S(2)}) async-start(bf16[16,16,4736]{2,1,0:T(8,128)(2,1)} %bitcast.15), calls=%async_computation.1 | async-start | bytes 4849664 | tf_op jit(solution)/shard_map/all_to_all | solution.py:493
  31.2 0.1 shard_map.116
  31.3 10.7 %collective-permute-start = (bf16[8,128,128]{2,1,0:T(8,128)(2,1)S(1)}, bf16[8,128,128]{2,1,0:T(8,128)(2,1)S(1)}, u32[]{:S(2)}, u32[]{:S(2)}) collective-permute-start(bf16[8,128,128]{2,1,0:T(8,128)(2,1)S(1)} %get-tuple-element.27), channel_id=1, source_target_pairs={{0,1},{1,2},{2,3},{3,4},{4,5},{5,6},{6,7},{8,9},{9,10},{10,11},{11... | collective-permute-start | bytes 786440 | tf_op jit(solution)/shard_map/ppermute | solution.py:434
  42.0 1.9 %collective-permute-start.1 = (bf16[8,128,128]{2,1,0:T(8,128)(2,1)S(1)}, bf16[8,128,128]{2,1,0:T(8,128)(2,1)S(1)}, u32[]{:S(2)}, u32[]{:S(2)}) collective-permute-start(bf16[8,128,128]{2,1,0:T(8,128)(2,1)S(1)} %get-tuple-element.28), channel_id=1, source_target_pairs={{1,0},{2,1},{3,2},{4,3},{5,4},{6,5},{7,6},{9,8},{10,9},{11,10},{12... | collective-permute-start | bytes 786440 | tf_op jit(solution)/shard_map/ppermute | solution.py:434
  43.9 1.4 %collective-permute-done.lo = bf16[8,128,128]{2,1,0:T(8,128)(2,1)S(1)} collective-permute-done((bf16[8,128,128]{2,1,0:T(8,128)(2,1)S(1)}, bf16[8,128,128]{2,1,0:T(8,128)(2,1)S(1)}, u32[]{:S(2)}, u32[]{:S(2)}) %collective-permute-start) | collective-permute-done | bytes 262176 | tf_op jit(solution)/shard_map/ppermute | solution.py:434
  45.3 16.7 %collective-permute-done.1.hi = bf16[8,128,128]{2,1,0:T(8,128)(2,1)S(1)} collective-permute-done((bf16[8,128,128]{2,1,0:T(8,128)(2,1)S(1)}, bf16[8,128,128]{2,1,0:T(8,128)(2,1)S(1)}, u32[]{:S(2)}, u32[]{:S(2)}) %collective-permute-start.1) | collective-permute-done | bytes 262176 | tf_op jit(solution)/shard_map/ppermute | solution.py:434
  62.1 3.2 %collective-permute-start.2 = (bf16[240,128]{1,0:T(8,128)(2,1)S(1)}, bf16[240,128]{1,0:T(8,128)(2,1)S(1)}, u32[]{:S(2)}, u32[]{:S(2)}) collective-permute-start(bf16[240,128]{1,0:T(8,128)(2,1)S(1)} %get-tuple-element.29), channel_id=1, source_target_pairs={{0,128},{128,256},{256,384},{1,129},{129,257},{257,385},{2,130},{1... | collective-permute-start | bytes 184328 | tf_op jit(solution)/shard_map/ppermute | solution.py:434
  65.2 1.3 %collective-permute-start.3 = (bf16[240,128]{1,0:T(8,128)(2,1)S(1)}, bf16[240,128]{1,0:T(8,128)(2,1)S(1)}, u32[]{:S(2)}, u32[]{:S(2)}) collective-permute-start(bf16[240,128]{1,0:T(8,128)(2,1)S(1)} %get-tuple-element.30), channel_id=1, source_target_pairs={{128,0},{256,128},{384,256},{129,1},{257,129},{385,257},{130,2},{2... | collective-permute-start | bytes 184328 | tf_op jit(solution)/shard_map/ppermute | solution.py:434
  66.5 0.7 shard_map.114.selector
  67.3 2.9 %collective-permute-done.3.below = bf16[240,128]{1,0:T(8,128)(2,1)S(1)} collective-permute-done((bf16[240,128]{1,0:T(8,128)(2,1)S(1)}, bf16[240,128]{1,0:T(8,128)(2,1)S(1)}, u32[]{:S(2)}, u32[]{:S(2)}) %collective-permute-start.3) | collective-permute-done | bytes 61472 | tf_op jit(solution)/shard_map/ppermute | solution.py:434
  70.2 0.6 shard_map.118
  70.8 1.4 %copy-done = f32[30,144,128]{2,1,0:T(8,128)} copy-done((f32[30,144,128]{2,1,0:T(8,128)}, f32[30,144,128]{2,1,0:T(8,128)S(1)}, u32[]{:S(2)}) %copy-start) | copy-done | bytes 2211864
  72.2 0.0 all-to-all-done.1
  72.2 0.6 shard_map.119
  72.8 0.9 convert_element_type.6
  73.7 3.6 %all-to-all-start.2 = ((f16[4,16,4480]{2,1,0:T(8,128)(2,1)}), f16[4,16,4480]{2,1,0:T(8,128)(2,1)S(1)}, u32[]{:S(2)}, u32[]{:S(2)}) async-start(f16[4,16,4480]{2,1,0:T(8,128)(2,1)} %bitcast.16), calls=%async_computation.2 | async-start | bytes 1146880 | tf_op jit(solution)/shard_map/all_to_all | solution.py:499
  77.3 1.3 %collective-permute-start.5 = (bf16[144,128]{1,0:T(8,128)(2,1)S(1)}, bf16[144,128]{1,0:T(8,128)(2,1)S(1)}, u32[]{:S(2)}, u32[]{:S(2)}) collective-permute-start(bf16[144,128]{1,0:T(8,128)(2,1)S(1)} %get-tuple-element.31._to_left), channel_id=1, source_target_pairs={{8,0},{16,8},{24,16},{32,24},{40,32},{48,40},{56,48},{64,56},{72,6... | collective-permute-start | bytes 110600 | tf_op jit(solution)/shard_map/ppermute | solution.py:434
  78.6 4.0 %collective-permute-start.4 = (bf16[144,128]{1,0:T(8,128)(2,1)S(1)}, bf16[144,128]{1,0:T(8,128)(2,1)S(1)}, u32[]{:S(2)}, u32[]{:S(2)}) collective-permute-start(bf16[144,128]{1,0:T(8,128)(2,1)S(1)} %get-tuple-element.32._to_right), channel_id=1, source_target_pairs={{0,8},{8,16},{16,24},{24,32},{32,40},{40,48},{48,56},{56,64},{64,7... | collective-permute-start | bytes 110600 | tf_op jit(solution)/shard_map/ppermute | solution.py:434
  82.6 4.7 %all-to-all-done.2 = f16[4,16,4480]{2,1,0:T(8,128)(2,1)S(1)} async-done(((f16[4,16,4480]{2,1,0:T(8,128)(2,1)}), f16[4,16,4480]{2,1,0:T(8,128)(2,1)S(1)}, u32[]{:S(2)}, u32[]{:S(2)}) %all-to-all-start.2) | async-done | bytes 573472 | tf_op jit(solution)/shard_map/all_to_all | solution.py:499
  87.3 0.1 convert_reduce_fusion.whole
  87.4 1.4 %shard_map.120 = (f32[512,128]{1,0:T(8,128)}, f32[576,128]{1,0:T(8,128)S(1)}, f32[576,128]{1,0:T(8,128)S(1)}, bf16[432,128]{1,0:T(8,128)(2,1)S(1)}, bf16[432,128]{1,0:T(8,128)(2,1)S(1)}) custom-call(f32[16,4480]{1,0:T(8,128)S(1)} %convert_reduce_fusion.whole, bf16[144,128]{1,0:T(8,128)(2,1)S(1)} %collective-permute-done.4._left.from_left, ...), custom_call_target="tpu_custom_call" | custom-call | tf_op jit(solution)/shard_map/pallas_call | solution.py:417
  88.8 9.0 %collective-permute-start.6 = (bf16[432,128]{1,0:T(8,128)(2,1)S(1)}, bf16[432,128]{1,0:T(8,128)(2,1)S(1)}, u32[]{:S(2)}, u32[]{:S(2)}) collective-permute-start(bf16[432,128]{1,0:T(8,128)(2,1)S(1)} %get-tuple-element.35), channel_id=1, source_target_pairs={{0,1},{1,2},{2,3},{3,4},{4,5},{5,6},{6,7},{8,9},{9,10},{10,11},{11... | collective-permute-start | bytes 331784 | tf_op jit(solution)/shard_map/ppermute | solution.py:434
  97.8 1.9 %collective-permute-start.7 = (bf16[432,128]{1,0:T(8,128)(2,1)S(1)}, bf16[432,128]{1,0:T(8,128)(2,1)S(1)}, u32[]{:S(2)}, u32[]{:S(2)}) collective-permute-start(bf16[432,128]{1,0:T(8,128)(2,1)S(1)} %get-tuple-element.36), channel_id=1, source_target_pairs={{1,0},{2,1},{3,2},{4,3},{5,4},{6,5},{7,6},{9,8},{10,9},{11,10},{12... | collective-permute-start | bytes 331784 | tf_op jit(solution)/shard_map/ppermute | solution.py:434
  99.7 2.9 %shard_map.121 = (f32[9,144,256]{2,1,0:T(8,128)S(1)}, f32[8,144,256]{2,1,0:T(8,128)S(1)}, f32[8,144,256]{2,1,0:T(8,128)S(1)}, f32[8,144,256]{2,1,0:T(8,128)S(1)}, f32[8,144,256]{2,1,0:T(8,128)S(1)}) custom-call(f32[30,144,128]{2,1,0:T(8,128)S(1)} %copy-done.1, bf16[144,128]{1,0:T(8,128)(2,1)S(1)} %collective-permute-done.4._left.from_left, ...), custom_call_target="tpu_custom_call" | custom-call | tf_op jit(solution)/shard_map/pallas_call | solution.py:417
  102.7 6.3 %collective-permute-done.7.hi = bf16[432,128]{1,0:T(8,128)(2,1)S(1)} collective-permute-done((bf16[432,128]{1,0:T(8,128)(2,1)S(1)}, bf16[432,128]{1,0:T(8,128)(2,1)S(1)}, u32[]{:S(2)}, u32[]{:S(2)}) %collective-permute-start.7) | collective-permute-done | bytes 110624 | tf_op jit(solution)/shard_map/ppermute | solution.py:434
  109.0 2.2 %shard_map.122 = f32[512,128]{1,0:T(8,128)} custom-call(f32[576,128]{1,0:T(8,128)S(1)} %get-tuple-element.33.main, f32[576,128]{1,0:T(8,128)S(1)} %get-tuple-element.34.side, bf16[432,128]{1,0:T(8,128)(2,1)S(1)} %collective-permute-done.6.lo, bf16[432,128]{1,0:T(8,128)(2,1)S(1)} %collective-permute-done.7.hi, f32[30,144,128]{2,1,0:T(8,128)S(1)} %copy-done.1, ...), custom_call_target="tpu_custom_call" | custom-call | tf_op jit(solution)/shard_map/pallas_call | solution.py:417
  (13 shorter events, 0.0 us)
Async XLA Ops:
  27.2 3.9 %copy-start.2 = (f32[4,128,128]{2,1,0:T(8,128)S(1)}, f32[4,128,128]{2,1,0:T(8,128)}, u32[]{:S(2)}) copy-start(f32[4,128,128]{2,1,0:T(8,128)} %temp.3) | copy-start | bytes 786436
  27.3 3.9 %copy-start.4 = (f32[4,128,128]{2,1,0:T(8,128)S(1)}, f32[4,128,128]{2,1,0:T(8,128)}, u32[]{:S(2)}) copy-start(f32[4,128,128]{2,1,0:T(8,128)} %cond.1) | copy-start | bytes 786436
  27.3 3.9 %copy-start.5 = (f32[4,128,128]{2,1,0:T(8,128)S(1)}, f32[4,128,128]{2,1,0:T(8,128)}, u32[]{:S(2)}) copy-start(f32[4,128,128]{2,1,0:T(8,128)} %mass.1) | copy-start | bytes 786436
  27.3 44.9 %all-to-all-start.1 = ((bf16[16,16,4736]{2,1,0:T(8,128)(2,1)}), bf16[16,16,4736]{2,1,0:T(8,128)(2,1)S(1)}, u32[]{:S(2)}, u32[]{:S(2)}) async-start(bf16[16,16,4736]{2,1,0:T(8,128)(2,1)} %bitcast.15), calls=%async_computation.1 | async-start | bytes 4849664 | tf_op jit(solution)/shard_map/all_to_all | solution.py:493
  31.2 35.3 %copy-start.3 = (f32[64,1,128]{2,1,0:T(1,128)S(1)}, f32[64,1,128]{2,1,0:T(1,128)}, u32[]{:S(2)}) copy-start(f32[64,1,128]{2,1,0:T(1,128)} %all_to_all.15) | copy-start | bytes 98308
  31.3 14.0 %collective-permute-start = (bf16[8,128,128]{2,1,0:T(8,128)(2,1)S(1)}, bf16[8,128,128]{2,1,0:T(8,128)(2,1)S(1)}, u32[]{:S(2)}, u32[]{:S(2)}) collective-permute-start(bf16[8,128,128]{2,1,0:T(8,128)(2,1)S(1)} %get-tuple-element.27), channel_id=1, source_target_pairs={{0,1},{1,2},{2,3},{3,4},{4,5},{5,6},{6,7},{8,9},{9,10},{10,11},{11... | collective-permute-start | bytes 786440 | tf_op jit(solution)/shard_map/ppermute | solution.py:434
  42.0 20.0 %collective-permute-start.1 = (bf16[8,128,128]{2,1,0:T(8,128)(2,1)S(1)}, bf16[8,128,128]{2,1,0:T(8,128)(2,1)S(1)}, u32[]{:S(2)}, u32[]{:S(2)}) collective-permute-start(bf16[8,128,128]{2,1,0:T(8,128)(2,1)S(1)} %get-tuple-element.28), channel_id=1, source_target_pairs={{1,0},{2,1},{3,2},{4,3},{5,4},{6,5},{7,6},{9,8},{10,9},{11,10},{12... | collective-permute-start | bytes 786440 | tf_op jit(solution)/shard_map/ppermute | solution.py:434
  62.1 5.2 %collective-permute-start.2 = (bf16[240,128]{1,0:T(8,128)(2,1)S(1)}, bf16[240,128]{1,0:T(8,128)(2,1)S(1)}, u32[]{:S(2)}, u32[]{:S(2)}) collective-permute-start(bf16[240,128]{1,0:T(8,128)(2,1)S(1)} %get-tuple-element.29), channel_id=1, source_target_pairs={{0,128},{128,256},{256,384},{1,129},{129,257},{257,385},{2,130},{1... | collective-permute-start | bytes 184328 | tf_op jit(solution)/shard_map/ppermute | solution.py:434
  65.2 5.0 %collective-permute-start.3 = (bf16[240,128]{1,0:T(8,128)(2,1)S(1)}, bf16[240,128]{1,0:T(8,128)(2,1)S(1)}, u32[]{:S(2)}, u32[]{:S(2)}) collective-permute-start(bf16[240,128]{1,0:T(8,128)(2,1)S(1)} %get-tuple-element.30), channel_id=1, source_target_pairs={{128,0},{256,128},{384,256},{129,1},{257,129},{385,257},{130,2},{2... | collective-permute-start | bytes 184328 | tf_op jit(solution)/shard_map/ppermute | solution.py:434
  70.8 1.4 %copy-start = (f32[30,144,128]{2,1,0:T(8,128)}, f32[30,144,128]{2,1,0:T(8,128)S(1)}, u32[]{:S(2)}) copy-start(f32[30,144,128]{2,1,0:T(8,128)S(1)} %get-tuple-element.37.grids) | copy-start | bytes 6635524
  73.7 26.1 %copy-start.1 = (f32[30,144,128]{2,1,0:T(8,128)S(1)}, f32[30,144,128]{2,1,0:T(8,128)}, u32[]{:S(2)}) copy-start(f32[30,144,128]{2,1,0:T(8,128)} %copy-done) | copy-start | bytes 6635524
  73.7 13.6 %all-to-all-start.2 = ((f16[4,16,4480]{2,1,0:T(8,128)(2,1)}), f16[4,16,4480]{2,1,0:T(8,128)(2,1)S(1)}, u32[]{:S(2)}, u32[]{:S(2)}) async-start(f16[4,16,4480]{2,1,0:T(8,128)(2,1)} %bitcast.16), calls=%async_computation.2 | async-start | bytes 1146880 | tf_op jit(solution)/shard_map/all_to_all | solution.py:499
  77.3 10.1 %collective-permute-start.5 = (bf16[144,128]{1,0:T(8,128)(2,1)S(1)}, bf16[144,128]{1,0:T(8,128)(2,1)S(1)}, u32[]{:S(2)}, u32[]{:S(2)}) collective-permute-start(bf16[144,128]{1,0:T(8,128)(2,1)S(1)} %get-tuple-element.31._to_left), channel_id=1, source_target_pairs={{8,0},{16,8},{24,16},{32,24},{40,32},{48,40},{56,48},{64,56},{72,6... | collective-permute-start | bytes 110600 | tf_op jit(solution)/shard_map/ppermute | solution.py:434
  78.6 8.8 %collective-permute-start.4 = (bf16[144,128]{1,0:T(8,128)(2,1)S(1)}, bf16[144,128]{1,0:T(8,128)(2,1)S(1)}, u32[]{:S(2)}, u32[]{:S(2)}) collective-permute-start(bf16[144,128]{1,0:T(8,128)(2,1)S(1)} %get-tuple-element.32._to_right), channel_id=1, source_target_pairs={{0,8},{8,16},{16,24},{24,32},{32,40},{40,48},{48,56},{56,64},{64,7... | collective-permute-start | bytes 110600 | tf_op jit(solution)/shard_map/ppermute | solution.py:434
  88.8 13.8 %collective-permute-start.6 = (bf16[432,128]{1,0:T(8,128)(2,1)S(1)}, bf16[432,128]{1,0:T(8,128)(2,1)S(1)}, u32[]{:S(2)}, u32[]{:S(2)}) collective-permute-start(bf16[432,128]{1,0:T(8,128)(2,1)S(1)} %get-tuple-element.35), channel_id=1, source_target_pairs={{0,1},{1,2},{2,3},{3,4},{4,5},{5,6},{6,7},{8,9},{9,10},{10,11},{11... | collective-permute-start | bytes 331784 | tf_op jit(solution)/shard_map/ppermute | solution.py:434
  97.8 11.2 %collective-permute-start.7 = (bf16[432,128]{1,0:T(8,128)(2,1)S(1)}, bf16[432,128]{1,0:T(8,128)(2,1)S(1)}, u32[]{:S(2)}, u32[]{:S(2)}) collective-permute-start(bf16[432,128]{1,0:T(8,128)(2,1)S(1)} %get-tuple-element.36), channel_id=1, source_target_pairs={{1,0},{2,1},{3,2},{4,3},{5,4},{6,5},{7,6},{9,8},{10,9},{11,10},{12... | collective-permute-start | bytes 331784 | tf_op jit(solution)/shard_map/ppermute | solution.py:434

commit v5 on v4

--- a/solution.py
+++ b/solution.py
@@ -56,8 +56,16 @@
     )
 
 
-def message_kernel(temp, panel, place, holder, tier, out, placing, columns, temp_v, panel_v, place_v, holder_v, tier_v, sems):
-    pairs = [(panel, panel_v), (place, place_v), (holder, holder_v), (tier, tier_v), (temp, temp_v)]
+def depth(a):
+    return 3 if a < 2 else 2
+
+
+def message_kernel(
+    temp, cond, mass, panel, place, holder, tier, out, placing, columns, own, up, down,
+    panel_v, place_v, holder_v, tier_v, sems,
+):
+    pairs = [(panel, panel_v), (place, place_v), (holder, holder_v), (tier, tier_v)]
+    pairs += [(grid, own.at[a]) for a, grid in enumerate((temp, cond, mass))]
     copies = [pltpu.make_async_copy(a, b, sems.at[i]) for i, (a, b) in enumerate(pairs)]
     for copy in copies:
         copy.start()
@@ -67,8 +75,12 @@
     pos, ident, dest = slot_rows(panel_row, place_v[...], holder_row, tier_v[...])
     place_slots(panel_row, pos, dest, holder_row, placing, columns)
     code = (dest * 64 + ident).astype(F32)
-    copies[4].wait()
-    sums = jnp.sum(temp_v[...].reshape(8, 64, 128), axis=1)
+    for a in range(3):
+        copies[4 + a].wait()
+        for k in range(depth(a)):
+            up[3 * a + k] = own[a, 4 - depth(a) + k].astype(BF16)
+            down[3 * a + k] = own[a, k].astype(BF16)
+    sums = jnp.sum(own[0].reshape(8, 64, 128), axis=1)
     lane = iota((8, 128), 1)
     first = jnp.sum(jnp.where(lane < 64, sums, 0.0), axis=1, keepdims=True)
     second = jnp.sum(jnp.where(lane < 64, 0.0, sums), axis=1, keepdims=True)
@@ -80,7 +92,7 @@
 
 
 def power_kernel(
-    far_messages, far_columns, far_warming, far_toggling, far_baseline, far_placing, out,
+    far_messages, far_columns, far_warming, far_toggling, far_baseline, far_placing, _lo, _hi, out,
     messages, columns, warming, toggling, baseline, placing, sent, sems,
 ):
     pairs = [
@@ -260,27 +272,12 @@
         out[288:432, :] = (side[first : first + 144, :] + pltpu.roll(second, 4, 1)).astype(BF16)
 
 
-def depth(a):
-    return 3 if a < 2 else 2
-
-
 def beyond(lo, hi, a, layer):
     if layer < 3:
         k = layer - 3 + depth(a)
         return (lo, 3 * a + k) if k >= 0 else None
     k = layer - 7
     return (hi, 3 * a + k) if k < depth(a) else None
-
-
-def layers_kernel(temp, cond, mass, own, up, down, sems):
-    copies = [pltpu.make_async_copy(a, own.at[i], sems.at[i]) for i, a in enumerate((temp, cond, mass))]
-    for copy in copies:
-        copy.start()
-    for a, copy in enumerate(copies):
-        copy.wait()
-        for k in range(depth(a)):
-            up[3 * a + k] = own[a, 4 - depth(a) + k].astype(BF16)
-            down[3 * a + k] = own[a, k].astype(BF16)
 
 
 def rows_kernel(own, lo, hi, last, first):
@@ -434,16 +431,8 @@
     return lax.ppermute(to_next, axis, up), lax.ppermute(to_last, axis, down)
 
 
-def extended_grids(temp, cond, mass):
-    eight, rows, edge = sds((8, 128, 128), BF16), sds((240, 128), BF16), sds((144, 128), BF16)
-    own, up, down = call(
-        layers_kernel,
-        (sds((3, 4, 128, 128), F32), eight, eight),
-        (temp, cond, mass),
-        scratch=[pltpu.SemaphoreType.DMA((3,))],
-        far=range(3),
-    )
-    lo, hi = exchange(up, down, LAYER)
+def extended_grids(own, lo, hi):
+    rows, edge = sds((240, 128), BF16), sds((144, 128), BF16)
     above, below = exchange(*call(rows_kernel, (rows, rows), (own, lo, hi)), "row")
     wide, to_left, to_right = call(
         gather_kernel, (sds((30, 144, 128), F32), edge, edge), (own, lo, hi, above, below), mib=24
@@ -464,35 +453,37 @@
 
 def shards(temp, cond, mass, toggling, baseline, panel, place, holder, tier, warming):
     row64 = pltpu.VMEM((1, 64), I32)
-    message, placing, columns = call(
+    eight = sds((8, 128, 128), BF16)
+    message, placing, columns, own, up, down = call(
         message_kernel,
-        (sds((64, 128), F32), sds((1024, 64), BF16), sds((64, 128), I32)),
-        (temp, panel.reshape(1, 64), place, holder, tier),
+        (
+            sds((64, 128), F32), sds((1024, 64), BF16), sds((64, 128), I32),
+            sds((3, 4, 128, 128), F32), eight, eight,
+        ),
+        (temp, cond, mass, panel.reshape(1, 64), place, holder, tier),
         mib=60,
-        scratch=[
-            pltpu.VMEM((4, 128, 128), F32), row64, row64, row64,
-            pltpu.VMEM((1, 16), I32), pltpu.SemaphoreType.DMA((5,)),
-        ],
-        far=range(5),
-    )
+        scratch=[row64, row64, row64, pltpu.VMEM((1, 16), I32), pltpu.SemaphoreType.DMA((7,))],
+        far=range(7),
+    )
+    lo, hi = exchange(up, down, LAYER)
     messages = lax.all_to_all(message.reshape(64, 1, 128), CUBE, split_axis=0, concat_axis=0, tiled=True)
     messages = messages.reshape(64, 128)
     send = call(
         power_kernel,
         sds((256, 4736), BF16),
-        (messages, columns, warming, toggling[0], baseline[0], placing),
+        (messages, columns, warming, toggling[0], baseline[0], placing, lo, hi),
         mib=60,
         scratch=[
             pltpu.VMEM((64, 128), F32), pltpu.VMEM((64, 128), I32), pltpu.VMEM((1, 16), F32),
             pltpu.VMEM((64, 4096), BF16), pltpu.VMEM((64, 4096), BF16), pltpu.VMEM((1024, 64), BF16),
             pltpu.VMEM((256, 4736), BF16), pltpu.SemaphoreType.DMA((15,)),
         ],
-        far=range(6),
+        far=range(8),
         far_out=True,
     )
     received = lax.all_to_all(send.reshape(16, 16, 4736), PLANE, split_axis=0, concat_axis=0, tiled=True)
     selector = call(selector_kernel, sds((576, 256), BF16), (messages,))
-    wide, edges, beside = extended_grids(temp, cond, mass)
+    wide, edges, beside = extended_grids(own, lo, hi)
     partial = call(
         combine_kernel, sds((64, 4480), F32), (selector, received.reshape(256, 4736), *edges)
     )

time: 112 us -> 124 us (1.11)
  the two profiles are of different devices: /device:TPU:1 before, /device:TPU:3 now
where the time goes in v5:
time: 124 us; the launch traced here: 123 us
  starting transfers between devices  50.1 us (40%)
  waiting for transfers between devices  30.5 us (25%)
  blocking collectives  22.6 us (18%)
  Pallas kernels  13.5 us (11%)
  local copies, waits for them, and re-layouts  4.78 us (4%)
    ppermute x8, starting transfers between devices, exchange(): return (lax.ppermute(to_next, axis, up), lax.ppermute(to_last, axis, down))  41.7 us
    ppermute x8, waiting for transfers between devices, exchange(): return (lax.ppermute(to_next, axis, up), lax.ppermute(to_last, axis, down))  24 us
    all_to_all x1, blocking collectives, shards(): lax.all_to_all(message.reshape(64, 1, 128), CUBE, split_axis=0, concat_ax...  22.6 us
    pallas_call x9, Pallas kernels, call(): pl.pallas_call(kernel, out_shape=shape, in_specs=[anywhere if i in far el...  13.5 us
    all_to_all x1, waiting for transfers between devices, shards(): lax.all_to_all(partial.astype(jnp.float16).reshape(4, 16, 4480), 'zlo', s...  6.49 us
    all_to_all x1, starting transfers between devices, shards(): lax.all_to_all(send.reshape(16, 16, 4736), PLANE, split_axis=0, concat_ax...  4.86 us
    unnamed x22, local copies, waits for them, and re-layouts  4.78 us
    all_to_all x1, starting transfers between devices, shards(): lax.all_to_all(partial.astype(jnp.float16).reshape(4, 16, 4480), 'zlo', s...  3.61 us
  transfers between devices with their start and end apart: 10, of which 4 were waited for; matrix products, arithmetic and copies ran while one was open for 0% of the time, Pallas kernels for 3%

profile of v5, /device:TPU:3, one launch (start us, length us, event | category | flops | bytes accessed | tf_op | source)
XLA Modules:
  0.0 123.4 jit_solution(10823591166202944566)
XLA Ops:
  0.6 2.4 %shard_map.113 = (f32[64,128]{1,0:T(8,128)}, bf16[1024,64]{1,0:T(8,128)(2,1)}, s32[64,128]{1,0:T(8,128)}, f32[3,4,128,128]{3,2,1,0:T(8,128)}, bf16[8,128,128]{2,...) custom-call(f32[4,128,128]{2,1,0:T(8,128)} %temp.1, f32[4,128,128]{2,1,0:T(8,128)} %cond.1, f32[4,128,128]{2,1,0:T(8,128)} %mass.1, ...), custom_call_target="tpu_custom_call" | custom-call | tf_op jit(solution)/shard_map/pallas_call | solution.py:414
  3.0 9.4 %collective-permute-start = (bf16[8,128,128]{2,1,0:T(8,128)(2,1)}, bf16[8,128,128]{2,1,0:T(8,128)(2,1)S(1)}, u32[]{:S(2)}, u32[]{:S(2)}) collective-permute-start(bf16[8,128,128]{2,1,0:T(8,128)(2,1)} %get-tuple-element.26), channel_id=1, source_target_pairs={{0,1},{1,2},{2,3},{3,4},{4,5},{5,6},{6,7},{8,9},{9,10},{10,11},{11... | collective-permute-start | bytes 786440 | tf_op jit(solution)/shard_map/ppermute | solution.py:431
  12.4 1.9 %collective-permute-start.1 = (bf16[8,128,128]{2,1,0:T(8,128)(2,1)}, bf16[8,128,128]{2,1,0:T(8,128)(2,1)S(1)}, u32[]{:S(2)}, u32[]{:S(2)}) collective-permute-start(bf16[8,128,128]{2,1,0:T(8,128)(2,1)} %get-tuple-element.27), channel_id=1, source_target_pairs={{1,0},{2,1},{3,2},{4,3},{5,4},{6,5},{7,6},{9,8},{10,9},{11,10},{12... | collective-permute-start | bytes 786440 | tf_op jit(solution)/shard_map/ppermute | solution.py:431
  14.3 22.6 %all_to_all.15 = f32[64,1,128]{2,1,0:T(1,128)} all-to-all(f32[64,1,128]{2,1,0:T(1,128)} %bitcast.19), channel_id=1, replica_groups=mesh['row'=4,'zlo'=4,'y'=4,'zhi'=4,'core'=2] {'row','zlo','y'}, dimensions={0} | all-to-all | bytes 65536 | tf_op jit(solution)/shard_map/all_to_all | solution.py:469
  37.0 0.7 copy-done.3
  37.7 0.1 copy-done.5
  37.8 3.2 %shard_map.115 = bf16[256,4736]{1,0:T(8,128)(2,1)} custom-call(f32[64,128]{1,0:T(8,128)} %bitcast.13, s32[64,128]{1,0:T(8,128)} %get-tuple-element.24.far_columns, f32[1,16]{1,0:T(1,128)} %far_warming.1, bf16[64,4096]{1,0:T(8,128)(2,1)} %bitcast.16, bf16[64,4096]{1,0:T(8,128)(2,1)} %bitcast.17, bf16[1024,64]{1,0:T(8,128)(2,1)} %get-tuple-element.25.far_placing, ...), custom_call_target="tpu_custom_call" | custom-call | tf_op jit(solution)/shard_map/pallas_call | solution.py:414
  41.0 0.0 copy-start.4
  41.0 4.9 %all-to-all-start.1 = ((bf16[16,16,4736]{2,1,0:T(8,128)(2,1)}), bf16[16,16,4736]{2,1,0:T(8,128)(2,1)S(1)}, u32[]{:S(2)}, u32[]{:S(2)}) async-start(bf16[16,16,4736]{2,1,0:T(8,128)(2,1)} %bitcast.15), calls=%async_computation.1 | async-start | bytes 4849664 | tf_op jit(solution)/shard_map/all_to_all | solution.py:484
  45.9 0.9 copy-done.6
  46.8 3.2 %collective-permute-start.2 = (bf16[240,128]{1,0:T(8,128)(2,1)S(1)}, bf16[240,128]{1,0:T(8,128)(2,1)S(1)}, u32[]{:S(2)}, u32[]{:S(2)}) collective-permute-start(bf16[240,128]{1,0:T(8,128)(2,1)S(1)} %get-tuple-element.29), channel_id=1, source_target_pairs={{0,128},{128,256},{256,384},{1,129},{129,257},{257,385},{2,130},{1... | collective-permute-start | bytes 184328 | tf_op jit(solution)/shard_map/ppermute | solution.py:431
  50.1 2.2 %collective-permute-start.3 = (bf16[240,128]{1,0:T(8,128)(2,1)S(1)}, bf16[240,128]{1,0:T(8,128)(2,1)S(1)}, u32[]{:S(2)}, u32[]{:S(2)}) collective-permute-start(bf16[240,128]{1,0:T(8,128)(2,1)S(1)} %get-tuple-element.30), channel_id=1, source_target_pairs={{128,0},{256,128},{384,256},{129,1},{257,129},{385,257},{130,2},{2... | collective-permute-start | bytes 184328 | tf_op jit(solution)/shard_map/ppermute | solution.py:431
  52.3 0.7 shard_map.114.selector
  53.0 0.7 copy-done.8
  53.8 14.7 %collective-permute-done.2.above = bf16[240,128]{1,0:T(8,128)(2,1)S(1)} collective-permute-done((bf16[240,128]{1,0:T(8,128)(2,1)S(1)}, bf16[240,128]{1,0:T(8,128)(2,1)S(1)}, u32[]{:S(2)}, u32[]{:S(2)}) %collective-permute-start.2) | collective-permute-done | bytes 61472 | tf_op jit(solution)/shard_map/ppermute | solution.py:431
  68.5 1.5 %collective-permute-done.3.below = bf16[240,128]{1,0:T(8,128)(2,1)S(1)} collective-permute-done((bf16[240,128]{1,0:T(8,128)(2,1)S(1)}, bf16[240,128]{1,0:T(8,128)(2,1)S(1)}, u32[]{:S(2)}, u32[]{:S(2)}) %collective-permute-start.3) | collective-permute-done | bytes 61472 | tf_op jit(solution)/shard_map/ppermute | solution.py:431
  70.0 0.6 shard_map.117
  70.7 1.4 %copy-done = f32[30,144,128]{2,1,0:T(8,128)} copy-done((f32[30,144,128]{2,1,0:T(8,128)}, f32[30,144,128]{2,1,0:T(8,128)S(1)}, u32[]{:S(2)}) %copy-start) | copy-done | bytes 2211864
  72.0 1.0 copy-done.9
  73.0 0.6 shard_map.118
  73.6 0.9 convert_element_type.6
  74.4 3.6 %all-to-all-start.2 = ((f16[4,16,4480]{2,1,0:T(8,128)(2,1)}), f16[4,16,4480]{2,1,0:T(8,128)(2,1)S(1)}, u32[]{:S(2)}, u32[]{:S(2)}) async-start(f16[4,16,4480]{2,1,0:T(8,128)(2,1)} %bitcast.8), calls=%async_computation.2 | async-start | bytes 1146880 | tf_op jit(solution)/shard_map/all_to_all | solution.py:490
  78.1 1.3 %collective-permute-start.5 = (bf16[144,128]{1,0:T(8,128)(2,1)S(1)}, bf16[144,128]{1,0:T(8,128)(2,1)S(1)}, u32[]{:S(2)}, u32[]{:S(2)}) collective-permute-start(bf16[144,128]{1,0:T(8,128)(2,1)S(1)} %get-tuple-element.31._to_left), channel_id=1, source_target_pairs={{8,0},{16,8},{24,16},{32,24},{40,32},{48,40},{56,48},{64,56},{72,6... | collective-permute-start | bytes 110600 | tf_op jit(solution)/shard_map/ppermute | solution.py:431
  79.4 4.0 %collective-permute-start.4 = (bf16[144,128]{1,0:T(8,128)(2,1)S(1)}, bf16[144,128]{1,0:T(8,128)(2,1)S(1)}, u32[]{:S(2)}, u32[]{:S(2)}) collective-permute-start(bf16[144,128]{1,0:T(8,128)(2,1)S(1)} %get-tuple-element.32._to_right), channel_id=1, source_target_pairs={{0,8},{8,16},{16,24},{24,32},{32,40},{40,48},{48,56},{56,64},{64,7... | collective-permute-start | bytes 110600 | tf_op jit(solution)/shard_map/ppermute | solution.py:431
  83.4 6.5 %all-to-all-done.2 = f16[4,16,4480]{2,1,0:T(8,128)(2,1)S(1)} async-done(((f16[4,16,4480]{2,1,0:T(8,128)(2,1)}), f16[4,16,4480]{2,1,0:T(8,128)(2,1)S(1)}, u32[]{:S(2)}, u32[]{:S(2)}) %all-to-all-start.2) | async-done | bytes 573472 | tf_op jit(solution)/shard_map/all_to_all | solution.py:490
  89.8 0.1 convert_reduce_fusion.whole
  89.9 1.4 %shard_map.119 = (f32[512,128]{1,0:T(8,128)}, f32[576,128]{1,0:T(8,128)S(1)}, f32[576,128]{1,0:T(8,128)S(1)}, bf16[432,128]{1,0:T(8,128)(2,1)S(1)}, bf16[432,128]{1,0:T(8,128)(2,1)S(1)}) custom-call(f32[16,4480]{1,0:T(8,128)S(1)} %convert_reduce_fusion.whole, bf16[144,128]{1,0:T(8,128)(2,1)S(1)} %collective-permute-done.4._left.from_left, ...), custom_call_target="tpu_custom_call" | custom-call | tf_op jit(solution)/shard_map/pallas_call | solution.py:414
  91.3 17.8 %collective-permute-start.6 = (bf16[432,128]{1,0:T(8,128)(2,1)S(1)}, bf16[432,128]{1,0:T(8,128)(2,1)S(1)}, u32[]{:S(2)}, u32[]{:S(2)}) collective-permute-start(bf16[432,128]{1,0:T(8,128)(2,1)S(1)} %get-tuple-element.35), channel_id=1, source_target_pairs={{0,1},{1,2},{2,3},{3,4},{4,5},{5,6},{6,7},{8,9},{9,10},{10,11},{11... | collective-permute-start | bytes 331784 | tf_op jit(solution)/shard_map/ppermute | solution.py:431
  109.1 1.9 %collective-permute-start.7 = (bf16[432,128]{1,0:T(8,128)(2,1)S(1)}, bf16[432,128]{1,0:T(8,128)(2,1)S(1)}, u32[]{:S(2)}, u32[]{:S(2)}) collective-permute-start(bf16[432,128]{1,0:T(8,128)(2,1)S(1)} %get-tuple-element.36), channel_id=1, source_target_pairs={{1,0},{2,1},{3,2},{4,3},{5,4},{6,5},{7,6},{9,8},{10,9},{11,10},{12... | collective-permute-start | bytes 331784 | tf_op jit(solution)/shard_map/ppermute | solution.py:431
  111.0 2.6 %shard_map.120 = (f32[9,144,256]{2,1,0:T(8,128)S(1)}, f32[8,144,256]{2,1,0:T(8,128)S(1)}, f32[8,144,256]{2,1,0:T(8,128)S(1)}, f32[8,144,256]{2,1,0:T(8,128)S(1)}, f32[8,144,256]{2,1,0:T(8,128)S(1)}) custom-call(f32[30,144,128]{2,1,0:T(8,128)S(1)} %copy-done.1, bf16[144,128]{1,0:T(8,128)(2,1)S(1)} %collective-permute-done.4._left.from_left, ...), custom_call_target="tpu_custom_call" | custom-call | tf_op jit(solution)/shard_map/pallas_call | solution.py:414
  113.7 7.8 %collective-permute-done.7.hi = bf16[432,128]{1,0:T(8,128)(2,1)S(1)} collective-permute-done((bf16[432,128]{1,0:T(8,128)(2,1)S(1)}, bf16[432,128]{1,0:T(8,128)(2,1)S(1)}, u32[]{:S(2)}, u32[]{:S(2)}) %collective-permute-start.7) | collective-permute-done | bytes 110624 | tf_op jit(solution)/shard_map/ppermute | solution.py:431
  121.4 1.9 %shard_map.121 = f32[512,128]{1,0:T(8,128)} custom-call(f32[576,128]{1,0:T(8,128)S(1)} %get-tuple-element.33.main, f32[576,128]{1,0:T(8,128)S(1)} %get-tuple-element.34.side, bf16[432,128]{1,0:T(8,128)(2,1)S(1)} %collective-permute-done.6.lo, bf16[432,128]{1,0:T(8,128)(2,1)S(1)} %collective-permute-done.7.hi, f32[30,144,128]{2,1,0:T(8,128)S(1)} %copy-done.1, ...), custom_call_target="tpu_custom_call" | custom-call | tf_op jit(solution)/shard_map/pallas_call | solution.py:414
  (22 shorter events, 0.1 us)
Async XLA Ops:
  3.0 34.0 %collective-permute-start = (bf16[8,128,128]{2,1,0:T(8,128)(2,1)}, bf16[8,128,128]{2,1,0:T(8,128)(2,1)S(1)}, u32[]{:S(2)}, u32[]{:S(2)}) collective-permute-start(bf16[8,128,128]{2,1,0:T(8,128)(2,1)} %get-tuple-element.26), channel_id=1, source_target_pairs={{0,1},{1,2},{2,3},{3,4},{4,5},{5,6},{6,7},{8,9},{9,10},{10,11},{11... | collective-permute-start | bytes 786440 | tf_op jit(solution)/shard_map/ppermute | solution.py:431
  12.4 24.6 %collective-permute-start.1 = (bf16[8,128,128]{2,1,0:T(8,128)(2,1)}, bf16[8,128,128]{2,1,0:T(8,128)(2,1)S(1)}, u32[]{:S(2)}, u32[]{:S(2)}) collective-permute-start(bf16[8,128,128]{2,1,0:T(8,128)(2,1)} %get-tuple-element.27), channel_id=1, source_target_pairs={{1,0},{2,1},{3,2},{4,3},{5,4},{6,5},{7,6},{9,8},{10,9},{11,10},{12... | collective-permute-start | bytes 786440 | tf_op jit(solution)/shard_map/ppermute | solution.py:431
  37.0 0.7 copy-start.3
  37.0 0.8 copy-start.5
  41.0 4.9 %copy-start.2 = (f32[3,4,128,128]{3,2,1,0:T(8,128)S(1)}, f32[3,4,128,128]{3,2,1,0:T(8,128)}, u32[]{:S(2)}) copy-start(f32[3,4,128,128]{3,2,1,0:T(8,128)} %get-tuple-element.28.own) | copy-start | bytes 2359300
  41.0 4.9 %copy-start.4 = (bf16[8,128,128]{2,1,0:T(8,128)(2,1)S(1)}, bf16[8,128,128]{2,1,0:T(8,128)(2,1)}, u32[]{:S(2)}) copy-start(bf16[8,128,128]{2,1,0:T(8,128)(2,1)} %copy-done.3) | copy-start | bytes 786436
  41.0 31.0 %all-to-all-start.1 = ((bf16[16,16,4736]{2,1,0:T(8,128)(2,1)}), bf16[16,16,4736]{2,1,0:T(8,128)(2,1)S(1)}, u32[]{:S(2)}, u32[]{:S(2)}) async-start(bf16[16,16,4736]{2,1,0:T(8,128)(2,1)} %bitcast.15), calls=%async_computation.1 | async-start | bytes 4849664 | tf_op jit(solution)/shard_map/all_to_all | solution.py:484
  45.9 1.0 copy-start.6
  46.8 5.5 %copy-start.10 = (f32[64,1,128]{2,1,0:T(1,128)S(1)}, f32[64,1,128]{2,1,0:T(1,128)}, u32[]{:S(2)}) copy-start(f32[64,1,128]{2,1,0:T(1,128)} %all_to_all.15) | copy-start | bytes 98308
  46.8 23.2 %copy-start.7 = (bf16[8,128,128]{2,1,0:T(8,128)(2,1)S(1)}, bf16[8,128,128]{2,1,0:T(8,128)(2,1)}, u32[]{:S(2)}) copy-start(bf16[8,128,128]{2,1,0:T(8,128)(2,1)} %copy-done.5) | copy-start | bytes 786436
  46.8 21.6 %collective-permute-start.2 = (bf16[240,128]{1,0:T(8,128)(2,1)S(1)}, bf16[240,128]{1,0:T(8,128)(2,1)S(1)}, u32[]{:S(2)}, u32[]{:S(2)}) collective-permute-start(bf16[240,128]{1,0:T(8,128)(2,1)S(1)} %get-tuple-element.29), channel_id=1, source_target_pairs={{0,128},{128,256},{256,384},{1,129},{129,257},{257,385},{2,130},{1... | collective-permute-start | bytes 184328 | tf_op jit(solution)/shard_map/ppermute | solution.py:431
  50.1 19.9 %collective-permute-start.3 = (bf16[240,128]{1,0:T(8,128)(2,1)S(1)}, bf16[240,128]{1,0:T(8,128)(2,1)S(1)}, u32[]{:S(2)}, u32[]{:S(2)}) collective-permute-start(bf16[240,128]{1,0:T(8,128)(2,1)S(1)} %get-tuple-element.30), channel_id=1, source_target_pairs={{128,0},{256,128},{384,256},{129,1},{257,129},{385,257},{130,2},{2... | collective-permute-start | bytes 184328 | tf_op jit(solution)/shard_map/ppermute | solution.py:431
  53.0 0.7 copy-start.8
  70.6 1.4 %copy-start = (f32[30,144,128]{2,1,0:T(8,128)}, f32[30,144,128]{2,1,0:T(8,128)S(1)}, u32[]{:S(2)}) copy-start(f32[30,144,128]{2,1,0:T(8,128)S(1)} %get-tuple-element.37.grids) | copy-start | bytes 6635524
  72.0 1.0 copy-start.9
  74.4 36.6 %copy-start.1 = (f32[30,144,128]{2,1,0:T(8,128)S(1)}, f32[30,144,128]{2,1,0:T(8,128)}, u32[]{:S(2)}) copy-start(f32[30,144,128]{2,1,0:T(8,128)} %copy-done) | copy-start | bytes 6635524
  74.4 15.4 %all-to-all-start.2 = ((f16[4,16,4480]{2,1,0:T(8,128)(2,1)}), f16[4,16,4480]{2,1,0:T(8,128)(2,1)S(1)}, u32[]{:S(2)}, u32[]{:S(2)}) async-start(f16[4,16,4480]{2,1,0:T(8,128)(2,1)} %bitcast.8), calls=%async_computation.2 | async-start | bytes 1146880 | tf_op jit(solution)/shard_map/all_to_all | solution.py:490
  78.1 11.9 %collective-permute-start.5 = (bf16[144,128]{1,0:T(8,128)(2,1)S(1)}, bf16[144,128]{1,0:T(8,128)(2,1)S(1)}, u32[]{:S(2)}, u32[]{:S(2)}) collective-permute-start(bf16[144,128]{1,0:T(8,128)(2,1)S(1)} %get-tuple-element.31._to_left), channel_id=1, source_target_pairs={{8,0},{16,8},{24,16},{32,24},{40,32},{48,40},{56,48},{64,56},{72,6... | collective-permute-start | bytes 110600 | tf_op jit(solution)/shard_map/ppermute | solution.py:431
  79.4 10.6 %collective-permute-start.4 = (bf16[144,128]{1,0:T(8,128)(2,1)S(1)}, bf16[144,128]{1,0:T(8,128)(2,1)S(1)}, u32[]{:S(2)}, u32[]{:S(2)}) collective-permute-start(bf16[144,128]{1,0:T(8,128)(2,1)S(1)} %get-tuple-element.32._to_right), channel_id=1, source_target_pairs={{0,8},{8,16},{16,24},{24,32},{32,40},{40,48},{48,56},{56,64},{64,7... | collective-permute-start | bytes 110600 | tf_op jit(solution)/shard_map/ppermute | solution.py:431
  91.3 22.3 %collective-permute-start.6 = (bf16[432,128]{1,0:T(8,128)(2,1)S(1)}, bf16[432,128]{1,0:T(8,128)(2,1)S(1)}, u32[]{:S(2)}, u32[]{:S(2)}) collective-permute-start(bf16[432,128]{1,0:T(8,128)(2,1)S(1)} %get-tuple-element.35), channel_id=1, source_target_pairs={{0,1},{1,2},{2,3},{3,4},{4,5},{5,6},{6,7},{8,9},{9,10},{10,11},{11... | collective-permute-start | bytes 331784 | tf_op jit(solution)/shard_map/ppermute | solution.py:431
  109.1 12.3 %collective-permute-start.7 = (bf16[432,128]{1,0:T(8,128)(2,1)S(1)}, bf16[432,128]{1,0:T(8,128)(2,1)S(1)}, u32[]{:S(2)}, u32[]{:S(2)}) collective-permute-start(bf16[432,128]{1,0:T(8,128)(2,1)S(1)} %get-tuple-element.36), channel_id=1, source_target_pairs={{1,0},{2,1},{3,2},{4,3},{5,4},{6,5},{7,6},{9,8},{10,9},{11,10},{12... | collective-permute-start | bytes 331784 | tf_op jit(solution)/shard_map/ppermute | solution.py:431

commit v6 on v4

--- a/solution.py
+++ b/solution.py
@@ -153,7 +153,7 @@
         copy.wait()
 
 
-def selector_kernel(messages, out):
+def selector_kernel(messages, _last, _first, out):
     x, y = lax.axis_index("row"), lax.axis_index("y")
     plane = lax.axis_index("zlo")
     code = jnp.concatenate([messages[pl.ds(r * 16 + plane * 4, 4), :] for r in range(4)], axis=0)
@@ -189,7 +189,7 @@
         put(5 + k, ids, z * 16 + layer)
 
 
-def combine_kernel(selector, received, _to_left, _to_right, out):
+def combine_kernel(selector, received, out):
     def add(k, start, width):
         return jnp.dot(
             selector[k * 64 : (k + 1) * 64, :],
@@ -208,7 +208,7 @@
     out[:, 4352:4480] = corners
 
 
-def unpack_kernel(whole, _left, _right, density, main, side, up, down, turned):
+def unpack_kernel(whole, _to_left, _to_right, density, main, side, up, down, turned):
     for k in range(32):
         turned[k * 16 : (k + 1) * 16, :] = whole[:, k * 128 : (k + 1) * 128]
     low = iota((32, 128), 1) < 64
@@ -444,11 +444,12 @@
         far=range(3),
     )
     lo, hi = exchange(up, down, LAYER)
-    above, below = exchange(*call(rows_kernel, (rows, rows), (own, lo, hi)), "row")
+    ends = call(rows_kernel, (rows, rows), (own, lo, hi))
+    above, below = exchange(*ends, "row")
     wide, to_left, to_right = call(
         gather_kernel, (sds((30, 144, 128), F32), edge, edge), (own, lo, hi, above, below), mib=24
     )
-    return wide, (to_left, to_right), exchange(to_right, to_left, COL)
+    return wide, ends, (to_left, to_right), exchange(to_right, to_left, COL)
 
 
 def operator(wide, from_left, from_right):
@@ -491,10 +492,10 @@
         far_out=True,
     )
     received = lax.all_to_all(send.reshape(16, 16, 4736), PLANE, split_axis=0, concat_axis=0, tiled=True)
-    selector = call(selector_kernel, sds((576, 256), BF16), (messages,))
-    wide, edges, beside = extended_grids(temp, cond, mass)
+    wide, ends, edges, beside = extended_grids(temp, cond, mass)
+    selector = call(selector_kernel, sds((576, 256), BF16), (messages, *ends))
     partial = call(
-        combine_kernel, sds((64, 4480), F32), (selector, received.reshape(256, 4736), *edges)
+        combine_kernel, sds((64, 4480), F32), (selector, received.reshape(256, 4736))
     )
     parts = lax.all_to_all(
         partial.astype(jnp.float16).reshape(4, 16, 4480), "zlo", split_axis=0, concat_axis=0, tiled=True
@@ -504,7 +505,7 @@
     density, main, side, up, down = call(
         unpack_kernel,
         (sds((512, 128), F32), block, block, strip, strip),
-        (jnp.sum(parts.astype(F32), axis=0), *beside),
+        (jnp.sum(parts.astype(F32), axis=0), *edges),
         scratch=[pltpu.VMEM((512, 128), F32)],
     )
     lo, hi = exchange(up, down, LAYER)

time: 112 us -> 114 us (1.018)
  the two profiles are of different devices: /device:TPU:1 before, /device:TPU:33 now
where the time goes in v6:
time: 114 us; the launch traced here: 113 us
  starting transfers between devices  46.4 us (41%)
  waiting for transfers between devices  26.6 us (23%)
  blocking collectives  19.2 us (17%)
  Pallas kernels  13 us (11%)
  local copies, waits for them, and re-layouts  4.76 us (4%)
  other arithmetic  2.05 us (2%)
    ppermute x8, starting transfers between devices, exchange(): return (lax.ppermute(to_next, axis, up), lax.ppermute(to_last, axis, down))  34.8 us
    ppermute x8, waiting for transfers between devices, exchange(): return (lax.ppermute(to_next, axis, up), lax.ppermute(to_last, axis, down))  24.5 us
    all_to_all x1, blocking collectives, shards(): lax.all_to_all(message.reshape(64, 1, 128), CUBE, split_axis=0, concat_ax...  19.2 us
    pallas_call x10, Pallas kernels, call(): pl.pallas_call(kernel, out_shape=shape, in_specs=[anywhere if i in far el...  13 us
    all_to_all x1, starting transfers between devices, shards(): lax.all_to_all(partial.astype(jnp.float16).reshape(4, 16, 4480), 'zlo', s...  7.67 us
    unnamed x24, local copies, waits for them, and re-layouts  4.76 us
    all_to_all x1, starting transfers between devices, shards(): lax.all_to_all(send.reshape(16, 16, 4736), PLANE, split_axis=0, concat_ax...  3.87 us
  transfers between devices with their start and end apart: 10, of which 5 were waited for; matrix products, arithmetic and copies ran while one was open for 0% of the time, Pallas kernels for 4%

profile of v6, /device:TPU:33, one launch (start us, length us, event | category | flops | bytes accessed | tf_op | source)
XLA Modules:
  0.0 112.9 jit_solution(6695800268876018009)
XLA Ops:
  0.6 1.8 %shard_map.113 = (f32[64,128]{1,0:T(8,128)}, bf16[1024,64]{1,0:T(8,128)(2,1)}, s32[64,128]{1,0:T(8,128)}) custom-call(f32[4,128,128]{2,1,0:T(8,128)} %temp.3, s32[1,64]{1,0:T(1,128)} %bitcast.20, s32[1,64]{1,0:T(1,128)} %place.1, s32[1,64]{1,0:T(1,128)} %holder.1, s32[1,16]{1,0:T(1,128)} %tier.1), custom_call_target="tpu_custom_call" | custom-call | tf_op jit(solution)/shard_map/pallas_call | solution.py:417
  2.4 19.2 %all_to_all.15 = f32[64,1,128]{2,1,0:T(1,128)} all-to-all(f32[64,1,128]{2,1,0:T(1,128)} %bitcast.19), channel_id=1, replica_groups=mesh['row'=4,'zlo'=4,'y'=4,'zhi'=4,'core'=2] {'row','zlo','y'}, dimensions={0} | all-to-all | bytes 65536 | tf_op jit(solution)/shard_map/all_to_all | solution.py:479
  21.6 3.2 %shard_map.117 = bf16[256,4736]{1,0:T(8,128)(2,1)} custom-call(f32[64,128]{1,0:T(8,128)} %bitcast.13, s32[64,128]{1,0:T(8,128)} %get-tuple-element.29.far_columns, f32[1,16]{1,0:T(1,128)} %far_warming.1, bf16[64,4096]{1,0:T(8,128)(2,1)} %bitcast.16, bf16[64,4096]{1,0:T(8,128)(2,1)} %bitcast.17, bf16[1024,64]{1,0:T(8,128)(2,1)} %get-tuple-element.30.far_placing), custom_call_target="tpu_custom_call" | custom-call | tf_op jit(solution)/shard_map/pallas_call | solution.py:417
  24.8 3.9 %all-to-all-start.1 = ((bf16[16,16,4736]{2,1,0:T(8,128)(2,1)}), bf16[16,16,4736]{2,1,0:T(8,128)(2,1)S(1)}, u32[]{:S(2)}, u32[]{:S(2)}) async-start(bf16[16,16,4736]{2,1,0:T(8,128)(2,1)} %bitcast.15), calls=%async_computation.1 | async-start | bytes 4849664 | tf_op jit(solution)/shard_map/all_to_all | solution.py:494
  28.7 0.9 copy-done.6
  29.7 0.9 copy-done.7
  30.7 11.0 %collective-permute-start = (bf16[8,128,128]{2,1,0:T(8,128)(2,1)S(1)}, bf16[8,128,128]{2,1,0:T(8,128)(2,1)S(1)}, u32[]{:S(2)}, u32[]{:S(2)}) collective-permute-start(bf16[8,128,128]{2,1,0:T(8,128)(2,1)S(1)} %get-tuple-element.25), channel_id=1, source_target_pairs={{0,1},{1,2},{2,3},{3,4},{4,5},{5,6},{6,7},{8,9},{9,10},{10,11},{11... | collective-permute-start | bytes 786440 | tf_op jit(solution)/shard_map/ppermute | solution.py:434
  41.7 1.9 %collective-permute-start.1 = (bf16[8,128,128]{2,1,0:T(8,128)(2,1)S(1)}, bf16[8,128,128]{2,1,0:T(8,128)(2,1)S(1)}, u32[]{:S(2)}, u32[]{:S(2)}) collective-permute-start(bf16[8,128,128]{2,1,0:T(8,128)(2,1)S(1)} %get-tuple-element.26), channel_id=1, source_target_pairs={{1,0},{2,1},{3,2},{4,3},{5,4},{6,5},{7,6},{9,8},{10,9},{11,10},{12... | collective-permute-start | bytes 786440 | tf_op jit(solution)/shard_map/ppermute | solution.py:434
  43.6 4.2 %collective-permute-done.lo = bf16[8,128,128]{2,1,0:T(8,128)(2,1)S(1)} collective-permute-done((bf16[8,128,128]{2,1,0:T(8,128)(2,1)S(1)}, bf16[8,128,128]{2,1,0:T(8,128)(2,1)S(1)}, u32[]{:S(2)}, u32[]{:S(2)}) %collective-permute-start) | collective-permute-done | bytes 262176 | tf_op jit(solution)/shard_map/ppermute | solution.py:434
  47.9 11.4 %collective-permute-done.1.hi = bf16[8,128,128]{2,1,0:T(8,128)(2,1)S(1)} collective-permute-done((bf16[8,128,128]{2,1,0:T(8,128)(2,1)S(1)}, bf16[8,128,128]{2,1,0:T(8,128)(2,1)S(1)}, u32[]{:S(2)}, u32[]{:S(2)}) %collective-permute-start.1) | collective-permute-done | bytes 262176 | tf_op jit(solution)/shard_map/ppermute | solution.py:434
  59.3 0.7 copy-done.3
  59.9 0.7 shard_map.116.selector
  60.7 0.6 copy-done.8
  61.3 0.6 copy-done.10
  61.9 0.6 shard_map.118
  62.5 0.9 convert_element_type.6
  63.4 7.7 %all-to-all-start.2 = ((f16[4,16,4480]{2,1,0:T(8,128)(2,1)}), f16[4,16,4480]{2,1,0:T(8,128)(2,1)}, u32[]{:S(2)}, u32[]{:S(2)}) async-start(f16[4,16,4480]{2,1,0:T(8,128)(2,1)} %bitcast.8), calls=%async_computation.2 | async-start | bytes 1146880 | tf_op jit(solution)/shard_map/all_to_all | solution.py:500
  71.1 3.4 %collective-permute-start.2 = (bf16[240,128]{1,0:T(8,128)(2,1)S(1)}, bf16[240,128]{1,0:T(8,128)(2,1)S(1)}, u32[]{:S(2)}, u32[]{:S(2)}) collective-permute-start(bf16[240,128]{1,0:T(8,128)(2,1)S(1)} %copy-done.11), channel_id=1, source_target_pairs={{0,128},{128,256},{256,384},{1,129},{129,257},{257,385},{2,130},{1... | collective-permute-start | bytes 184328 | tf_op jit(solution)/shard_map/ppermute | solution.py:434
  74.5 1.3 %collective-permute-start.3 = (bf16[240,128]{1,0:T(8,128)(2,1)S(1)}, bf16[240,128]{1,0:T(8,128)(2,1)S(1)}, u32[]{:S(2)}, u32[]{:S(2)}) collective-permute-start(bf16[240,128]{1,0:T(8,128)(2,1)S(1)} %copy-done.9), channel_id=1, source_target_pairs={{128,0},{256,128},{384,256},{129,1},{257,129},{385,257},{130,2},{2... | collective-permute-start | bytes 184328 | tf_op jit(solution)/shard_map/ppermute | solution.py:434
  75.8 4.1 %collective-permute-done.3.below = bf16[240,128]{1,0:T(8,128)(2,1)S(1)} collective-permute-done((bf16[240,128]{1,0:T(8,128)(2,1)S(1)}, bf16[240,128]{1,0:T(8,128)(2,1)S(1)}, u32[]{:S(2)}, u32[]{:S(2)}) %collective-permute-start.3) | collective-permute-done | bytes 61472 | tf_op jit(solution)/shard_map/ppermute | solution.py:434
  79.9 0.9 copy-done.4
  80.9 0.6 shard_map.119
  81.5 2.1 %all-to-all-done.2 = f16[4,16,4480]{2,1,0:T(8,128)(2,1)} async-done(((f16[4,16,4480]{2,1,0:T(8,128)(2,1)}), f16[4,16,4480]{2,1,0:T(8,128)(2,1)}, u32[]{:S(2)}, u32[]{:S(2)}) %all-to-all-start.2) | async-done | bytes 573472 | tf_op jit(solution)/shard_map/all_to_all | solution.py:500
  83.6 1.2 %convert_reduce_fusion.whole = f32[16,4480]{1,0:T(8,128)S(1)} fusion(f16[4,16,4480]{2,1,0:T(8,128)(2,1)} %all-to-all-done.2), kind=kLoop, calls=%fused_computation | loop fusion | flops 501760 | bytes 860160 | tf_op jit(solution)/shard_map/reduce_sum | solution.py:508
  84.8 1.4 %shard_map.120 = (f32[512,128]{1,0:T(8,128)}, f32[576,128]{1,0:T(8,128)S(1)}, f32[576,128]{1,0:T(8,128)S(1)}, bf16[432,128]{1,0:T(8,128)(2,1)S(1)}, bf16[432,128]{1,0:T(8,128)(2,1)S(1)}) custom-call(f32[16,4480]{1,0:T(8,128)S(1)} %convert_reduce_fusion.whole, bf16[144,128]{1,0:T(8,128)(2,1)S(1)} %get-tuple-element.31._to_left, ...), custom_call_target="tpu_custom_call" | custom-call | tf_op jit(solution)/shard_map/pallas_call | solution.py:417
  86.1 7.3 %collective-permute-start.4 = (bf16[432,128]{1,0:T(8,128)(2,1)S(1)}, bf16[432,128]{1,0:T(8,128)(2,1)S(1)}, u32[]{:S(2)}, u32[]{:S(2)}) collective-permute-start(bf16[432,128]{1,0:T(8,128)(2,1)S(1)} %get-tuple-element.35), channel_id=1, source_target_pairs={{0,1},{1,2},{2,3},{3,4},{4,5},{5,6},{6,7},{8,9},{9,10},{10,11},{11... | collective-permute-start | bytes 331784 | tf_op jit(solution)/shard_map/ppermute | solution.py:434
  93.4 1.9 %collective-permute-start.5 = (bf16[432,128]{1,0:T(8,128)(2,1)S(1)}, bf16[432,128]{1,0:T(8,128)(2,1)S(1)}, u32[]{:S(2)}, u32[]{:S(2)}) collective-permute-start(bf16[432,128]{1,0:T(8,128)(2,1)S(1)} %get-tuple-element.36), channel_id=1, source_target_pairs={{1,0},{2,1},{3,2},{4,3},{5,4},{6,5},{7,6},{9,8},{10,9},{11,10},{12... | collective-permute-start | bytes 331784 | tf_op jit(solution)/shard_map/ppermute | solution.py:434
  95.4 6.1 %collective-permute-start.7 = (bf16[144,128]{1,0:T(8,128)(2,1)S(1)}, bf16[144,128]{1,0:T(8,128)(2,1)S(1)}, u32[]{:S(2)}, u32[]{:S(2)}) collective-permute-start(bf16[144,128]{1,0:T(8,128)(2,1)S(1)} %get-tuple-element.31._to_left), channel_id=1, source_target_pairs={{8,0},{16,8},{24,16},{32,24},{40,32},{48,40},{56,48},{64,56},{72,6... | collective-permute-start | bytes 110600 | tf_op jit(solution)/shard_map/ppermute | solution.py:434
  101.5 1.9 %collective-permute-start.6 = (bf16[144,128]{1,0:T(8,128)(2,1)S(1)}, bf16[144,128]{1,0:T(8,128)(2,1)S(1)}, u32[]{:S(2)}, u32[]{:S(2)}) collective-permute-start(bf16[144,128]{1,0:T(8,128)(2,1)S(1)} %get-tuple-element.32._to_right), channel_id=1, source_target_pairs={{0,8},{8,16},{16,24},{24,32},{32,40},{40,48},{48,56},{56,64},{64,7... | collective-permute-start | bytes 110600 | tf_op jit(solution)/shard_map/ppermute | solution.py:434
  103.4 4.9 %collective-permute-done.6.from_left = bf16[144,128]{1,0:T(8,128)(2,1)S(1)} collective-permute-done((bf16[144,128]{1,0:T(8,128)(2,1)S(1)}, bf16[144,128]{1,0:T(8,128)(2,1)S(1)}, u32[]{:S(2)}, u32[]{:S(2)}) %collective-permute-start.6) | collective-permute-done | bytes 36896 | tf_op jit(solution)/shard_map/ppermute | solution.py:434
  108.3 2.6 %shard_map.121 = (f32[9,144,256]{2,1,0:T(8,128)S(1)}, f32[8,144,256]{2,1,0:T(8,128)S(1)}, f32[8,144,256]{2,1,0:T(8,128)S(1)}, f32[8,144,256]{2,1,0:T(8,128)S(1)}, f32[8,144,256]{2,1,0:T(8,128)S(1)}) custom-call(f32[30,144,128]{2,1,0:T(8,128)S(1)} %get-tuple-element.37.grids, bf16[144,128]{1,0:T(8,128)(2,1)S(1)} %collective-permute-done.6.from_left, ...), custom_call_target="tpu_custom_call" | custom-call | tf_op jit(solution)/shard_map/pallas_call | solution.py:417
  110.9 1.9 %shard_map.122 = f32[512,128]{1,0:T(8,128)} custom-call(f32[576,128]{1,0:T(8,128)S(1)} %get-tuple-element.33.main, f32[576,128]{1,0:T(8,128)S(1)} %get-tuple-element.34.side, bf16[432,128]{1,0:T(8,128)(2,1)S(1)} %collective-permute-done.4.lo, bf16[432,128]{1,0:T(8,128)(2,1)S(1)} %collective-permute-done.5.hi, f32[30,144,128]{2,1,0:T(8,128)S(1)} %get-tuple-element.37.grids, ...), custom_call_target="tpu_custom_call" | custom-call | tf_op jit(solution)/shard_map/pallas_call | solution.py:417
  (25 shorter events, 0.2 us)
Async XLA Ops:
  24.8 3.9 %copy-start = (f32[4,128,128]{2,1,0:T(8,128)S(1)}, f32[4,128,128]{2,1,0:T(8,128)}, u32[]{:S(2)}) copy-start(f32[4,128,128]{2,1,0:T(8,128)} %temp.3) | copy-start | bytes 786436
  24.8 37.1 %all-to-all-start.1 = ((bf16[16,16,4736]{2,1,0:T(8,128)(2,1)}), bf16[16,16,4736]{2,1,0:T(8,128)(2,1)S(1)}, u32[]{:S(2)}, u32[]{:S(2)}) async-start(bf16[16,16,4736]{2,1,0:T(8,128)(2,1)} %bitcast.15), calls=%async_computation.1 | async-start | bytes 4849664 | tf_op jit(solution)/shard_map/all_to_all | solution.py:494
  28.7 1.0 copy-start.6
  29.7 0.9 copy-start.7
  30.6 29.3 %copy-start.5 = (f32[64,1,128]{2,1,0:T(1,128)S(1)}, f32[64,1,128]{2,1,0:T(1,128)}, u32[]{:S(2)}) copy-start(f32[64,1,128]{2,1,0:T(1,128)} %all_to_all.15) | copy-start | bytes 98308
  30.7 17.1 %collective-permute-start = (bf16[8,128,128]{2,1,0:T(8,128)(2,1)S(1)}, bf16[8,128,128]{2,1,0:T(8,128)(2,1)S(1)}, u32[]{:S(2)}, u32[]{:S(2)}) collective-permute-start(bf16[8,128,128]{2,1,0:T(8,128)(2,1)S(1)} %get-tuple-element.25), channel_id=1, source_target_pairs={{0,1},{1,2},{2,3},{3,4},{4,5},{5,6},{6,7},{8,9},{9,10},{10,11},{11... | collective-permute-start | bytes 786440 | tf_op jit(solution)/shard_map/ppermute | solution.py:434
  41.7 17.5 %collective-permute-start.1 = (bf16[8,128,128]{2,1,0:T(8,128)(2,1)S(1)}, bf16[8,128,128]{2,1,0:T(8,128)(2,1)S(1)}, u32[]{:S(2)}, u32[]{:S(2)}) collective-permute-start(bf16[8,128,128]{2,1,0:T(8,128)(2,1)S(1)} %get-tuple-element.26), channel_id=1, source_target_pairs={{1,0},{2,1},{3,2},{4,3},{5,4},{6,5},{7,6},{9,8},{10,9},{11,10},{12... | collective-permute-start | bytes 786440 | tf_op jit(solution)/shard_map/ppermute | solution.py:434
  47.9 11.4 %copy-start.1 = (bf16[8,128,128]{2,1,0:T(8,128)(2,1)}, bf16[8,128,128]{2,1,0:T(8,128)(2,1)S(1)}, u32[]{:S(2)}) copy-start(bf16[8,128,128]{2,1,0:T(8,128)(2,1)S(1)} %collective-permute-done.lo) | copy-start | bytes 786436
  59.2 0.7 copy-start.3
  60.7 0.6 copy-start.8
  61.3 0.6 copy-start.10
  62.5 8.6 %copy-start.11 = (bf16[240,128]{1,0:T(8,128)(2,1)S(1)}, bf16[240,128]{1,0:T(8,128)(2,1)}, u32[]{:S(2)}) copy-start(bf16[240,128]{1,0:T(8,128)(2,1)} %copy-done.10) | copy-start | bytes 184324
  62.5 12.0 %copy-start.9 = (bf16[240,128]{1,0:T(8,128)(2,1)S(1)}, bf16[240,128]{1,0:T(8,128)(2,1)}, u32[]{:S(2)}) copy-start(bf16[240,128]{1,0:T(8,128)(2,1)} %copy-done.8) | copy-start | bytes 184324
  62.5 17.4 %copy-start.2 = (bf16[8,128,128]{2,1,0:T(8,128)(2,1)S(1)}, bf16[8,128,128]{2,1,0:T(8,128)(2,1)}, u32[]{:S(2)}) copy-start(bf16[8,128,128]{2,1,0:T(8,128)(2,1)} %copy-done.1) | copy-start | bytes 786436
  63.4 20.2 %all-to-all-start.2 = ((f16[4,16,4480]{2,1,0:T(8,128)(2,1)}), f16[4,16,4480]{2,1,0:T(8,128)(2,1)}, u32[]{:S(2)}, u32[]{:S(2)}) async-start(f16[4,16,4480]{2,1,0:T(8,128)(2,1)} %bitcast.8), calls=%async_computation.2 | async-start | bytes 1146880 | tf_op jit(solution)/shard_map/all_to_all | solution.py:500
  71.1 4.8 %collective-permute-start.2 = (bf16[240,128]{1,0:T(8,128)(2,1)S(1)}, bf16[240,128]{1,0:T(8,128)(2,1)S(1)}, u32[]{:S(2)}, u32[]{:S(2)}) collective-permute-start(bf16[240,128]{1,0:T(8,128)(2,1)S(1)} %copy-done.11), channel_id=1, source_target_pairs={{0,128},{128,256},{256,384},{1,129},{129,257},{257,385},{2,130},{1... | collective-permute-start | bytes 184328 | tf_op jit(solution)/shard_map/ppermute | solution.py:434
  74.5 5.4 %collective-permute-start.3 = (bf16[240,128]{1,0:T(8,128)(2,1)S(1)}, bf16[240,128]{1,0:T(8,128)(2,1)S(1)}, u32[]{:S(2)}, u32[]{:S(2)}) collective-permute-start(bf16[240,128]{1,0:T(8,128)(2,1)S(1)} %copy-done.9), channel_id=1, source_target_pairs={{128,0},{256,128},{384,256},{129,1},{257,129},{385,257},{130,2},{2... | collective-permute-start | bytes 184328 | tf_op jit(solution)/shard_map/ppermute | solution.py:434
  79.9 1.0 copy-start.4
  86.1 24.7 %collective-permute-start.4 = (bf16[432,128]{1,0:T(8,128)(2,1)S(1)}, bf16[432,128]{1,0:T(8,128)(2,1)S(1)}, u32[]{:S(2)}, u32[]{:S(2)}) collective-permute-start(bf16[432,128]{1,0:T(8,128)(2,1)S(1)} %get-tuple-element.35), channel_id=1, source_target_pairs={{0,1},{1,2},{2,3},{3,4},{4,5},{5,6},{6,7},{8,9},{9,10},{10,11},{11... | collective-permute-start | bytes 331784 | tf_op jit(solution)/shard_map/ppermute | solution.py:434
  93.4 17.5 %collective-permute-start.5 = (bf16[432,128]{1,0:T(8,128)(2,1)S(1)}, bf16[432,128]{1,0:T(8,128)(2,1)S(1)}, u32[]{:S(2)}, u32[]{:S(2)}) collective-permute-start(bf16[432,128]{1,0:T(8,128)(2,1)S(1)} %get-tuple-element.36), channel_id=1, source_target_pairs={{1,0},{2,1},{3,2},{4,3},{5,4},{6,5},{7,6},{9,8},{10,9},{11,10},{12... | collective-permute-start | bytes 331784 | tf_op jit(solution)/shard_map/ppermute | solution.py:434
  95.4 8.0 %collective-permute-start.7 = (bf16[144,128]{1,0:T(8,128)(2,1)S(1)}, bf16[144,128]{1,0:T(8,128)(2,1)S(1)}, u32[]{:S(2)}, u32[]{:S(2)}) collective-permute-start(bf16[144,128]{1,0:T(8,128)(2,1)S(1)} %get-tuple-element.31._to_left), channel_id=1, source_target_pairs={{8,0},{16,8},{24,16},{32,24},{40,32},{48,40},{56,48},{64,56},{72,6... | collective-permute-start | bytes 110600 | tf_op jit(solution)/shard_map/ppermute | solution.py:434
  101.5 6.8 %collective-permute-start.6 = (bf16[144,128]{1,0:T(8,128)(2,1)S(1)}, bf16[144,128]{1,0:T(8,128)(2,1)S(1)}, u32[]{:S(2)}, u32[]{:S(2)}) collective-permute-start(bf16[144,128]{1,0:T(8,128)(2,1)S(1)} %get-tuple-element.32._to_right), channel_id=1, source_target_pairs={{0,8},{8,16},{16,24},{24,32},{32,40},{40,48},{48,56},{56,64},{64,7... | collective-permute-start | bytes 110600 | tf_op jit(solution)/shard_map/ppermute | solution.py:434

commit v7 on v6

--- a/solution.py
+++ b/solution.py
@@ -208,7 +208,7 @@
     out[:, 4352:4480] = corners
 
 
-def unpack_kernel(whole, _to_left, _to_right, density, main, side, up, down, turned):
+def unpack_kernel(whole, _left, _right, density, main, side, up, down, turned):
     for k in range(32):
         turned[k * 16 : (k + 1) * 16, :] = whole[:, k * 128 : (k + 1) * 128]
     low = iota((32, 128), 1) < 64
@@ -412,7 +412,7 @@
     return jax.ShapeDtypeStruct(shape, dtype)
 
 
-def call(kernel, shape, args, mib=16, scratch=(), far=(), far_out=False):
+def call(kernel, shape, args, mib=12, scratch=(), far=(), far_out=False):
     vmem, anywhere = pl.BlockSpec(memory_space=pltpu.VMEM), pl.BlockSpec(memory_space=pltpu.HBM)
     return pl.pallas_call(
         kernel,
@@ -447,9 +447,9 @@
     ends = call(rows_kernel, (rows, rows), (own, lo, hi))
     above, below = exchange(*ends, "row")
     wide, to_left, to_right = call(
-        gather_kernel, (sds((30, 144, 128), F32), edge, edge), (own, lo, hi, above, below), mib=24
-    )
-    return wide, ends, (to_left, to_right), exchange(to_right, to_left, COL)
+        gather_kernel, (sds((30, 144, 128), F32), edge, edge), (own, lo, hi, above, below), mib=12
+    )
+    return wide, ends, exchange(to_right, to_left, COL)
 
 
 def operator(wide, from_left, from_right):
@@ -458,7 +458,7 @@
         operator_kernel,
         (sds((9, 144, 256), F32), eight, eight, eight, eight),
         (wide, from_left, from_right),
-        mib=32,
+        mib=12,
         scratch=[pltpu.VMEM((30, 144, 256), F32)],
     )
 
@@ -492,7 +492,7 @@
         far_out=True,
     )
     received = lax.all_to_all(send.reshape(16, 16, 4736), PLANE, split_axis=0, concat_axis=0, tiled=True)
-    wide, ends, edges, beside = extended_grids(temp, cond, mass)
+    wide, ends, beside = extended_grids(temp, cond, mass)
     selector = call(selector_kernel, sds((576, 256), BF16), (messages, *ends))
     partial = call(
         combine_kernel, sds((64, 4480), F32), (selector, received.reshape(256, 4736))
@@ -505,7 +505,7 @@
     density, main, side, up, down = call(
         unpack_kernel,
         (sds((512, 128), F32), block, block, strip, strip),
-        (jnp.sum(parts.astype(F32), axis=0), *edges),
+        (jnp.sum(parts.astype(F32), axis=0), *beside),
         scratch=[pltpu.VMEM((512, 128), F32)],
     )
     lo, hi = exchange(up, down, LAYER)
@@ -514,7 +514,7 @@
         sweep_kernel,
         sds((512, 128), F32),
         (main, side, lo, hi, wide, *terms),
-        mib=40,
+        mib=12,
         scratch=[eight, eight, eight],
     )
     return guess.reshape(4, 128, 128), density.reshape(4, 128, 128)

time: 114 us -> 116 us (1.018)
  the two profiles are of different devices: /device:TPU:33 before, /device:TPU:25 now
where the time goes in v7:
time: 116 us
  starting transfers between devices  42.8 us (37%)
  waiting for transfers between devices  33.3 us (29%)
  blocking collectives  18.8 us (16%)
  Pallas kernels  13 us (11%)
  local copies, waits for them, and re-layouts  4.76 us (4%)
  other arithmetic  2.05 us (2%)
    ppermute x8, waiting for transfers between devices, exchange(): return (lax.ppermute(to_next, axis, up), lax.ppermute(to_last, axis, down))  33.3 us
    ppermute x8, starting transfers between devices, exchange(): return (lax.ppermute(to_next, axis, up), lax.ppermute(to_last, axis, down))  33.1 us
    all_to_all x1, blocking collectives, shards(): lax.all_to_all(message.reshape(64, 1, 128), CUBE, split_axis=0, concat_ax...  18.8 us
    pallas_call x10, Pallas kernels, call(): pl.pallas_call(kernel, out_shape=shape, in_specs=[anywhere if i in far el...  13 us
    all_to_all x1, starting transfers between devices, shards(): lax.all_to_all(send.reshape(16, 16, 4736), PLANE, split_axis=0, concat_ax...  5.46 us
    unnamed x24, local copies, waits for them, and re-layouts  4.76 us
    all_to_all x1, starting transfers between devices, shards(): lax.all_to_all(partial.astype(jnp.float16).reshape(4, 16, 4480), 'zlo', s...  4.16 us
  transfers between devices with their start and end apart: 10, of which 5 were waited for; matrix products, arithmetic and copies ran while one was open for 1% of the time, Pallas kernels for 4%

profile of v7, /device:TPU:25, one launch (start us, length us, event | category | flops | bytes accessed | tf_op | source)
XLA Modules:
  0.0 115.5 jit_solution(956975935657834041)
XLA Ops:
  0.6 1.8 %shard_map.113 = (f32[64,128]{1,0:T(8,128)}, bf16[1024,64]{1,0:T(8,128)(2,1)}, s32[64,128]{1,0:T(8,128)}) custom-call(f32[4,128,128]{2,1,0:T(8,128)} %temp.3, s32[1,64]{1,0:T(1,128)} %bitcast.20, s32[1,64]{1,0:T(1,128)} %place.1, s32[1,64]{1,0:T(1,128)} %holder.1, s32[1,16]{1,0:T(1,128)} %tier.1), custom_call_target="tpu_custom_call" | custom-call | tf_op jit(solution)/shard_map/pallas_call | solution.py:417
  2.4 18.8 %all_to_all.15 = f32[64,1,128]{2,1,0:T(1,128)} all-to-all(f32[64,1,128]{2,1,0:T(1,128)} %bitcast.19), channel_id=1, replica_groups=mesh['row'=4,'zlo'=4,'y'=4,'zhi'=4,'core'=2] {'row','zlo','y'}, dimensions={0} | all-to-all | bytes 65536 | tf_op jit(solution)/shard_map/all_to_all | solution.py:479
  21.2 3.2 %shard_map.117 = bf16[256,4736]{1,0:T(8,128)(2,1)} custom-call(f32[64,128]{1,0:T(8,128)} %bitcast.13, s32[64,128]{1,0:T(8,128)} %get-tuple-element.29.far_columns, f32[1,16]{1,0:T(1,128)} %far_warming.1, bf16[64,4096]{1,0:T(8,128)(2,1)} %bitcast.16, bf16[64,4096]{1,0:T(8,128)(2,1)} %bitcast.17, bf16[1024,64]{1,0:T(8,128)(2,1)} %get-tuple-element.30.far_placing), custom_call_target="tpu_custom_call" | custom-call | tf_op jit(solution)/shard_map/pallas_call | solution.py:417
  24.5 5.5 %all-to-all-start.1 = ((bf16[16,16,4736]{2,1,0:T(8,128)(2,1)}), bf16[16,16,4736]{2,1,0:T(8,128)(2,1)S(1)}, u32[]{:S(2)}, u32[]{:S(2)}) async-start(bf16[16,16,4736]{2,1,0:T(8,128)(2,1)} %bitcast.15), calls=%async_computation.1 | async-start | bytes 4849664 | tf_op jit(solution)/shard_map/all_to_all | solution.py:494
  29.9 0.9 copy-done.6
  30.9 0.9 copy-done.7
  32.0 11.2 %collective-permute-start = (bf16[8,128,128]{2,1,0:T(8,128)(2,1)S(1)}, bf16[8,128,128]{2,1,0:T(8,128)(2,1)S(1)}, u32[]{:S(2)}, u32[]{:S(2)}) collective-permute-start(bf16[8,128,128]{2,1,0:T(8,128)(2,1)S(1)} %get-tuple-element.25), channel_id=1, source_target_pairs={{0,1},{1,2},{2,3},{3,4},{4,5},{5,6},{6,7},{8,9},{9,10},{10,11},{11... | collective-permute-start | bytes 786440 | tf_op jit(solution)/shard_map/ppermute | solution.py:434
  43.2 1.9 %collective-permute-start.1 = (bf16[8,128,128]{2,1,0:T(8,128)(2,1)S(1)}, bf16[8,128,128]{2,1,0:T(8,128)(2,1)S(1)}, u32[]{:S(2)}, u32[]{:S(2)}) collective-permute-start(bf16[8,128,128]{2,1,0:T(8,128)(2,1)S(1)} %get-tuple-element.26), channel_id=1, source_target_pairs={{1,0},{2,1},{3,2},{4,3},{5,4},{6,5},{7,6},{9,8},{10,9},{11,10},{12... | collective-permute-start | bytes 786440 | tf_op jit(solution)/shard_map/ppermute | solution.py:434
  45.2 1.4 %collective-permute-done.lo = bf16[8,128,128]{2,1,0:T(8,128)(2,1)S(1)} collective-permute-done((bf16[8,128,128]{2,1,0:T(8,128)(2,1)S(1)}, bf16[8,128,128]{2,1,0:T(8,128)(2,1)S(1)}, u32[]{:S(2)}, u32[]{:S(2)}) %collective-permute-start) | collective-permute-done | bytes 262176 | tf_op jit(solution)/shard_map/ppermute | solution.py:434
  46.6 16.4 %collective-permute-done.1.hi = bf16[8,128,128]{2,1,0:T(8,128)(2,1)S(1)} collective-permute-done((bf16[8,128,128]{2,1,0:T(8,128)(2,1)S(1)}, bf16[8,128,128]{2,1,0:T(8,128)(2,1)S(1)}, u32[]{:S(2)}, u32[]{:S(2)}) %collective-permute-start.1) | collective-permute-done | bytes 262176 | tf_op jit(solution)/shard_map/ppermute | solution.py:434
  63.0 0.7 copy-done.3
  63.7 0.7 shard_map.116.selector
  64.4 0.6 copy-done.8
  65.0 0.6 copy-done.10
  65.6 0.6 shard_map.118
  66.3 0.9 convert_element_type.6
  67.1 4.2 %all-to-all-start.2 = ((f16[4,16,4480]{2,1,0:T(8,128)(2,1)}), f16[4,16,4480]{2,1,0:T(8,128)(2,1)}, u32[]{:S(2)}, u32[]{:S(2)}) async-start(f16[4,16,4480]{2,1,0:T(8,128)(2,1)} %bitcast.8), calls=%async_computation.2 | async-start | bytes 1146880 | tf_op jit(solution)/shard_map/all_to_all | solution.py:500
  71.3 3.1 %collective-permute-start.2 = (bf16[240,128]{1,0:T(8,128)(2,1)S(1)}, bf16[240,128]{1,0:T(8,128)(2,1)S(1)}, u32[]{:S(2)}, u32[]{:S(2)}) collective-permute-start(bf16[240,128]{1,0:T(8,128)(2,1)S(1)} %copy-done.11), channel_id=1, source_target_pairs={{0,128},{128,256},{256,384},{1,129},{129,257},{257,385},{2,130},{1... | collective-permute-start | bytes 184328 | tf_op jit(solution)/shard_map/ppermute | solution.py:434
  74.5 1.3 %collective-permute-start.3 = (bf16[240,128]{1,0:T(8,128)(2,1)S(1)}, bf16[240,128]{1,0:T(8,128)(2,1)S(1)}, u32[]{:S(2)}, u32[]{:S(2)}) collective-permute-start(bf16[240,128]{1,0:T(8,128)(2,1)S(1)} %copy-done.9), channel_id=1, source_target_pairs={{128,0},{256,128},{384,256},{129,1},{257,129},{385,257},{130,2},{2... | collective-permute-start | bytes 184328 | tf_op jit(solution)/shard_map/ppermute | solution.py:434
  75.8 4.1 %collective-permute-done.3.below = bf16[240,128]{1,0:T(8,128)(2,1)S(1)} collective-permute-done((bf16[240,128]{1,0:T(8,128)(2,1)S(1)}, bf16[240,128]{1,0:T(8,128)(2,1)S(1)}, u32[]{:S(2)}, u32[]{:S(2)}) %collective-permute-start.3) | collective-permute-done | bytes 61472 | tf_op jit(solution)/shard_map/ppermute | solution.py:434
  79.8 0.9 copy-done.4
  80.8 0.6 shard_map.119
  81.4 3.3 %collective-permute-start.4 = (bf16[144,128]{1,0:T(8,128)(2,1)S(1)}, bf16[144,128]{1,0:T(8,128)(2,1)S(1)}, u32[]{:S(2)}, u32[]{:S(2)}) collective-permute-start(bf16[144,128]{1,0:T(8,128)(2,1)S(1)} %get-tuple-element.31), channel_id=1, source_target_pairs={{0,8},{8,16},{16,24},{24,32},{32,40},{40,48},{48,56},{56,64},{64,7... | collective-permute-start | bytes 110600 | tf_op jit(solution)/shard_map/ppermute | solution.py:434
  84.7 2.0 %collective-permute-start.5 = (bf16[144,128]{1,0:T(8,128)(2,1)S(1)}, bf16[144,128]{1,0:T(8,128)(2,1)S(1)}, u32[]{:S(2)}, u32[]{:S(2)}) collective-permute-start(bf16[144,128]{1,0:T(8,128)(2,1)S(1)} %get-tuple-element.32), channel_id=1, source_target_pairs={{8,0},{16,8},{24,16},{32,24},{40,32},{48,40},{56,48},{64,56},{72,6... | collective-permute-start | bytes 110600 | tf_op jit(solution)/shard_map/ppermute | solution.py:434
  86.7 1.2 %convert_reduce_fusion.whole = f32[16,4480]{1,0:T(8,128)S(1)} fusion(f16[4,16,4480]{2,1,0:T(8,128)(2,1)} %all-to-all-done.2), kind=kLoop, calls=%fused_computation | loop fusion | flops 501760 | bytes 860160 | tf_op jit(solution)/shard_map/reduce_sum | solution.py:508
  87.9 3.6 %collective-permute-done.5._right.from_right = bf16[144,128]{1,0:T(8,128)(2,1)S(1)} collective-permute-done((bf16[144,128]{1,0:T(8,128)(2,1)S(1)}, bf16[144,128]{1,0:T(8,128)(2,1)S(1)}, u32[]{:S(2)}, u32[]{:S(2)}) %collective-permute-start.5) | collective-permute-done | bytes 36896 | tf_op jit(solution)/shard_map/ppermute | solution.py:434
  91.5 1.4 %shard_map.120 = (f32[512,128]{1,0:T(8,128)}, f32[576,128]{1,0:T(8,128)S(1)}, f32[576,128]{1,0:T(8,128)S(1)}, bf16[432,128]{1,0:T(8,128)(2,1)S(1)}, bf16[432,128]{1,0:T(8,128)(2,1)S(1)}) custom-call(f32[16,4480]{1,0:T(8,128)S(1)} %convert_reduce_fusion.whole, bf16[144,128]{1,0:T(8,128)(2,1)S(1)} %collective-permute-done.4._left.from_left, ...), custom_call_target="tpu_custom_call" | custom-call | tf_op jit(solution)/shard_map/pallas_call | solution.py:417
  92.9 8.4 %collective-permute-start.6 = (bf16[432,128]{1,0:T(8,128)(2,1)S(1)}, bf16[432,128]{1,0:T(8,128)(2,1)S(1)}, u32[]{:S(2)}, u32[]{:S(2)}) collective-permute-start(bf16[432,128]{1,0:T(8,128)(2,1)S(1)} %get-tuple-element.35), channel_id=1, source_target_pairs={{0,1},{1,2},{2,3},{3,4},{4,5},{5,6},{6,7},{8,9},{9,10},{10,11},{11... | collective-permute-start | bytes 331784 | tf_op jit(solution)/shard_map/ppermute | solution.py:434
  101.3 1.9 %collective-permute-start.7 = (bf16[432,128]{1,0:T(8,128)(2,1)S(1)}, bf16[432,128]{1,0:T(8,128)(2,1)S(1)}, u32[]{:S(2)}, u32[]{:S(2)}) collective-permute-start(bf16[432,128]{1,0:T(8,128)(2,1)S(1)} %get-tuple-element.36), channel_id=1, source_target_pairs={{1,0},{2,1},{3,2},{4,3},{5,4},{6,5},{7,6},{9,8},{10,9},{11,10},{12... | collective-permute-start | bytes 331784 | tf_op jit(solution)/shard_map/ppermute | solution.py:434
  103.2 2.6 %shard_map.121 = (f32[9,144,256]{2,1,0:T(8,128)S(1)}, f32[8,144,256]{2,1,0:T(8,128)S(1)}, f32[8,144,256]{2,1,0:T(8,128)S(1)}, f32[8,144,256]{2,1,0:T(8,128)S(1)}, f32[8,144,256]{2,1,0:T(8,128)S(1)}) custom-call(f32[30,144,128]{2,1,0:T(8,128)S(1)} %get-tuple-element.37.grids, bf16[144,128]{1,0:T(8,128)(2,1)S(1)} %collective-permute-done.4._left.from_left, ...), custom_call_target="tpu_custom_call" | custom-call | tf_op jit(solution)/shard_map/pallas_call | solution.py:417
  105.8 7.8 %collective-permute-done.7.hi = bf16[432,128]{1,0:T(8,128)(2,1)S(1)} collective-permute-done((bf16[432,128]{1,0:T(8,128)(2,1)S(1)}, bf16[432,128]{1,0:T(8,128)(2,1)S(1)}, u32[]{:S(2)}, u32[]{:S(2)}) %collective-permute-start.7) | collective-permute-done | bytes 110624 | tf_op jit(solution)/shard_map/ppermute | solution.py:434
  113.6 1.9 %shard_map.122 = f32[512,128]{1,0:T(8,128)} custom-call(f32[576,128]{1,0:T(8,128)S(1)} %get-tuple-element.33.main, f32[576,128]{1,0:T(8,128)S(1)} %get-tuple-element.34.side, bf16[432,128]{1,0:T(8,128)(2,1)S(1)} %collective-permute-done.6.lo, bf16[432,128]{1,0:T(8,128)(2,1)S(1)} %collective-permute-done.7.hi, f32[30,144,128]{2,1,0:T(8,128)S(1)} %get-tuple-element.37.grids, ...), custom_call_target="tpu_custom_call" | custom-call | tf_op jit(solution)/shard_map/pallas_call | solution.py:417
  (25 shorter events, 0.2 us)
Async XLA Ops:
  24.5 5.5 %copy-start = (f32[4,128,128]{2,1,0:T(8,128)S(1)}, f32[4,128,128]{2,1,0:T(8,128)}, u32[]{:S(2)}) copy-start(f32[4,128,128]{2,1,0:T(8,128)} %temp.3) | copy-start | bytes 786436
  24.5 41.2 %all-to-all-start.1 = ((bf16[16,16,4736]{2,1,0:T(8,128)(2,1)}), bf16[16,16,4736]{2,1,0:T(8,128)(2,1)S(1)}, u32[]{:S(2)}, u32[]{:S(2)}) async-start(bf16[16,16,4736]{2,1,0:T(8,128)(2,1)} %bitcast.15), calls=%async_computation.1 | async-start | bytes 4849664 | tf_op jit(solution)/shard_map/all_to_all | solution.py:494
  29.9 1.0 copy-start.6
  30.9 0.9 copy-start.7
  31.8 31.8 %copy-start.5 = (f32[64,1,128]{2,1,0:T(1,128)S(1)}, f32[64,1,128]{2,1,0:T(1,128)}, u32[]{:S(2)}) copy-start(f32[64,1,128]{2,1,0:T(1,128)} %all_to_all.15) | copy-start | bytes 98308
  32.0 14.6 %collective-permute-start = (bf16[8,128,128]{2,1,0:T(8,128)(2,1)S(1)}, bf16[8,128,128]{2,1,0:T(8,128)(2,1)S(1)}, u32[]{:S(2)}, u32[]{:S(2)}) collective-permute-start(bf16[8,128,128]{2,1,0:T(8,128)(2,1)S(1)} %get-tuple-element.25), channel_id=1, source_target_pairs={{0,1},{1,2},{2,3},{3,4},{4,5},{5,6},{6,7},{8,9},{9,10},{10,11},{11... | collective-permute-start | bytes 786440 | tf_op jit(solution)/shard_map/ppermute | solution.py:434
  43.2 19.7 %collective-permute-start.1 = (bf16[8,128,128]{2,1,0:T(8,128)(2,1)S(1)}, bf16[8,128,128]{2,1,0:T(8,128)(2,1)S(1)}, u32[]{:S(2)}, u32[]{:S(2)}) collective-permute-start(bf16[8,128,128]{2,1,0:T(8,128)(2,1)S(1)} %get-tuple-element.26), channel_id=1, source_target_pairs={{1,0},{2,1},{3,2},{4,3},{5,4},{6,5},{7,6},{9,8},{10,9},{11,10},{12... | collective-permute-start | bytes 786440 | tf_op jit(solution)/shard_map/ppermute | solution.py:434
  46.6 16.4 %copy-start.1 = (bf16[8,128,128]{2,1,0:T(8,128)(2,1)}, bf16[8,128,128]{2,1,0:T(8,128)(2,1)S(1)}, u32[]{:S(2)}) copy-start(bf16[8,128,128]{2,1,0:T(8,128)(2,1)S(1)} %collective-permute-done.lo) | copy-start | bytes 786436
  63.0 0.7 copy-start.3
  64.4 0.6 copy-start.8
  65.0 0.6 copy-start.10
  66.2 5.1 %copy-start.11 = (bf16[240,128]{1,0:T(8,128)(2,1)S(1)}, bf16[240,128]{1,0:T(8,128)(2,1)}, u32[]{:S(2)}) copy-start(bf16[240,128]{1,0:T(8,128)(2,1)} %copy-done.10) | copy-start | bytes 184324
  66.2 8.2 %copy-start.9 = (bf16[240,128]{1,0:T(8,128)(2,1)S(1)}, bf16[240,128]{1,0:T(8,128)(2,1)}, u32[]{:S(2)}) copy-start(bf16[240,128]{1,0:T(8,128)(2,1)} %copy-done.8) | copy-start | bytes 184324
  66.2 13.6 %copy-start.2 = (bf16[8,128,128]{2,1,0:T(8,128)(2,1)S(1)}, bf16[8,128,128]{2,1,0:T(8,128)(2,1)}, u32[]{:S(2)}) copy-start(bf16[8,128,128]{2,1,0:T(8,128)(2,1)} %copy-done.1) | copy-start | bytes 786436
  67.1 19.6 %all-to-all-start.2 = ((f16[4,16,4480]{2,1,0:T(8,128)(2,1)}), f16[4,16,4480]{2,1,0:T(8,128)(2,1)}, u32[]{:S(2)}, u32[]{:S(2)}) async-start(f16[4,16,4480]{2,1,0:T(8,128)(2,1)} %bitcast.8), calls=%async_computation.2 | async-start | bytes 1146880 | tf_op jit(solution)/shard_map/all_to_all | solution.py:500
  71.3 4.4 %collective-permute-start.2 = (bf16[240,128]{1,0:T(8,128)(2,1)S(1)}, bf16[240,128]{1,0:T(8,128)(2,1)S(1)}, u32[]{:S(2)}, u32[]{:S(2)}) collective-permute-start(bf16[240,128]{1,0:T(8,128)(2,1)S(1)} %copy-done.11), channel_id=1, source_target_pairs={{0,128},{128,256},{256,384},{1,129},{129,257},{257,385},{2,130},{1... | collective-permute-start | bytes 184328 | tf_op jit(solution)/shard_map/ppermute | solution.py:434
  74.5 5.4 %collective-permute-start.3 = (bf16[240,128]{1,0:T(8,128)(2,1)S(1)}, bf16[240,128]{1,0:T(8,128)(2,1)S(1)}, u32[]{:S(2)}, u32[]{:S(2)}) collective-permute-start(bf16[240,128]{1,0:T(8,128)(2,1)S(1)} %copy-done.9), channel_id=1, source_target_pairs={{128,0},{256,128},{384,256},{129,1},{257,129},{385,257},{130,2},{2... | collective-permute-start | bytes 184328 | tf_op jit(solution)/shard_map/ppermute | solution.py:434
  79.8 1.0 copy-start.4
  81.4 6.5 %collective-permute-start.4 = (bf16[144,128]{1,0:T(8,128)(2,1)S(1)}, bf16[144,128]{1,0:T(8,128)(2,1)S(1)}, u32[]{:S(2)}, u32[]{:S(2)}) collective-permute-start(bf16[144,128]{1,0:T(8,128)(2,1)S(1)} %get-tuple-element.31), channel_id=1, source_target_pairs={{0,8},{8,16},{16,24},{24,32},{32,40},{40,48},{48,56},{56,64},{64,7... | collective-permute-start | bytes 110600 | tf_op jit(solution)/shard_map/ppermute | solution.py:434
  84.7 6.8 %collective-permute-start.5 = (bf16[144,128]{1,0:T(8,128)(2,1)S(1)}, bf16[144,128]{1,0:T(8,128)(2,1)S(1)}, u32[]{:S(2)}, u32[]{:S(2)}) collective-permute-start(bf16[144,128]{1,0:T(8,128)(2,1)S(1)} %get-tuple-element.32), channel_id=1, source_target_pairs={{8,0},{16,8},{24,16},{32,24},{40,32},{48,40},{56,48},{64,56},{72,6... | collective-permute-start | bytes 110600 | tf_op jit(solution)/shard_map/ppermute | solution.py:434
  92.9 12.9 %collective-permute-start.6 = (bf16[432,128]{1,0:T(8,128)(2,1)S(1)}, bf16[432,128]{1,0:T(8,128)(2,1)S(1)}, u32[]{:S(2)}, u32[]{:S(2)}) collective-permute-start(bf16[432,128]{1,0:T(8,128)(2,1)S(1)} %get-tuple-element.35), channel_id=1, source_target_pairs={{0,1},{1,2},{2,3},{3,4},{4,5},{5,6},{6,7},{8,9},{9,10},{10,11},{11... | collective-permute-start | bytes 331784 | tf_op jit(solution)/shard_map/ppermute | solution.py:434
  101.3 12.3 %collective-permute-start.7 = (bf16[432,128]{1,0:T(8,128)(2,1)S(1)}, bf16[432,128]{1,0:T(8,128)(2,1)S(1)}, u32[]{:S(2)}, u32[]{:S(2)}) collective-permute-start(bf16[432,128]{1,0:T(8,128)(2,1)S(1)} %get-tuple-element.36), channel_id=1, source_target_pairs={{1,0},{2,1},{3,2},{4,3},{5,4},{6,5},{7,6},{9,8},{10,9},{11,10},{12... | collective-permute-start | bytes 331784 | tf_op jit(solution)/shard_map/ppermute | solution.py:434

commit v8 on v5

--- a/solution.py
+++ b/solution.py
@@ -56,12 +56,8 @@
     )
 
 
-def depth(a):
-    return 3 if a < 2 else 2
-
-
 def message_kernel(
-    temp, cond, mass, panel, place, holder, tier, out, placing, columns, own, up, down,
+    temp, cond, mass, panel, place, holder, tier, out, placing, columns, own, last, first,
     panel_v, place_v, holder_v, tier_v, sems,
 ):
     pairs = [(panel, panel_v), (place, place_v), (holder, holder_v), (tier, tier_v)]
@@ -75,11 +71,11 @@
     pos, ident, dest = slot_rows(panel_row, place_v[...], holder_row, tier_v[...])
     place_slots(panel_row, pos, dest, holder_row, placing, columns)
     code = (dest * 64 + ident).astype(F32)
-    for a in range(3):
-        copies[4 + a].wait()
-        for k in range(depth(a)):
-            up[3 * a + k] = own[a, 4 - depth(a) + k].astype(BF16)
-            down[3 * a + k] = own[a, k].astype(BF16)
+    for copy in copies[4:]:
+        copy.wait()
+    grids = own[...].reshape(12, 128, 128)
+    last[...] = grids[:, 120:128, :].reshape(96, 128).astype(BF16)
+    first[...] = grids[:, 0:8, :].reshape(96, 128).astype(BF16)
     sums = jnp.sum(own[0].reshape(8, 64, 128), axis=1)
     lane = iota((8, 128), 1)
     first = jnp.sum(jnp.where(lane < 64, sums, 0.0), axis=1, keepdims=True)
@@ -92,7 +88,7 @@
 
 
 def power_kernel(
-    far_messages, far_columns, far_warming, far_toggling, far_baseline, far_placing, _lo, _hi, out,
+    far_messages, far_columns, far_warming, far_toggling, far_baseline, far_placing, _above, _below, out,
     messages, columns, warming, toggling, baseline, placing, sent, sems,
 ):
     pairs = [
@@ -165,7 +161,7 @@
         copy.wait()
 
 
-def selector_kernel(messages, out):
+def selector_kernel(messages, _to_left, _to_right, out):
     x, y = lax.axis_index("row"), lax.axis_index("y")
     plane = lax.axis_index("zlo")
     code = jnp.concatenate([messages[pl.ds(r * 16 + plane * 4, 4), :] for r in range(4)], axis=0)
@@ -201,7 +197,7 @@
         put(5 + k, ids, z * 16 + layer)
 
 
-def combine_kernel(selector, received, _to_left, _to_right, out):
+def combine_kernel(selector, received, out):
     def add(k, start, width):
         return jnp.dot(
             selector[k * 64 : (k + 1) * 64, :],
@@ -272,6 +268,10 @@
         out[288:432, :] = (side[first : first + 144, :] + pltpu.roll(second, 4, 1)).astype(BF16)
 
 
+def depth(a):
+    return 3 if a < 2 else 2
+
+
 def beyond(lo, hi, a, layer):
     if layer < 3:
         k = layer - 3 + depth(a)
@@ -280,22 +280,17 @@
     return (hi, 3 * a + k) if k < depth(a) else None
 
 
-def rows_kernel(own, lo, hi, last, first):
-    lasts, firsts = [], []
+def with_rows(own, above, below, a, layer):
+    at = (a * 4 + layer) * 8
+    return jnp.concatenate([own[a, layer], below[at : at + 8], above[at : at + 8]], axis=0)
+
+
+def layers_kernel(own, above, below, up, down):
+    over, under = above[...].astype(F32), below[...].astype(F32)
     for a in range(3):
-        for layer in range(10):
-            if 3 <= layer < 7:
-                lasts.append(own[a, layer - 3, 120:128, :])
-                firsts.append(own[a, layer - 3, 0:8, :])
-            elif found := beyond(lo, hi, a, layer):
-                source, k = found
-                lasts.append(source[k, 112:128, :].astype(F32)[8:16])
-                firsts.append(source[k, 0:16, :].astype(F32)[0:8])
-            else:
-                lasts.append(jnp.zeros((8, 128), F32))
-                firsts.append(jnp.zeros((8, 128), F32))
-    last[...] = jnp.concatenate(lasts, axis=0).astype(BF16)
-    first[...] = jnp.concatenate(firsts, axis=0).astype(BF16)
+        for k in range(depth(a)):
+            up[3 * a + k] = with_rows(own, over, under, a, 4 - depth(a) + k).astype(BF16)
+            down[3 * a + k] = with_rows(own, over, under, a, k).astype(BF16)
 
 
 def gather_kernel(own, lo, hi, above, below, out, to_left, to_right):
@@ -306,12 +301,11 @@
         for layer in range(10):
             i = a * 10 + layer
             if 3 <= layer < 7:
-                source = own[a, layer - 3]
+                piece = with_rows(own, over, under, a, layer - 3)
             elif found := beyond(lo, hi, a, layer):
-                source = found[0][found[1]].astype(F32)
+                piece = found[0][found[1]].astype(F32)
             else:
-                source = jnp.zeros((128, 128), F32)
-            piece = jnp.concatenate([source, under[8 * i : 8 * i + 8], over[8 * i : 8 * i + 8]], axis=0)
+                piece = jnp.zeros((144, 128), F32)
             out[i] = piece
             base = a * 40 + layer * 4
             here = (lane >= base) & (lane < base + 3)
@@ -409,7 +403,7 @@
     return jax.ShapeDtypeStruct(shape, dtype)
 
 
-def call(kernel, shape, args, mib=16, scratch=(), far=(), far_out=False):
+def call(kernel, shape, args, mib=12, scratch=(), far=(), far_out=False):
     vmem, anywhere = pl.BlockSpec(memory_space=pltpu.VMEM), pl.BlockSpec(memory_space=pltpu.HBM)
     return pl.pallas_call(
         kernel,
@@ -431,13 +425,14 @@
     return lax.ppermute(to_next, axis, up), lax.ppermute(to_last, axis, down)
 
 
-def extended_grids(own, lo, hi):
-    rows, edge = sds((240, 128), BF16), sds((144, 128), BF16)
-    above, below = exchange(*call(rows_kernel, (rows, rows), (own, lo, hi)), "row")
-    wide, to_left, to_right = call(
-        gather_kernel, (sds((30, 144, 128), F32), edge, edge), (own, lo, hi, above, below), mib=24
-    )
-    return wide, (to_left, to_right), exchange(to_right, to_left, COL)
+def extended_grids(own, above, below):
+    eight, edge = sds((8, 144, 128), BF16), sds((144, 128), BF16)
+    lo, hi = exchange(*call(layers_kernel, (eight, eight), (own, above, below)), LAYER)
+    wide, *edges = call(
+        gather_kernel, (sds((30, 144, 128), F32), edge, edge), (own, lo, hi, above, below)
+    )
+    to_left, to_right = edges
+    return wide, edges, exchange(to_right, to_left, COL)
 
 
 def operator(wide, from_left, from_right):
@@ -446,32 +441,32 @@
         operator_kernel,
         (sds((9, 144, 256), F32), eight, eight, eight, eight),
         (wide, from_left, from_right),
-        mib=32,
+        mib=12,
         scratch=[pltpu.VMEM((30, 144, 256), F32)],
     )
 
 
 def shards(temp, cond, mass, toggling, baseline, panel, place, holder, tier, warming):
     row64 = pltpu.VMEM((1, 64), I32)
-    eight = sds((8, 128, 128), BF16)
-    message, placing, columns, own, up, down = call(
+    ends = sds((96, 128), BF16)
+    message, placing, columns, own, last, first = call(
         message_kernel,
         (
             sds((64, 128), F32), sds((1024, 64), BF16), sds((64, 128), I32),
-            sds((3, 4, 128, 128), F32), eight, eight,
+            sds((3, 4, 128, 128), F32), ends, ends,
         ),
         (temp, cond, mass, panel.reshape(1, 64), place, holder, tier),
         mib=60,
         scratch=[row64, row64, row64, pltpu.VMEM((1, 16), I32), pltpu.SemaphoreType.DMA((7,))],
         far=range(7),
     )
-    lo, hi = exchange(up, down, LAYER)
+    above, below = exchange(last, first, "row")
     messages = lax.all_to_all(message.reshape(64, 1, 128), CUBE, split_axis=0, concat_axis=0, tiled=True)
     messages = messages.reshape(64, 128)
     send = call(
         power_kernel,
         sds((256, 4736), BF16),
-        (messages, columns, warming, toggling[0], baseline[0], placing, lo, hi),
+        (messages, columns, warming, toggling[0], baseline[0], placing, above, below),
         mib=60,
         scratch=[
             pltpu.VMEM((64, 128), F32), pltpu.VMEM((64, 128), I32), pltpu.VMEM((1, 16), F32),
@@ -482,10 +477,10 @@
         far_out=True,
     )
     received = lax.all_to_all(send.reshape(16, 16, 4736), PLANE, split_axis=0, concat_axis=0, tiled=True)
-    selector = call(selector_kernel, sds((576, 256), BF16), (messages,))
-    wide, edges, beside = extended_grids(own, lo, hi)
+    wide, edges, beside = extended_grids(own, above, below)
+    selector = call(selector_kernel, sds((576, 256), BF16), (messages, *edges))
     partial = call(
-        combine_kernel, sds((64, 4480), F32), (selector, received.reshape(256, 4736), *edges)
+        combine_kernel, sds((64, 4480), F32), (selector, received.reshape(256, 4736))
     )
     parts = lax.all_to_all(
         partial.astype(jnp.float16).reshape(4, 16, 4480), "zlo", split_axis=0, concat_axis=0, tiled=True
@@ -504,7 +499,7 @@
         sweep_kernel,
         sds((512, 128), F32),
         (main, side, lo, hi, wide, *terms),
-        mib=40,
+        mib=12,
         scratch=[eight, eight, eight],
     )
     return guess.reshape(4, 128, 128), density.reshape(4, 128, 128)

time: 124 us -> 112 us (0.903)
  the two profiles are of different devices: /device:TPU:3 before, /device:TPU:1 now
where the time goes in v8:
time: 112 us; the launch traced here: 111 us
  starting transfers between devices  54 us (48%)
  waiting for transfers between devices  40.1 us (36%)
  Pallas kernels  13.3 us (12%)
  local copies, waits for them, and re-layouts  2 us (2%)
    ppermute x8, starting transfers between devices, exchange(): return (lax.ppermute(to_next, axis, up), lax.ppermute(to_last, axis, down))  32.4 us
    ppermute x8, waiting for transfers between devices, exchange(): return (lax.ppermute(to_next, axis, up), lax.ppermute(to_last, axis, down))  28.7 us
    pallas_call x9, Pallas kernels, call(): pl.pallas_call(kernel, out_shape=shape, in_specs=[anywhere if i in far el...  13.3 us
    all_to_all x1, starting transfers between devices, shards(): lax.all_to_all(message.reshape(64, 1, 128), CUBE, split_axis=0, concat_ax...  12.6 us
    all_to_all x1, waiting for transfers between devices, shards(): lax.all_to_all(partial.astype(jnp.float16).reshape(4, 16, 4480), 'zlo', s...  10.5 us
    all_to_all x1, starting transfers between devices, shards(): lax.all_to_all(send.reshape(16, 16, 4736), PLANE, split_axis=0, concat_ax...  5.45 us
    all_to_all x1, starting transfers between devices, shards(): lax.all_to_all(partial.astype(jnp.float16).reshape(4, 16, 4480), 'zlo', s...  3.61 us
  transfers between devices with their start and end apart: 11, of which 6 were waited for; matrix products, arithmetic and copies ran while one was open for 0% of the time, Pallas kernels for 4%

profile of v8, /device:TPU:1, one launch (start us, length us, event | category | flops | bytes accessed | tf_op | source)
XLA Modules:
  0.0 111.2 jit_solution(11869117171108536996)
XLA Ops:
  0.6 2.2 %shard_map.113 = (f32[64,128]{1,0:T(8,128)}, bf16[1024,64]{1,0:T(8,128)(2,1)}, s32[64,128]{1,0:T(8,128)}, f32[3,4,128,128]{3,2,1,0:T(8,128)}, bf16[96,128]{1,0:T(8,128)(2,1)}, /*index=5*/bf16[96,128]{1,0:T(8,128)(2,1)}) custom-call(f32[4,128,128]{2,1,0:T(8,128)} %temp.1, f32[4,128,128]{2,1,0:T(8,128)} %cond.1, f32[4,128,128]{2,1,0:T(8,128)} %mass.1, ...), custom_call_target="tpu_custom_call" | custom-call | tf_op jit(solution)/shard_map/pallas_call | solution.py:408
  2.9 12.6 %all-to-all-start = ((f32[64,1,128]{2,1,0:T(1,128)}), f32[64,1,128]{2,1,0:T(1,128)S(1)}, u32[]{:S(2)}, u32[]{:S(2)}) async-start(f32[64,1,128]{2,1,0:T(1,128)} %bitcast.20), calls=%async_computation | async-start | bytes 65536 | tf_op jit(solution)/shard_map/all_to_all | solution.py:464
  15.4 2.9 %collective-permute-start = (bf16[96,128]{1,0:T(8,128)(2,1)}, bf16[96,128]{1,0:T(8,128)(2,1)S(1)}, u32[]{:S(2)}, u32[]{:S(2)}) collective-permute-start(bf16[96,128]{1,0:T(8,128)(2,1)} %get-tuple-element.25), channel_id=1, source_target_pairs={{0,128},{128,256},{256,384},{1,129},{129,257},{257,385},{2,130},{1... | collective-permute-start | bytes 73736 | tf_op jit(solution)/shard_map/ppermute | solution.py:425
  18.4 1.3 %collective-permute-start.1 = (bf16[96,128]{1,0:T(8,128)(2,1)}, bf16[96,128]{1,0:T(8,128)(2,1)S(1)}, u32[]{:S(2)}, u32[]{:S(2)}) collective-permute-start(bf16[96,128]{1,0:T(8,128)(2,1)} %get-tuple-element.26), channel_id=1, source_target_pairs={{128,0},{256,128},{384,256},{129,1},{257,129},{385,257},{130,2},{2... | collective-permute-start | bytes 73736 | tf_op jit(solution)/shard_map/ppermute | solution.py:425
  19.7 0.0 collective-permute-done.above._above
  19.7 3.8 %collective-permute-done.1.below._below = bf16[96,128]{1,0:T(8,128)(2,1)S(1)} collective-permute-done((bf16[96,128]{1,0:T(8,128)(2,1)}, bf16[96,128]{1,0:T(8,128)(2,1)S(1)}, u32[]{:S(2)}, u32[]{:S(2)}) %collective-permute-start.1) | collective-permute-done | bytes 24608 | tf_op jit(solution)/shard_map/ppermute | solution.py:425
  23.4 0.8 all-to-all-done
  24.3 0.6 copy-done.3
  24.9 3.2 %shard_map.117 = bf16[256,4736]{1,0:T(8,128)(2,1)} custom-call(f32[64,128]{1,0:T(8,128)} %bitcast.13, s32[64,128]{1,0:T(8,128)} %get-tuple-element.31.far_columns, f32[1,16]{1,0:T(1,128)} %far_warming.1, bf16[64,4096]{1,0:T(8,128)(2,1)} %bitcast.17, bf16[64,4096]{1,0:T(8,128)(2,1)} %bitcast.18, bf16[1024,64]{1,0:T(8,128)(2,1)} %get-tuple-element.32.far_placing, ...), custom_call_target="tpu_custom_call" | custom-call | tf_op jit(solution)/shard_map/pallas_call | solution.py:408
  28.1 5.5 %all-to-all-start.1 = ((bf16[16,16,4736]{2,1,0:T(8,128)(2,1)}), bf16[16,16,4736]{2,1,0:T(8,128)(2,1)S(1)}, u32[]{:S(2)}, u32[]{:S(2)}) async-start(bf16[16,16,4736]{2,1,0:T(8,128)(2,1)} %bitcast.15), calls=%async_computation.1 | async-start | bytes 4849664 | tf_op jit(solution)/shard_map/all_to_all | solution.py:479
  33.5 0.0 copy-start.4
  33.6 0.1 shard_map.114
  33.6 11.6 %collective-permute-start.2 = (bf16[8,144,128]{2,1,0:T(8,128)(2,1)S(1)}, bf16[8,144,128]{2,1,0:T(8,128)(2,1)S(1)}, u32[]{:S(2)}, u32[]{:S(2)}) collective-permute-start(bf16[8,144,128]{2,1,0:T(8,128)(2,1)S(1)} %get-tuple-element.27), channel_id=1, source_target_pairs={{0,1},{1,2},{2,3},{3,4},{4,5},{5,6},{6,7},{8,9},{9,10},{10,11},{11... | collective-permute-start | bytes 884744 | tf_op jit(solution)/shard_map/ppermute | solution.py:425
  45.3 1.9 %collective-permute-start.3 = (bf16[8,144,128]{2,1,0:T(8,128)(2,1)S(1)}, bf16[8,144,128]{2,1,0:T(8,128)(2,1)S(1)}, u32[]{:S(2)}, u32[]{:S(2)}) collective-permute-start(bf16[8,144,128]{2,1,0:T(8,128)(2,1)S(1)} %get-tuple-element.28), channel_id=1, source_target_pairs={{1,0},{2,1},{3,2},{4,3},{5,4},{6,5},{7,6},{9,8},{10,9},{11,10},{12... | collective-permute-start | bytes 884744 | tf_op jit(solution)/shard_map/ppermute | solution.py:425
  47.2 1.8 %collective-permute-done.2.lo = bf16[8,144,128]{2,1,0:T(8,128)(2,1)S(1)} collective-permute-done((bf16[8,144,128]{2,1,0:T(8,128)(2,1)S(1)}, bf16[8,144,128]{2,1,0:T(8,128)(2,1)S(1)}, u32[]{:S(2)}, u32[]{:S(2)}) %collective-permute-start.2) | collective-permute-done | bytes 294944 | tf_op jit(solution)/shard_map/ppermute | solution.py:425
  49.0 17.7 %collective-permute-done.3.hi = bf16[8,144,128]{2,1,0:T(8,128)(2,1)S(1)} collective-permute-done((bf16[8,144,128]{2,1,0:T(8,128)(2,1)S(1)}, bf16[8,144,128]{2,1,0:T(8,128)(2,1)S(1)}, u32[]{:S(2)}, u32[]{:S(2)}) %collective-permute-start.3) | collective-permute-done | bytes 294944 | tf_op jit(solution)/shard_map/ppermute | solution.py:425
  66.7 0.6 shard_map.115
  67.4 1.4 %copy-done = f32[30,144,128]{2,1,0:T(8,128)} copy-done((f32[30,144,128]{2,1,0:T(8,128)}, f32[30,144,128]{2,1,0:T(8,128)S(1)}, u32[]{:S(2)}) %copy-start) | copy-done | bytes 2211864
  68.7 0.7 shard_map.116.selector
  69.5 0.6 shard_map.118
  70.1 0.9 convert_element_type.6
  70.9 3.6 %all-to-all-start.2 = ((f16[4,16,4480]{2,1,0:T(8,128)(2,1)}), f16[4,16,4480]{2,1,0:T(8,128)(2,1)S(1)}, u32[]{:S(2)}, u32[]{:S(2)}) async-start(f16[4,16,4480]{2,1,0:T(8,128)(2,1)} %bitcast.16), calls=%async_computation.2 | async-start | bytes 1146880 | tf_op jit(solution)/shard_map/all_to_all | solution.py:485
  74.6 1.3 %collective-permute-start.5 = (bf16[144,128]{1,0:T(8,128)(2,1)S(1)}, bf16[144,128]{1,0:T(8,128)(2,1)S(1)}, u32[]{:S(2)}, u32[]{:S(2)}) collective-permute-start(bf16[144,128]{1,0:T(8,128)(2,1)S(1)} %get-tuple-element.29._to_left), channel_id=1, source_target_pairs={{8,0},{16,8},{24,16},{32,24},{40,32},{48,40},{56,48},{64,56},{72,6... | collective-permute-start | bytes 110600 | tf_op jit(solution)/shard_map/ppermute | solution.py:425
  75.9 4.2 %collective-permute-start.4 = (bf16[144,128]{1,0:T(8,128)(2,1)S(1)}, bf16[144,128]{1,0:T(8,128)(2,1)S(1)}, u32[]{:S(2)}, u32[]{:S(2)}) collective-permute-start(bf16[144,128]{1,0:T(8,128)(2,1)S(1)} %get-tuple-element.30._to_right), channel_id=1, source_target_pairs={{0,8},{8,16},{16,24},{24,32},{32,40},{40,48},{48,56},{56,64},{64,7... | collective-permute-start | bytes 110600 | tf_op jit(solution)/shard_map/ppermute | solution.py:425
  80.0 10.5 %all-to-all-done.2 = f16[4,16,4480]{2,1,0:T(8,128)(2,1)S(1)} async-done(((f16[4,16,4480]{2,1,0:T(8,128)(2,1)}), f16[4,16,4480]{2,1,0:T(8,128)(2,1)S(1)}, u32[]{:S(2)}, u32[]{:S(2)}) %all-to-all-start.2) | async-done | bytes 573472 | tf_op jit(solution)/shard_map/all_to_all | solution.py:485
  90.6 0.1 convert_reduce_fusion.whole
  90.7 1.4 %shard_map.119 = (f32[512,128]{1,0:T(8,128)}, f32[576,128]{1,0:T(8,128)S(1)}, f32[576,128]{1,0:T(8,128)S(1)}, bf16[432,128]{1,0:T(8,128)(2,1)S(1)}, bf16[432,128]{1,0:T(8,128)(2,1)S(1)}) custom-call(f32[16,4480]{1,0:T(8,128)S(1)} %convert_reduce_fusion.whole, bf16[144,128]{1,0:T(8,128)(2,1)S(1)} %collective-permute-done.4._left.from_left, ...), custom_call_target="tpu_custom_call" | custom-call | tf_op jit(solution)/shard_map/pallas_call | solution.py:408
  92.1 7.2 %collective-permute-start.6 = (bf16[432,128]{1,0:T(8,128)(2,1)S(1)}, bf16[432,128]{1,0:T(8,128)(2,1)S(1)}, u32[]{:S(2)}, u32[]{:S(2)}) collective-permute-start(bf16[432,128]{1,0:T(8,128)(2,1)S(1)} %get-tuple-element.35), channel_id=1, source_target_pairs={{0,1},{1,2},{2,3},{3,4},{4,5},{5,6},{6,7},{8,9},{9,10},{10,11},{11... | collective-permute-start | bytes 331784 | tf_op jit(solution)/shard_map/ppermute | solution.py:425
  99.3 1.9 %collective-permute-start.7 = (bf16[432,128]{1,0:T(8,128)(2,1)S(1)}, bf16[432,128]{1,0:T(8,128)(2,1)S(1)}, u32[]{:S(2)}, u32[]{:S(2)}) collective-permute-start(bf16[432,128]{1,0:T(8,128)(2,1)S(1)} %get-tuple-element.36), channel_id=1, source_target_pairs={{1,0},{2,1},{3,2},{4,3},{5,4},{6,5},{7,6},{9,8},{10,9},{11,10},{12... | collective-permute-start | bytes 331784 | tf_op jit(solution)/shard_map/ppermute | solution.py:425
  101.2 2.6 %shard_map.120 = (f32[9,144,256]{2,1,0:T(8,128)S(1)}, f32[8,144,256]{2,1,0:T(8,128)S(1)}, f32[8,144,256]{2,1,0:T(8,128)S(1)}, f32[8,144,256]{2,1,0:T(8,128)S(1)}, f32[8,144,256]{2,1,0:T(8,128)S(1)}) custom-call(f32[30,144,128]{2,1,0:T(8,128)S(1)} %copy-done.1, bf16[144,128]{1,0:T(8,128)(2,1)S(1)} %collective-permute-done.4._left.from_left, ...), custom_call_target="tpu_custom_call" | custom-call | tf_op jit(solution)/shard_map/pallas_call | solution.py:408
  103.8 5.5 %collective-permute-done.7.hi = bf16[432,128]{1,0:T(8,128)(2,1)S(1)} collective-permute-done((bf16[432,128]{1,0:T(8,128)(2,1)S(1)}, bf16[432,128]{1,0:T(8,128)(2,1)S(1)}, u32[]{:S(2)}, u32[]{:S(2)}) %collective-permute-start.7) | collective-permute-done | bytes 110624 | tf_op jit(solution)/shard_map/ppermute | solution.py:425
  109.3 1.9 %shard_map.121 = f32[512,128]{1,0:T(8,128)} custom-call(f32[576,128]{1,0:T(8,128)S(1)} %get-tuple-element.33.main, f32[576,128]{1,0:T(8,128)S(1)} %get-tuple-element.34.side, bf16[432,128]{1,0:T(8,128)(2,1)S(1)} %collective-permute-done.6.lo, bf16[432,128]{1,0:T(8,128)(2,1)S(1)} %collective-permute-done.7.hi, f32[30,144,128]{2,1,0:T(8,128)S(1)} %copy-done.1, ...), custom_call_target="tpu_custom_call" | custom-call | tf_op jit(solution)/shard_map/pallas_call | solution.py:408
  (19 shorter events, 0.0 us)
Async XLA Ops:
  2.9 21.4 %all-to-all-start = ((f32[64,1,128]{2,1,0:T(1,128)}), f32[64,1,128]{2,1,0:T(1,128)S(1)}, u32[]{:S(2)}, u32[]{:S(2)}) async-start(f32[64,1,128]{2,1,0:T(1,128)} %bitcast.20), calls=%async_computation | async-start | bytes 65536 | tf_op jit(solution)/shard_map/all_to_all | solution.py:464
  15.4 4.2 %collective-permute-start = (bf16[96,128]{1,0:T(8,128)(2,1)}, bf16[96,128]{1,0:T(8,128)(2,1)S(1)}, u32[]{:S(2)}, u32[]{:S(2)}) collective-permute-start(bf16[96,128]{1,0:T(8,128)(2,1)} %get-tuple-element.25), channel_id=1, source_target_pairs={{0,128},{128,256},{256,384},{1,129},{129,257},{257,385},{2,130},{1... | collective-permute-start | bytes 73736 | tf_op jit(solution)/shard_map/ppermute | solution.py:425
  18.4 5.1 %collective-permute-start.1 = (bf16[96,128]{1,0:T(8,128)(2,1)}, bf16[96,128]{1,0:T(8,128)(2,1)S(1)}, u32[]{:S(2)}, u32[]{:S(2)}) collective-permute-start(bf16[96,128]{1,0:T(8,128)(2,1)} %get-tuple-element.26), channel_id=1, source_target_pairs={{128,0},{256,128},{384,256},{129,1},{257,129},{385,257},{130,2},{2... | collective-permute-start | bytes 73736 | tf_op jit(solution)/shard_map/ppermute | solution.py:425
  19.7 4.6 %copy-start.5 = (bf16[96,128]{1,0:T(8,128)(2,1)}, bf16[96,128]{1,0:T(8,128)(2,1)S(1)}, u32[]{:S(2)}) copy-start(bf16[96,128]{1,0:T(8,128)(2,1)S(1)} %collective-permute-done.above._above) | copy-start | bytes 73732
  23.4 0.8 copy-start.7
  24.2 0.6 copy-start.3
  28.1 5.5 %copy-start.2 = (f32[3,4,128,128]{3,2,1,0:T(8,128)S(1)}, f32[3,4,128,128]{3,2,1,0:T(8,128)}, u32[]{:S(2)}) copy-start(f32[3,4,128,128]{3,2,1,0:T(8,128)} %get-tuple-element.24.own) | copy-start | bytes 2359300
  28.1 5.5 %copy-start.6 = (bf16[96,128]{1,0:T(8,128)(2,1)S(1)}, bf16[96,128]{1,0:T(8,128)(2,1)}, u32[]{:S(2)}) copy-start(bf16[96,128]{1,0:T(8,128)(2,1)} %copy-done.5) | copy-start | bytes 73732
  28.1 5.5 %copy-start.8 = (bf16[96,128]{1,0:T(8,128)(2,1)S(1)}, bf16[96,128]{1,0:T(8,128)(2,1)}, u32[]{:S(2)}) copy-start(bf16[96,128]{1,0:T(8,128)(2,1)} %copy-done.7) | copy-start | bytes 73732
  28.1 41.4 %all-to-all-start.1 = ((bf16[16,16,4736]{2,1,0:T(8,128)(2,1)}), bf16[16,16,4736]{2,1,0:T(8,128)(2,1)S(1)}, u32[]{:S(2)}, u32[]{:S(2)}) async-start(bf16[16,16,4736]{2,1,0:T(8,128)(2,1)} %bitcast.15), calls=%async_computation.1 | async-start | bytes 4849664 | tf_op jit(solution)/shard_map/all_to_all | solution.py:479
  33.5 35.2 %copy-start.4 = (f32[64,1,128]{2,1,0:T(1,128)S(1)}, f32[64,1,128]{2,1,0:T(1,128)}, u32[]{:S(2)}) copy-start(f32[64,1,128]{2,1,0:T(1,128)} %copy-done.3) | copy-start | bytes 98308
  33.6 15.4 %collective-permute-start.2 = (bf16[8,144,128]{2,1,0:T(8,128)(2,1)S(1)}, bf16[8,144,128]{2,1,0:T(8,128)(2,1)S(1)}, u32[]{:S(2)}, u32[]{:S(2)}) collective-permute-start(bf16[8,144,128]{2,1,0:T(8,128)(2,1)S(1)} %get-tuple-element.27), channel_id=1, source_target_pairs={{0,1},{1,2},{2,3},{3,4},{4,5},{5,6},{6,7},{8,9},{9,10},{10,11},{11... | collective-permute-start | bytes 884744 | tf_op jit(solution)/shard_map/ppermute | solution.py:425
  45.3 21.4 %collective-permute-start.3 = (bf16[8,144,128]{2,1,0:T(8,128)(2,1)S(1)}, bf16[8,144,128]{2,1,0:T(8,128)(2,1)S(1)}, u32[]{:S(2)}, u32[]{:S(2)}) collective-permute-start(bf16[8,144,128]{2,1,0:T(8,128)(2,1)S(1)} %get-tuple-element.28), channel_id=1, source_target_pairs={{1,0},{2,1},{3,2},{4,3},{5,4},{6,5},{7,6},{9,8},{10,9},{11,10},{12... | collective-permute-start | bytes 884744 | tf_op jit(solution)/shard_map/ppermute | solution.py:425
  67.4 1.4 %copy-start = (f32[30,144,128]{2,1,0:T(8,128)}, f32[30,144,128]{2,1,0:T(8,128)S(1)}, u32[]{:S(2)}) copy-start(f32[30,144,128]{2,1,0:T(8,128)S(1)} %get-tuple-element.37.grids) | copy-start | bytes 6635524
  70.9 30.2 %copy-start.1 = (f32[30,144,128]{2,1,0:T(8,128)S(1)}, f32[30,144,128]{2,1,0:T(8,128)}, u32[]{:S(2)}) copy-start(f32[30,144,128]{2,1,0:T(8,128)} %copy-done) | copy-start | bytes 6635524
  70.9 19.6 %all-to-all-start.2 = ((f16[4,16,4480]{2,1,0:T(8,128)(2,1)}), f16[4,16,4480]{2,1,0:T(8,128)(2,1)S(1)}, u32[]{:S(2)}, u32[]{:S(2)}) async-start(f16[4,16,4480]{2,1,0:T(8,128)(2,1)} %bitcast.16), calls=%async_computation.2 | async-start | bytes 1146880 | tf_op jit(solution)/shard_map/all_to_all | solution.py:485
  74.6 16.1 %collective-permute-start.5 = (bf16[144,128]{1,0:T(8,128)(2,1)S(1)}, bf16[144,128]{1,0:T(8,128)(2,1)S(1)}, u32[]{:S(2)}, u32[]{:S(2)}) collective-permute-start(bf16[144,128]{1,0:T(8,128)(2,1)S(1)} %get-tuple-element.29._to_left), channel_id=1, source_target_pairs={{8,0},{16,8},{24,16},{32,24},{40,32},{48,40},{56,48},{64,56},{72,6... | collective-permute-start | bytes 110600 | tf_op jit(solution)/shard_map/ppermute | solution.py:425
  75.9 14.8 %collective-permute-start.4 = (bf16[144,128]{1,0:T(8,128)(2,1)S(1)}, bf16[144,128]{1,0:T(8,128)(2,1)S(1)}, u32[]{:S(2)}, u32[]{:S(2)}) collective-permute-start(bf16[144,128]{1,0:T(8,128)(2,1)S(1)} %get-tuple-element.30._to_right), channel_id=1, source_target_pairs={{0,8},{8,16},{16,24},{24,32},{32,40},{40,48},{48,56},{56,64},{64,7... | collective-permute-start | bytes 110600 | tf_op jit(solution)/shard_map/ppermute | solution.py:425
  92.1 11.8 %collective-permute-start.6 = (bf16[432,128]{1,0:T(8,128)(2,1)S(1)}, bf16[432,128]{1,0:T(8,128)(2,1)S(1)}, u32[]{:S(2)}, u32[]{:S(2)}) collective-permute-start(bf16[432,128]{1,0:T(8,128)(2,1)S(1)} %get-tuple-element.35), channel_id=1, source_target_pairs={{0,1},{1,2},{2,3},{3,4},{4,5},{5,6},{6,7},{8,9},{9,10},{10,11},{11... | collective-permute-start | bytes 331784 | tf_op jit(solution)/shard_map/ppermute | solution.py:425
  99.3 10.0 %collective-permute-start.7 = (bf16[432,128]{1,0:T(8,128)(2,1)S(1)}, bf16[432,128]{1,0:T(8,128)(2,1)S(1)}, u32[]{:S(2)}, u32[]{:S(2)}) collective-permute-start(bf16[432,128]{1,0:T(8,128)(2,1)S(1)} %get-tuple-element.36), channel_id=1, source_target_pairs={{1,0},{2,1},{3,2},{4,3},{5,4},{6,5},{7,6},{9,8},{10,9},{11,10},{12... | collective-permute-start | bytes 331784 | tf_op jit(solution)/shard_map/ppermute | solution.py:425

commit v9 on v4

--- a/solution.py
+++ b/solution.py
@@ -208,7 +208,7 @@
     out[:, 4352:4480] = corners
 
 
-def unpack_kernel(whole, _left, _right, density, main, side, up, down, turned):
+def unpack_kernel(whole, _left, _right, density, main, side, far, near, turned):
     for k in range(32):
         turned[k * 16 : (k + 1) * 16, :] = whole[:, k * 128 : (k + 1) * 128]
     low = iota((32, 128), 1) < 64
@@ -254,54 +254,63 @@
             block = jnp.where((row16 == r) & (lane16 == at_lane), value, block)
         side[base + 128 : base + 144, :] = block
         density[layer * 128 : (layer + 1) * 128, :] = main[base : base + 128, :]
-    for out, first in ((up, 288), (down, 0)):
-        out[0:288, :] = main[first : first + 288, :].astype(BF16)
-        second = side[first + 144 : first + 288, :]
-        out[288:432, :] = (side[first : first + 144, :] + pltpu.roll(second, 4, 1)).astype(BF16)
+    upper = jnp.where(lax.axis_index("core") == 1, 288, 0)
+    for out, first in ((far, upper), (near, 288 - upper)):
+        first = pl.multiple_of(first, 144)
+        out[0:288, :] = main[pl.ds(first, 288), :].astype(BF16)
+        second = side[pl.ds(first + 144, 144), :]
+        out[288:432, :] = (side[pl.ds(first, 144), :] + pltpu.roll(second, 4, 1)).astype(BF16)
 
 
 def depth(a):
     return 3 if a < 2 else 2
 
 
-def beyond(lo, hi, a, layer):
-    if layer < 3:
-        k = layer - 3 + depth(a)
-        return (lo, 3 * a + k) if k >= 0 else None
-    k = layer - 7
-    return (hi, 3 * a + k) if k < depth(a) else None
-
-
-def layers_kernel(temp, cond, mass, own, up, down, sems):
+def beyond(a, layer):
+    k = layer - 3 + depth(a) if layer < 3 else layer - 7
+    return 3 * a + k if 0 <= k < depth(a) else None
+
+
+def from_layer(far, near, a, layer, at):
+    k = beyond(a, layer)
+    if k is None:
+        return None
+    same, other = (near, far) if layer < 3 else (far, near)
+    upper = lax.axis_index("core") == 1
+    return jnp.where(upper, same[k, at, :].astype(F32), other[k, at, :].astype(F32))
+
+
+def layers_kernel(temp, cond, mass, own, far, near, sems):
+    upper = lax.axis_index("core") == 1
     copies = [pltpu.make_async_copy(a, own.at[i], sems.at[i]) for i, a in enumerate((temp, cond, mass))]
     for copy in copies:
         copy.start()
     for a, copy in enumerate(copies):
         copy.wait()
         for k in range(depth(a)):
-            up[3 * a + k] = own[a, 4 - depth(a) + k].astype(BF16)
-            down[3 * a + k] = own[a, k].astype(BF16)
-
-
-def rows_kernel(own, lo, hi, last, first):
+            last, first = own[a, 4 - depth(a) + k], own[a, k]
+            far[3 * a + k] = jnp.where(upper, last, first).astype(BF16)
+            near[3 * a + k] = jnp.where(upper, first, last).astype(BF16)
+
+
+def rows_kernel(own, far, near, last, first):
     lasts, firsts = [], []
     for a in range(3):
         for layer in range(10):
             if 3 <= layer < 7:
                 lasts.append(own[a, layer - 3, 120:128, :])
                 firsts.append(own[a, layer - 3, 0:8, :])
-            elif found := beyond(lo, hi, a, layer):
-                source, k = found
-                lasts.append(source[k, 112:128, :].astype(F32)[8:16])
-                firsts.append(source[k, 0:16, :].astype(F32)[0:8])
             else:
-                lasts.append(jnp.zeros((8, 128), F32))
-                firsts.append(jnp.zeros((8, 128), F32))
+                zeros = jnp.zeros((8, 128), F32)
+                ends = from_layer(far, near, a, layer, slice(112, 128))
+                lasts.append(zeros if ends is None else ends[8:16])
+                ends = from_layer(far, near, a, layer, slice(0, 16))
+                firsts.append(zeros if ends is None else ends[0:8])
     last[...] = jnp.concatenate(lasts, axis=0).astype(BF16)
     first[...] = jnp.concatenate(firsts, axis=0).astype(BF16)
 
 
-def gather_kernel(own, lo, hi, above, below, out, to_left, to_right):
+def gather_kernel(own, far, near, above, below, out, to_left, to_right):
     over, under = above[...].astype(F32), below[...].astype(F32)
     lane = iota((144, 128), 1)
     left, right = jnp.zeros((144, 128), F32), jnp.zeros((144, 128), F32)
@@ -310,10 +319,9 @@
             i = a * 10 + layer
             if 3 <= layer < 7:
                 source = own[a, layer - 3]
-            elif found := beyond(lo, hi, a, layer):
-                source = found[0][found[1]].astype(F32)
             else:
-                source = jnp.zeros((128, 128), F32)
+                source = from_layer(far, near, a, layer, slice(0, 128))
+                source = jnp.zeros((128, 128), F32) if source is None else source
             piece = jnp.concatenate([source, under[8 * i : 8 * i + 8], over[8 * i : 8 * i + 8]], axis=0)
             out[i] = piece
             base = a * 40 + layer * 4
@@ -369,20 +377,26 @@
 W2 = 1.0 / (2.0 * MIDDLE / SPREAD - W1)
 
 
-def sweep_kernel(main, side, lo, hi, grids, face_layer, face_row, face_col, inverse, residual, out, d0, d1, rest):
+def sweep_kernel(main, side, far, near, grids, face_layer, face_row, face_col, inverse, residual, out, d0, d1, rest):
     lane = iota((144, 128), 1)
     kept = (lane < 2) | (lane >= 126)
+    upper = lax.axis_index("core") == 1
 
     def supplied(i):
         if 3 <= i <= 6:
             at = (i - 3) * 144
             return main[at : at + 144, :], side[at : at + 144, :]
-        source, second = (lo, i == 2) if i < 3 else (hi, i == 8)
+        second = i in (2, 8)
         at = 144 if second else 0
-        beside = source[288:432, :].astype(F32)
-        if second:
-            beside = turned_by(beside, -4, 1)
-        return source[at : at + 144, :].astype(F32), jnp.where(kept, beside, 0.0)
+        same, other = (near, far) if i < 3 else (far, near)
+
+        def rows(at):
+            return jnp.where(
+                upper, same[at : at + 144, :].astype(F32), other[at : at + 144, :].astype(F32)
+            )
+
+        beside = turned_by(rows(288), -4, 1) if second else rows(288)
+        return rows(at), jnp.where(kept, beside, 0.0)
 
     for i in range(1, 9):
         start = residual[i - 1] + jnp.concatenate(supplied(i), axis=1)
@@ -434,19 +448,27 @@
     return lax.ppermute(to_next, axis, up), lax.ppermute(to_last, axis, down)
 
 
+def swap_layers(far, near):
+    apart = [(i, i + 1) for i in range(1, lax.axis_size(LAYER) - 1, 2)]
+    return (
+        lax.ppermute(far, LAYER, apart + [(b, a) for a, b in apart]),
+        lax.ppermute(near, "core", [(0, 1), (1, 0)]),
+    )
+
+
 def extended_grids(temp, cond, mass):
     eight, rows, edge = sds((8, 128, 128), BF16), sds((240, 128), BF16), sds((144, 128), BF16)
-    own, up, down = call(
+    own, far, near = call(
         layers_kernel,
         (sds((3, 4, 128, 128), F32), eight, eight),
         (temp, cond, mass),
         scratch=[pltpu.SemaphoreType.DMA((3,))],
         far=range(3),
     )
-    lo, hi = exchange(up, down, LAYER)
-    above, below = exchange(*call(rows_kernel, (rows, rows), (own, lo, hi)), "row")
+    far, near = swap_layers(far, near)
+    above, below = exchange(*call(rows_kernel, (rows, rows), (own, far, near)), "row")
     wide, to_left, to_right = call(
-        gather_kernel, (sds((30, 144, 128), F32), edge, edge), (own, lo, hi, above, below), mib=24
+        gather_kernel, (sds((30, 144, 128), F32), edge, edge), (own, far, near, above, below), mib=24
     )
     return wide, (to_left, to_right), exchange(to_right, to_left, COL)
 
@@ -501,18 +523,18 @@
     )
     terms = operator(wide, *beside)
     block, strip = sds((576, 128), F32), sds((432, 128), BF16)
-    density, main, side, up, down = call(
+    density, main, side, far, near = call(
         unpack_kernel,
         (sds((512, 128), F32), block, block, strip, strip),
         (jnp.sum(parts.astype(F32), axis=0), *beside),
         scratch=[pltpu.VMEM((512, 128), F32)],
     )
-    lo, hi = exchange(up, down, LAYER)
+    far, near = swap_layers(far, near)
     eight = pltpu.VMEM((8, 144, 256), F32)
     guess = call(
         sweep_kernel,
         sds((512, 128), F32),
-        (main, side, lo, hi, wide, *terms),
+        (main, side, far, near, wide, *terms),
         mib=40,
         scratch=[eight, eight, eight],
     )

time: 112 us -> 103 us (0.920)
  waiting for transfers between devices: 32.1 us -> 23.2 us
    ppermute x8 -> x4, waiting for transfers between devices: 27.3 us -> 3.2 us  [exchange(): return (lax.ppermute(to_next, axis, up), lax.ppermute(to_last, axis, down))]
    ppermute x8 -> x4, starting transfers between devices: 33.2 us -> 10 us  [exchange(): return (lax.ppermute(to_next, axis, up), lax.ppermute(to_last, axis, down))]
    ppermute x0 -> x4, starting transfers between devices: none -> 23 us  [the longest x2 19.2 us: swap_layers(): lax.ppermute(far, LAYER, apart + [(b, a) for a, b in apart])]
    ppermute x0 -> x4, waiting for transfers between devices: none -> 10.3 us  [the longest x2 10.3 us: swap_layers(): lax.ppermute(far, LAYER, apart + [(b, a) for a, b in apart])]
    all_to_all x1, waiting for transfers between devices: 4.73 us -> 9.76 us  [shards(): lax.all_to_all(partial.astype(jnp.float16).reshape(4, 16, 4480), 'zlo', s...]
  transfers between devices with their start and end apart: 10 -> 10, of which waited for: 5 -> 3; matrix products, arithmetic and copies ran while one was open for 0% -> 0% of each run, Pallas kernels for 4% -> 4%
where the time goes in v9:
time: 103 us; the launch traced here: 102 us
  starting transfers between devices  40.5 us (39%)
  waiting for transfers between devices  23.2 us (23%)
  blocking collectives  21.6 us (21%)
  Pallas kernels  13.6 us (13%)
  local copies, waits for them, and re-layouts  1.39 us (1%)
    all_to_all x1, blocking collectives, shards(): lax.all_to_all(message.reshape(64, 1, 128), CUBE, split_axis=0, concat_ax...  21.6 us
    ppermute x2, starting transfers between devices, swap_layers(): lax.ppermute(far, LAYER, apart + [(b, a) for a, b in apart])  19.2 us
    pallas_call x10, Pallas kernels, call(): pl.pallas_call(kernel, out_shape=shape, in_specs=[anywhere if i in far el...  13.6 us
    ppermute x2, waiting for transfers between devices, swap_layers(): lax.ppermute(far, LAYER, apart + [(b, a) for a, b in apart])  10.3 us
    ppermute x4, starting transfers between devices, exchange(): return (lax.ppermute(to_next, axis, up), lax.ppermute(to_last, axis, down))  10 us
    all_to_all x1, waiting for transfers between devices, shards(): lax.all_to_all(partial.astype(jnp.float16).reshape(4, 16, 4480), 'zlo', s...  9.76 us
    all_to_all x1, starting transfers between devices, shards(): lax.all_to_all(send.reshape(16, 16, 4736), PLANE, split_axis=0, concat_ax...  3.87 us
    ppermute x2, starting transfers between devices, swap_layers(): lax.ppermute(near, 'core', [(0, 1), (1, 0)])  3.84 us
  transfers between devices with their start and end apart: 10, of which 3 were waited for; matrix products, arithmetic and copies ran while one was open for 0% of the time, Pallas kernels for 4%

profile of v9, /device:TPU:1, one launch (start us, length us, event | category | flops | bytes accessed | tf_op | source)
XLA Modules:
  0.0 102.2 jit_solution(176374217719097250)
XLA Ops:
  0.6 1.8 %shard_map.113 = (f32[64,128]{1,0:T(8,128)}, bf16[1024,64]{1,0:T(8,128)(2,1)}, s32[64,128]{1,0:T(8,128)}) custom-call(f32[4,128,128]{2,1,0:T(8,128)} %temp.3, s32[1,64]{1,0:T(1,128)} %bitcast.21, s32[1,64]{1,0:T(1,128)} %place.1, s32[1,64]{1,0:T(1,128)} %holder.1, s32[1,16]{1,0:T(1,128)} %tier.1), custom_call_target="tpu_custom_call" | custom-call | tf_op jit(solution)/shard_map/pallas_call | solution.py:431
  2.4 21.6 %all_to_all.15 = f32[64,1,128]{2,1,0:T(1,128)} all-to-all(f32[64,1,128]{2,1,0:T(1,128)} %bitcast.20), channel_id=1, replica_groups=mesh['row'=4,'zlo'=4,'y'=4,'zhi'=4,'core'=2] {'row','zlo','y'}, dimensions={0} | all-to-all | bytes 65536 | tf_op jit(solution)/shard_map/all_to_all | solution.py:500
  24.1 3.2 %shard_map.115 = bf16[256,4736]{1,0:T(8,128)(2,1)} custom-call(f32[64,128]{1,0:T(8,128)} %bitcast.13, s32[64,128]{1,0:T(8,128)} %get-tuple-element.24.far_columns, f32[1,16]{1,0:T(1,128)} %far_warming.1, bf16[64,4096]{1,0:T(8,128)(2,1)} %bitcast.17, bf16[64,4096]{1,0:T(8,128)(2,1)} %bitcast.18, bf16[1024,64]{1,0:T(8,128)(2,1)} %get-tuple-element.25.far_placing), custom_call_target="tpu_custom_call" | custom-call | tf_op jit(solution)/shard_map/pallas_call | solution.py:431
  27.2 0.0 copy-start.2
  27.3 0.0 copy-start.4
  27.3 0.0 copy-start.5
  27.3 3.9 %all-to-all-start.1 = ((bf16[16,16,4736]{2,1,0:T(8,128)(2,1)}), bf16[16,16,4736]{2,1,0:T(8,128)(2,1)S(1)}, u32[]{:S(2)}, u32[]{:S(2)}) async-start(bf16[16,16,4736]{2,1,0:T(8,128)(2,1)} %bitcast.15), calls=%async_computation.1 | async-start | bytes 4849664 | tf_op jit(solution)/shard_map/all_to_all | solution.py:515
  31.2 0.2 shard_map.116
  31.4 10.7 %collective-permute-start = (bf16[8,128,128]{2,1,0:T(8,128)(2,1)S(1)}, bf16[8,128,128]{2,1,0:T(8,128)(2,1)S(1)}, u32[]{:S(2)}, u32[]{:S(2)}) collective-permute-start(bf16[8,128,128]{2,1,0:T(8,128)(2,1)S(1)} %get-tuple-element.27), channel_id=1, source_target_pairs={{1,2},{3,4},{5,6},{2,1},{4,3},{6,5},{9,10},{11,12},{13,14},{10,9},... | collective-permute-start | bytes 786440 | tf_op jit(solution)/shard_map/ppermute | solution.py:454
  42.0 1.9 %collective-permute-start.1 = (bf16[8,128,128]{2,1,0:T(8,128)(2,1)S(1)}, bf16[8,128,128]{2,1,0:T(8,128)(2,1)S(1)}, u32[]{:S(2)}, u32[]{:S(2)}) collective-permute-start(bf16[8,128,128]{2,1,0:T(8,128)(2,1)S(1)} %get-tuple-element.28), channel_id=1, source_target_pairs={{0,1},{1,0},{2,3},{3,2},{4,5},{5,4},{6,7},{7,6},{8,9},{9,8},{10,11... | collective-permute-start | bytes 786440 | tf_op jit(solution)/shard_map/ppermute | solution.py:455
  44.0 10.3 %collective-permute-done.far = bf16[8,128,128]{2,1,0:T(8,128)(2,1)S(1)} collective-permute-done((bf16[8,128,128]{2,1,0:T(8,128)(2,1)S(1)}, bf16[8,128,128]{2,1,0:T(8,128)(2,1)S(1)}, u32[]{:S(2)}, u32[]{:S(2)}) %collective-permute-start) | collective-permute-done | bytes 262176 | tf_op jit(solution)/shard_map/ppermute | solution.py:454
  54.2 0.0 collective-permute-done.1.near
  54.3 3.4 %collective-permute-start.2 = (bf16[240,128]{1,0:T(8,128)(2,1)S(1)}, bf16[240,128]{1,0:T(8,128)(2,1)S(1)}, u32[]{:S(2)}, u32[]{:S(2)}) collective-permute-start(bf16[240,128]{1,0:T(8,128)(2,1)S(1)} %get-tuple-element.29), channel_id=1, source_target_pairs={{0,128},{128,256},{256,384},{1,129},{129,257},{257,385},{2,130},{1... | collective-permute-start | bytes 184328 | tf_op jit(solution)/shard_map/ppermute | solution.py:448
  57.7 1.3 %collective-permute-start.3 = (bf16[240,128]{1,0:T(8,128)(2,1)S(1)}, bf16[240,128]{1,0:T(8,128)(2,1)S(1)}, u32[]{:S(2)}, u32[]{:S(2)}) collective-permute-start(bf16[240,128]{1,0:T(8,128)(2,1)S(1)} %get-tuple-element.30), channel_id=1, source_target_pairs={{128,0},{256,128},{384,256},{129,1},{257,129},{385,257},{130,2},{2... | collective-permute-start | bytes 184328 | tf_op jit(solution)/shard_map/ppermute | solution.py:448
  59.0 0.7 shard_map.114.selector
  59.8 0.0 collective-permute-done.2.above
  59.8 3.2 %collective-permute-done.3.below = bf16[240,128]{1,0:T(8,128)(2,1)S(1)} collective-permute-done((bf16[240,128]{1,0:T(8,128)(2,1)S(1)}, bf16[240,128]{1,0:T(8,128)(2,1)S(1)}, u32[]{:S(2)}, u32[]{:S(2)}) %collective-permute-start.3) | collective-permute-done | bytes 61472 | tf_op jit(solution)/shard_map/ppermute | solution.py:448
  63.0 0.6 shard_map.118
  63.6 1.4 %copy-done = f32[30,144,128]{2,1,0:T(8,128)} copy-done((f32[30,144,128]{2,1,0:T(8,128)}, f32[30,144,128]{2,1,0:T(8,128)S(1)}, u32[]{:S(2)}) %copy-start) | copy-done | bytes 2211864
  65.0 0.6 shard_map.119
  65.6 0.9 convert_element_type.6
  66.5 3.6 %all-to-all-start.2 = ((f16[4,16,4480]{2,1,0:T(8,128)(2,1)}), f16[4,16,4480]{2,1,0:T(8,128)(2,1)S(1)}, u32[]{:S(2)}, u32[]{:S(2)}) async-start(f16[4,16,4480]{2,1,0:T(8,128)(2,1)} %bitcast.16), calls=%async_computation.2 | async-start | bytes 1146880 | tf_op jit(solution)/shard_map/all_to_all | solution.py:521
  70.1 1.3 %collective-permute-start.5 = (bf16[144,128]{1,0:T(8,128)(2,1)S(1)}, bf16[144,128]{1,0:T(8,128)(2,1)S(1)}, u32[]{:S(2)}, u32[]{:S(2)}) collective-permute-start(bf16[144,128]{1,0:T(8,128)(2,1)S(1)} %get-tuple-element.31._to_left), channel_id=1, source_target_pairs={{8,0},{16,8},{24,16},{32,24},{40,32},{48,40},{56,48},{64,56},{72,6... | collective-permute-start | bytes 110600 | tf_op jit(solution)/shard_map/ppermute | solution.py:448
  71.4 4.0 %collective-permute-start.4 = (bf16[144,128]{1,0:T(8,128)(2,1)S(1)}, bf16[144,128]{1,0:T(8,128)(2,1)S(1)}, u32[]{:S(2)}, u32[]{:S(2)}) collective-permute-start(bf16[144,128]{1,0:T(8,128)(2,1)S(1)} %get-tuple-element.32._to_right), channel_id=1, source_target_pairs={{0,8},{8,16},{16,24},{24,32},{32,40},{40,48},{48,56},{56,64},{64,7... | collective-permute-start | bytes 110600 | tf_op jit(solution)/shard_map/ppermute | solution.py:448
  75.4 9.8 %all-to-all-done.2 = f16[4,16,4480]{2,1,0:T(8,128)(2,1)S(1)} async-done(((f16[4,16,4480]{2,1,0:T(8,128)(2,1)}), f16[4,16,4480]{2,1,0:T(8,128)(2,1)S(1)}, u32[]{:S(2)}, u32[]{:S(2)}) %all-to-all-start.2) | async-done | bytes 573472 | tf_op jit(solution)/shard_map/all_to_all | solution.py:521
  85.1 0.1 convert_reduce_fusion.whole
  85.2 0.0 collective-permute-done.5._right.from_right
  85.2 1.4 %shard_map.120 = (f32[512,128]{1,0:T(8,128)}, f32[576,128]{1,0:T(8,128)S(1)}, f32[576,128]{1,0:T(8,128)S(1)}, bf16[432,128]{1,0:T(8,128)(2,1)S(1)}, bf16[432,128]{1,0:T(8,128)(2,1)S(1)}) custom-call(f32[16,4480]{1,0:T(8,128)S(1)} %convert_reduce_fusion.whole, bf16[144,128]{1,0:T(8,128)(2,1)S(1)} %collective-permute-done.4._left.from_left, ...), custom_call_target="tpu_custom_call" | custom-call | tf_op jit(solution)/shard_map/pallas_call | solution.py:431
  86.6 8.6 %collective-permute-start.6 = (bf16[432,128]{1,0:T(8,128)(2,1)S(1)}, bf16[432,128]{1,0:T(8,128)(2,1)S(1)}, u32[]{:S(2)}, u32[]{:S(2)}) collective-permute-start(bf16[432,128]{1,0:T(8,128)(2,1)S(1)} %get-tuple-element.35), channel_id=1, source_target_pairs={{1,2},{3,4},{5,6},{2,1},{4,3},{6,5},{9,10},{11,12},{13,14},{10,9},... | collective-permute-start | bytes 331784 | tf_op jit(solution)/shard_map/ppermute | solution.py:454
  95.2 1.9 %collective-permute-start.7 = (bf16[432,128]{1,0:T(8,128)(2,1)S(1)}, bf16[432,128]{1,0:T(8,128)(2,1)S(1)}, u32[]{:S(2)}, u32[]{:S(2)}) collective-permute-start(bf16[432,128]{1,0:T(8,128)(2,1)S(1)} %get-tuple-element.36), channel_id=1, source_target_pairs={{0,1},{1,0},{2,3},{3,2},{4,5},{5,4},{6,7},{7,6},{8,9},{9,8},{10,11... | collective-permute-start | bytes 331784 | tf_op jit(solution)/shard_map/ppermute | solution.py:455
  97.1 2.9 %shard_map.121 = (f32[9,144,256]{2,1,0:T(8,128)S(1)}, f32[8,144,256]{2,1,0:T(8,128)S(1)}, f32[8,144,256]{2,1,0:T(8,128)S(1)}, f32[8,144,256]{2,1,0:T(8,128)S(1)}, f32[8,144,256]{2,1,0:T(8,128)S(1)}) custom-call(f32[30,144,128]{2,1,0:T(8,128)S(1)} %copy-done.1, bf16[144,128]{1,0:T(8,128)(2,1)S(1)} %collective-permute-done.4._left.from_left, ...), custom_call_target="tpu_custom_call" | custom-call | tf_op jit(solution)/shard_map/pallas_call | solution.py:431
  100.0 2.2 %shard_map.122 = f32[512,128]{1,0:T(8,128)} custom-call(f32[576,128]{1,0:T(8,128)S(1)} %get-tuple-element.33.main, f32[576,128]{1,0:T(8,128)S(1)} %get-tuple-element.34.side, bf16[432,128]{1,0:T(8,128)(2,1)S(1)} %collective-permute-done.6.far, bf16[432,128]{1,0:T(8,128)(2,1)S(1)} %collective-permute-done.7.near, f32[30,144,128]{2,1,0:T(8,128)S(1)} %copy-done.1, ...), custom_call_target="tpu_custom_call" | custom-call | tf_op jit(solution)/shard_map/pallas_call | solution.py:431
  (13 shorter events, 0.1 us)
Async XLA Ops:
  27.2 3.9 %copy-start.2 = (f32[4,128,128]{2,1,0:T(8,128)S(1)}, f32[4,128,128]{2,1,0:T(8,128)}, u32[]{:S(2)}) copy-start(f32[4,128,128]{2,1,0:T(8,128)} %temp.3) | copy-start | bytes 786436
  27.3 3.9 %copy-start.4 = (f32[4,128,128]{2,1,0:T(8,128)S(1)}, f32[4,128,128]{2,1,0:T(8,128)}, u32[]{:S(2)}) copy-start(f32[4,128,128]{2,1,0:T(8,128)} %cond.1) | copy-start | bytes 786436
  27.3 3.9 %copy-start.5 = (f32[4,128,128]{2,1,0:T(8,128)S(1)}, f32[4,128,128]{2,1,0:T(8,128)}, u32[]{:S(2)}) copy-start(f32[4,128,128]{2,1,0:T(8,128)} %mass.1) | copy-start | bytes 786436
  27.3 37.7 %all-to-all-start.1 = ((bf16[16,16,4736]{2,1,0:T(8,128)(2,1)}), bf16[16,16,4736]{2,1,0:T(8,128)(2,1)S(1)}, u32[]{:S(2)}, u32[]{:S(2)}) async-start(bf16[16,16,4736]{2,1,0:T(8,128)(2,1)} %bitcast.15), calls=%async_computation.1 | async-start | bytes 4849664 | tf_op jit(solution)/shard_map/all_to_all | solution.py:515
  31.2 27.8 %copy-start.3 = (f32[64,1,128]{2,1,0:T(1,128)S(1)}, f32[64,1,128]{2,1,0:T(1,128)}, u32[]{:S(2)}) copy-start(f32[64,1,128]{2,1,0:T(1,128)} %all_to_all.15) | copy-start | bytes 98308
  31.4 22.9 %collective-permute-start = (bf16[8,128,128]{2,1,0:T(8,128)(2,1)S(1)}, bf16[8,128,128]{2,1,0:T(8,128)(2,1)S(1)}, u32[]{:S(2)}, u32[]{:S(2)}) collective-permute-start(bf16[8,128,128]{2,1,0:T(8,128)(2,1)S(1)} %get-tuple-element.27), channel_id=1, source_target_pairs={{1,2},{3,4},{5,6},{2,1},{4,3},{6,5},{9,10},{11,12},{13,14},{10,9},... | collective-permute-start | bytes 786440 | tf_op jit(solution)/shard_map/ppermute | solution.py:454
  42.0 12.2 %collective-permute-start.1 = (bf16[8,128,128]{2,1,0:T(8,128)(2,1)S(1)}, bf16[8,128,128]{2,1,0:T(8,128)(2,1)S(1)}, u32[]{:S(2)}, u32[]{:S(2)}) collective-permute-start(bf16[8,128,128]{2,1,0:T(8,128)(2,1)S(1)} %get-tuple-element.28), channel_id=1, source_target_pairs={{0,1},{1,0},{2,3},{3,2},{4,5},{5,4},{6,7},{7,6},{8,9},{9,8},{10,11... | collective-permute-start | bytes 786440 | tf_op jit(solution)/shard_map/ppermute | solution.py:455
  54.3 5.5 %collective-permute-start.2 = (bf16[240,128]{1,0:T(8,128)(2,1)S(1)}, bf16[240,128]{1,0:T(8,128)(2,1)S(1)}, u32[]{:S(2)}, u32[]{:S(2)}) collective-permute-start(bf16[240,128]{1,0:T(8,128)(2,1)S(1)} %get-tuple-element.29), channel_id=1, source_target_pairs={{0,128},{128,256},{256,384},{1,129},{129,257},{257,385},{2,130},{1... | collective-permute-start | bytes 184328 | tf_op jit(solution)/shard_map/ppermute | solution.py:448
  57.7 5.3 %collective-permute-start.3 = (bf16[240,128]{1,0:T(8,128)(2,1)S(1)}, bf16[240,128]{1,0:T(8,128)(2,1)S(1)}, u32[]{:S(2)}, u32[]{:S(2)}) collective-permute-start(bf16[240,128]{1,0:T(8,128)(2,1)S(1)} %get-tuple-element.30), channel_id=1, source_target_pairs={{128,0},{256,128},{384,256},{129,1},{257,129},{385,257},{130,2},{2... | collective-permute-start | bytes 184328 | tf_op jit(solution)/shard_map/ppermute | solution.py:448
  63.6 1.4 %copy-start = (f32[30,144,128]{2,1,0:T(8,128)}, f32[30,144,128]{2,1,0:T(8,128)S(1)}, u32[]{:S(2)}) copy-start(f32[30,144,128]{2,1,0:T(8,128)S(1)} %get-tuple-element.37.grids) | copy-start | bytes 6635524
  66.5 30.6 %copy-start.1 = (f32[30,144,128]{2,1,0:T(8,128)S(1)}, f32[30,144,128]{2,1,0:T(8,128)}, u32[]{:S(2)}) copy-start(f32[30,144,128]{2,1,0:T(8,128)} %copy-done) | copy-start | bytes 6635524
  66.5 18.7 %all-to-all-start.2 = ((f16[4,16,4480]{2,1,0:T(8,128)(2,1)}), f16[4,16,4480]{2,1,0:T(8,128)(2,1)S(1)}, u32[]{:S(2)}, u32[]{:S(2)}) async-start(f16[4,16,4480]{2,1,0:T(8,128)(2,1)} %bitcast.16), calls=%async_computation.2 | async-start | bytes 1146880 | tf_op jit(solution)/shard_map/all_to_all | solution.py:521
  70.1 15.1 %collective-permute-start.5 = (bf16[144,128]{1,0:T(8,128)(2,1)S(1)}, bf16[144,128]{1,0:T(8,128)(2,1)S(1)}, u32[]{:S(2)}, u32[]{:S(2)}) collective-permute-start(bf16[144,128]{1,0:T(8,128)(2,1)S(1)} %get-tuple-element.31._to_left), channel_id=1, source_target_pairs={{8,0},{16,8},{24,16},{32,24},{40,32},{48,40},{56,48},{64,56},{72,6... | collective-permute-start | bytes 110600 | tf_op jit(solution)/shard_map/ppermute | solution.py:448
  71.4 13.8 %collective-permute-start.4 = (bf16[144,128]{1,0:T(8,128)(2,1)S(1)}, bf16[144,128]{1,0:T(8,128)(2,1)S(1)}, u32[]{:S(2)}, u32[]{:S(2)}) collective-permute-start(bf16[144,128]{1,0:T(8,128)(2,1)S(1)} %get-tuple-element.32._to_right), channel_id=1, source_target_pairs={{0,8},{8,16},{16,24},{24,32},{32,40},{40,48},{48,56},{56,64},{64,7... | collective-permute-start | bytes 110600 | tf_op jit(solution)/shard_map/ppermute | solution.py:448
  86.6 13.4 %collective-permute-start.6 = (bf16[432,128]{1,0:T(8,128)(2,1)S(1)}, bf16[432,128]{1,0:T(8,128)(2,1)S(1)}, u32[]{:S(2)}, u32[]{:S(2)}) collective-permute-start(bf16[432,128]{1,0:T(8,128)(2,1)S(1)} %get-tuple-element.35), channel_id=1, source_target_pairs={{1,2},{3,4},{5,6},{2,1},{4,3},{6,5},{9,10},{11,12},{13,14},{10,9},... | collective-permute-start | bytes 331784 | tf_op jit(solution)/shard_map/ppermute | solution.py:454
  95.2 4.9 %collective-permute-start.7 = (bf16[432,128]{1,0:T(8,128)(2,1)S(1)}, bf16[432,128]{1,0:T(8,128)(2,1)S(1)}, u32[]{:S(2)}, u32[]{:S(2)}) collective-permute-start(bf16[432,128]{1,0:T(8,128)(2,1)S(1)} %get-tuple-element.36), channel_id=1, source_target_pairs={{0,1},{1,0},{2,3},{3,2},{4,5},{5,4},{6,7},{7,6},{8,9},{9,8},{10,11... | collective-permute-start | bytes 331784 | tf_op jit(solution)/shard_map/ppermute | solution.py:455

commit v10 on v9

--- a/solution.py
+++ b/solution.py
@@ -189,7 +189,7 @@
         put(5 + k, ids, z * 16 + layer)
 
 
-def combine_kernel(selector, received, _to_left, _to_right, out):
+def combine_kernel(selector, received, _outer, _inner, out):
     def add(k, start, width):
         return jnp.dot(
             selector[k * 64 : (k + 1) * 64, :],
@@ -208,7 +208,7 @@
     out[:, 4352:4480] = corners
 
 
-def unpack_kernel(whole, _left, _right, density, main, side, far, near, turned):
+def unpack_kernel(whole, _outer, _inner, density, main, side, far, near, turned):
     for k in range(32):
         turned[k * 16 : (k + 1) * 16, :] = whole[:, k * 128 : (k + 1) * 128]
     low = iota((32, 128), 1) < 64
@@ -293,7 +293,7 @@
             near[3 * a + k] = jnp.where(upper, first, last).astype(BF16)
 
 
-def rows_kernel(own, far, near, last, first):
+def rows_kernel(own, far, near, outer, inner):
     lasts, firsts = [], []
     for a in range(3):
         for layer in range(10):
@@ -306,12 +306,14 @@
                 lasts.append(zeros if ends is None else ends[8:16])
                 ends = from_layer(far, near, a, layer, slice(0, 16))
                 firsts.append(zeros if ends is None else ends[0:8])
-    last[...] = jnp.concatenate(lasts, axis=0).astype(BF16)
-    first[...] = jnp.concatenate(firsts, axis=0).astype(BF16)
-
-
-def gather_kernel(own, far, near, above, below, out, to_left, to_right):
-    over, under = above[...].astype(F32), below[...].astype(F32)
+    last, first = jnp.concatenate(lasts, axis=0), jnp.concatenate(firsts, axis=0)
+    odd = is_odd("row")
+    outer[...] = jnp.where(odd, last, first).astype(BF16)
+    inner[...] = jnp.where(odd, first, last).astype(BF16)
+
+
+def gather_kernel(own, far, near, outer, inner, out, to_outer, to_inner):
+    over, under = sides(is_odd("row"), outer, inner)
     lane = iota((144, 128), 1)
     left, right = jnp.zeros((144, 128), F32), jnp.zeros((144, 128), F32)
     for a in range(3):
@@ -328,8 +330,9 @@
             here = (lane >= base) & (lane < base + 3)
             left = jnp.where(here, pltpu.roll(piece, base, 1) if base else piece, left)
             right = jnp.where(here, pltpu.roll(piece, base + 3, 1), right)
-    to_left[...] = left.astype(BF16)
-    to_right[...] = right.astype(BF16)
+    odd = is_odd("y")
+    to_outer[...] = jnp.where(odd, right, left).astype(BF16)
+    to_inner[...] = jnp.where(odd, left, right).astype(BF16)
 
 
 def turned_by(x, shift, axis):
@@ -345,8 +348,8 @@
     )
 
 
-def operator_kernel(grids, from_left, from_right, face_layer, face_row, face_col, inverse, residual, wide):
-    left, right = from_left[...].astype(F32), from_right[...].astype(F32)
+def operator_kernel(grids, outer, inner, face_layer, face_row, face_col, inverse, residual, wide):
+    left, right = sides(is_odd("y"), outer, inner)
     lane = iota((144, 128), 1)
     for a in range(3):
         for layer in range(10):
@@ -438,14 +441,23 @@
     )(*args)
 
 
-def pairs(axis):
-    up = [(i, i + 1) for i in range(lax.axis_size(axis) - 1)]
-    return up, [(b, a) for a, b in up]
-
-
-def exchange(to_next, to_last, axis):
-    up, down = pairs(axis)
-    return lax.ppermute(to_next, axis, up), lax.ppermute(to_last, axis, down)
+def swap_sides(to_outer, to_inner, axis):
+    count = lax.axis_size(axis)
+
+    def swapped(data, first):
+        apart = [(i, i + 1) for i in range(first, count - 1, 2)]
+        return lax.ppermute(data, axis, apart + [(b, a) for a, b in apart])
+
+    return swapped(to_outer, 1), swapped(to_inner, 0)
+
+
+def is_odd(axis):
+    return (lax.axis_index(axis) & 1) == 1
+
+
+def sides(odd, outer, inner):
+    outer, inner = outer[...].astype(F32), inner[...].astype(F32)
+    return jnp.where(odd, inner, outer), jnp.where(odd, outer, inner)
 
 
 def swap_layers(far, near):
@@ -466,19 +478,19 @@
         far=range(3),
     )
     far, near = swap_layers(far, near)
-    above, below = exchange(*call(rows_kernel, (rows, rows), (own, far, near)), "row")
-    wide, to_left, to_right = call(
-        gather_kernel, (sds((30, 144, 128), F32), edge, edge), (own, far, near, above, below), mib=24
-    )
-    return wide, (to_left, to_right), exchange(to_right, to_left, COL)
-
-
-def operator(wide, from_left, from_right):
+    beside = swap_sides(*call(rows_kernel, (rows, rows), (own, far, near)), "row")
+    wide, *edges = call(
+        gather_kernel, (sds((30, 144, 128), F32), edge, edge), (own, far, near, *beside), mib=24
+    )
+    return wide, edges, swap_sides(*edges, COL)
+
+
+def operator(wide, outer, inner):
     eight = sds((8, 144, 256), F32)
     return call(
         operator_kernel,
         (sds((9, 144, 256), F32), eight, eight, eight, eight),
-        (wide, from_left, from_right),
+        (wide, outer, inner),
         mib=32,
         scratch=[pltpu.VMEM((30, 144, 256), F32)],
     )

time: 103 us -> 103 us (level)
  waiting for transfers between devices: 23.2 us -> 20.5 us
  starting transfers between devices: 40.5 us -> 43 us
    ppermute x4, starting transfers between devices: 10 us -> 12.5 us  [swapped(): return lax.ppermute(data, axis, apart + [(b, a) for a, b in apart])]
    ppermute x4, waiting for transfers between devices: 3.2 us -> 1.13 us  [swapped(): return lax.ppermute(data, axis, apart + [(b, a) for a, b in apart])]
where the time goes in v10:
time: 103 us; the launch traced here: 102 us
  starting transfers between devices  43 us (42%)
  blocking collectives  21.6 us (21%)
  waiting for transfers between devices  20.5 us (20%)
  Pallas kernels  13.6 us (13%)
  local copies, waits for them, and re-layouts  1.39 us (1%)
    all_to_all x1, blocking collectives, shards(): lax.all_to_all(message.reshape(64, 1, 128), CUBE, split_axis=0, concat_ax...  21.6 us
    ppermute x2, starting transfers between devices, swap_layers(): lax.ppermute(far, LAYER, apart + [(b, a) for a, b in apart])  19.2 us
    pallas_call x10, Pallas kernels, call(): pl.pallas_call(kernel, out_shape=shape, in_specs=[anywhere if i in far el...  13.6 us
    ppermute x4, starting transfers between devices, swapped(): return lax.ppermute(data, axis, apart + [(b, a) for a, b in apart])  12.5 us
    ppermute x2, waiting for transfers between devices, swap_layers(): lax.ppermute(far, LAYER, apart + [(b, a) for a, b in apart])  10.3 us
    all_to_all x1, waiting for transfers between devices, shards(): lax.all_to_all(partial.astype(jnp.float16).reshape(4, 16, 4480), 'zlo', s...  9.1 us
    all_to_all x1, starting transfers between devices, shards(): lax.all_to_all(send.reshape(16, 16, 4736), PLANE, split_axis=0, concat_ax...  3.87 us
    ppermute x2, starting transfers between devices, swap_layers(): lax.ppermute(near, 'core', [(0, 1), (1, 0)])  3.84 us
  transfers between devices with their start and end apart: 10, of which 3 were waited for; matrix products, arithmetic and copies ran while one was open for 0% of the time, Pallas kernels for 4%

profile of v10, /device:TPU:1, one launch (start us, length us, event | category | flops | bytes accessed | tf_op | source)
XLA Modules:
  0.0 102.0 jit_solution(5027827492048836373)
XLA Ops:
  0.6 1.8 %shard_map.113 = (f32[64,128]{1,0:T(8,128)}, bf16[1024,64]{1,0:T(8,128)(2,1)}, s32[64,128]{1,0:T(8,128)}) custom-call(f32[4,128,128]{2,1,0:T(8,128)} %temp.3, s32[1,64]{1,0:T(1,128)} %bitcast.21, s32[1,64]{1,0:T(1,128)} %place.1, s32[1,64]{1,0:T(1,128)} %holder.1, s32[1,16]{1,0:T(1,128)} %tier.1), custom_call_target="tpu_custom_call" | custom-call | tf_op jit(solution)/shard_map/pallas_call | solution.py:434
  2.4 21.6 %all_to_all.15 = f32[64,1,128]{2,1,0:T(1,128)} all-to-all(f32[64,1,128]{2,1,0:T(1,128)} %bitcast.20), channel_id=1, replica_groups=mesh['row'=4,'zlo'=4,'y'=4,'zhi'=4,'core'=2] {'row','zlo','y'}, dimensions={0} | all-to-all | bytes 65536 | tf_op jit(solution)/shard_map/all_to_all | solution.py:512
  24.1 3.2 %shard_map.115 = bf16[256,4736]{1,0:T(8,128)(2,1)} custom-call(f32[64,128]{1,0:T(8,128)} %bitcast.13, s32[64,128]{1,0:T(8,128)} %get-tuple-element.24.far_columns, f32[1,16]{1,0:T(1,128)} %far_warming.1, bf16[64,4096]{1,0:T(8,128)(2,1)} %bitcast.17, bf16[64,4096]{1,0:T(8,128)(2,1)} %bitcast.18, bf16[1024,64]{1,0:T(8,128)(2,1)} %get-tuple-element.25.far_placing), custom_call_target="tpu_custom_call" | custom-call | tf_op jit(solution)/shard_map/pallas_call | solution.py:434
  27.2 0.0 copy-start.2
  27.3 0.0 copy-start.4
  27.3 0.0 copy-start.5
  27.3 3.9 %all-to-all-start.1 = ((bf16[16,16,4736]{2,1,0:T(8,128)(2,1)}), bf16[16,16,4736]{2,1,0:T(8,128)(2,1)S(1)}, u32[]{:S(2)}, u32[]{:S(2)}) async-start(bf16[16,16,4736]{2,1,0:T(8,128)(2,1)} %bitcast.15), calls=%async_computation.1 | async-start | bytes 4849664 | tf_op jit(solution)/shard_map/all_to_all | solution.py:527
  31.2 0.2 shard_map.116
  31.4 10.7 %collective-permute-start = (bf16[8,128,128]{2,1,0:T(8,128)(2,1)S(1)}, bf16[8,128,128]{2,1,0:T(8,128)(2,1)S(1)}, u32[]{:S(2)}, u32[]{:S(2)}) collective-permute-start(bf16[8,128,128]{2,1,0:T(8,128)(2,1)S(1)} %get-tuple-element.27), channel_id=1, source_target_pairs={{1,2},{3,4},{5,6},{2,1},{4,3},{6,5},{9,10},{11,12},{13,14},{10,9},... | collective-permute-start | bytes 786440 | tf_op jit(solution)/shard_map/ppermute | solution.py:466
  42.0 1.9 %collective-permute-start.1 = (bf16[8,128,128]{2,1,0:T(8,128)(2,1)S(1)}, bf16[8,128,128]{2,1,0:T(8,128)(2,1)S(1)}, u32[]{:S(2)}, u32[]{:S(2)}) collective-permute-start(bf16[8,128,128]{2,1,0:T(8,128)(2,1)S(1)} %get-tuple-element.28), channel_id=1, source_target_pairs={{0,1},{1,0},{2,3},{3,2},{4,5},{5,4},{6,7},{7,6},{8,9},{9,8},{10,11... | collective-permute-start | bytes 786440 | tf_op jit(solution)/shard_map/ppermute | solution.py:467
  44.0 10.3 %collective-permute-done.far = bf16[8,128,128]{2,1,0:T(8,128)(2,1)S(1)} collective-permute-done((bf16[8,128,128]{2,1,0:T(8,128)(2,1)S(1)}, bf16[8,128,128]{2,1,0:T(8,128)(2,1)S(1)}, u32[]{:S(2)}, u32[]{:S(2)}) %collective-permute-start) | collective-permute-done | bytes 262176 | tf_op jit(solution)/shard_map/ppermute | solution.py:466
  54.2 0.0 collective-permute-done.1.near
  54.3 0.7 collective-permute-start.2
  54.9 5.9 %collective-permute-start.3 = (bf16[240,128]{1,0:T(8,128)(2,1)S(1)}, bf16[240,128]{1,0:T(8,128)(2,1)S(1)}, u32[]{:S(2)}, u32[]{:S(2)}) collective-permute-start(bf16[240,128]{1,0:T(8,128)(2,1)S(1)} %get-tuple-element.30), channel_id=1, source_target_pairs={{0,128},{256,384},{128,0},{384,256},{1,129},{257,385},{129,1},{385... | collective-permute-start | bytes 184328 | tf_op jit(solution)/shard_map/ppermute | solution.py:449
  60.9 0.7 shard_map.114.selector
  61.6 0.0 collective-permute-done.2.outer
  61.6 1.1 %collective-permute-done.3.inner = bf16[240,128]{1,0:T(8,128)(2,1)S(1)} collective-permute-done((bf16[240,128]{1,0:T(8,128)(2,1)S(1)}, bf16[240,128]{1,0:T(8,128)(2,1)S(1)}, u32[]{:S(2)}, u32[]{:S(2)}) %collective-permute-start.3) | collective-permute-done | bytes 61472 | tf_op jit(solution)/shard_map/ppermute | solution.py:449
  62.7 0.6 shard_map.118
  63.4 1.4 %copy-done = f32[30,144,128]{2,1,0:T(8,128)} copy-done((f32[30,144,128]{2,1,0:T(8,128)}, f32[30,144,128]{2,1,0:T(8,128)S(1)}, u32[]{:S(2)}) %copy-start) | copy-done | bytes 2211864
  64.7 0.0 all-to-all-done.1
  64.7 0.6 shard_map.119
  65.3 0.9 convert_element_type.6
  66.2 3.6 %all-to-all-start.2 = ((f16[4,16,4480]{2,1,0:T(8,128)(2,1)}), f16[4,16,4480]{2,1,0:T(8,128)(2,1)S(1)}, u32[]{:S(2)}, u32[]{:S(2)}) async-start(f16[4,16,4480]{2,1,0:T(8,128)(2,1)} %bitcast.16), calls=%async_computation.2 | async-start | bytes 1146880 | tf_op jit(solution)/shard_map/all_to_all | solution.py:533
  69.8 0.7 collective-permute-start.4
  70.5 5.2 %collective-permute-start.5 = (bf16[144,128]{1,0:T(8,128)(2,1)S(1)}, bf16[144,128]{1,0:T(8,128)(2,1)S(1)}, u32[]{:S(2)}, u32[]{:S(2)}) collective-permute-start(bf16[144,128]{1,0:T(8,128)(2,1)S(1)} %get-tuple-element.32._inner), channel_id=1, source_target_pairs={{0,8},{16,24},{32,40},{48,56},{64,72},{80,88},{96,104},{112,120},{... | collective-permute-start | bytes 110600 | tf_op jit(solution)/shard_map/ppermute | solution.py:449
  75.8 9.1 %all-to-all-done.2 = f16[4,16,4480]{2,1,0:T(8,128)(2,1)S(1)} async-done(((f16[4,16,4480]{2,1,0:T(8,128)(2,1)}), f16[4,16,4480]{2,1,0:T(8,128)(2,1)S(1)}, u32[]{:S(2)}, u32[]{:S(2)}) %all-to-all-start.2) | async-done | bytes 573472 | tf_op jit(solution)/shard_map/all_to_all | solution.py:533
  84.9 0.1 convert_reduce_fusion.whole
  85.0 1.4 %shard_map.120 = (f32[512,128]{1,0:T(8,128)}, f32[576,128]{1,0:T(8,128)S(1)}, f32[576,128]{1,0:T(8,128)S(1)}, bf16[432,128]{1,0:T(8,128)(2,1)S(1)}, bf16[432,128]{1,0:T(8,128)(2,1)S(1)}) custom-call(f32[16,4480]{1,0:T(8,128)S(1)} %convert_reduce_fusion.whole, bf16[144,128]{1,0:T(8,128)(2,1)S(1)} %collective-permute-done.4._outer.outer, ...), custom_call_target="tpu_custom_call" | custom-call | tf_op jit(solution)/shard_map/pallas_call | solution.py:434
  86.3 8.6 %collective-permute-start.6 = (bf16[432,128]{1,0:T(8,128)(2,1)S(1)}, bf16[432,128]{1,0:T(8,128)(2,1)S(1)}, u32[]{:S(2)}, u32[]{:S(2)}) collective-permute-start(bf16[432,128]{1,0:T(8,128)(2,1)S(1)} %get-tuple-element.35), channel_id=1, source_target_pairs={{1,2},{3,4},{5,6},{2,1},{4,3},{6,5},{9,10},{11,12},{13,14},{10,9},... | collective-permute-start | bytes 331784 | tf_op jit(solution)/shard_map/ppermute | solution.py:466
  94.9 1.9 %collective-permute-start.7 = (bf16[432,128]{1,0:T(8,128)(2,1)S(1)}, bf16[432,128]{1,0:T(8,128)(2,1)S(1)}, u32[]{:S(2)}, u32[]{:S(2)}) collective-permute-start(bf16[432,128]{1,0:T(8,128)(2,1)S(1)} %get-tuple-element.36), channel_id=1, source_target_pairs={{0,1},{1,0},{2,3},{3,2},{4,5},{5,4},{6,7},{7,6},{8,9},{9,8},{10,11... | collective-permute-start | bytes 331784 | tf_op jit(solution)/shard_map/ppermute | solution.py:467
  96.9 2.9 %shard_map.121 = (f32[9,144,256]{2,1,0:T(8,128)S(1)}, f32[8,144,256]{2,1,0:T(8,128)S(1)}, f32[8,144,256]{2,1,0:T(8,128)S(1)}, f32[8,144,256]{2,1,0:T(8,128)S(1)}, f32[8,144,256]{2,1,0:T(8,128)S(1)}) custom-call(f32[30,144,128]{2,1,0:T(8,128)S(1)} %copy-done.1, bf16[144,128]{1,0:T(8,128)(2,1)S(1)} %collective-permute-done.4._outer.outer, ...), custom_call_target="tpu_custom_call" | custom-call | tf_op jit(solution)/shard_map/pallas_call | solution.py:434
  99.8 2.2 %shard_map.122 = f32[512,128]{1,0:T(8,128)} custom-call(f32[576,128]{1,0:T(8,128)S(1)} %get-tuple-element.33.main, f32[576,128]{1,0:T(8,128)S(1)} %get-tuple-element.34.side, bf16[432,128]{1,0:T(8,128)(2,1)S(1)} %collective-permute-done.6.far, bf16[432,128]{1,0:T(8,128)(2,1)S(1)} %collective-permute-done.7.near, f32[30,144,128]{2,1,0:T(8,128)S(1)} %copy-done.1, ...), custom_call_target="tpu_custom_call" | custom-call | tf_op jit(solution)/shard_map/pallas_call | solution.py:434
  (13 shorter events, 0.1 us)
Async XLA Ops:
  27.2 3.9 %copy-start.2 = (f32[4,128,128]{2,1,0:T(8,128)S(1)}, f32[4,128,128]{2,1,0:T(8,128)}, u32[]{:S(2)}) copy-start(f32[4,128,128]{2,1,0:T(8,128)} %temp.3) | copy-start | bytes 786436
  27.3 3.9 %copy-start.4 = (f32[4,128,128]{2,1,0:T(8,128)S(1)}, f32[4,128,128]{2,1,0:T(8,128)}, u32[]{:S(2)}) copy-start(f32[4,128,128]{2,1,0:T(8,128)} %cond.1) | copy-start | bytes 786436
  27.3 3.9 %copy-start.5 = (f32[4,128,128]{2,1,0:T(8,128)S(1)}, f32[4,128,128]{2,1,0:T(8,128)}, u32[]{:S(2)}) copy-start(f32[4,128,128]{2,1,0:T(8,128)} %mass.1) | copy-start | bytes 786436
  27.3 37.5 %all-to-all-start.1 = ((bf16[16,16,4736]{2,1,0:T(8,128)(2,1)}), bf16[16,16,4736]{2,1,0:T(8,128)(2,1)S(1)}, u32[]{:S(2)}, u32[]{:S(2)}) async-start(bf16[16,16,4736]{2,1,0:T(8,128)(2,1)} %bitcast.15), calls=%async_computation.1 | async-start | bytes 4849664 | tf_op jit(solution)/shard_map/all_to_all | solution.py:527
  31.2 29.7 %copy-start.3 = (f32[64,1,128]{2,1,0:T(1,128)S(1)}, f32[64,1,128]{2,1,0:T(1,128)}, u32[]{:S(2)}) copy-start(f32[64,1,128]{2,1,0:T(1,128)} %all_to_all.15) | copy-start | bytes 98308
  31.4 22.9 %collective-permute-start = (bf16[8,128,128]{2,1,0:T(8,128)(2,1)S(1)}, bf16[8,128,128]{2,1,0:T(8,128)(2,1)S(1)}, u32[]{:S(2)}, u32[]{:S(2)}) collective-permute-start(bf16[8,128,128]{2,1,0:T(8,128)(2,1)S(1)} %get-tuple-element.27), channel_id=1, source_target_pairs={{1,2},{3,4},{5,6},{2,1},{4,3},{6,5},{9,10},{11,12},{13,14},{10,9},... | collective-permute-start | bytes 786440 | tf_op jit(solution)/shard_map/ppermute | solution.py:466
  42.0 12.2 %collective-permute-start.1 = (bf16[8,128,128]{2,1,0:T(8,128)(2,1)S(1)}, bf16[8,128,128]{2,1,0:T(8,128)(2,1)S(1)}, u32[]{:S(2)}, u32[]{:S(2)}) collective-permute-start(bf16[8,128,128]{2,1,0:T(8,128)(2,1)S(1)} %get-tuple-element.28), channel_id=1, source_target_pairs={{0,1},{1,0},{2,3},{3,2},{4,5},{5,4},{6,7},{7,6},{8,9},{9,8},{10,11... | collective-permute-start | bytes 786440 | tf_op jit(solution)/shard_map/ppermute | solution.py:467
  54.3 7.3 %collective-permute-start.2 = (bf16[240,128]{1,0:T(8,128)(2,1)S(1)}, bf16[240,128]{1,0:T(8,128)(2,1)S(1)}, u32[]{:S(2)}, u32[]{:S(2)}) collective-permute-start(bf16[240,128]{1,0:T(8,128)(2,1)S(1)} %get-tuple-element.29), channel_id=1, source_target_pairs={{128,256},{256,128},{129,257},{257,129},{130,258},{258,130},{131,2... | collective-permute-start | bytes 184328 | tf_op jit(solution)/shard_map/ppermute | solution.py:449
  54.9 7.8 %collective-permute-start.3 = (bf16[240,128]{1,0:T(8,128)(2,1)S(1)}, bf16[240,128]{1,0:T(8,128)(2,1)S(1)}, u32[]{:S(2)}, u32[]{:S(2)}) collective-permute-start(bf16[240,128]{1,0:T(8,128)(2,1)S(1)} %get-tuple-element.30), channel_id=1, source_target_pairs={{0,128},{256,384},{128,0},{384,256},{1,129},{257,385},{129,1},{385... | collective-permute-start | bytes 184328 | tf_op jit(solution)/shard_map/ppermute | solution.py:449
  63.4 1.4 %copy-start = (f32[30,144,128]{2,1,0:T(8,128)}, f32[30,144,128]{2,1,0:T(8,128)S(1)}, u32[]{:S(2)}) copy-start(f32[30,144,128]{2,1,0:T(8,128)S(1)} %get-tuple-element.37.grids) | copy-start | bytes 6635524
  66.2 30.6 %copy-start.1 = (f32[30,144,128]{2,1,0:T(8,128)S(1)}, f32[30,144,128]{2,1,0:T(8,128)}, u32[]{:S(2)}) copy-start(f32[30,144,128]{2,1,0:T(8,128)} %copy-done) | copy-start | bytes 6635524
  66.2 18.6 %all-to-all-start.2 = ((f16[4,16,4480]{2,1,0:T(8,128)(2,1)}), f16[4,16,4480]{2,1,0:T(8,128)(2,1)S(1)}, u32[]{:S(2)}, u32[]{:S(2)}) async-start(f16[4,16,4480]{2,1,0:T(8,128)(2,1)} %bitcast.16), calls=%async_computation.2 | async-start | bytes 1146880 | tf_op jit(solution)/shard_map/all_to_all | solution.py:533
  69.8 15.1 %collective-permute-start.4 = (bf16[144,128]{1,0:T(8,128)(2,1)S(1)}, bf16[144,128]{1,0:T(8,128)(2,1)S(1)}, u32[]{:S(2)}, u32[]{:S(2)}) collective-permute-start(bf16[144,128]{1,0:T(8,128)(2,1)S(1)} %get-tuple-element.31._outer), channel_id=1, source_target_pairs={{8,16},{24,32},{40,48},{56,64},{72,80},{88,96},{104,112},{16,8},{3... | collective-permute-start | bytes 110600 | tf_op jit(solution)/shard_map/ppermute | solution.py:449
  70.5 14.4 %collective-permute-start.5 = (bf16[144,128]{1,0:T(8,128)(2,1)S(1)}, bf16[144,128]{1,0:T(8,128)(2,1)S(1)}, u32[]{:S(2)}, u32[]{:S(2)}) collective-permute-start(bf16[144,128]{1,0:T(8,128)(2,1)S(1)} %get-tuple-element.32._inner), channel_id=1, source_target_pairs={{0,8},{16,24},{32,40},{48,56},{64,72},{80,88},{96,104},{112,120},{... | collective-permute-start | bytes 110600 | tf_op jit(solution)/shard_map/ppermute | solution.py:449
  86.3 13.4 %collective-permute-start.6 = (bf16[432,128]{1,0:T(8,128)(2,1)S(1)}, bf16[432,128]{1,0:T(8,128)(2,1)S(1)}, u32[]{:S(2)}, u32[]{:S(2)}) collective-permute-start(bf16[432,128]{1,0:T(8,128)(2,1)S(1)} %get-tuple-element.35), channel_id=1, source_target_pairs={{1,2},{3,4},{5,6},{2,1},{4,3},{6,5},{9,10},{11,12},{13,14},{10,9},... | collective-permute-start | bytes 331784 | tf_op jit(solution)/shard_map/ppermute | solution.py:466
  94.9 4.9 %collective-permute-start.7 = (bf16[432,128]{1,0:T(8,128)(2,1)S(1)}, bf16[432,128]{1,0:T(8,128)(2,1)S(1)}, u32[]{:S(2)}, u32[]{:S(2)}) collective-permute-start(bf16[432,128]{1,0:T(8,128)(2,1)S(1)} %get-tuple-element.36), channel_id=1, source_target_pairs={{0,1},{1,0},{2,3},{3,2},{4,5},{5,4},{6,7},{7,6},{8,9},{9,8},{10,11... | collective-permute-start | bytes 331784 | tf_op jit(solution)/shard_map/ppermute | solution.py:467

commit v11 on v10

--- a/solution.py
+++ b/solution.py
@@ -255,11 +255,18 @@
         side[base + 128 : base + 144, :] = block
         density[layer * 128 : (layer + 1) * 128, :] = main[base : base + 128, :]
     upper = jnp.where(lax.axis_index("core") == 1, 288, 0)
+    lane8 = iota((8, 128), 1)
     for out, first in ((far, upper), (near, 288 - upper)):
+        nearest = pl.multiple_of(jnp.where(first == 0, 0, 432), 144)
         first = pl.multiple_of(first, 144)
-        out[0:288, :] = main[pl.ds(first, 288), :].astype(BF16)
-        second = side[pl.ds(first + 144, 144), :]
-        out[288:432, :] = (side[pl.ds(first, 144), :] + pltpu.roll(second, 4, 1)).astype(BF16)
+        out[0:128, :] = main[pl.ds(first, 128), :].astype(BF16)
+        out[128:256, :] = main[pl.ds(first + 144, 128), :].astype(BF16)
+        out[256:272, :] = main[pl.ds(nearest + 128, 16), :].astype(BF16)
+        folded = jnp.zeros((8, 128), F32)
+        for k in range(16):
+            piece = pltpu.roll(side[pl.ds(nearest + 8 * k, 8), :], 4 * k + 2, 1)
+            folded = jnp.where(lane8 >> 2 == k, piece, folded)
+        out[272:288, :] = jnp.concatenate([folded, jnp.zeros((8, 128), F32)], axis=0).astype(BF16)
 
 
 def depth(a):
@@ -381,7 +388,7 @@
 
 
 def sweep_kernel(main, side, far, near, grids, face_layer, face_row, face_col, inverse, residual, out, d0, d1, rest):
-    lane = iota((144, 128), 1)
+    lane = iota((8, 128), 1)
     kept = (lane < 2) | (lane >= 126)
     upper = lax.axis_index("core") == 1
 
@@ -389,17 +396,23 @@
         if 3 <= i <= 6:
             at = (i - 3) * 144
             return main[at : at + 144, :], side[at : at + 144, :]
-        second = i in (2, 8)
-        at = 144 if second else 0
+        at = 128 if i in (2, 8) else 0
         same, other = (near, far) if i < 3 else (far, near)
 
-        def rows(at):
+        def rows(at, size):
             return jnp.where(
-                upper, same[at : at + 144, :].astype(F32), other[at : at + 144, :].astype(F32)
+                upper, same[at : at + size, :].astype(F32), other[at : at + size, :].astype(F32)
             )
 
-        beside = turned_by(rows(288), -4, 1) if second else rows(288)
-        return rows(at), jnp.where(kept, beside, 0.0)
+        ends = jnp.zeros((16, 128), F32)
+        if i in (1, 8):
+            return jnp.concatenate([rows(at, 128), ends], axis=0), jnp.zeros((144, 128), F32)
+        folded = rows(272, 16)[0:8]
+        beside = [jnp.where(kept, turned_by(folded, -4 * k - 2, 1), 0.0) for k in range(16)]
+        return (
+            jnp.concatenate([rows(at, 128), rows(256, 16)], axis=0),
+            jnp.concatenate([*beside, ends], axis=0),
+        )
 
     for i in range(1, 9):
         start = residual[i - 1] + jnp.concatenate(supplied(i), axis=1)
@@ -534,7 +547,7 @@
         partial.astype(jnp.float16).reshape(4, 16, 4480), "zlo", split_axis=0, concat_axis=0, tiled=True
     )
     terms = operator(wide, *beside)
-    block, strip = sds((576, 128), F32), sds((432, 128), BF16)
+    block, strip = sds((576, 128), F32), sds((288, 128), BF16)
     density, main, side, far, near = call(
         unpack_kernel,
         (sds((512, 128), F32), block, block, strip, strip),

time: 103 us -> 102 us (level)
  no operation moved by 1% of the time
where the time goes in v11:
time: 102 us; the launch traced here: 101 us
  starting transfers between devices  43 us (42%)
  blocking collectives  21.6 us (21%)
  waiting for transfers between devices  20.5 us (20%)
  Pallas kernels  13 us (13%)
  local copies, waits for them, and re-layouts  1.39 us (1%)
    all_to_all x1, blocking collectives, shards(): lax.all_to_all(message.reshape(64, 1, 128), CUBE, split_axis=0, concat_ax...  21.6 us
    ppermute x2, starting transfers between devices, swap_layers(): lax.ppermute(far, LAYER, apart + [(b, a) for a, b in apart])  19.2 us
    pallas_call x10, Pallas kernels, call(): pl.pallas_call(kernel, out_shape=shape, in_specs=[anywhere if i in far el...  13 us
    ppermute x4, starting transfers between devices, swapped(): return lax.ppermute(data, axis, apart + [(b, a) for a, b in apart])  12.5 us
    ppermute x2, waiting for transfers between devices, swap_layers(): lax.ppermute(far, LAYER, apart + [(b, a) for a, b in apart])  10.3 us
    all_to_all x1, waiting for transfers between devices, shards(): lax.all_to_all(partial.astype(jnp.float16).reshape(4, 16, 4480), 'zlo', s...  9.1 us
    all_to_all x1, starting transfers between devices, shards(): lax.all_to_all(send.reshape(16, 16, 4736), PLANE, split_axis=0, concat_ax...  3.87 us
    ppermute x2, starting transfers between devices, swap_layers(): lax.ppermute(near, 'core', [(0, 1), (1, 0)])  3.84 us
  transfers between devices with their start and end apart: 10, of which 3 were waited for; matrix products, arithmetic and copies ran while one was open for 0% of the time, Pallas kernels for 4%

profile of v11, /device:TPU:1, one launch (start us, length us, event | category | flops | bytes accessed | tf_op | source)
XLA Modules:
  0.0 101.4 jit_solution(16325397021699561376)
XLA Ops:
  0.6 1.8 %shard_map.113 = (f32[64,128]{1,0:T(8,128)}, bf16[1024,64]{1,0:T(8,128)(2,1)}, s32[64,128]{1,0:T(8,128)}) custom-call(f32[4,128,128]{2,1,0:T(8,128)} %temp.3, s32[1,64]{1,0:T(1,128)} %bitcast.21, s32[1,64]{1,0:T(1,128)} %place.1, s32[1,64]{1,0:T(1,128)} %holder.1, s32[1,16]{1,0:T(1,128)} %tier.1), custom_call_target="tpu_custom_call" | custom-call | tf_op jit(solution)/shard_map/pallas_call | solution.py:447
  2.4 21.6 %all_to_all.15 = f32[64,1,128]{2,1,0:T(1,128)} all-to-all(f32[64,1,128]{2,1,0:T(1,128)} %bitcast.20), channel_id=1, replica_groups=mesh['row'=4,'zlo'=4,'y'=4,'zhi'=4,'core'=2] {'row','zlo','y'}, dimensions={0} | all-to-all | bytes 65536 | tf_op jit(solution)/shard_map/all_to_all | solution.py:525
  24.1 3.2 %shard_map.115 = bf16[256,4736]{1,0:T(8,128)(2,1)} custom-call(f32[64,128]{1,0:T(8,128)} %bitcast.13, s32[64,128]{1,0:T(8,128)} %get-tuple-element.24.far_columns, f32[1,16]{1,0:T(1,128)} %far_warming.1, bf16[64,4096]{1,0:T(8,128)(2,1)} %bitcast.17, bf16[64,4096]{1,0:T(8,128)(2,1)} %bitcast.18, bf16[1024,64]{1,0:T(8,128)(2,1)} %get-tuple-element.25.far_placing), custom_call_target="tpu_custom_call" | custom-call | tf_op jit(solution)/shard_map/pallas_call | solution.py:447
  27.2 0.0 copy-start.2
  27.3 0.0 copy-start.4
  27.3 0.0 copy-start.5
  27.3 3.9 %all-to-all-start.1 = ((bf16[16,16,4736]{2,1,0:T(8,128)(2,1)}), bf16[16,16,4736]{2,1,0:T(8,128)(2,1)S(1)}, u32[]{:S(2)}, u32[]{:S(2)}) async-start(bf16[16,16,4736]{2,1,0:T(8,128)(2,1)} %bitcast.15), calls=%async_computation.1 | async-start | bytes 4849664 | tf_op jit(solution)/shard_map/all_to_all | solution.py:540
  31.2 0.2 shard_map.116
  31.4 10.7 %collective-permute-start = (bf16[8,128,128]{2,1,0:T(8,128)(2,1)S(1)}, bf16[8,128,128]{2,1,0:T(8,128)(2,1)S(1)}, u32[]{:S(2)}, u32[]{:S(2)}) collective-permute-start(bf16[8,128,128]{2,1,0:T(8,128)(2,1)S(1)} %get-tuple-element.27), channel_id=1, source_target_pairs={{1,2},{3,4},{5,6},{2,1},{4,3},{6,5},{9,10},{11,12},{13,14},{10,9},... | collective-permute-start | bytes 786440 | tf_op jit(solution)/shard_map/ppermute | solution.py:479
  42.0 1.9 %collective-permute-start.1 = (bf16[8,128,128]{2,1,0:T(8,128)(2,1)S(1)}, bf16[8,128,128]{2,1,0:T(8,128)(2,1)S(1)}, u32[]{:S(2)}, u32[]{:S(2)}) collective-permute-start(bf16[8,128,128]{2,1,0:T(8,128)(2,1)S(1)} %get-tuple-element.28), channel_id=1, source_target_pairs={{0,1},{1,0},{2,3},{3,2},{4,5},{5,4},{6,7},{7,6},{8,9},{9,8},{10,11... | collective-permute-start | bytes 786440 | tf_op jit(solution)/shard_map/ppermute | solution.py:480
  44.0 10.3 %collective-permute-done.far = bf16[8,128,128]{2,1,0:T(8,128)(2,1)S(1)} collective-permute-done((bf16[8,128,128]{2,1,0:T(8,128)(2,1)S(1)}, bf16[8,128,128]{2,1,0:T(8,128)(2,1)S(1)}, u32[]{:S(2)}, u32[]{:S(2)}) %collective-permute-start) | collective-permute-done | bytes 262176 | tf_op jit(solution)/shard_map/ppermute | solution.py:479
  54.2 0.0 collective-permute-done.1.near
  54.3 0.7 collective-permute-start.2
  54.9 5.9 %collective-permute-start.3 = (bf16[240,128]{1,0:T(8,128)(2,1)S(1)}, bf16[240,128]{1,0:T(8,128)(2,1)S(1)}, u32[]{:S(2)}, u32[]{:S(2)}) collective-permute-start(bf16[240,128]{1,0:T(8,128)(2,1)S(1)} %get-tuple-element.30), channel_id=1, source_target_pairs={{0,128},{256,384},{128,0},{384,256},{1,129},{257,385},{129,1},{385... | collective-permute-start | bytes 184328 | tf_op jit(solution)/shard_map/ppermute | solution.py:462
  60.9 0.7 shard_map.114.selector
  61.6 1.1 %collective-permute-done.3.inner = bf16[240,128]{1,0:T(8,128)(2,1)S(1)} collective-permute-done((bf16[240,128]{1,0:T(8,128)(2,1)S(1)}, bf16[240,128]{1,0:T(8,128)(2,1)S(1)}, u32[]{:S(2)}, u32[]{:S(2)}) %collective-permute-start.3) | collective-permute-done | bytes 61472 | tf_op jit(solution)/shard_map/ppermute | solution.py:462
  62.7 0.6 shard_map.118
  63.4 1.4 %copy-done = f32[30,144,128]{2,1,0:T(8,128)} copy-done((f32[30,144,128]{2,1,0:T(8,128)}, f32[30,144,128]{2,1,0:T(8,128)S(1)}, u32[]{:S(2)}) %copy-start) | copy-done | bytes 2211864
  64.7 0.6 shard_map.119
  65.3 0.9 convert_element_type.6
  66.2 3.6 %all-to-all-start.2 = ((f16[4,16,4480]{2,1,0:T(8,128)(2,1)}), f16[4,16,4480]{2,1,0:T(8,128)(2,1)S(1)}, u32[]{:S(2)}, u32[]{:S(2)}) async-start(f16[4,16,4480]{2,1,0:T(8,128)(2,1)} %bitcast.16), calls=%async_computation.2 | async-start | bytes 1146880 | tf_op jit(solution)/shard_map/all_to_all | solution.py:546
  69.8 0.7 collective-permute-start.4
  70.5 5.2 %collective-permute-start.5 = (bf16[144,128]{1,0:T(8,128)(2,1)S(1)}, bf16[144,128]{1,0:T(8,128)(2,1)S(1)}, u32[]{:S(2)}, u32[]{:S(2)}) collective-permute-start(bf16[144,128]{1,0:T(8,128)(2,1)S(1)} %get-tuple-element.32._inner), channel_id=1, source_target_pairs={{0,8},{16,24},{32,40},{48,56},{64,72},{80,88},{96,104},{112,120},{... | collective-permute-start | bytes 110600 | tf_op jit(solution)/shard_map/ppermute | solution.py:462
  75.8 9.1 %all-to-all-done.2 = f16[4,16,4480]{2,1,0:T(8,128)(2,1)S(1)} async-done(((f16[4,16,4480]{2,1,0:T(8,128)(2,1)}), f16[4,16,4480]{2,1,0:T(8,128)(2,1)S(1)}, u32[]{:S(2)}, u32[]{:S(2)}) %all-to-all-start.2) | async-done | bytes 573472 | tf_op jit(solution)/shard_map/all_to_all | solution.py:546
  84.9 0.1 convert_reduce_fusion.whole
  84.9 0.0 collective-permute-done.4._outer.outer
  85.0 1.3 %shard_map.120 = (f32[512,128]{1,0:T(8,128)}, f32[576,128]{1,0:T(8,128)S(1)}, f32[576,128]{1,0:T(8,128)S(1)}, bf16[288,128]{1,0:T(8,128)(2,1)S(1)}, bf16[288,128]{1,0:T(8,128)(2,1)S(1)}) custom-call(f32[16,4480]{1,0:T(8,128)S(1)} %convert_reduce_fusion.whole, bf16[144,128]{1,0:T(8,128)(2,1)S(1)} %collective-permute-done.4._outer.outer, ...), custom_call_target="tpu_custom_call" | custom-call | tf_op jit(solution)/shard_map/pallas_call | solution.py:447
  86.3 8.6 %collective-permute-start.6 = (bf16[288,128]{1,0:T(8,128)(2,1)S(1)}, bf16[288,128]{1,0:T(8,128)(2,1)S(1)}, u32[]{:S(2)}, u32[]{:S(2)}) collective-permute-start(bf16[288,128]{1,0:T(8,128)(2,1)S(1)} %get-tuple-element.35), channel_id=1, source_target_pairs={{1,2},{3,4},{5,6},{2,1},{4,3},{6,5},{9,10},{11,12},{13,14},{10,9},... | collective-permute-start | bytes 221192 | tf_op jit(solution)/shard_map/ppermute | solution.py:479
  94.9 1.9 %collective-permute-start.7 = (bf16[288,128]{1,0:T(8,128)(2,1)S(1)}, bf16[288,128]{1,0:T(8,128)(2,1)S(1)}, u32[]{:S(2)}, u32[]{:S(2)}) collective-permute-start(bf16[288,128]{1,0:T(8,128)(2,1)S(1)} %get-tuple-element.36), channel_id=1, source_target_pairs={{0,1},{1,0},{2,3},{3,2},{4,5},{5,4},{6,7},{7,6},{8,9},{9,8},{10,11... | collective-permute-start | bytes 221192 | tf_op jit(solution)/shard_map/ppermute | solution.py:480
  96.8 2.6 %shard_map.121 = (f32[9,144,256]{2,1,0:T(8,128)S(1)}, f32[8,144,256]{2,1,0:T(8,128)S(1)}, f32[8,144,256]{2,1,0:T(8,128)S(1)}, f32[8,144,256]{2,1,0:T(8,128)S(1)}, f32[8,144,256]{2,1,0:T(8,128)S(1)}) custom-call(f32[30,144,128]{2,1,0:T(8,128)S(1)} %copy-done.1, bf16[144,128]{1,0:T(8,128)(2,1)S(1)} %collective-permute-done.4._outer.outer, ...), custom_call_target="tpu_custom_call" | custom-call | tf_op jit(solution)/shard_map/pallas_call | solution.py:447
  99.5 0.0 collective-permute-done.6.far
  99.5 1.9 %shard_map.122 = f32[512,128]{1,0:T(8,128)} custom-call(f32[576,128]{1,0:T(8,128)S(1)} %get-tuple-element.33.main, f32[576,128]{1,0:T(8,128)S(1)} %get-tuple-element.34.side, bf16[288,128]{1,0:T(8,128)(2,1)S(1)} %collective-permute-done.6.far, bf16[288,128]{1,0:T(8,128)(2,1)S(1)} %collective-permute-done.7.near, f32[30,144,128]{2,1,0:T(8,128)S(1)} %copy-done.1, ...), custom_call_target="tpu_custom_call" | custom-call | tf_op jit(solution)/shard_map/pallas_call | solution.py:447
  (13 shorter events, 0.1 us)
Async XLA Ops:
  27.2 3.9 %copy-start.2 = (f32[4,128,128]{2,1,0:T(8,128)S(1)}, f32[4,128,128]{2,1,0:T(8,128)}, u32[]{:S(2)}) copy-start(f32[4,128,128]{2,1,0:T(8,128)} %temp.3) | copy-start | bytes 786436
  27.3 3.9 %copy-start.4 = (f32[4,128,128]{2,1,0:T(8,128)S(1)}, f32[4,128,128]{2,1,0:T(8,128)}, u32[]{:S(2)}) copy-start(f32[4,128,128]{2,1,0:T(8,128)} %cond.1) | copy-start | bytes 786436
  27.3 3.9 %copy-start.5 = (f32[4,128,128]{2,1,0:T(8,128)S(1)}, f32[4,128,128]{2,1,0:T(8,128)}, u32[]{:S(2)}) copy-start(f32[4,128,128]{2,1,0:T(8,128)} %mass.1) | copy-start | bytes 786436
  27.3 37.5 %all-to-all-start.1 = ((bf16[16,16,4736]{2,1,0:T(8,128)(2,1)}), bf16[16,16,4736]{2,1,0:T(8,128)(2,1)S(1)}, u32[]{:S(2)}, u32[]{:S(2)}) async-start(bf16[16,16,4736]{2,1,0:T(8,128)(2,1)} %bitcast.15), calls=%async_computation.1 | async-start | bytes 4849664 | tf_op jit(solution)/shard_map/all_to_all | solution.py:540
  31.2 29.7 %copy-start.3 = (f32[64,1,128]{2,1,0:T(1,128)S(1)}, f32[64,1,128]{2,1,0:T(1,128)}, u32[]{:S(2)}) copy-start(f32[64,1,128]{2,1,0:T(1,128)} %all_to_all.15) | copy-start | bytes 98308
  31.4 22.9 %collective-permute-start = (bf16[8,128,128]{2,1,0:T(8,128)(2,1)S(1)}, bf16[8,128,128]{2,1,0:T(8,128)(2,1)S(1)}, u32[]{:S(2)}, u32[]{:S(2)}) collective-permute-start(bf16[8,128,128]{2,1,0:T(8,128)(2,1)S(1)} %get-tuple-element.27), channel_id=1, source_target_pairs={{1,2},{3,4},{5,6},{2,1},{4,3},{6,5},{9,10},{11,12},{13,14},{10,9},... | collective-permute-start | bytes 786440 | tf_op jit(solution)/shard_map/ppermute | solution.py:479
  42.0 12.2 %collective-permute-start.1 = (bf16[8,128,128]{2,1,0:T(8,128)(2,1)S(1)}, bf16[8,128,128]{2,1,0:T(8,128)(2,1)S(1)}, u32[]{:S(2)}, u32[]{:S(2)}) collective-permute-start(bf16[8,128,128]{2,1,0:T(8,128)(2,1)S(1)} %get-tuple-element.28), channel_id=1, source_target_pairs={{0,1},{1,0},{2,3},{3,2},{4,5},{5,4},{6,7},{7,6},{8,9},{9,8},{10,11... | collective-permute-start | bytes 786440 | tf_op jit(solution)/shard_map/ppermute | solution.py:480
  54.3 7.3 %collective-permute-start.2 = (bf16[240,128]{1,0:T(8,128)(2,1)S(1)}, bf16[240,128]{1,0:T(8,128)(2,1)S(1)}, u32[]{:S(2)}, u32[]{:S(2)}) collective-permute-start(bf16[240,128]{1,0:T(8,128)(2,1)S(1)} %get-tuple-element.29), channel_id=1, source_target_pairs={{128,256},{256,128},{129,257},{257,129},{130,258},{258,130},{131,2... | collective-permute-start | bytes 184328 | tf_op jit(solution)/shard_map/ppermute | solution.py:462
  54.9 7.8 %collective-permute-start.3 = (bf16[240,128]{1,0:T(8,128)(2,1)S(1)}, bf16[240,128]{1,0:T(8,128)(2,1)S(1)}, u32[]{:S(2)}, u32[]{:S(2)}) collective-permute-start(bf16[240,128]{1,0:T(8,128)(2,1)S(1)} %get-tuple-element.30), channel_id=1, source_target_pairs={{0,128},{256,384},{128,0},{384,256},{1,129},{257,385},{129,1},{385... | collective-permute-start | bytes 184328 | tf_op jit(solution)/shard_map/ppermute | solution.py:462
  63.4 1.4 %copy-start = (f32[30,144,128]{2,1,0:T(8,128)}, f32[30,144,128]{2,1,0:T(8,128)S(1)}, u32[]{:S(2)}) copy-start(f32[30,144,128]{2,1,0:T(8,128)S(1)} %get-tuple-element.37.grids) | copy-start | bytes 6635524
  66.2 30.6 %copy-start.1 = (f32[30,144,128]{2,1,0:T(8,128)S(1)}, f32[30,144,128]{2,1,0:T(8,128)}, u32[]{:S(2)}) copy-start(f32[30,144,128]{2,1,0:T(8,128)} %copy-done) | copy-start | bytes 6635524
  66.2 18.6 %all-to-all-start.2 = ((f16[4,16,4480]{2,1,0:T(8,128)(2,1)}), f16[4,16,4480]{2,1,0:T(8,128)(2,1)S(1)}, u32[]{:S(2)}, u32[]{:S(2)}) async-start(f16[4,16,4480]{2,1,0:T(8,128)(2,1)} %bitcast.16), calls=%async_computation.2 | async-start | bytes 1146880 | tf_op jit(solution)/shard_map/all_to_all | solution.py:546
  69.8 15.1 %collective-permute-start.4 = (bf16[144,128]{1,0:T(8,128)(2,1)S(1)}, bf16[144,128]{1,0:T(8,128)(2,1)S(1)}, u32[]{:S(2)}, u32[]{:S(2)}) collective-permute-start(bf16[144,128]{1,0:T(8,128)(2,1)S(1)} %get-tuple-element.31._outer), channel_id=1, source_target_pairs={{8,16},{24,32},{40,48},{56,64},{72,80},{88,96},{104,112},{16,8},{3... | collective-permute-start | bytes 110600 | tf_op jit(solution)/shard_map/ppermute | solution.py:462
  70.5 14.4 %collective-permute-start.5 = (bf16[144,128]{1,0:T(8,128)(2,1)S(1)}, bf16[144,128]{1,0:T(8,128)(2,1)S(1)}, u32[]{:S(2)}, u32[]{:S(2)}) collective-permute-start(bf16[144,128]{1,0:T(8,128)(2,1)S(1)} %get-tuple-element.32._inner), channel_id=1, source_target_pairs={{0,8},{16,24},{32,40},{48,56},{64,72},{80,88},{96,104},{112,120},{... | collective-permute-start | bytes 110600 | tf_op jit(solution)/shard_map/ppermute | solution.py:462
  86.3 13.2 %collective-permute-start.6 = (bf16[288,128]{1,0:T(8,128)(2,1)S(1)}, bf16[288,128]{1,0:T(8,128)(2,1)S(1)}, u32[]{:S(2)}, u32[]{:S(2)}) collective-permute-start(bf16[288,128]{1,0:T(8,128)(2,1)S(1)} %get-tuple-element.35), channel_id=1, source_target_pairs={{1,2},{3,4},{5,6},{2,1},{4,3},{6,5},{9,10},{11,12},{13,14},{10,9},... | collective-permute-start | bytes 221192 | tf_op jit(solution)/shard_map/ppermute | solution.py:479
  94.9 4.6 %collective-permute-start.7 = (bf16[288,128]{1,0:T(8,128)(2,1)S(1)}, bf16[288,128]{1,0:T(8,128)(2,1)S(1)}, u32[]{:S(2)}, u32[]{:S(2)}) collective-permute-start(bf16[288,128]{1,0:T(8,128)(2,1)S(1)} %get-tuple-element.36), channel_id=1, source_target_pairs={{0,1},{1,0},{2,3},{3,2},{4,5},{5,4},{6,7},{7,6},{8,9},{9,8},{10,11... | collective-permute-start | bytes 221192 | tf_op jit(solution)/shard_map/ppermute | solution.py:480

commit v12 on v11

--- a/solution.py
+++ b/solution.py
@@ -552,7 +552,7 @@
         unpack_kernel,
         (sds((512, 128), F32), block, block, strip, strip),
         (jnp.sum(parts.astype(F32), axis=0), *beside),
-        scratch=[pltpu.VMEM((512, 128), F32)],
+        scratch=[pltpu.VMEM((528, 128), F32)],
     )
     far, near = swap_layers(far, near)
     eight = pltpu.VMEM((8, 144, 256), F32)

time: 102 us -> 102 us (level)
  no operation moved by 1% of the time
where the time goes in v12:
time: 102 us; the launch traced here: 101 us
  starting transfers between devices  43 us (42%)
  blocking collectives  21.6 us (21%)
  waiting for transfers between devices  20.5 us (20%)
  Pallas kernels  13 us (13%)
  local copies, waits for them, and re-layouts  1.39 us (1%)
    all_to_all x1, blocking collectives, shards(): lax.all_to_all(message.reshape(64, 1, 128), CUBE, split_axis=0, concat_ax...  21.6 us
    ppermute x2, starting transfers between devices, swap_layers(): lax.ppermute(far, LAYER, apart + [(b, a) for a, b in apart])  19.2 us
    pallas_call x10, Pallas kernels, call(): pl.pallas_call(kernel, out_shape=shape, in_specs=[anywhere if i in far el...  13 us
    ppermute x4, starting transfers between devices, swapped(): return lax.ppermute(data, axis, apart + [(b, a) for a, b in apart])  12.5 us
    ppermute x2, waiting for transfers between devices, swap_layers(): lax.ppermute(far, LAYER, apart + [(b, a) for a, b in apart])  10.3 us
    all_to_all x1, waiting for transfers between devices, shards(): lax.all_to_all(partial.astype(jnp.float16).reshape(4, 16, 4480), 'zlo', s...  9.1 us
    all_to_all x1, starting transfers between devices, shards(): lax.all_to_all(send.reshape(16, 16, 4736), PLANE, split_axis=0, concat_ax...  3.87 us
    ppermute x2, starting transfers between devices, swap_layers(): lax.ppermute(near, 'core', [(0, 1), (1, 0)])  3.84 us
  transfers between devices with their start and end apart: 10, of which 3 were waited for; matrix products, arithmetic and copies ran while one was open for 0% of the time, Pallas kernels for 4%

profile of v12, /device:TPU:1, one launch (start us, length us, event | category | flops | bytes accessed | tf_op | source)
XLA Modules:
  0.0 101.4 jit_solution(11765247874570635851)
XLA Ops:
  0.6 1.8 %shard_map.113 = (f32[64,128]{1,0:T(8,128)}, bf16[1024,64]{1,0:T(8,128)(2,1)}, s32[64,128]{1,0:T(8,128)}) custom-call(f32[4,128,128]{2,1,0:T(8,128)} %temp.3, s32[1,64]{1,0:T(1,128)} %bitcast.21, s32[1,64]{1,0:T(1,128)} %place.1, s32[1,64]{1,0:T(1,128)} %holder.1, s32[1,16]{1,0:T(1,128)} %tier.1), custom_call_target="tpu_custom_call" | custom-call | tf_op jit(solution)/shard_map/pallas_call | solution.py:447
  2.4 21.6 %all_to_all.15 = f32[64,1,128]{2,1,0:T(1,128)} all-to-all(f32[64,1,128]{2,1,0:T(1,128)} %bitcast.20), channel_id=1, replica_groups=mesh['row'=4,'zlo'=4,'y'=4,'zhi'=4,'core'=2] {'row','zlo','y'}, dimensions={0} | all-to-all | bytes 65536 | tf_op jit(solution)/shard_map/all_to_all | solution.py:525
  24.1 3.2 %shard_map.115 = bf16[256,4736]{1,0:T(8,128)(2,1)} custom-call(f32[64,128]{1,0:T(8,128)} %bitcast.13, s32[64,128]{1,0:T(8,128)} %get-tuple-element.24.far_columns, f32[1,16]{1,0:T(1,128)} %far_warming.1, bf16[64,4096]{1,0:T(8,128)(2,1)} %bitcast.17, bf16[64,4096]{1,0:T(8,128)(2,1)} %bitcast.18, bf16[1024,64]{1,0:T(8,128)(2,1)} %get-tuple-element.25.far_placing), custom_call_target="tpu_custom_call" | custom-call | tf_op jit(solution)/shard_map/pallas_call | solution.py:447
  27.2 0.0 copy-start.2
  27.3 0.0 copy-start.4
  27.3 0.0 copy-start.5
  27.3 3.9 %all-to-all-start.1 = ((bf16[16,16,4736]{2,1,0:T(8,128)(2,1)}), bf16[16,16,4736]{2,1,0:T(8,128)(2,1)S(1)}, u32[]{:S(2)}, u32[]{:S(2)}) async-start(bf16[16,16,4736]{2,1,0:T(8,128)(2,1)} %bitcast.15), calls=%async_computation.1 | async-start | bytes 4849664 | tf_op jit(solution)/shard_map/all_to_all | solution.py:540
  31.2 0.2 shard_map.116
  31.4 10.7 %collective-permute-start = (bf16[8,128,128]{2,1,0:T(8,128)(2,1)S(1)}, bf16[8,128,128]{2,1,0:T(8,128)(2,1)S(1)}, u32[]{:S(2)}, u32[]{:S(2)}) collective-permute-start(bf16[8,128,128]{2,1,0:T(8,128)(2,1)S(1)} %get-tuple-element.27), channel_id=1, source_target_pairs={{1,2},{3,4},{5,6},{2,1},{4,3},{6,5},{9,10},{11,12},{13,14},{10,9},... | collective-permute-start | bytes 786440 | tf_op jit(solution)/shard_map/ppermute | solution.py:479
  42.0 1.9 %collective-permute-start.1 = (bf16[8,128,128]{2,1,0:T(8,128)(2,1)S(1)}, bf16[8,128,128]{2,1,0:T(8,128)(2,1)S(1)}, u32[]{:S(2)}, u32[]{:S(2)}) collective-permute-start(bf16[8,128,128]{2,1,0:T(8,128)(2,1)S(1)} %get-tuple-element.28), channel_id=1, source_target_pairs={{0,1},{1,0},{2,3},{3,2},{4,5},{5,4},{6,7},{7,6},{8,9},{9,8},{10,11... | collective-permute-start | bytes 786440 | tf_op jit(solution)/shard_map/ppermute | solution.py:480
  44.0 10.3 %collective-permute-done.far = bf16[8,128,128]{2,1,0:T(8,128)(2,1)S(1)} collective-permute-done((bf16[8,128,128]{2,1,0:T(8,128)(2,1)S(1)}, bf16[8,128,128]{2,1,0:T(8,128)(2,1)S(1)}, u32[]{:S(2)}, u32[]{:S(2)}) %collective-permute-start) | collective-permute-done | bytes 262176 | tf_op jit(solution)/shard_map/ppermute | solution.py:479
  54.2 0.0 collective-permute-done.1.near
  54.3 0.7 collective-permute-start.2
  54.9 5.9 %collective-permute-start.3 = (bf16[240,128]{1,0:T(8,128)(2,1)S(1)}, bf16[240,128]{1,0:T(8,128)(2,1)S(1)}, u32[]{:S(2)}, u32[]{:S(2)}) collective-permute-start(bf16[240,128]{1,0:T(8,128)(2,1)S(1)} %get-tuple-element.30), channel_id=1, source_target_pairs={{0,128},{256,384},{128,0},{384,256},{1,129},{257,385},{129,1},{385... | collective-permute-start | bytes 184328 | tf_op jit(solution)/shard_map/ppermute | solution.py:462
  60.9 0.7 shard_map.114.selector
  61.6 1.1 %collective-permute-done.3.inner = bf16[240,128]{1,0:T(8,128)(2,1)S(1)} collective-permute-done((bf16[240,128]{1,0:T(8,128)(2,1)S(1)}, bf16[240,128]{1,0:T(8,128)(2,1)S(1)}, u32[]{:S(2)}, u32[]{:S(2)}) %collective-permute-start.3) | collective-permute-done | bytes 61472 | tf_op jit(solution)/shard_map/ppermute | solution.py:462
  62.7 0.6 shard_map.118
  63.4 1.4 %copy-done = f32[30,144,128]{2,1,0:T(8,128)} copy-done((f32[30,144,128]{2,1,0:T(8,128)}, f32[30,144,128]{2,1,0:T(8,128)S(1)}, u32[]{:S(2)}) %copy-start) | copy-done | bytes 2211864
  64.7 0.6 shard_map.119
  65.3 0.9 convert_element_type.6
  66.2 3.6 %all-to-all-start.2 = ((f16[4,16,4480]{2,1,0:T(8,128)(2,1)}), f16[4,16,4480]{2,1,0:T(8,128)(2,1)S(1)}, u32[]{:S(2)}, u32[]{:S(2)}) async-start(f16[4,16,4480]{2,1,0:T(8,128)(2,1)} %bitcast.16), calls=%async_computation.2 | async-start | bytes 1146880 | tf_op jit(solution)/shard_map/all_to_all | solution.py:546
  69.8 0.7 collective-permute-start.4
  70.5 5.2 %collective-permute-start.5 = (bf16[144,128]{1,0:T(8,128)(2,1)S(1)}, bf16[144,128]{1,0:T(8,128)(2,1)S(1)}, u32[]{:S(2)}, u32[]{:S(2)}) collective-permute-start(bf16[144,128]{1,0:T(8,128)(2,1)S(1)} %get-tuple-element.32._inner), channel_id=1, source_target_pairs={{0,8},{16,24},{32,40},{48,56},{64,72},{80,88},{96,104},{112,120},{... | collective-permute-start | bytes 110600 | tf_op jit(solution)/shard_map/ppermute | solution.py:462
  75.8 9.1 %all-to-all-done.2 = f16[4,16,4480]{2,1,0:T(8,128)(2,1)S(1)} async-done(((f16[4,16,4480]{2,1,0:T(8,128)(2,1)}), f16[4,16,4480]{2,1,0:T(8,128)(2,1)S(1)}, u32[]{:S(2)}, u32[]{:S(2)}) %all-to-all-start.2) | async-done | bytes 573472 | tf_op jit(solution)/shard_map/all_to_all | solution.py:546
  84.9 0.1 convert_reduce_fusion.whole
  84.9 0.0 collective-permute-done.4._outer.outer
  85.0 1.3 %shard_map.120 = (f32[512,128]{1,0:T(8,128)}, f32[576,128]{1,0:T(8,128)S(1)}, f32[576,128]{1,0:T(8,128)S(1)}, bf16[288,128]{1,0:T(8,128)(2,1)S(1)}, bf16[288,128]{1,0:T(8,128)(2,1)S(1)}) custom-call(f32[16,4480]{1,0:T(8,128)S(1)} %convert_reduce_fusion.whole, bf16[144,128]{1,0:T(8,128)(2,1)S(1)} %collective-permute-done.4._outer.outer, ...), custom_call_target="tpu_custom_call" | custom-call | tf_op jit(solution)/shard_map/pallas_call | solution.py:447
  86.3 8.6 %collective-permute-start.6 = (bf16[288,128]{1,0:T(8,128)(2,1)S(1)}, bf16[288,128]{1,0:T(8,128)(2,1)S(1)}, u32[]{:S(2)}, u32[]{:S(2)}) collective-permute-start(bf16[288,128]{1,0:T(8,128)(2,1)S(1)} %get-tuple-element.35), channel_id=1, source_target_pairs={{1,2},{3,4},{5,6},{2,1},{4,3},{6,5},{9,10},{11,12},{13,14},{10,9},... | collective-permute-start | bytes 221192 | tf_op jit(solution)/shard_map/ppermute | solution.py:479
  94.9 1.9 %collective-permute-start.7 = (bf16[288,128]{1,0:T(8,128)(2,1)S(1)}, bf16[288,128]{1,0:T(8,128)(2,1)S(1)}, u32[]{:S(2)}, u32[]{:S(2)}) collective-permute-start(bf16[288,128]{1,0:T(8,128)(2,1)S(1)} %get-tuple-element.36), channel_id=1, source_target_pairs={{0,1},{1,0},{2,3},{3,2},{4,5},{5,4},{6,7},{7,6},{8,9},{9,8},{10,11... | collective-permute-start | bytes 221192 | tf_op jit(solution)/shard_map/ppermute | solution.py:480
  96.8 2.6 %shard_map.121 = (f32[9,144,256]{2,1,0:T(8,128)S(1)}, f32[8,144,256]{2,1,0:T(8,128)S(1)}, f32[8,144,256]{2,1,0:T(8,128)S(1)}, f32[8,144,256]{2,1,0:T(8,128)S(1)}, f32[8,144,256]{2,1,0:T(8,128)S(1)}) custom-call(f32[30,144,128]{2,1,0:T(8,128)S(1)} %copy-done.1, bf16[144,128]{1,0:T(8,128)(2,1)S(1)} %collective-permute-done.4._outer.outer, ...), custom_call_target="tpu_custom_call" | custom-call | tf_op jit(solution)/shard_map/pallas_call | solution.py:447
  99.5 0.0 collective-permute-done.6.far
  99.5 1.9 %shard_map.122 = f32[512,128]{1,0:T(8,128)} custom-call(f32[576,128]{1,0:T(8,128)S(1)} %get-tuple-element.33.main, f32[576,128]{1,0:T(8,128)S(1)} %get-tuple-element.34.side, bf16[288,128]{1,0:T(8,128)(2,1)S(1)} %collective-permute-done.6.far, bf16[288,128]{1,0:T(8,128)(2,1)S(1)} %collective-permute-done.7.near, f32[30,144,128]{2,1,0:T(8,128)S(1)} %copy-done.1, ...), custom_call_target="tpu_custom_call" | custom-call | tf_op jit(solution)/shard_map/pallas_call | solution.py:447
  (13 shorter events, 0.1 us)
Async XLA Ops:
  27.2 3.9 %copy-start.2 = (f32[4,128,128]{2,1,0:T(8,128)S(1)}, f32[4,128,128]{2,1,0:T(8,128)}, u32[]{:S(2)}) copy-start(f32[4,128,128]{2,1,0:T(8,128)} %temp.3) | copy-start | bytes 786436
  27.3 3.9 %copy-start.4 = (f32[4,128,128]{2,1,0:T(8,128)S(1)}, f32[4,128,128]{2,1,0:T(8,128)}, u32[]{:S(2)}) copy-start(f32[4,128,128]{2,1,0:T(8,128)} %cond.1) | copy-start | bytes 786436
  27.3 3.9 %copy-start.5 = (f32[4,128,128]{2,1,0:T(8,128)S(1)}, f32[4,128,128]{2,1,0:T(8,128)}, u32[]{:S(2)}) copy-start(f32[4,128,128]{2,1,0:T(8,128)} %mass.1) | copy-start | bytes 786436
  27.3 37.5 %all-to-all-start.1 = ((bf16[16,16,4736]{2,1,0:T(8,128)(2,1)}), bf16[16,16,4736]{2,1,0:T(8,128)(2,1)S(1)}, u32[]{:S(2)}, u32[]{:S(2)}) async-start(bf16[16,16,4736]{2,1,0:T(8,128)(2,1)} %bitcast.15), calls=%async_computation.1 | async-start | bytes 4849664 | tf_op jit(solution)/shard_map/all_to_all | solution.py:540
  31.2 29.7 %copy-start.3 = (f32[64,1,128]{2,1,0:T(1,128)S(1)}, f32[64,1,128]{2,1,0:T(1,128)}, u32[]{:S(2)}) copy-start(f32[64,1,128]{2,1,0:T(1,128)} %all_to_all.15) | copy-start | bytes 98308
  31.4 22.9 %collective-permute-start = (bf16[8,128,128]{2,1,0:T(8,128)(2,1)S(1)}, bf16[8,128,128]{2,1,0:T(8,128)(2,1)S(1)}, u32[]{:S(2)}, u32[]{:S(2)}) collective-permute-start(bf16[8,128,128]{2,1,0:T(8,128)(2,1)S(1)} %get-tuple-element.27), channel_id=1, source_target_pairs={{1,2},{3,4},{5,6},{2,1},{4,3},{6,5},{9,10},{11,12},{13,14},{10,9},... | collective-permute-start | bytes 786440 | tf_op jit(solution)/shard_map/ppermute | solution.py:479
  42.0 12.2 %collective-permute-start.1 = (bf16[8,128,128]{2,1,0:T(8,128)(2,1)S(1)}, bf16[8,128,128]{2,1,0:T(8,128)(2,1)S(1)}, u32[]{:S(2)}, u32[]{:S(2)}) collective-permute-start(bf16[8,128,128]{2,1,0:T(8,128)(2,1)S(1)} %get-tuple-element.28), channel_id=1, source_target_pairs={{0,1},{1,0},{2,3},{3,2},{4,5},{5,4},{6,7},{7,6},{8,9},{9,8},{10,11... | collective-permute-start | bytes 786440 | tf_op jit(solution)/shard_map/ppermute | solution.py:480
  54.3 7.3 %collective-permute-start.2 = (bf16[240,128]{1,0:T(8,128)(2,1)S(1)}, bf16[240,128]{1,0:T(8,128)(2,1)S(1)}, u32[]{:S(2)}, u32[]{:S(2)}) collective-permute-start(bf16[240,128]{1,0:T(8,128)(2,1)S(1)} %get-tuple-element.29), channel_id=1, source_target_pairs={{128,256},{256,128},{129,257},{257,129},{130,258},{258,130},{131,2... | collective-permute-start | bytes 184328 | tf_op jit(solution)/shard_map/ppermute | solution.py:462
  54.9 7.8 %collective-permute-start.3 = (bf16[240,128]{1,0:T(8,128)(2,1)S(1)}, bf16[240,128]{1,0:T(8,128)(2,1)S(1)}, u32[]{:S(2)}, u32[]{:S(2)}) collective-permute-start(bf16[240,128]{1,0:T(8,128)(2,1)S(1)} %get-tuple-element.30), channel_id=1, source_target_pairs={{0,128},{256,384},{128,0},{384,256},{1,129},{257,385},{129,1},{385... | collective-permute-start | bytes 184328 | tf_op jit(solution)/shard_map/ppermute | solution.py:462
  63.4 1.4 %copy-start = (f32[30,144,128]{2,1,0:T(8,128)}, f32[30,144,128]{2,1,0:T(8,128)S(1)}, u32[]{:S(2)}) copy-start(f32[30,144,128]{2,1,0:T(8,128)S(1)} %get-tuple-element.37.grids) | copy-start | bytes 6635524
  66.2 30.6 %copy-start.1 = (f32[30,144,128]{2,1,0:T(8,128)S(1)}, f32[30,144,128]{2,1,0:T(8,128)}, u32[]{:S(2)}) copy-start(f32[30,144,128]{2,1,0:T(8,128)} %copy-done) | copy-start | bytes 6635524
  66.2 18.6 %all-to-all-start.2 = ((f16[4,16,4480]{2,1,0:T(8,128)(2,1)}), f16[4,16,4480]{2,1,0:T(8,128)(2,1)S(1)}, u32[]{:S(2)}, u32[]{:S(2)}) async-start(f16[4,16,4480]{2,1,0:T(8,128)(2,1)} %bitcast.16), calls=%async_computation.2 | async-start | bytes 1146880 | tf_op jit(solution)/shard_map/all_to_all | solution.py:546
  69.8 15.1 %collective-permute-start.4 = (bf16[144,128]{1,0:T(8,128)(2,1)S(1)}, bf16[144,128]{1,0:T(8,128)(2,1)S(1)}, u32[]{:S(2)}, u32[]{:S(2)}) collective-permute-start(bf16[144,128]{1,0:T(8,128)(2,1)S(1)} %get-tuple-element.31._outer), channel_id=1, source_target_pairs={{8,16},{24,32},{40,48},{56,64},{72,80},{88,96},{104,112},{16,8},{3... | collective-permute-start | bytes 110600 | tf_op jit(solution)/shard_map/ppermute | solution.py:462
  70.5 14.4 %collective-permute-start.5 = (bf16[144,128]{1,0:T(8,128)(2,1)S(1)}, bf16[144,128]{1,0:T(8,128)(2,1)S(1)}, u32[]{:S(2)}, u32[]{:S(2)}) collective-permute-start(bf16[144,128]{1,0:T(8,128)(2,1)S(1)} %get-tuple-element.32._inner), channel_id=1, source_target_pairs={{0,8},{16,24},{32,40},{48,56},{64,72},{80,88},{96,104},{112,120},{... | collective-permute-start | bytes 110600 | tf_op jit(solution)/shard_map/ppermute | solution.py:462
  86.3 13.2 %collective-permute-start.6 = (bf16[288,128]{1,0:T(8,128)(2,1)S(1)}, bf16[288,128]{1,0:T(8,128)(2,1)S(1)}, u32[]{:S(2)}, u32[]{:S(2)}) collective-permute-start(bf16[288,128]{1,0:T(8,128)(2,1)S(1)} %get-tuple-element.35), channel_id=1, source_target_pairs={{1,2},{3,4},{5,6},{2,1},{4,3},{6,5},{9,10},{11,12},{13,14},{10,9},... | collective-permute-start | bytes 221192 | tf_op jit(solution)/shard_map/ppermute | solution.py:479
  94.9 4.6 %collective-permute-start.7 = (bf16[288,128]{1,0:T(8,128)(2,1)S(1)}, bf16[288,128]{1,0:T(8,128)(2,1)S(1)}, u32[]{:S(2)}, u32[]{:S(2)}) collective-permute-start(bf16[288,128]{1,0:T(8,128)(2,1)S(1)} %get-tuple-element.36), channel_id=1, source_target_pairs={{0,1},{1,0},{2,3},{3,2},{4,5},{5,4},{6,7},{7,6},{8,9},{9,8},{10,11... | collective-permute-start | bytes 221192 | tf_op jit(solution)/shard_map/ppermute | solution.py:480

commit v13 on v12

--- a/solution.py
+++ b/solution.py
@@ -153,7 +153,7 @@
         copy.wait()
 
 
-def selector_kernel(messages, out):
+def selector_kernel(messages, _outer, _inner, out):
     x, y = lax.axis_index("row"), lax.axis_index("y")
     plane = lax.axis_index("zlo")
     code = jnp.concatenate([messages[pl.ds(r * 16 + plane * 4, 4), :] for r in range(4)], axis=0)
@@ -189,7 +189,7 @@
         put(5 + k, ids, z * 16 + layer)
 
 
-def combine_kernel(selector, received, _outer, _inner, out):
+def combine_kernel(selector, received, out):
     def add(k, start, width):
         return jnp.dot(
             selector[k * 64 : (k + 1) * 64, :],
@@ -495,7 +495,7 @@
     wide, *edges = call(
         gather_kernel, (sds((30, 144, 128), F32), edge, edge), (own, far, near, *beside), mib=24
     )
-    return wide, edges, swap_sides(*edges, COL)
+    return wide, beside, swap_sides(*edges, COL)
 
 
 def operator(wide, outer, inner):
@@ -538,10 +538,10 @@
         far_out=True,
     )
     received = lax.all_to_all(send.reshape(16, 16, 4736), PLANE, split_axis=0, concat_axis=0, tiled=True)
-    selector = call(selector_kernel, sds((576, 256), BF16), (messages,))
-    wide, edges, beside = extended_grids(temp, cond, mass)
+    wide, rows, beside = extended_grids(temp, cond, mass)
+    selector = call(selector_kernel, sds((576, 256), BF16), (messages, *rows))
     partial = call(
-        combine_kernel, sds((64, 4480), F32), (selector, received.reshape(256, 4736), *edges)
+        combine_kernel, sds((64, 4480), F32), (selector, received.reshape(256, 4736))
     )
     parts = lax.all_to_all(
         partial.astype(jnp.float16).reshape(4, 16, 4480), "zlo", split_axis=0, concat_axis=0, tiled=True

time: 102 us -> 105 us (1.029)
  local copies, waits for them, and re-layouts: 1.39 us -> 4.09 us
  other arithmetic: 0.96 us -> 2.05 us
    unnamed x12 -> x24, local copies, waits for them, and re-layouts: 1.39 us -> 4.09 us
    all_to_all x1, waiting for transfers between devices: 9.1 us -> 7.86 us  [shards(): lax.all_to_all(partial.astype(jnp.float16).reshape(4, 16, 4480), 'zlo', s...]
    reduce_sum x1, other arithmetic: 0.08 us -> 1.16 us  [shards(): jnp.sum(parts.astype(F32), axis=0)]
  transfers between devices with their start and end apart: 10 -> 10, of which waited for: 3 -> 3; matrix products, arithmetic and copies ran while one was open for 0% -> 1% of each run, Pallas kernels for 4% -> 4%
where the time goes in v13:
time: 105 us; the launch traced here: 104 us
  starting transfers between devices  42.9 us (41%)
  blocking collectives  21.5 us (20%)
  waiting for transfers between devices  20 us (19%)
  Pallas kernels  13 us (12%)
  local copies, waits for them, and re-layouts  4.09 us (4%)
  other arithmetic  2.05 us (2%)
    all_to_all x1, blocking collectives, shards(): lax.all_to_all(message.reshape(64, 1, 128), CUBE, split_axis=0, concat_ax...  21.5 us
    ppermute x2, starting transfers between devices, swap_layers(): lax.ppermute(far, LAYER, apart + [(b, a) for a, b in apart])  18.5 us
    pallas_call x10, Pallas kernels, call(): pl.pallas_call(kernel, out_shape=shape, in_specs=[anywhere if i in far el...  13 us
    ppermute x4, starting transfers between devices, swapped(): return lax.ppermute(data, axis, apart + [(b, a) for a, b in apart])  12.5 us
    ppermute x2, waiting for transfers between devices, swap_layers(): lax.ppermute(far, LAYER, apart + [(b, a) for a, b in apart])  10.6 us
    all_to_all x1, waiting for transfers between devices, shards(): lax.all_to_all(partial.astype(jnp.float16).reshape(4, 16, 4480), 'zlo', s...  7.86 us
    all_to_all x1, starting transfers between devices, shards(): lax.all_to_all(partial.astype(jnp.float16).reshape(4, 16, 4480), 'zlo', s...  4.16 us
    unnamed x24, local copies, waits for them, and re-layouts  4.09 us
  transfers between devices with their start and end apart: 10, of which 3 were waited for; matrix products, arithmetic and copies ran while one was open for 1% of the time, Pallas kernels for 4%

profile of v13, /device:TPU:1, one launch (start us, length us, event | category | flops | bytes accessed | tf_op | source)
XLA Modules:
  0.0 104.4 jit_solution(13600750123263324515)
XLA Ops:
  0.6 1.8 %shard_map.113 = (f32[64,128]{1,0:T(8,128)}, bf16[1024,64]{1,0:T(8,128)(2,1)}, s32[64,128]{1,0:T(8,128)}) custom-call(f32[4,128,128]{2,1,0:T(8,128)} %temp.3, s32[1,64]{1,0:T(1,128)} %bitcast.20, s32[1,64]{1,0:T(1,128)} %place.1, s32[1,64]{1,0:T(1,128)} %holder.1, s32[1,16]{1,0:T(1,128)} %tier.1), custom_call_target="tpu_custom_call" | custom-call | tf_op jit(solution)/shard_map/pallas_call | solution.py:447
  2.4 21.5 %all_to_all.15 = f32[64,1,128]{2,1,0:T(1,128)} all-to-all(f32[64,1,128]{2,1,0:T(1,128)} %bitcast.19), channel_id=1, replica_groups=mesh['row'=4,'zlo'=4,'y'=4,'zhi'=4,'core'=2] {'row','zlo','y'}, dimensions={0} | all-to-all | bytes 65536 | tf_op jit(solution)/shard_map/all_to_all | solution.py:525
  23.9 3.2 %shard_map.117 = bf16[256,4736]{1,0:T(8,128)(2,1)} custom-call(f32[64,128]{1,0:T(8,128)} %bitcast.13, s32[64,128]{1,0:T(8,128)} %get-tuple-element.29.far_columns, f32[1,16]{1,0:T(1,128)} %far_warming.1, bf16[64,4096]{1,0:T(8,128)(2,1)} %bitcast.16, bf16[64,4096]{1,0:T(8,128)(2,1)} %bitcast.17, bf16[1024,64]{1,0:T(8,128)(2,1)} %get-tuple-element.30.far_placing), custom_call_target="tpu_custom_call" | custom-call | tf_op jit(solution)/shard_map/pallas_call | solution.py:447
  27.1 0.0 copy-start
  27.1 3.9 %all-to-all-start.1 = ((bf16[16,16,4736]{2,1,0:T(8,128)(2,1)}), bf16[16,16,4736]{2,1,0:T(8,128)(2,1)S(1)}, u32[]{:S(2)}, u32[]{:S(2)}) async-start(bf16[16,16,4736]{2,1,0:T(8,128)(2,1)} %bitcast.15), calls=%async_computation.1 | async-start | bytes 4849664 | tf_op jit(solution)/shard_map/all_to_all | solution.py:540
  31.0 0.9 copy-done.6
  32.0 0.9 copy-done.7
  32.9 0.1 shard_map.114
  33.1 11.0 %collective-permute-start = (bf16[8,128,128]{2,1,0:T(8,128)(2,1)S(1)}, bf16[8,128,128]{2,1,0:T(8,128)(2,1)S(1)}, u32[]{:S(2)}, u32[]{:S(2)}) collective-permute-start(bf16[8,128,128]{2,1,0:T(8,128)(2,1)S(1)} %get-tuple-element.25), channel_id=1, source_target_pairs={{1,2},{3,4},{5,6},{2,1},{4,3},{6,5},{9,10},{11,12},{13,14},{10,9},... | collective-permute-start | bytes 786440 | tf_op jit(solution)/shard_map/ppermute | solution.py:479
  44.1 1.9 %collective-permute-start.1 = (bf16[8,128,128]{2,1,0:T(8,128)(2,1)S(1)}, bf16[8,128,128]{2,1,0:T(8,128)(2,1)S(1)}, u32[]{:S(2)}, u32[]{:S(2)}) collective-permute-start(bf16[8,128,128]{2,1,0:T(8,128)(2,1)S(1)} %get-tuple-element.26), channel_id=1, source_target_pairs={{0,1},{1,0},{2,3},{3,2},{4,5},{5,4},{6,7},{7,6},{8,9},{9,8},{10,11... | collective-permute-start | bytes 786440 | tf_op jit(solution)/shard_map/ppermute | solution.py:480
  46.0 10.6 %collective-permute-done.far = bf16[8,128,128]{2,1,0:T(8,128)(2,1)S(1)} collective-permute-done((bf16[8,128,128]{2,1,0:T(8,128)(2,1)S(1)}, bf16[8,128,128]{2,1,0:T(8,128)(2,1)S(1)}, u32[]{:S(2)}, u32[]{:S(2)}) %collective-permute-start) | collective-permute-done | bytes 262176 | tf_op jit(solution)/shard_map/ppermute | solution.py:479
  56.6 0.7 collective-permute-start.2
  57.3 5.6 %collective-permute-start.3 = (bf16[240,128]{1,0:T(8,128)(2,1)S(1)}, bf16[240,128]{1,0:T(8,128)(2,1)S(1)}, u32[]{:S(2)}, u32[]{:S(2)}) collective-permute-start(bf16[240,128]{1,0:T(8,128)(2,1)S(1)} %get-tuple-element.28), channel_id=1, source_target_pairs={{0,128},{256,384},{128,0},{384,256},{1,129},{257,385},{129,1},{385... | collective-permute-start | bytes 184328 | tf_op jit(solution)/shard_map/ppermute | solution.py:462
  62.9 1.6 %collective-permute-done.3._inner.inner = bf16[240,128]{1,0:T(8,128)(2,1)S(1)} collective-permute-done((bf16[240,128]{1,0:T(8,128)(2,1)S(1)}, bf16[240,128]{1,0:T(8,128)(2,1)S(1)}, u32[]{:S(2)}, u32[]{:S(2)}) %collective-permute-start.3) | collective-permute-done | bytes 61472 | tf_op jit(solution)/shard_map/ppermute | solution.py:462
  64.5 0.7 shard_map.116.selector
  65.2 0.6 copy-done.8
  65.8 0.6 copy-done.10
  66.4 0.6 shard_map.118
  67.1 0.9 convert_element_type.6
  67.9 4.2 %all-to-all-start.2 = ((f16[4,16,4480]{2,1,0:T(8,128)(2,1)}), f16[4,16,4480]{2,1,0:T(8,128)(2,1)}, u32[]{:S(2)}, u32[]{:S(2)}) async-start(f16[4,16,4480]{2,1,0:T(8,128)(2,1)} %bitcast.8), calls=%async_computation.2 | async-start | bytes 1146880 | tf_op jit(solution)/shard_map/all_to_all | solution.py:546
  72.1 0.0 copy-start.4
  72.2 0.9 copy-done.4
  73.1 0.6 shard_map.119
  73.7 0.7 collective-permute-start.4
  74.4 5.5 %collective-permute-start.5 = (bf16[144,128]{1,0:T(8,128)(2,1)S(1)}, bf16[144,128]{1,0:T(8,128)(2,1)S(1)}, u32[]{:S(2)}, u32[]{:S(2)}) collective-permute-start(bf16[144,128]{1,0:T(8,128)(2,1)S(1)} %get-tuple-element.32), channel_id=1, source_target_pairs={{0,8},{16,24},{32,40},{48,56},{64,72},{80,88},{96,104},{112,120},{... | collective-permute-start | bytes 110600 | tf_op jit(solution)/shard_map/ppermute | solution.py:462
  79.9 7.9 %all-to-all-done.2 = f16[4,16,4480]{2,1,0:T(8,128)(2,1)} async-done(((f16[4,16,4480]{2,1,0:T(8,128)(2,1)}), f16[4,16,4480]{2,1,0:T(8,128)(2,1)}, u32[]{:S(2)}, u32[]{:S(2)}) %all-to-all-start.2) | async-done | bytes 573472 | tf_op jit(solution)/shard_map/all_to_all | solution.py:546
  87.8 1.2 %convert_reduce_fusion.whole = f32[16,4480]{1,0:T(8,128)S(1)} fusion(f16[4,16,4480]{2,1,0:T(8,128)(2,1)} %all-to-all-done.2), kind=kLoop, calls=%fused_computation | loop fusion | flops 501760 | bytes 860160 | tf_op jit(solution)/shard_map/reduce_sum | solution.py:554
  89.0 1.3 %shard_map.120 = (f32[512,128]{1,0:T(8,128)}, f32[576,128]{1,0:T(8,128)S(1)}, f32[576,128]{1,0:T(8,128)S(1)}, bf16[288,128]{1,0:T(8,128)(2,1)S(1)}, bf16[288,128]{1,0:T(8,128)(2,1)S(1)}) custom-call(f32[16,4480]{1,0:T(8,128)S(1)} %convert_reduce_fusion.whole, bf16[144,128]{1,0:T(8,128)(2,1)S(1)} %collective-permute-done.4._outer.outer, ...), custom_call_target="tpu_custom_call" | custom-call | tf_op jit(solution)/shard_map/pallas_call | solution.py:447
  90.3 7.6 %collective-permute-start.6 = (bf16[288,128]{1,0:T(8,128)(2,1)S(1)}, bf16[288,128]{1,0:T(8,128)(2,1)S(1)}, u32[]{:S(2)}, u32[]{:S(2)}) collective-permute-start(bf16[288,128]{1,0:T(8,128)(2,1)S(1)} %get-tuple-element.35), channel_id=1, source_target_pairs={{1,2},{3,4},{5,6},{2,1},{4,3},{6,5},{9,10},{11,12},{13,14},{10,9},... | collective-permute-start | bytes 221192 | tf_op jit(solution)/shard_map/ppermute | solution.py:479
  97.9 1.9 %collective-permute-start.7 = (bf16[288,128]{1,0:T(8,128)(2,1)S(1)}, bf16[288,128]{1,0:T(8,128)(2,1)S(1)}, u32[]{:S(2)}, u32[]{:S(2)}) collective-permute-start(bf16[288,128]{1,0:T(8,128)(2,1)S(1)} %get-tuple-element.36), channel_id=1, source_target_pairs={{0,1},{1,0},{2,3},{3,2},{4,5},{5,4},{6,7},{7,6},{8,9},{9,8},{10,11... | collective-permute-start | bytes 221192 | tf_op jit(solution)/shard_map/ppermute | solution.py:480
  99.8 2.6 %shard_map.121 = (f32[9,144,256]{2,1,0:T(8,128)S(1)}, f32[8,144,256]{2,1,0:T(8,128)S(1)}, f32[8,144,256]{2,1,0:T(8,128)S(1)}, f32[8,144,256]{2,1,0:T(8,128)S(1)}, f32[8,144,256]{2,1,0:T(8,128)S(1)}) custom-call(f32[30,144,128]{2,1,0:T(8,128)S(1)} %get-tuple-element.37.grids, bf16[144,128]{1,0:T(8,128)(2,1)S(1)} %collective-permute-done.4._outer.outer, ...), custom_call_target="tpu_custom_call" | custom-call | tf_op jit(solution)/shard_map/pallas_call | solution.py:447
  102.5 1.9 %shard_map.122 = f32[512,128]{1,0:T(8,128)} custom-call(f32[576,128]{1,0:T(8,128)S(1)} %get-tuple-element.33.main, f32[576,128]{1,0:T(8,128)S(1)} %get-tuple-element.34.side, bf16[288,128]{1,0:T(8,128)(2,1)S(1)} %collective-permute-done.6.far, bf16[288,128]{1,0:T(8,128)(2,1)S(1)} %collective-permute-done.7.near, ...), custom_call_target="tpu_custom_call" | custom-call | tf_op jit(solution)/shard_map/pallas_call | solution.py:447
  (25 shorter events, 0.1 us)
Async XLA Ops:
  27.1 3.9 %copy-start = (f32[4,128,128]{2,1,0:T(8,128)S(1)}, f32[4,128,128]{2,1,0:T(8,128)}, u32[]{:S(2)}) copy-start(f32[4,128,128]{2,1,0:T(8,128)} %temp.3) | copy-start | bytes 786436
  27.1 39.3 %all-to-all-start.1 = ((bf16[16,16,4736]{2,1,0:T(8,128)(2,1)}), bf16[16,16,4736]{2,1,0:T(8,128)(2,1)S(1)}, u32[]{:S(2)}, u32[]{:S(2)}) async-start(bf16[16,16,4736]{2,1,0:T(8,128)(2,1)} %bitcast.15), calls=%async_computation.1 | async-start | bytes 4849664 | tf_op jit(solution)/shard_map/all_to_all | solution.py:540
  31.0 1.0 copy-start.6
  32.0 0.9 copy-start.7
  32.9 31.5 %copy-start.5 = (f32[64,1,128]{2,1,0:T(1,128)S(1)}, f32[64,1,128]{2,1,0:T(1,128)}, u32[]{:S(2)}) copy-start(f32[64,1,128]{2,1,0:T(1,128)} %all_to_all.15) | copy-start | bytes 98308
  33.1 23.5 %collective-permute-start = (bf16[8,128,128]{2,1,0:T(8,128)(2,1)S(1)}, bf16[8,128,128]{2,1,0:T(8,128)(2,1)S(1)}, u32[]{:S(2)}, u32[]{:S(2)}) collective-permute-start(bf16[8,128,128]{2,1,0:T(8,128)(2,1)S(1)} %get-tuple-element.25), channel_id=1, source_target_pairs={{1,2},{3,4},{5,6},{2,1},{4,3},{6,5},{9,10},{11,12},{13,14},{10,9},... | collective-permute-start | bytes 786440 | tf_op jit(solution)/shard_map/ppermute | solution.py:479
  44.1 12.5 %collective-permute-start.1 = (bf16[8,128,128]{2,1,0:T(8,128)(2,1)S(1)}, bf16[8,128,128]{2,1,0:T(8,128)(2,1)S(1)}, u32[]{:S(2)}, u32[]{:S(2)}) collective-permute-start(bf16[8,128,128]{2,1,0:T(8,128)(2,1)S(1)} %get-tuple-element.26), channel_id=1, source_target_pairs={{0,1},{1,0},{2,3},{3,2},{4,5},{5,4},{6,7},{7,6},{8,9},{9,8},{10,11... | collective-permute-start | bytes 786440 | tf_op jit(solution)/shard_map/ppermute | solution.py:480
  56.5 6.3 %copy-start.1 = (bf16[8,128,128]{2,1,0:T(8,128)(2,1)}, bf16[8,128,128]{2,1,0:T(8,128)(2,1)S(1)}, u32[]{:S(2)}) copy-start(bf16[8,128,128]{2,1,0:T(8,128)(2,1)S(1)} %collective-permute-done.far) | copy-start | bytes 786436
  56.5 7.9 %copy-start.3 = (bf16[8,128,128]{2,1,0:T(8,128)(2,1)}, bf16[8,128,128]{2,1,0:T(8,128)(2,1)S(1)}, u32[]{:S(2)}) copy-start(bf16[8,128,128]{2,1,0:T(8,128)(2,1)S(1)} %collective-permute-done.1.near) | copy-start | bytes 786436
  56.6 6.3 %collective-permute-start.2 = (bf16[240,128]{1,0:T(8,128)(2,1)S(1)}, bf16[240,128]{1,0:T(8,128)(2,1)S(1)}, u32[]{:S(2)}, u32[]{:S(2)}) collective-permute-start(bf16[240,128]{1,0:T(8,128)(2,1)S(1)} %get-tuple-element.27), channel_id=1, source_target_pairs={{128,256},{256,128},{129,257},{257,129},{130,258},{258,130},{131,2... | collective-permute-start | bytes 184328 | tf_op jit(solution)/shard_map/ppermute | solution.py:462
  57.3 7.2 %collective-permute-start.3 = (bf16[240,128]{1,0:T(8,128)(2,1)S(1)}, bf16[240,128]{1,0:T(8,128)(2,1)S(1)}, u32[]{:S(2)}, u32[]{:S(2)}) collective-permute-start(bf16[240,128]{1,0:T(8,128)(2,1)S(1)} %get-tuple-element.28), channel_id=1, source_target_pairs={{0,128},{256,384},{128,0},{384,256},{1,129},{257,385},{129,1},{385... | collective-permute-start | bytes 184328 | tf_op jit(solution)/shard_map/ppermute | solution.py:462
  65.2 0.6 copy-start.8
  65.8 0.6 copy-start.10
  67.0 5.1 %copy-start.2 = (bf16[8,128,128]{2,1,0:T(8,128)(2,1)S(1)}, bf16[8,128,128]{2,1,0:T(8,128)(2,1)}, u32[]{:S(2)}) copy-start(bf16[8,128,128]{2,1,0:T(8,128)(2,1)} %copy-done.1) | copy-start | bytes 786436
  67.0 5.1 %copy-start.9 = (bf16[240,128]{1,0:T(8,128)(2,1)S(1)}, bf16[240,128]{1,0:T(8,128)(2,1)}, u32[]{:S(2)}) copy-start(bf16[240,128]{1,0:T(8,128)(2,1)} %copy-done.8) | copy-start | bytes 184324
  67.0 5.1 %copy-start.11 = (bf16[240,128]{1,0:T(8,128)(2,1)S(1)}, bf16[240,128]{1,0:T(8,128)(2,1)}, u32[]{:S(2)}) copy-start(bf16[240,128]{1,0:T(8,128)(2,1)} %copy-done.10) | copy-start | bytes 184324
  67.9 19.9 %all-to-all-start.2 = ((f16[4,16,4480]{2,1,0:T(8,128)(2,1)}), f16[4,16,4480]{2,1,0:T(8,128)(2,1)}, u32[]{:S(2)}, u32[]{:S(2)}) async-start(f16[4,16,4480]{2,1,0:T(8,128)(2,1)} %bitcast.8), calls=%async_computation.2 | async-start | bytes 1146880 | tf_op jit(solution)/shard_map/all_to_all | solution.py:546
  72.1 1.0 copy-start.4
  73.7 15.2 %collective-permute-start.4 = (bf16[144,128]{1,0:T(8,128)(2,1)S(1)}, bf16[144,128]{1,0:T(8,128)(2,1)S(1)}, u32[]{:S(2)}, u32[]{:S(2)}) collective-permute-start(bf16[144,128]{1,0:T(8,128)(2,1)S(1)} %get-tuple-element.31), channel_id=1, source_target_pairs={{8,16},{24,32},{40,48},{56,64},{72,80},{88,96},{104,112},{16,8},{3... | collective-permute-start | bytes 110600 | tf_op jit(solution)/shard_map/ppermute | solution.py:462
  74.4 14.6 %collective-permute-start.5 = (bf16[144,128]{1,0:T(8,128)(2,1)S(1)}, bf16[144,128]{1,0:T(8,128)(2,1)S(1)}, u32[]{:S(2)}, u32[]{:S(2)}) collective-permute-start(bf16[144,128]{1,0:T(8,128)(2,1)S(1)} %get-tuple-element.32), channel_id=1, source_target_pairs={{0,8},{16,24},{32,40},{48,56},{64,72},{80,88},{96,104},{112,120},{... | collective-permute-start | bytes 110600 | tf_op jit(solution)/shard_map/ppermute | solution.py:462
  90.3 12.1 %collective-permute-start.6 = (bf16[288,128]{1,0:T(8,128)(2,1)S(1)}, bf16[288,128]{1,0:T(8,128)(2,1)S(1)}, u32[]{:S(2)}, u32[]{:S(2)}) collective-permute-start(bf16[288,128]{1,0:T(8,128)(2,1)S(1)} %get-tuple-element.35), channel_id=1, source_target_pairs={{1,2},{3,4},{5,6},{2,1},{4,3},{6,5},{9,10},{11,12},{13,14},{10,9},... | collective-permute-start | bytes 221192 | tf_op jit(solution)/shard_map/ppermute | solution.py:479
  97.9 4.6 %collective-permute-start.7 = (bf16[288,128]{1,0:T(8,128)(2,1)S(1)}, bf16[288,128]{1,0:T(8,128)(2,1)S(1)}, u32[]{:S(2)}, u32[]{:S(2)}) collective-permute-start(bf16[288,128]{1,0:T(8,128)(2,1)S(1)} %get-tuple-element.36), channel_id=1, source_target_pairs={{0,1},{1,0},{2,3},{3,2},{4,5},{5,4},{6,7},{7,6},{8,9},{9,8},{10,11... | collective-permute-start | bytes 221192 | tf_op jit(solution)/shard_map/ppermute | solution.py:480
